TPU v7x, 1024 devices: a whole 8x8x8 slice. The times are simulated.
1024 devices in a mesh: dp: 128 (over x, z_hi, y), mp: 8 (over z_lo, core).
Axes of the slice: x: 8, y: 8, z: 8 (z_hi: 2, z_lo: 4; z = z_hi * 4 + z_lo), core: 2. Of those that a mesh axis runs over, the one named last changes fastest.
Arguments:
- picture_tower_activations: bfloat16 [131072, 1152], P(('dp', 'mp')), may hold values from -6 to 6
- caption_tower_activations: bfloat16 [131072, 1152], P(('dp', 'mp')), may hold values from -6 to 6
- picture_mapping_kernel: bfloat16 [1152, 1152], replicated, may hold values from -0.1875 to 0.1875
- caption_mapping_kernel: bfloat16 [1152, 1152], replicated, may hold values from -0.1875 to 0.1875
- sigmoid_sharpness: float32 [1], replicated, may hold values from 5 to 20
- sigmoid_shift_term: float32 [1], replicated, may hold values from -4 to -1
Outputs:
- image_head_grad: float32 [128, 1152, 1152], P('dp', 'mp')
- text_head_grad: float32 [128, 1152, 1152], P('dp', 'mp')
All inputs are finite; a program needn't handle non-finite values.
Results may differ from a plain program's by a relative error of at most 0.017.
Values may be sent and summed in bfloat16 or wider, within the bound.
No kernel may reach another device: no remote copies, remote signals or barrier semaphores. Data moves between devices by JAX's collectives and lax.ppermute only.
A program may use at most 64 MiB of HBM per device.

v0:
```python
import jax
import jax.numpy as jnp
from jax import lax
from jax.sharding import PartitionSpec as P

SHIFTS = 3


epsilon = 1e-06


def passed_along(value, axis, steps):
    count = lax.axis_size(axis)
    pairs = [(source, (source + steps) % count) for source in range(count)]
    return lax.ppermute(value, axis, pairs)


def project_rows(features, projection):
    x_values = jnp.dot(features, projection, preferred_element_type=jnp.float32)
    norm_rows = jnp.sqrt(jnp.sum(x_values * x_values, axis=-1, keepdims=True) + epsilon)
    return (x_values, norm_rows)


def rounded(values):
    return lax.optimization_barrier(values.astype(jnp.bfloat16)).astype(jnp.float32)


def paired_blocks(
    image_embedded, text_embedded, multiplier_coefficient, block_offset, positive_pairs
):
    logit_matrix = (
        multiplier_coefficient
        * jnp.dot(image_embedded, text_embedded.T, preferred_element_type=jnp.float32)
        + block_offset
    )
    prob_values = jax.nn.sigmoid(logit_matrix)
    if positive_pairs:
        prob_values = prob_values - jnp.eye(image_embedded.shape[0], dtype=jnp.float32)
    head_weights = (prob_values / image_embedded.shape[0]).astype(jnp.bfloat16)
    image_projection = multiplier_coefficient * jnp.dot(
        head_weights, text_embedded, preferred_element_type=jnp.float32
    )
    text_projection = multiplier_coefficient * jnp.dot(
        head_weights.T, image_embedded, preferred_element_type=jnp.float32
    )
    return (image_projection, text_projection)


def tangent(unit_rows, norm_rows, dz_rows):
    inner = jnp.sum(unit_rows * dz_rows, axis=-1, keepdims=True)
    return ((dz_rows - unit_rows * inner) / norm_rows).astype(jnp.bfloat16)


def on_device(
    picture_tower_activations,
    caption_tower_activations,
    picture_mapping_kernel,
    caption_mapping_kernel,
    sigmoid_sharpness,
    sigmoid_shift_term,
):
    multiplier_coefficient = sigmoid_sharpness[0]
    block_offset = sigmoid_shift_term[0]
    x_image, norm_image = project_rows(picture_tower_activations, picture_mapping_kernel)
    x_text, norm_text = project_rows(caption_tower_activations, caption_mapping_kernel)
    unit_image = x_image / norm_image
    unit_text = x_text / norm_text
    image_embedded = unit_image.astype(jnp.bfloat16)
    text_embedded = unit_text.astype(jnp.bfloat16)
    image_embedding_grad, text_embedding_grad = paired_blocks(
        image_embedded, text_embedded, multiplier_coefficient, block_offset, True
    )
    present_block = text_embedded
    for shift_step in range(1, SHIFTS + 1):
        outgoing = present_block
        present_block = passed_along(outgoing, "dp", 1)
        image_projection, text_projection = paired_blocks(
            image_embedded, present_block, multiplier_coefficient, block_offset, False
        )
        image_embedding_grad = image_embedding_grad + rounded(image_projection)
        returned = passed_along(text_projection.astype(jnp.bfloat16), "dp", -shift_step)
        text_embedding_grad = text_embedding_grad + returned.astype(jnp.float32)
    dx_image = tangent(unit_image, norm_image, image_embedding_grad)
    dx_text = tangent(unit_text, norm_text, text_embedding_grad)
    columns = picture_tower_activations
    image_grad = lax.psum_scatter(
        jnp.dot(columns.T, dx_image, preferred_element_type=jnp.float32).astype(jnp.bfloat16),
        "mp",
        scatter_dimension=0,
        tiled=True,
    ).astype(jnp.float32)
    columns = caption_tower_activations
    text_grad = lax.psum_scatter(
        jnp.dot(columns.T, dx_text, preferred_element_type=jnp.float32).astype(jnp.bfloat16),
        "mp",
        scatter_dimension=0,
        tiled=True,
    ).astype(jnp.float32)
    return (image_grad[None], text_grad[None])


def solution(mesh):
    return jax.shard_map(
        on_device,
        mesh=mesh,
        in_specs=(P(("dp", "mp"), None), P(("dp", "mp"), None), P(), P(), P(), P()),
        out_specs=(P("dp", "mp", None), P("dp", "mp", None)),
        check_vma=False,
    )
```

profile of v0, /device:TPU:1, one launch (start us, length us, event | category | flops | bytes accessed | tf_op | source)
XLA Modules:
  0.0 215.5 jit_solution(10423672465628570889)
XLA Ops:
  7.2 0.0 copy-start
  7.2 0.0 copy-start.2
  7.2 0.0 reduce-scatter.7.cloned.1.call-start
  7.2 1.7 copy-done
  8.9 0.0 copy-start.1
  8.9 1.8 multiply_reduce_fusion.2
  10.7 0.1 fusion.42
  10.9 4.2 %collective-permute-start = (bf16[128,1152]{1,0:T(8,128)(2,1)S(1)}, bf16[128,1152]{1,0:T(8,128)(2,1)S(1)}, u32[]{:S(2)}, u32[]{:S(2)}) collective-permute-start(bf16[128,1152]{1,0:T(8,128)(2,1)S(1)} %fusion.42), channel_id=1, source_target_pairs={{0,8},{8,16},{16,24},{24,32},{32,40},{40,48},{48,56},{56,64},{64,7... | collective-permute-start | bytes 884744 | tf_op jit(solution)/shard_map/ppermute | solution.py:15
  15.0 0.0 copy-done.2
  15.0 0.0 copy-done.1
  15.0 0.7 multiply_reduce_fusion.3
  15.7 0.1 fusion.41
  17.2 0.3 fusion.33
  17.4 0.0 copy-start.8
  17.5 20.1 %collective-permute-done = bf16[128,1152]{1,0:T(8,128)(2,1)S(1)} collective-permute-done((bf16[128,1152]{1,0:T(8,128)(2,1)S(1)}, bf16[128,1152]{1,0:T(8,128)(2,1)S(1)}, u32[]{:S(2)}, u32[]{:S(2)}) %collective-permute-start) | collective-permute-done | bytes 294944 | tf_op jit(solution)/shard_map/ppermute | solution.py:15
  37.5 1.9 collective-permute-start.1
  39.5 0.3 fusion.34
  39.7 0.0 copy-start.5
  39.7 0.2 fusion.2
  40.0 13.2 %collective-permute-done.1 = bf16[128,1152]{1,0:T(8,128)(2,1)S(1)} collective-permute-done((bf16[128,1152]{1,0:T(8,128)(2,1)S(1)}, bf16[128,1152]{1,0:T(8,128)(2,1)S(1)}, u32[]{:S(2)}, u32[]{:S(2)}) %collective-permute-start.1) | collective-permute-done | bytes 294944 | tf_op jit(solution)/shard_map/ppermute | solution.py:15
  53.1 1.9 collective-permute-start.2
  55.0 0.3 fusion.35
  55.3 0.0 copy-start.6
  55.3 0.0 copy-start.3
  55.3 0.2 fusion.3
  55.6 16.0 %collective-permute-done.2 = bf16[128,1152]{1,0:T(8,128)(2,1)S(1)} collective-permute-done((bf16[128,1152]{1,0:T(8,128)(2,1)S(1)}, bf16[128,1152]{1,0:T(8,128)(2,1)S(1)}, u32[]{:S(2)}, u32[]{:S(2)}) %collective-permute-start.2) | collective-permute-done | bytes 294944 | tf_op jit(solution)/shard_map/ppermute | solution.py:15
  71.6 0.3 fusion.36
  71.9 0.0 copy-done.6
  71.9 0.0 copy-start.7
  71.9 0.2 fusion.4
  72.1 0.4 multiply_reduce_fusion.1
  72.6 0.0 copy-done.8
  72.6 0.0 copy-done.5
  72.6 0.0 copy-done.7
  72.6 0.0 copy-done.3
  72.6 2.5 %fusion = bf16[1152,1152]{0,1:T(8,128)(2,1)} fusion(bf16[128,1152]{1,0:T(8,128)(2,1)S(1)} %copy-done.3, f32[128]{0:T(128)S(1)} %get-tuple-element.10, f32[128]{0:T(128)S(1)} %add_sqrt_fusion.1, bf16[128,1152]{1,0:T(8,128)(2,1)S(1)} %fusion.4, bf16[128,1152]{1,0:T(8,128)(2,1)S(1)} %fusion.3, f32[128,1152]{1,0:T(8,128)S(1)} %get-tuple-element.11, ...), kind=kOutput, calls=%fused_computation.2 | convolution fusion | flops 342687744 | bytes 5014528 | tf_op jit(solution)/shard_map/dot_general | solution.py:87
  75.1 5.2 %copy.12 = bf16[1152,1152]{1,0:T(8,128)(2,1)} copy(bf16[1152,1152]{0,1:T(8,128)(2,1)} %fusion) | data formatting | bytes 5308416
  80.4 0.0 reduce-scatter.7.cloned.1.call-update
  80.4 0.0 reduce-scatter.9.cloned.1.call-start
  80.4 0.0 copy-start.4
  80.4 1.1 fusion.5
  81.5 1.9 collective-permute-start.3
  83.4 1.0 fusion.6
  84.5 1.9 collective-permute-start.4
  86.4 1.0 fusion.7
  87.4 1.9 collective-permute-start.5
  89.4 0.0 collective-permute-done.3
  89.4 41.2 %collective-permute-done.4 = bf16[128,1152]{1,0:T(8,128)(2,1)S(1)} collective-permute-done((bf16[128,1152]{1,0:T(8,128)(2,1)S(1)}, bf16[128,1152]{1,0:T(8,128)(2,1)S(1)}, u32[]{:S(2)}, u32[]{:S(2)}) %collective-permute-start.4) | collective-permute-done | bytes 294944 | tf_op jit(solution)/shard_map/ppermute | solution.py:15
  130.6 0.0 collective-permute-done.5
  130.6 1.2 multiply_reduce_fusion
  131.9 0.0 copy-done.4
  131.9 2.5 %fusion.1 = bf16[1152,1152]{0,1:T(8,128)(2,1)} fusion(bf16[128,1152]{1,0:T(8,128)(2,1)S(1)} %copy-done.4, f32[128,1152]{1,0:T(8,128)S(1)} %get-tuple-element.13, f32[128]{0:T(128)S(1)} %get-tuple-element.12, f32[128]{0:T(128)S(1)} %add_sqrt_fusion, f32[128,1152]{1,0:T(8,128)S(1)} %get-tuple-element.9), kind=kOutput, calls=%fused_computation.3 | convolution fusion | flops 341803008 | bytes 4129792 | tf_op jit(solution)/shard_map/dot_general | solution.py:94
  134.4 5.2 %copy.14 = bf16[1152,1152]{1,0:T(8,128)(2,1)} copy(bf16[1152,1152]{0,1:T(8,128)(2,1)} %fusion.1) | data formatting | bytes 5308416
  139.6 0.0 reduce-scatter.9.cloned.1.call-update
  139.6 0.0 reduce-scatter.7.cloned.1.call-done
  139.6 1.2 copy.13
  140.9 1.1 bitcast_convert_fusion.1
  142.0 2.4 %copy.10 = f32[1,144,1152]{2,1,0:T(8,128)} copy(f32[1,144,1152]{1,2,0:T(8,128)} %bitcast_convert_fusion.1) | data formatting | bytes 1327104
  144.4 59.5 %reduce-scatter.9.cloned.1.call-done = bf16[144,1152]{1,0:T(8,128)(2,1)} async-done(((bf16[1152,1152]{1,0:T(8,128)(2,1)}), bf16[144,1152]{1,0:T(8,128)(2,1)}) %reduce-scatter.9.cloned.1.call-update) | async-done | bytes 331792
  203.9 1.2 copy.15
  205.1 1.1 bitcast_convert_fusion
  206.2 2.4 %copy.11 = f32[1,144,1152]{2,1,0:T(8,128)} copy(f32[1,144,1152]{1,2,0:T(8,128)} %bitcast_convert_fusion) | data formatting | bytes 1327104
  (2 shorter events, 0.0 us)
Async XLA Ops:
  7.2 1.8 copy-start
  7.2 7.8 %copy-start.2 = (bf16[128,1152]{1,0:T(8,128)(2,1)S(1)}, bf16[128,1152]{1,0:T(8,128)(2,1)}, u32[]{:S(2)}) copy-start(bf16[128,1152]{1,0:T(8,128)(2,1)} %param.6) | copy-start | bytes 884740
  7.2 132.4 %reduce-scatter.7.cloned.1.call-start = ((), (), s32[]{:S(2)}) async-start(), calls=%async_computation.2 | async-start | bytes 2985984
  8.9 6.1 %copy-start.1 = (bf16[1152,1152]{1,0:T(8,128)(2,1)S(1)}, bf16[1152,1152]{1,0:T(8,128)(2,1)}, u32[]{:S(2)}) copy-start(bf16[1152,1152]{1,0:T(8,128)(2,1)} %param.8) | copy-start | bytes 7962628
  10.9 26.7 %collective-permute-start = (bf16[128,1152]{1,0:T(8,128)(2,1)S(1)}, bf16[128,1152]{1,0:T(8,128)(2,1)S(1)}, u32[]{:S(2)}, u32[]{:S(2)}) collective-permute-start(bf16[128,1152]{1,0:T(8,128)(2,1)S(1)} %fusion.42), channel_id=1, source_target_pairs={{0,8},{8,16},{16,24},{24,32},{32,40},{40,48},{48,56},{56,64},{64,7... | collective-permute-start | bytes 884744 | tf_op jit(solution)/shard_map/ppermute | solution.py:15
  17.4 55.1 %copy-start.8 = (bf16[128,128]{1,0:T(8,128)(2,1)}, bf16[128,128]{1,0:T(8,128)(2,1)S(1)}, u32[]{:S(2)}) copy-start(bf16[128,128]{1,0:T(8,128)(2,1)S(1)} %fusion.33) | copy-start | bytes 98308
  37.5 15.6 %collective-permute-start.1 = (bf16[128,1152]{1,0:T(8,128)(2,1)S(1)}, bf16[128,1152]{1,0:T(8,128)(2,1)S(1)}, u32[]{:S(2)}, u32[]{:S(2)}) collective-permute-start(bf16[128,1152]{1,0:T(8,128)(2,1)S(1)} %collective-permute-done), channel_id=1, source_target_pairs={{0,8},{8,16},{16,24},{24,32},{32,40},{40,48},{48,56},{56,64},{64,7... | collective-permute-start | bytes 884744 | tf_op jit(solution)/shard_map/ppermute | solution.py:15
  39.7 32.9 %copy-start.5 = (bf16[128,128]{1,0:T(8,128)(2,1)}, bf16[128,128]{1,0:T(8,128)(2,1)S(1)}, u32[]{:S(2)}) copy-start(bf16[128,128]{1,0:T(8,128)(2,1)S(1)} %fusion.34) | copy-start | bytes 98308
  53.1 18.5 %collective-permute-start.2 = (bf16[128,1152]{1,0:T(8,128)(2,1)S(1)}, bf16[128,1152]{1,0:T(8,128)(2,1)S(1)}, u32[]{:S(2)}, u32[]{:S(2)}) collective-permute-start(bf16[128,1152]{1,0:T(8,128)(2,1)S(1)} %collective-permute-done.1), channel_id=1, source_target_pairs={{0,8},{8,16},{16,24},{24,32},{32,40},{40,48},{48,56},{56,64},{64,7... | collective-permute-start | bytes 884744 | tf_op jit(solution)/shard_map/ppermute | solution.py:15
  55.3 16.6 %copy-start.6 = (bf16[128,128]{1,0:T(8,128)(2,1)}, bf16[128,128]{1,0:T(8,128)(2,1)S(1)}, u32[]{:S(2)}) copy-start(bf16[128,128]{1,0:T(8,128)(2,1)S(1)} %fusion.35) | copy-start | bytes 98308
  55.3 17.3 %copy-start.3 = (bf16[128,1152]{1,0:T(8,128)(2,1)S(1)}, bf16[128,1152]{1,0:T(8,128)(2,1)}, u32[]{:S(2)}) copy-start(bf16[128,1152]{1,0:T(8,128)(2,1)} %param.6) | copy-start | bytes 884740
  71.9 0.7 copy-start.7
  80.4 123.5 %reduce-scatter.9.cloned.1.call-start = ((), (), s32[]{:S(2)}) async-start(), calls=%async_computation.3 | async-start | bytes 2985984
  80.4 51.4 %copy-start.4 = (bf16[128,1152]{1,0:T(8,128)(2,1)S(1)}, bf16[128,1152]{1,0:T(8,128)(2,1)}, u32[]{:S(2)}) copy-start(bf16[128,1152]{1,0:T(8,128)(2,1)} %param.7) | copy-start | bytes 884740
  81.5 7.8 %collective-permute-start.3 = (bf16[128,1152]{1,0:T(8,128)(2,1)S(1)}, bf16[128,1152]{1,0:T(8,128)(2,1)S(1)}, u32[]{:S(2)}, u32[]{:S(2)}) collective-permute-start(bf16[128,1152]{1,0:T(8,128)(2,1)S(1)} %fusion.5), channel_id=1, source_target_pairs={{0,1016},{8,0},{16,8},{24,16},{32,24},{40,32},{48,40},{56,48},{64,... | collective-permute-start | bytes 884744 | tf_op jit(solution)/shard_map/ppermute | solution.py:15
  84.5 46.1 %collective-permute-start.4 = (bf16[128,1152]{1,0:T(8,128)(2,1)S(1)}, bf16[128,1152]{1,0:T(8,128)(2,1)S(1)}, u32[]{:S(2)}, u32[]{:S(2)}) collective-permute-start(bf16[128,1152]{1,0:T(8,128)(2,1)S(1)} %fusion.6), channel_id=1, source_target_pairs={{0,1008},{8,1016},{16,0},{24,8},{32,16},{40,24},{48,32},{56,40},{6... | collective-permute-start | bytes 884744 | tf_op jit(solution)/shard_map/ppermute | solution.py:15
  87.4 43.2 %collective-permute-start.5 = (bf16[128,1152]{1,0:T(8,128)(2,1)S(1)}, bf16[128,1152]{1,0:T(8,128)(2,1)S(1)}, u32[]{:S(2)}, u32[]{:S(2)}) collective-permute-start(bf16[128,1152]{1,0:T(8,128)(2,1)S(1)} %fusion.7), channel_id=1, source_target_pairs={{0,1000},{8,1008},{16,1016},{24,0},{32,8},{40,16},{48,24},{56,32},... | collective-permute-start | bytes 884744 | tf_op jit(solution)/shard_map/ppermute | solution.py:15
Sparse Core Ops, SparseCore 0:
  80.5 54.3 reduce-scatter.6
  139.7 64.1 reduce-scatter.8
where the time goes:
time: 218 us; the launch traced here: 215 us
  waiting for transfers between devices  150 us (69%)
  local copies, waits for them, and re-layouts  19.5 us (9%)
  between operations  15.7 us (7%)
  matrix products  14 us (6%)
  starting transfers between devices  13.8 us (6%)
  other arithmetic  2.46 us (1%)
    ppermute x6, waiting for transfers between devices, passed_along(): return lax.ppermute(value, axis, pairs)  90.5 us
    unnamed x4, waiting for transfers between devices  59.5 us
    unnamed x24, local copies, waits for them, and re-layouts  19.5 us
    ppermute x6, starting transfers between devices, passed_along(): return lax.ppermute(value, axis, pairs)  13.7 us
  transfers between devices with their start and end apart: 8, of which 5 were waited for; matrix products, arithmetic and copies ran while one was open for 9% of the time, Pallas kernels for 0%

commit v1 on v0

v1 whole, which is shorter than its diff:
```python
import functools

import jax
import jax.numpy as jnp
from jax import lax
from jax.experimental import pallas as pl
from jax.experimental.pallas import tpu as pltpu
from jax.sharding import Mesh, PartitionSpec as P

NAMES = ("x", "zh", "y", "zl", "c")
NX, NZH, NY, NZL, NC = SIZES = (8, 2, 8, 4, 2)
ROWS = 128
D = 1152
CHIP = 288
CORE = 144
LEFT = 640
EPS = 1e-06
BF = jnp.bfloat16
F32 = jnp.float32
VMEM = pl.BlockSpec(memory_space=pltpu.VMEM)
SMEM = pl.BlockSpec(memory_space=pltpu.SMEM)
ANY = pl.BlockSpec(memory_space=pl.ANY)
PARAMS = pltpu.CompilerParams(vmem_limit_bytes=32 * 1024 * 1024)


def index_of(x, zh, y, zl, c):
    return (((x * NZH + zh) * NY + y) * NZL + zl) * NC + c


def pairs_of(rule):
    found = []
    for x in range(NX):
        for zh in range(NZH):
            for y in range(NY):
                for zl in range(NZL):
                    for c in range(NC):
                        target = rule(x, zh, y, zl, c)
                        if target is not None:
                            found.append((index_of(x, zh, y, zl, c), index_of(*target)))
    return found


def send(value, rule):
    return lax.ppermute(value, NAMES, pairs_of(rule))


def other_core(x, zh, y, zl, c):
    return (x, zh, y, zl, 1 - c)


def first_hop(x, zh, y, zl, c):
    if c == 1:
        return (x, zh, y + 1, zl, 0) if y < 7 else None
    return (x, zh, y - 1, zl, 1) if y > 0 else None


def second_hop(x, zh, y, zl, c):
    if not 1 <= y <= 6:
        return None
    return (x, zh, y + 1 if c == 0 else y - 1, zl, c)


def third_hop(x, zh, y, zl, c):
    if c == 0:
        return (x, zh, y + 1, zl, 0) if y < 7 else None
    return (x, zh, y - 1, zl, 1) if y > 0 else None


def crossing(x, zh, y, zl, c):
    if c == 1 and y >= 5:
        column = {7: 1, 6: 0, 5: 2}[y]
        return (x, 1, column, zl, 0) if zh == 0 else ((x + 1) % NX, 0, column, zl, 0)
    if c == 0 and y <= 2:
        column = {0: 6, 1: 7, 2: 5}[y]
        return (x, 0, column, zl, 1) if zh == 1 else ((x - 1) % NX, 1, column, zl, 1)
    return None


def from_second(x, zh, y, zl, c):
    if c == 0 and y == 1:
        return (x, zh, 0, zl, 0)
    if c == 1 and y == 6:
        return (x, zh, 7, zl, 1)
    return None


def from_third(x, zh, y, zl, c):
    if c == 0 and y == 2:
        return (x, zh, 0, zl, 0)
    if c == 1 and y == 5:
        return (x, zh, 7, zl, 1)
    return None


def inward(x, zh, y, zl, c):
    return {0: (x, zh, y, 1, c), 3: (x, zh, y, 2, c)}.get(zl)


def middle(x, zh, y, zl, c):
    return {1: (x, zh, y, 2, c), 2: (x, zh, y, 1, c)}.get(zl)


def outward(x, zh, y, zl, c):
    return {1: (x, zh, y, 0, c), 2: (x, zh, y, 3, c)}.get(zl)


def outward_cross(x, zh, y, zl, c):
    return {1: (x, zh, y, 0, 1 - c), 2: (x, zh, y, 3, 1 - c)}.get(zl)


def normalised(x):
    total = jnp.sum(x * x, axis=-1, keepdims=True)
    rn = 1.0 / jnp.sqrt(total + EPS)
    u = x * rn
    return u, jnp.broadcast_to(rn, (ROWS, 128))


def project_own_kernel(
    flags, pictures, captions, wp, wc, w_ref, z_ref, u_ref, rn_ref, f_ref, sems
):
    c = flags[0]
    parts = 3
    width = D // parts

    def fetch(feats, head):
        pltpu.make_async_copy(feats, f_ref, sems.at[parts]).start()
        for j in range(parts):
            cols = pl.ds(j * width, width)
            pltpu.make_async_copy(head.at[:, cols], w_ref.at[:, cols], sems.at[j]).start()

    @pl.when(c == 0)
    def _():
        fetch(pictures, wp)

    @pl.when(c == 1)
    def _():
        fetch(captions, wc)

    pltpu.make_async_copy(pictures, f_ref, sems.at[parts]).wait()
    for j in range(parts):
        cols = pl.ds(j * width, width)
        pltpu.make_async_copy(wp.at[:, cols], w_ref.at[:, cols], sems.at[j]).wait()
        u_ref[:, cols] = jnp.dot(f_ref[...], w_ref[:, cols], preferred_element_type=F32)
    u, rn_ref[...] = normalised(u_ref[...])
    u_ref[...] = u
    z_ref[...] = u.astype(BF)


def project_own(flags, pictures, captions, wp, wc):
    return pl.pallas_call(
        project_own_kernel,
        name="project_own",
        out_shape=(
            jax.ShapeDtypeStruct((D, D), BF),
            jax.ShapeDtypeStruct((ROWS, D), BF),
            jax.ShapeDtypeStruct((ROWS, D), F32),
            jax.ShapeDtypeStruct((ROWS, 128), F32),
        ),
        in_specs=[SMEM, ANY, ANY, ANY, ANY],
        out_specs=(VMEM,) * 4,
        scratch_shapes=[pltpu.VMEM((ROWS, D), BF), pltpu.SemaphoreType.DMA((4,))],
        compiler_params=PARAMS,
        cost_estimate=pl.CostEstimate(
            flops=2 * ROWS * D * D, bytes_accessed=4 * D * D + 8 * ROWS * D, transcendentals=0
        ),
    )(flags, pictures, captions, wp, wc)


def project_other_kernel(recv, w_ref, z_own, z_ref, u_ref, rn_ref):
    z_ref[:ROWS] = z_own[...]
    u, rn_ref[...] = normalised(
        jnp.dot(recv[...], w_ref[...], preferred_element_type=F32)
    )
    u_ref[...] = u
    z_ref[ROWS:] = u.astype(BF)


def project_other(recv, w, z_own):
    return pl.pallas_call(
        project_other_kernel,
        name="project_other",
        out_shape=(
            jax.ShapeDtypeStruct((2 * ROWS, D), BF),
            jax.ShapeDtypeStruct((ROWS, D), F32),
            jax.ShapeDtypeStruct((ROWS, 128), F32),
        ),
        in_specs=[VMEM] * 3,
        out_specs=(VMEM,) * 3,
        compiler_params=PARAMS,
        cost_estimate=pl.CostEstimate(
            flops=2 * ROWS * D * D, bytes_accessed=2 * D * D + 8 * ROWS * D, transcendentals=0
        ),
    )(recv, w, z_own)


def turn_kernel(flags, pictures, captions, recv, after, ft_ref, turned, f_ref, sem):
    del after
    mirror = flags[3]

    @pl.when(flags[0] == 0)
    def _():
        pltpu.make_async_copy(pictures, f_ref, sem).start()

    @pl.when(flags[0] == 1)
    def _():
        pltpu.make_async_copy(captions, f_ref, sem).start()

    turned[:, ROWS:] = recv[...].T
    pltpu.make_async_copy(pictures, f_ref, sem).wait()
    turned[:, :ROWS] = f_ref[...].T
    for j in range(4):
        start = pl.multiple_of(jnp.where(mirror == 1, 3 - j, j) * CHIP, CHIP)
        ft_ref[j * CHIP : (j + 1) * CHIP] = turned[pl.ds(start, CHIP)]


def turn(flags, pictures, captions, recv, after):
    return pl.pallas_call(
        turn_kernel,
        name="turn",
        out_shape=jax.ShapeDtypeStruct((D, 2 * ROWS), BF),
        in_specs=[SMEM, ANY, ANY, VMEM, ANY],
        out_specs=VMEM,
        scratch_shapes=[
            pltpu.VMEM((D, 2 * ROWS), BF),
            pltpu.VMEM((ROWS, D), BF),
            pltpu.SemaphoreType.DMA(()),
        ],
        compiler_params=PARAMS,
        cost_estimate=pl.CostEstimate(
            flops=0, bytes_accessed=8 * ROWS * D, transcendentals=0
        ),
    )(flags, pictures, captions, recv, after)


def pairs_kernel(
    flags, scale, z_ref, u_own, u_other, rn_own, rn_other,
    here, one, two, three, cross, second, third, early_end, early_mid,
    dx_ref, others, sems,
):
    del early_end, early_mid

    def fetch(source, s):
        for b in range(2):
            pltpu.make_async_copy(
                source.at[pl.ds((1 - b) * ROWS, ROWS)],
                others.at[b, pl.ds(s * ROWS, ROWS)],
                sems.at[2 * s + b],
            ).start()

    fetch(here, 0)

    @pl.when(flags[1] == 0)
    def _():
        fetch(one, 1)

    @pl.when(flags[1] == 1)
    def _():
        fetch(second, 1)

    @pl.when(flags[2] == 0)
    def _():
        fetch(two, 2)

    @pl.when(flags[2] == 1)
    def _():
        fetch(cross, 2)

    @pl.when(flags[1] == 0)
    def _():
        fetch(three, 3)

    @pl.when(flags[1] == 1)
    def _():
        fetch(third, 3)

    t = scale[0]
    bias = scale[1]
    for s in range(4):
        for b in range(2):
            pltpu.make_async_copy(
                here.at[pl.ds(0, ROWS)],
                others.at[b, pl.ds(s * ROWS, ROWS)],
                sems.at[2 * s + b],
            ).wait()
    row = lax.broadcasted_iota(jnp.int32, (ROWS, 4 * ROWS), 0)
    col = lax.broadcasted_iota(jnp.int32, (ROWS, 4 * ROWS), 1)
    for b in range(2):
        mine = z_ref[b * ROWS : (b + 1) * ROWS]
        logits = t * lax.dot_general(
            mine, others[b], (((1,), (1,)), ((), ())), preferred_element_type=F32
        ) + bias
        prob = jax.nn.sigmoid(logits) - jnp.where(row == col, 1.0, 0.0)
        weight = (prob * (1.0 / ROWS)).astype(BF)
        dz = t * jnp.dot(weight, others[b], preferred_element_type=F32)
        u = (u_own, u_other)[b][...]
        rn = (rn_own, rn_other)[b][:, :1]
        inner = jnp.sum(u * dz, axis=-1, keepdims=True)
        dx_ref[b * ROWS : (b + 1) * ROWS] = ((dz - u * inner) * rn).astype(BF)


def pairs(flags, scale, z, *rest):
    rows = 2 * ROWS
    return pl.pallas_call(
        pairs_kernel,
        name="pairs",
        out_shape=jax.ShapeDtypeStruct((rows, D), BF),
        in_specs=[SMEM, SMEM] + [VMEM] * 5 + [ANY] * 9,
        out_specs=VMEM,
        scratch_shapes=[
            pltpu.VMEM((2, 4 * ROWS, D), BF),
            pltpu.SemaphoreType.DMA((8,)),
        ],
        compiler_params=PARAMS,
        cost_estimate=pl.CostEstimate(
            flops=16 * rows * ROWS * D, bytes_accessed=14 * rows * D, transcendentals=rows * 512
        ),
    )(flags, scale, z, *rest)


def near_kernel(ft, dx, feats_end, dx_end, feats_mid, dx_mid, inner_ref, outer_ref):
    dx_own = dx[...]
    dx_other = dx_mid[...]
    inner_ref[...] = (
        jnp.dot(ft[CHIP : 2 * CHIP], dx_own, preferred_element_type=F32)
        + jnp.dot(feats_end[:CHIP], dx_end[...], preferred_element_type=F32)
        + jnp.dot(feats_mid[:CHIP], dx_other, preferred_element_type=F32)
    )
    outer_ref[...] = jnp.dot(ft[:CHIP], dx_own, preferred_element_type=F32) + jnp.dot(
        feats_mid[CHIP:], dx_other, preferred_element_type=F32
    )


def near(ft, dx, feats_end, dx_end, feats_mid, dx_mid):
    return pl.pallas_call(
        near_kernel,
        name="near",
        out_shape=(
            jax.ShapeDtypeStruct((CHIP, D), F32),
            jax.ShapeDtypeStruct((CHIP, D), F32),
        ),
        in_specs=[VMEM] * 6,
        out_specs=(VMEM, VMEM),
        compiler_params=PARAMS,
        cost_estimate=pl.CostEstimate(
            flops=20 * CHIP * ROWS * D, bytes_accessed=14 * CHIP * D, transcendentals=0
        ),
    )(ft, dx, feats_end, dx_end, feats_mid, dx_mid)


def far_kernel(first, flags, inner_ref, outer_ref, feats, dx, *refs):
    keep, swap, same, crossed, total, part = refs[-6:]
    c = flags[0]
    cols = slice(0, LEFT) if first else slice(LEFT, D)
    dx_far = dx[...]
    part[...] = outer_ref[:, cols] + jnp.dot(
        feats[CHIP:], dx_far, preferred_element_type=F32
    )
    total[...] = inner_ref[:, cols] + jnp.dot(
        feats[:CHIP], dx_far, preferred_element_type=F32
    )
    mine = pl.ds(pl.multiple_of(c * CORE, CORE), CORE)
    theirs = pl.ds(pl.multiple_of((1 - c) * CORE, CORE), CORE)
    same[...] = part[mine].astype(BF)
    crossed[...] = part[theirs].astype(BF)
    if not first:
        keep[:, :LEFT] = refs[0][...]
        swap[:, :LEFT] = refs[1][...]
    into = slice(0, LEFT) if first else slice(LEFT, D)

    @pl.when(flags[4] == 1)
    def _():
        keep[:, into] = total[mine]
        swap[:, into] = total[theirs].astype(BF)

    @pl.when(flags[4] == 0)
    def _():
        keep[:, into] = part[mine]
        swap[:, into] = part[theirs].astype(BF)


def far(flags, inner, outer, feats, dx, *earlier):
    first = not earlier
    cols = LEFT if first else D - LEFT
    kept = LEFT if first else D
    return pl.pallas_call(
        functools.partial(far_kernel, first),
        name="far_left" if first else "far_right",
        out_shape=(
            jax.ShapeDtypeStruct((CORE, kept), F32),
            jax.ShapeDtypeStruct((CORE, kept), BF),
            jax.ShapeDtypeStruct((CORE, cols), BF),
            jax.ShapeDtypeStruct((CORE, cols), BF),
        ),
        in_specs=[SMEM] + [VMEM] * (4 + len(earlier)),
        out_specs=(VMEM,) * 4,
        scratch_shapes=[pltpu.VMEM((CHIP, cols), F32), pltpu.VMEM((CHIP, cols), F32)],
        compiler_params=PARAMS,
        cost_estimate=pl.CostEstimate(
            flops=8 * CHIP * ROWS * cols, bytes_accessed=14 * CHIP * cols, transcendentals=0
        ),
    )(flags, inner, outer, feats, dx, *earlier)


def finish_kernel(
    flags, keep, swap, same_left, crossed_left, same_right, crossed_right, image_ref, text_ref
):
    def put(own_ref, other_ref):
        for cols, same, crossed in (
            (slice(0, LEFT), same_left, crossed_left),
            (slice(LEFT, D), same_right, crossed_right),
        ):
            own_ref[0, :, cols] = keep[:, cols] + same[...].astype(F32)
            other_ref[0, :, cols] = swap[:, cols].astype(F32) + crossed[...].astype(F32)

    @pl.when(flags[0] == 0)
    def _():
        put(image_ref, text_ref)

    @pl.when(flags[0] == 1)
    def _():
        put(text_ref, image_ref)


def finish(flags, *parts):
    shape = jax.ShapeDtypeStruct((1, CORE, D), F32)
    return pl.pallas_call(
        finish_kernel,
        name="finish",
        out_shape=(shape, shape),
        in_specs=[SMEM] + [VMEM] * 6,
        out_specs=(VMEM, VMEM),
        compiler_params=PARAMS,
        cost_estimate=pl.CostEstimate(
            flops=4 * CORE * D, bytes_accessed=18 * CORE * D, transcendentals=0
        ),
    )(flags, *parts)


def on_device(pictures, captions, picture_head, caption_head, sharpness, shift_term):
    c = lax.axis_index("c")
    y = lax.axis_index("y")
    zl = lax.axis_index("zl")
    yy = jnp.where(c == 0, y, 7 - y)
    flags = jnp.stack(
        [c, yy == 0, yy <= 1, zl >= 2, (zl == 1) | (zl == 2)]
    ).astype(jnp.int32)
    scale = jnp.concatenate([sharpness, shift_term])

    received = send(jnp.where(c == 0, captions, pictures), other_core)
    head, z_own, u_own, rn_own = project_own(
        flags, pictures, captions, picture_head, caption_head
    )
    z, u_other, rn_other = project_other(received, head, z_own)

    cross = send(z, crossing)
    one = send(z, first_hop)
    here = send(z, other_core)
    two = send(one, second_hop)
    three = send(jnp.where(yy <= 1, cross, two), third_hop)
    second = send(cross, from_second)
    third = send(cross, from_third)
    ft = turn(flags, pictures, captions, received, two)
    ft_end = send(ft[CHIP:], inward)
    ft_mid = send(ft[2 * CHIP :], middle)
    ft_far = send(ft_end[CHIP:], middle)
    dx = pairs(
        flags, scale, z, u_own, u_other, rn_own, rn_other,
        here, one, two, three, cross, second, third, ft_end, ft_mid,
    )

    dx_end = send(dx, inward)
    dx_mid = send(dx, middle)
    far_left = send(dx_end[:, :LEFT], middle)
    far_right = send(dx_end[:, LEFT:], middle)
    inner, outer = near(ft, dx, ft_end, dx_end, ft_mid, dx_mid)
    keep, swap, same_left, crossed_left = far(flags, inner, outer, ft_far, far_left)
    crossed_left = send(crossed_left, outward_cross)
    same_left = send(same_left, outward)
    keep, swap, same_right, crossed_right = far(
        flags, inner, outer, ft_far, far_right, keep, swap
    )
    crossed_right = send(crossed_right, outward_cross)
    same_right = send(same_right, outward)
    swap = send(swap, other_core)
    return finish(flags, keep, swap, same_left, crossed_left, same_right, crossed_right)


def solution(mesh):
    physical = Mesh(mesh.devices.reshape(SIZES), NAMES)
    rows = P(NAMES, None)
    grad = P(("x", "zh", "y"), ("zl", "c"), None)
    return jax.shard_map(
        on_device,
        mesh=physical,
        in_specs=(rows, rows, P(), P(), P(), P()),
        out_specs=(grad, grad),
        check_vma=False,
    )
```

time: 218 us -> 137 us (0.63)
  waiting for transfers between devices: 150 us -> 75.4 us
  starting transfers between devices: 13.8 us -> 40.5 us
  matrix products: 14 us -> 0 us
  local copies, waits for them, and re-layouts: 19.5 us -> 5.64 us
  between operations: 15.7 us -> 2.31 us
  Pallas kernels: 0 us -> 11.5 us
    unnamed x4 -> x0, waiting for transfers between devices: 59.5 us -> none
    ppermute x6 -> x20, starting transfers between devices: 13.7 us -> 40.5 us  [send(): return lax.ppermute(value, NAMES, pairs_of(rule))]
    ppermute x6 -> x20, waiting for transfers between devices: 90.5 us -> 75.4 us  [send(): return lax.ppermute(value, NAMES, pairs_of(rule))]
    unnamed x24 -> x12, local copies, waits for them, and re-layouts: 19.5 us -> 5.43 us
    dot_general x16 -> x0, matrix products: 14 us -> none  [the longest x4 4.34 us: paired_blocks(): jnp.dot(head_weights.T, image_embedded, preferred_element_type=jnp.float32)]
    pallas_call x0 -> x8, Pallas kernels: none -> 11.5 us  [the longest x1 2.85 us: pairs(): pl.pallas_call(pairs_kernel, name='pairs', out_shape=jax.ShapeDtypeStruct...]
    broadcast_in_dim x2 -> x0, other arithmetic: 2.21 us -> none  [on_device(): return (image_grad[None], text_grad[None])]
  transfers between devices with their start and end apart: 8 -> 20, of which waited for: 5 -> 7; matrix products, arithmetic and copies ran while one was open for 9% -> 0% of each run, Pallas kernels for 0% -> 4%
where the time goes in v1:
time: 137 us; the launch traced here: 136 us
  waiting for transfers between devices  75.4 us (55%)
  starting transfers between devices  40.5 us (30%)
  Pallas kernels  11.5 us (8%)
  local copies, waits for them, and re-layouts  5.64 us (4%)
  between operations  2.31 us (2%)
    ppermute x20, waiting for transfers between devices, send(): return lax.ppermute(value, NAMES, pairs_of(rule))  75.4 us
    ppermute x20, starting transfers between devices, send(): return lax.ppermute(value, NAMES, pairs_of(rule))  40.5 us
    unnamed x12, local copies, waits for them, and re-layouts  5.43 us
    pallas_call x1, Pallas kernels, pairs(): pl.pallas_call(pairs_kernel, name='pairs', out_shape=jax.ShapeDtypeStruct...  2.85 us
  transfers between devices with their start and end apart: 20, of which 7 were waited for; matrix products, arithmetic and copies ran while one was open for 0% of the time, Pallas kernels for 4%

profile of v1, /device:TPU:1, one launch (start us, length us, event | category | flops | bytes accessed | tf_op | source)
XLA Modules:
  0.0 136.5 jit_solution(8628932502308759011)
XLA Ops:
  0.6 1.0 broadcast_select_fusion.1
  1.6 16.1 %collective-permute-start = (bf16[128,1152]{1,0:T(8,128)(2,1)S(1)}, bf16[128,1152]{1,0:T(8,128)(2,1)S(1)}, u32[]{:S(2)}, u32[]{:S(2)}) collective-permute-start(bf16[128,1152]{1,0:T(8,128)(2,1)S(1)} %broadcast_select_fusion.1), channel_id=1, source_target_pairs={{0,1},{1,0},{2,3},{3,2},{4,5},{5,4},{6,7},{7,6},{8,9},{9,8},{10,11... | collective-permute-start | bytes 884744 | tf_op jit(solution)/shard_map/ppermute | solution.py:44
  17.7 0.1 stack.39.flags
  17.8 0.0 copy-start
  17.8 1.0 copy-done
  18.8 0.0 copy-start.2
  18.8 1.0 copy-done.2
  19.8 0.0 copy-start.4
  19.8 1.7 %copy-done.4 = bf16[1152,1152]{1,0:T(8,128)(2,1)S(1)} copy-done((bf16[1152,1152]{1,0:T(8,128)(2,1)S(1)}, bf16[1152,1152]{1,0:T(8,128)(2,1)}, u32[]{:S(2)}) %copy-start.4) | copy-done | bytes 2654232
  21.5 0.0 copy-start.5
  21.5 1.7 %copy-done.5 = bf16[1152,1152]{1,0:T(8,128)(2,1)S(1)} copy-done((bf16[1152,1152]{1,0:T(8,128)(2,1)S(1)}, bf16[1152,1152]{1,0:T(8,128)(2,1)}, u32[]{:S(2)}) %copy-start.5) | copy-done | bytes 2654232
  23.3 2.1 %project_own.1 = (bf16[1152,1152]{1,0:T(8,128)(2,1)S(1)}, bf16[128,1152]{1,0:T(8,128)(2,1)S(1)}, f32[128,1152]{1,0:T(8,128)S(1)}, f32[128,128]{1,0:T(8,128)S(1)}) custom-call(s32[5]{0:T(128)S(1)} %stack.39.flags, bf16[128,1152]{1,0:T(8,128)(2,1)S(1)} %copy-done, bf16[128,1152]{1,0:T(8,128)(2,1)S(1)} %copy-done.2, bf16[1152,1152]{1,0:T(8,128)(2,1)S(1)} %copy-done.4, ...), custom_call_target="tpu_custom_call" | custom-call | flops 339738624 | bytes 6488064 | tf_op jit(solution)/shard_map/project_own/pallas_call | solution.py:150
  25.3 0.0 copy-start.1
  25.3 0.0 copy-start.3
  25.4 0.0 collective-permute-done.recv
  25.4 0.8 project_other.1
  26.1 1.9 %collective-permute-start.1 = (bf16[256,1152]{1,0:T(8,128)(2,1)S(1)}, bf16[256,1152]{1,0:T(8,128)(2,1)S(1)}, u32[]{:S(2)}, u32[]{:S(2)}) collective-permute-start(bf16[256,1152]{1,0:T(8,128)(2,1)S(1)} %get-tuple-element.21.z_ref), channel_id=1, source_target_pairs={{1,8},{3,10},{5,12},{7,14},{8,1},{9,16},{10,3},{11,18},{12,5},{13,... | collective-permute-start | bytes 1769480 | tf_op jit(solution)/shard_map/ppermute | solution.py:44
  28.1 0.7 collective-permute-start.4
  28.8 12.9 %collective-permute-done.1.one = bf16[256,1152]{1,0:T(8,128)(2,1)S(1)} collective-permute-done((bf16[256,1152]{1,0:T(8,128)(2,1)S(1)}, bf16[256,1152]{1,0:T(8,128)(2,1)S(1)}, u32[]{:S(2)}, u32[]{:S(2)}) %collective-permute-start.1) | collective-permute-done | bytes 589856 | tf_op jit(solution)/shard_map/ppermute | solution.py:44
  41.6 1.3 collective-permute-start.2
  42.9 1.9 %collective-permute-start.3 = (bf16[256,1152]{1,0:T(8,128)(2,1)S(1)}, bf16[256,1152]{1,0:T(8,128)(2,1)S(1)}, u32[]{:S(2)}, u32[]{:S(2)}) collective-permute-start(bf16[256,1152]{1,0:T(8,128)(2,1)S(1)} %get-tuple-element.21.z_ref), channel_id=1, source_target_pairs={{0,1},{1,0},{2,3},{3,2},{4,5},{5,4},{6,7},{7,6},{8,9},{9,8},{10,11... | collective-permute-start | bytes 1769480 | tf_op jit(solution)/shard_map/ppermute | solution.py:44
  44.9 0.0 collective-permute-done.4.cross
  44.9 0.7 collective-permute-start.6
  45.6 0.7 collective-permute-start.7
  46.3 6.0 %collective-permute-done.2.after.two = bf16[256,1152]{1,0:T(8,128)(2,1)S(1)} collective-permute-done((bf16[256,1152]{1,0:T(8,128)(2,1)S(1)}, bf16[256,1152]{1,0:T(8,128)(2,1)S(1)}, u32[]{:S(2)}, u32[]{:S(2)}) %collective-permute-start.2) | collective-permute-done | bytes 589856 | tf_op jit(solution)/shard_map/ppermute | solution.py:44
  52.3 0.1 broadcast_select_fusion
  52.4 1.3 collective-permute-start.5
  53.7 0.0 copy-done.1
  53.7 0.0 copy-done.3
  53.7 1.0 turn.1.ft
  54.7 1.3 collective-permute-start.8
  56.0 0.0 collective-permute-done.3.here
  56.0 0.7 collective-permute-start.9
  58.0 0.1 pad_maximum_fusion.scale
  58.1 0.0 collective-permute-done.6.second
  58.1 0.0 collective-permute-done.7.third
  58.1 0.0 collective-permute-done.9.early_mid.feats_mid
  58.1 3.1 %collective-permute-done.8.early_end.feats_end = bf16[864,256]{1,0:T(8,128)(2,1)S(1)} collective-permute-done((bf16[864,256]{1,0:T(8,128)(2,1)S(1)}, bf16[864,256]{1,0:T(8,128)(2,1)S(1)}, u32[]{:S(2)}, u32[]{:S(2)}) %collective-permute-start.8) | collective-permute-done | bytes 442400 | tf_op jit(solution)/shard_map/ppermute | solution.py:44
  61.2 13.0 %collective-permute-done.5.three = bf16[256,1152]{1,0:T(8,128)(2,1)S(1)} collective-permute-done((bf16[256,1152]{1,0:T(8,128)(2,1)S(1)}, bf16[256,1152]{1,0:T(8,128)(2,1)S(1)}, u32[]{:S(2)}, u32[]{:S(2)}) %collective-permute-start.5) | collective-permute-done | bytes 589856 | tf_op jit(solution)/shard_map/ppermute | solution.py:44
  74.2 2.8 %pairs.1.dx = bf16[256,1152]{1,0:T(8,128)(2,1)S(1)} custom-call(s32[5]{0:T(128)S(1)} %stack.39.flags, f32[2]{0:T(128)S(1)} %pad_maximum_fusion.scale, bf16[256,1152]{1,0:T(8,128)(2,1)S(1)} %get-tuple-element.21.z_ref, f32[128,1152]{1,0:T(8,128)S(1)} %get-tuple-element.22.u_own, f32[128,1152]{1,0:T(8,128)S(1)} %get-tuple-element.23.u_other, ...), custom_call_target="tpu_custom_call" | custom-call | flops 603979776 | bytes 4128768 | tf_op jit(solution)/shard_map/pairs/pallas_call | solution.py:303
  77.1 1.3 collective-permute-start.10
  78.4 0.7 collective-permute-start.11
  79.1 10.0 %collective-permute-done.10.dx_end = bf16[256,1152]{1,0:T(8,128)(2,1)S(1)} collective-permute-done((bf16[256,1152]{1,0:T(8,128)(2,1)S(1)}, bf16[256,1152]{1,0:T(8,128)(2,1)S(1)}, u32[]{:S(2)}, u32[]{:S(2)}) %collective-permute-start.10) | collective-permute-done | bytes 589856 | tf_op jit(solution)/shard_map/ppermute | solution.py:44
  89.1 0.7 collective-permute-start.14
  89.9 0.7 collective-permute-start.12
  90.6 0.7 collective-permute-start.13
  91.3 0.0 collective-permute-done.11.dx_mid
  91.3 1.2 near.1
  92.4 0.0 collective-permute-done.12.feats
  92.4 0.0 collective-permute-done.14.dx
  92.4 1.0 far_left.1
  93.4 0.0 collective-permute-done.13.dx
  93.5 0.9 far_right.1
  94.4 4.7 %collective-permute-start.15 = (bf16[144,1152]{1,0:T(8,128)(2,1)S(1)}, bf16[144,1152]{1,0:T(8,128)(2,1)S(1)}, u32[]{:S(2)}, u32[]{:S(2)}) collective-permute-start(bf16[144,1152]{1,0:T(8,128)(2,1)S(1)} %get-tuple-element.31), channel_id=1, source_target_pairs={{0,1},{1,0},{2,3},{3,2},{4,5},{5,4},{6,7},{7,6},{8,9},{9,8},{10,11... | collective-permute-start | bytes 995336 | tf_op jit(solution)/shard_map/ppermute | solution.py:44
  99.1 1.3 collective-permute-start.16
  100.4 1.3 collective-permute-start.17
  101.7 1.3 collective-permute-start.18
  103.0 1.3 collective-permute-start.19
  104.3 27.2 %collective-permute-done.18.same_right = bf16[144,512]{1,0:T(8,128)(2,1)S(1)} collective-permute-done((bf16[144,512]{1,0:T(8,128)(2,1)S(1)}, bf16[144,512]{1,0:T(8,128)(2,1)S(1)}, u32[]{:S(2)}, u32[]{:S(2)}) %collective-permute-start.18) | collective-permute-done | bytes 147488 | tf_op jit(solution)/shard_map/ppermute | solution.py:44
  131.5 3.2 %collective-permute-done.19.crossed_right = bf16[144,512]{1,0:T(8,128)(2,1)S(1)} collective-permute-done((bf16[144,512]{1,0:T(8,128)(2,1)S(1)}, bf16[144,512]{1,0:T(8,128)(2,1)S(1)}, u32[]{:S(2)}, u32[]{:S(2)}) %collective-permute-start.19) | collective-permute-done | bytes 147488 | tf_op jit(solution)/shard_map/ppermute | solution.py:44
  134.7 0.0 collective-permute-done.16.same_left
  134.7 0.0 collective-permute-done.17.crossed_left
  134.7 0.0 collective-permute-done.15.swap
  134.7 1.8 %finish.1 = (f32[1,144,1152]{2,1,0:T(8,128)}, f32[1,144,1152]{2,1,0:T(8,128)}) custom-call(s32[5]{0:T(128)S(1)} %stack.39.flags, f32[144,1152]{1,0:T(8,128)S(1)} %get-tuple-element.30.keep, bf16[144,1152]{1,0:T(8,128)(2,1)S(1)} %collective-permute-done.15.swap, bf16[144,640]{1,0:T(8,128)(2,1)S(1)} %collective-permute-done.16.same_left, ...), custom_call_target="tpu_custom_call" | custom-call | flops 663552 | bytes 2985984 | tf_op jit(solution)/shard_map/finish/pallas_call | solution.py:426
  (5 shorter events, 0.1 us)
Async XLA Ops:
  1.6 23.7 %collective-permute-start = (bf16[128,1152]{1,0:T(8,128)(2,1)S(1)}, bf16[128,1152]{1,0:T(8,128)(2,1)S(1)}, u32[]{:S(2)}, u32[]{:S(2)}) collective-permute-start(bf16[128,1152]{1,0:T(8,128)(2,1)S(1)} %broadcast_select_fusion.1), channel_id=1, source_target_pairs={{0,1},{1,0},{2,3},{3,2},{4,5},{5,4},{6,7},{7,6},{8,9},{9,8},{10,11... | collective-permute-start | bytes 884744 | tf_op jit(solution)/shard_map/ppermute | solution.py:44
  17.8 1.0 copy-start
  18.8 1.0 copy-start.2
  19.8 1.7 %copy-start.4 = (bf16[1152,1152]{1,0:T(8,128)(2,1)S(1)}, bf16[1152,1152]{1,0:T(8,128)(2,1)}, u32[]{:S(2)}) copy-start(bf16[1152,1152]{1,0:T(8,128)(2,1)} %wp.1) | copy-start | bytes 7962628
  21.5 1.7 %copy-start.5 = (bf16[1152,1152]{1,0:T(8,128)(2,1)S(1)}, bf16[1152,1152]{1,0:T(8,128)(2,1)}, u32[]{:S(2)}) copy-start(bf16[1152,1152]{1,0:T(8,128)(2,1)} %wc.1) | copy-start | bytes 7962628
  25.3 28.3 %copy-start.1 = (bf16[128,1152]{1,0:T(8,128)(2,1)S(1)}, bf16[128,1152]{1,0:T(8,128)(2,1)}, u32[]{:S(2)}) copy-start(bf16[128,1152]{1,0:T(8,128)(2,1)} %pictures.3) | copy-start | bytes 884740
  25.3 28.3 %copy-start.3 = (bf16[128,1152]{1,0:T(8,128)(2,1)S(1)}, bf16[128,1152]{1,0:T(8,128)(2,1)}, u32[]{:S(2)}) copy-start(bf16[128,1152]{1,0:T(8,128)(2,1)} %captions.3) | copy-start | bytes 884740
  26.1 15.5 %collective-permute-start.1 = (bf16[256,1152]{1,0:T(8,128)(2,1)S(1)}, bf16[256,1152]{1,0:T(8,128)(2,1)S(1)}, u32[]{:S(2)}, u32[]{:S(2)}) collective-permute-start(bf16[256,1152]{1,0:T(8,128)(2,1)S(1)} %get-tuple-element.21.z_ref), channel_id=1, source_target_pairs={{1,8},{3,10},{5,12},{7,14},{8,1},{9,16},{10,3},{11,18},{12,5},{13,... | collective-permute-start | bytes 1769480 | tf_op jit(solution)/shard_map/ppermute | solution.py:44
  28.1 16.8 %collective-permute-start.4 = (bf16[256,1152]{1,0:T(8,128)(2,1)S(1)}, bf16[256,1152]{1,0:T(8,128)(2,1)S(1)}, u32[]{:S(2)}, u32[]{:S(2)}) collective-permute-start(bf16[256,1152]{1,0:T(8,128)(2,1)S(1)} %get-tuple-element.21.z_ref), channel_id=1, source_target_pairs={{0,1009},{2,1011},{4,1013},{6,1015},{8,1017},{10,1019},{12,1021},{... | collective-permute-start | bytes 1769480 | tf_op jit(solution)/shard_map/ppermute | solution.py:44
  41.6 10.6 %collective-permute-start.2 = (bf16[256,1152]{1,0:T(8,128)(2,1)S(1)}, bf16[256,1152]{1,0:T(8,128)(2,1)S(1)}, u32[]{:S(2)}, u32[]{:S(2)}) collective-permute-start(bf16[256,1152]{1,0:T(8,128)(2,1)S(1)} %collective-permute-done.1.one), channel_id=1, source_target_pairs={{8,16},{9,1},{10,18},{11,3},{12,20},{13,5},{14,22},{15,7},{16,24},... | collective-permute-start | bytes 1769480 | tf_op jit(solution)/shard_map/ppermute | solution.py:44
  42.9 13.1 %collective-permute-start.3 = (bf16[256,1152]{1,0:T(8,128)(2,1)S(1)}, bf16[256,1152]{1,0:T(8,128)(2,1)S(1)}, u32[]{:S(2)}, u32[]{:S(2)}) collective-permute-start(bf16[256,1152]{1,0:T(8,128)(2,1)S(1)} %get-tuple-element.21.z_ref), channel_id=1, source_target_pairs={{0,1},{1,0},{2,3},{3,2},{4,5},{5,4},{6,7},{7,6},{8,9},{9,8},{10,11... | collective-permute-start | bytes 1769480 | tf_op jit(solution)/shard_map/ppermute | solution.py:44
  44.9 13.2 %collective-permute-start.6 = (bf16[256,1152]{1,0:T(8,128)(2,1)S(1)}, bf16[256,1152]{1,0:T(8,128)(2,1)S(1)}, u32[]{:S(2)}, u32[]{:S(2)}) collective-permute-start(bf16[256,1152]{1,0:T(8,128)(2,1)S(1)} %collective-permute-done.4.cross), channel_id=1, source_target_pairs={{8,0},{10,2},{12,4},{14,6},{49,57},{51,59},{53,61},{55,63},{72,64}... | collective-permute-start | bytes 1769480 | tf_op jit(solution)/shard_map/ppermute | solution.py:44
  45.6 12.5 %collective-permute-start.7 = (bf16[256,1152]{1,0:T(8,128)(2,1)S(1)}, bf16[256,1152]{1,0:T(8,128)(2,1)S(1)}, u32[]{:S(2)}, u32[]{:S(2)}) collective-permute-start(bf16[256,1152]{1,0:T(8,128)(2,1)S(1)} %collective-permute-done.4.cross), channel_id=1, source_target_pairs={{16,0},{18,2},{20,4},{22,6},{41,57},{43,59},{45,61},{47,63},{80,64... | collective-permute-start | bytes 1769480 | tf_op jit(solution)/shard_map/ppermute | solution.py:44
  52.4 21.8 %collective-permute-start.5 = (bf16[256,1152]{1,0:T(8,128)(2,1)S(1)}, bf16[256,1152]{1,0:T(8,128)(2,1)S(1)}, u32[]{:S(2)}, u32[]{:S(2)}) collective-permute-start(bf16[256,1152]{1,0:T(8,128)(2,1)S(1)} %broadcast_select_fusion), channel_id=1, source_target_pairs={{0,8},{2,10},{4,12},{6,14},{8,16},{9,1},{10,18},{11,3},{12,20},{13... | collective-permute-start | bytes 1769480 | tf_op jit(solution)/shard_map/ppermute | solution.py:44
  54.7 6.5 %collective-permute-start.8 = (bf16[864,256]{1,0:T(8,128)(2,1)S(1)}, bf16[864,256]{1,0:T(8,128)(2,1)S(1)}, u32[]{:S(2)}, u32[]{:S(2)}) collective-permute-start(bf16[864,256]{1,0:T(8,128)(2,1)S(1)} %slice.20), channel_id=1, source_target_pairs={{0,2},{1,3},{6,4},{7,5},{8,10},{9,11},{14,12},{15,13},{16,18},{17,... | collective-permute-start | bytes 1327112 | tf_op jit(solution)/shard_map/ppermute | solution.py:44
  56.0 2.1 %collective-permute-start.9 = (bf16[576,256]{1,0:T(8,128)(2,1)S(1)}, bf16[576,256]{1,0:T(8,128)(2,1)S(1)}, u32[]{:S(2)}, u32[]{:S(2)}) collective-permute-start(bf16[576,256]{1,0:T(8,128)(2,1)S(1)} %slice.21), channel_id=1, source_target_pairs={{2,4},{3,5},{4,2},{5,3},{10,12},{11,13},{12,10},{13,11},{18,20},{1... | collective-permute-start | bytes 884744 | tf_op jit(solution)/shard_map/ppermute | solution.py:44
  77.1 12.0 %collective-permute-start.10 = (bf16[256,1152]{1,0:T(8,128)(2,1)S(1)}, bf16[256,1152]{1,0:T(8,128)(2,1)S(1)}, u32[]{:S(2)}, u32[]{:S(2)}) collective-permute-start(bf16[256,1152]{1,0:T(8,128)(2,1)S(1)} %pairs.1.dx), channel_id=1, source_target_pairs={{0,2},{1,3},{6,4},{7,5},{8,10},{9,11},{14,12},{15,13},{16,18},{17,... | collective-permute-start | bytes 1769480 | tf_op jit(solution)/shard_map/ppermute | solution.py:44
  78.4 12.9 %collective-permute-start.11 = (bf16[256,1152]{1,0:T(8,128)(2,1)S(1)}, bf16[256,1152]{1,0:T(8,128)(2,1)S(1)}, u32[]{:S(2)}, u32[]{:S(2)}) collective-permute-start(bf16[256,1152]{1,0:T(8,128)(2,1)S(1)} %pairs.1.dx), channel_id=1, source_target_pairs={{2,4},{3,5},{4,2},{5,3},{10,12},{11,13},{12,10},{13,11},{18,20},{1... | collective-permute-start | bytes 1769480 | tf_op jit(solution)/shard_map/ppermute | solution.py:44
  89.1 3.3 %collective-permute-start.14 = (bf16[256,640]{1,0:T(8,128)(2,1)S(1)}, bf16[256,640]{1,0:T(8,128)(2,1)S(1)}, u32[]{:S(2)}, u32[]{:S(2)}) collective-permute-start(bf16[256,640]{1,0:T(8,128)(2,1)S(1)} %slice.24), channel_id=1, source_target_pairs={{2,4},{3,5},{4,2},{5,3},{10,12},{11,13},{12,10},{13,11},{18,20},{1... | collective-permute-start | bytes 983048 | tf_op jit(solution)/shard_map/ppermute | solution.py:44
  89.9 2.6 %collective-permute-start.12 = (bf16[576,256]{1,0:T(8,128)(2,1)S(1)}, bf16[576,256]{1,0:T(8,128)(2,1)S(1)}, u32[]{:S(2)}, u32[]{:S(2)}) collective-permute-start(bf16[576,256]{1,0:T(8,128)(2,1)S(1)} %slice.22), channel_id=1, source_target_pairs={{2,4},{3,5},{4,2},{5,3},{10,12},{11,13},{12,10},{13,11},{18,20},{1... | collective-permute-start | bytes 884744 | tf_op jit(solution)/shard_map/ppermute | solution.py:44
  90.6 2.9 %collective-permute-start.13 = (bf16[256,512]{1,0:T(8,128)(2,1)S(1)}, bf16[256,512]{1,0:T(8,128)(2,1)S(1)}, u32[]{:S(2)}, u32[]{:S(2)}) collective-permute-start(bf16[256,512]{1,0:T(8,128)(2,1)S(1)} %slice.23), channel_id=1, source_target_pairs={{2,4},{3,5},{4,2},{5,3},{10,12},{11,13},{12,10},{13,11},{18,20},{1... | collective-permute-start | bytes 786440 | tf_op jit(solution)/shard_map/ppermute | solution.py:44
  94.4 40.3 %collective-permute-start.15 = (bf16[144,1152]{1,0:T(8,128)(2,1)S(1)}, bf16[144,1152]{1,0:T(8,128)(2,1)S(1)}, u32[]{:S(2)}, u32[]{:S(2)}) collective-permute-start(bf16[144,1152]{1,0:T(8,128)(2,1)S(1)} %get-tuple-element.31), channel_id=1, source_target_pairs={{0,1},{1,0},{2,3},{3,2},{4,5},{5,4},{6,7},{7,6},{8,9},{9,8},{10,11... | collective-permute-start | bytes 995336 | tf_op jit(solution)/shard_map/ppermute | solution.py:44
  99.1 35.6 %collective-permute-start.16 = (bf16[144,640]{1,0:T(8,128)(2,1)S(1)}, bf16[144,640]{1,0:T(8,128)(2,1)S(1)}, u32[]{:S(2)}, u32[]{:S(2)}) collective-permute-start(bf16[144,640]{1,0:T(8,128)(2,1)S(1)} %get-tuple-element.32), channel_id=1, source_target_pairs={{2,0},{3,1},{4,6},{5,7},{10,8},{11,9},{12,14},{13,15},{18,16},{19,... | collective-permute-start | bytes 552968 | tf_op jit(solution)/shard_map/ppermute | solution.py:44
  100.4 34.3 %collective-permute-start.17 = (bf16[144,640]{1,0:T(8,128)(2,1)S(1)}, bf16[144,640]{1,0:T(8,128)(2,1)S(1)}, u32[]{:S(2)}, u32[]{:S(2)}) collective-permute-start(bf16[144,640]{1,0:T(8,128)(2,1)S(1)} %get-tuple-element.33), channel_id=1, source_target_pairs={{2,1},{3,0},{4,7},{5,6},{10,9},{11,8},{12,15},{13,14},{18,17},{19,... | collective-permute-start | bytes 552968 | tf_op jit(solution)/shard_map/ppermute | solution.py:44
  101.7 29.8 %collective-permute-start.18 = (bf16[144,512]{1,0:T(8,128)(2,1)S(1)}, bf16[144,512]{1,0:T(8,128)(2,1)S(1)}, u32[]{:S(2)}, u32[]{:S(2)}) collective-permute-start(bf16[144,512]{1,0:T(8,128)(2,1)S(1)} %get-tuple-element.34), channel_id=1, source_target_pairs={{2,0},{3,1},{4,6},{5,7},{10,8},{11,9},{12,14},{13,15},{18,16},{19,... | collective-permute-start | bytes 442376 | tf_op jit(solution)/shard_map/ppermute | solution.py:44
  103.0 31.7 %collective-permute-start.19 = (bf16[144,512]{1,0:T(8,128)(2,1)S(1)}, bf16[144,512]{1,0:T(8,128)(2,1)S(1)}, u32[]{:S(2)}, u32[]{:S(2)}) collective-permute-start(bf16[144,512]{1,0:T(8,128)(2,1)S(1)} %get-tuple-element.35), channel_id=1, source_target_pairs={{2,1},{3,0},{4,7},{5,6},{10,9},{11,8},{12,15},{13,14},{18,17},{19,... | collective-permute-start | bytes 442376 | tf_op jit(solution)/shard_map/ppermute | solution.py:44

commit v2 on v1

v2 whole, which is shorter than its diff:
```python
import jax
import jax.numpy as jnp
from jax import lax
from jax.experimental import pallas as pl
from jax.experimental.pallas import tpu as pltpu
from jax.sharding import Mesh, PartitionSpec as P

NAMES = ("x", "zh", "y", "zl", "c")
NX, NZH, NY, NZL, NC = SIZES = (8, 2, 8, 4, 2)
ROWS = 128
D = 1152
CHIP = 288
CORE = 144
EPS = 1e-06
BF = jnp.bfloat16
F32 = jnp.float32
PROJECT_LIMIT = 58
VMEM = pl.BlockSpec(memory_space=pltpu.VMEM)
SMEM = pl.BlockSpec(memory_space=pltpu.SMEM)
ANY = pl.BlockSpec(memory_space=pl.ANY)
HBM = pl.BlockSpec(memory_space=pltpu.HBM)
PARAMS = pltpu.CompilerParams(vmem_limit_bytes=32 * 1024 * 1024)


def index_of(x, zh, y, zl, c):
    return (((x * NZH + zh) * NY + y) * NZL + zl) * NC + c


def pairs_of(rule):
    found = []
    for x in range(NX):
        for zh in range(NZH):
            for y in range(NY):
                for zl in range(NZL):
                    for c in range(NC):
                        target = rule(x, zh, y, zl, c)
                        if target is not None:
                            found.append((index_of(x, zh, y, zl, c), index_of(*target)))
    return found


def send(value, rule):
    return lax.ppermute(value, NAMES, pairs_of(rule))


def other_core(x, zh, y, zl, c):
    return (x, zh, y, zl, 1 - c)


def first_hop(x, zh, y, zl, c):
    if c == 1:
        return (x, zh, y + 1, zl, 0) if y < 7 else None
    return (x, zh, y - 1, zl, 1) if y > 0 else None


def second_hop(x, zh, y, zl, c):
    if not 1 <= y <= 6:
        return None
    return (x, zh, y + 1 if c == 0 else y - 1, zl, c)


def third_hop(x, zh, y, zl, c):
    if c == 0:
        return (x, zh, y + 1, zl, 0) if y < 7 else None
    return (x, zh, y - 1, zl, 1) if y > 0 else None


def above(x, zh, column):
    return (x, 1, column) if zh == 0 else ((x + 1) % NX, 0, column)


def below(x, zh, column):
    return (x, 0, column) if zh == 1 else ((x - 1) % NX, 1, column)


def first_crossing(x, zh, y, zl, c):
    if c == 1 and y == 7:
        return (*above(x, zh, 1), zl, 0)
    if c == 0 and y == 0:
        return (*below(x, zh, 6), zl, 1)
    return None


def later_crossing(x, zh, y, zl, c):
    if c == 0 and y == 7:
        return (*above(x, zh, 0), zl, 0)
    if c == 1 and y == 0:
        return (*below(x, zh, 7), zl, 1)
    return None


def from_second(x, zh, y, zl, c):
    if c == 0 and y == 1:
        return (x, zh, 0, zl, 0)
    if c == 1 and y == 6:
        return (x, zh, 7, zl, 1)
    return None


def inward(x, zh, y, zl, c):
    return {0: (x, zh, y, 1, c), 3: (x, zh, y, 2, c)}.get(zl)


def middle(x, zh, y, zl, c):
    return {1: (x, zh, y, 2, c), 2: (x, zh, y, 1, c)}.get(zl)


def outward(x, zh, y, zl, c):
    return {1: (x, zh, y, 0, c), 2: (x, zh, y, 3, c)}.get(zl)


def outward_cross(x, zh, y, zl, c):
    return {1: (x, zh, y, 0, 1 - c), 2: (x, zh, y, 3, 1 - c)}.get(zl)


def project_kernel(
    flags, pictures, captions, recv, wp, wc, z_ref, u_ref, rn_ref, f_ref, w_ref, sems
):
    c = flags[0]
    parts = 3
    width = D // parts

    def fetch(feats, head):
        pltpu.make_async_copy(feats, f_ref.at[pl.ds(0, ROWS)], sems.at[parts]).start()
        for j in range(parts):
            cols = pl.ds(j * width, width)
            pltpu.make_async_copy(head.at[:, cols], w_ref.at[j], sems.at[j]).start()

    @pl.when(c == 0)
    def _():
        fetch(pictures, wp)

    @pl.when(c == 1)
    def _():
        fetch(captions, wc)

    f_ref[ROWS:] = recv[...]
    pltpu.make_async_copy(pictures, f_ref.at[pl.ds(0, ROWS)], sems.at[parts]).wait()
    total = jnp.zeros((2 * ROWS, 1), F32)
    for j in range(parts):
        cols = pl.ds(j * width, width)
        pltpu.make_async_copy(wp.at[:, cols], w_ref.at[j], sems.at[j]).wait()
        x = jnp.dot(f_ref[...], w_ref[j], preferred_element_type=F32)
        u_ref[:, cols] = x
        total = total + jnp.sum(x * x, axis=-1, keepdims=True)
    rn = 1.0 / jnp.sqrt(total + EPS)
    rn_ref[...] = jnp.broadcast_to(rn, (2 * ROWS, 128))
    u = u_ref[...] * rn
    u_ref[...] = u
    z_ref[...] = u.astype(BF)


def project(flags, pictures, captions, recv, wp, wc):
    rows = 2 * ROWS
    return pl.pallas_call(
        project_kernel,
        name="project",
        out_shape=(
            jax.ShapeDtypeStruct((rows, D), BF),
            jax.ShapeDtypeStruct((rows, D), F32),
            jax.ShapeDtypeStruct((rows, 128), F32),
        ),
        in_specs=[SMEM, HBM, HBM, VMEM, HBM, HBM],
        out_specs=(VMEM,) * 3,
        scratch_shapes=[
            pltpu.VMEM((rows, D), BF),
            pltpu.VMEM((3, D, D // 3), BF),
            pltpu.SemaphoreType.DMA((4,)),
        ],
        compiler_params=pltpu.CompilerParams(vmem_limit_bytes=PROJECT_LIMIT * 1024 * 1024),
        cost_estimate=pl.CostEstimate(
            flops=2 * rows * D * D, bytes_accessed=2 * D * D + 8 * rows * D, transcendentals=0
        ),
    )(flags, pictures, captions, recv, wp, wc)


def turn_kernel(flags, pictures, captions, recv, ft_ref, turned, f_ref, sem):
    mirror = flags[3]

    @pl.when(flags[0] == 0)
    def _():
        pltpu.make_async_copy(pictures, f_ref, sem).start()

    @pl.when(flags[0] == 1)
    def _():
        pltpu.make_async_copy(captions, f_ref, sem).start()

    turned[:, ROWS:] = recv[...].T
    pltpu.make_async_copy(pictures, f_ref, sem).wait()
    turned[:, :ROWS] = f_ref[...].T
    for j in range(4):
        start = pl.multiple_of(jnp.where(mirror == 1, 3 - j, j) * CHIP, CHIP)
        ft_ref[j * CHIP : (j + 1) * CHIP] = turned[pl.ds(start, CHIP)]


def turn(flags, pictures, captions, recv):
    return pl.pallas_call(
        turn_kernel,
        name="turn",
        out_shape=jax.ShapeDtypeStruct((D, 2 * ROWS), BF),
        in_specs=[SMEM, HBM, HBM, VMEM],
        out_specs=VMEM,
        scratch_shapes=[
            pltpu.VMEM((D, 2 * ROWS), BF),
            pltpu.VMEM((ROWS, D), BF),
            pltpu.SemaphoreType.DMA(()),
        ],
        compiler_params=PARAMS,
        cost_estimate=pl.CostEstimate(
            flops=0, bytes_accessed=8 * ROWS * D, transcendentals=0
        ),
    )(flags, pictures, captions, recv)


def choose_kernel(flags, two, cross_one, cross_two, out_ref, sem):
    place = flags[1]

    @pl.when(place == 0)
    def _():
        pltpu.make_async_copy(cross_two, out_ref, sem).start()

    @pl.when(place == 1)
    def _():
        pltpu.make_async_copy(cross_one, out_ref, sem).start()

    @pl.when(place > 1)
    def _():
        pltpu.make_async_copy(two, out_ref, sem).start()

    pltpu.make_async_copy(two, out_ref, sem).wait()


def choose(flags, two, cross_one, cross_two):
    return pl.pallas_call(
        choose_kernel,
        name="choose",
        out_shape=jax.ShapeDtypeStruct((2 * ROWS, D), BF),
        in_specs=[SMEM] + [ANY] * 3,
        out_specs=VMEM,
        scratch_shapes=[pltpu.SemaphoreType.DMA(())],
        compiler_params=PARAMS,
        cost_estimate=pl.CostEstimate(
            flops=0, bytes_accessed=8 * ROWS * D, transcendentals=0
        ),
    )(flags, two, cross_one, cross_two)


def pairs_kernel(
    flags, scale, z_ref, u_ref, rn_ref,
    here, one, two, three, cross_one, cross_two, cross_three, second, early_mid, early_far,
    dx_ref, others, sems,
):
    del early_mid, early_far
    place = flags[1]

    def fetch(source, s):
        for b in range(2):
            pltpu.make_async_copy(
                source.at[pl.ds((1 - b) * ROWS, ROWS)],
                others.at[b, pl.ds(s * ROWS, ROWS)],
                sems.at[2 * s + b],
            ).start()

    fetch(here, 0)

    @pl.when(place > 0)
    def _():
        fetch(one, 1)
        fetch(three, 3)

    @pl.when(place == 0)
    def _():
        fetch(second, 1)
        fetch(cross_two, 2)
        fetch(cross_three, 3)

    @pl.when(place == 1)
    def _():
        fetch(cross_one, 2)

    @pl.when(place > 1)
    def _():
        fetch(two, 2)

    t = scale[0]
    bias = scale[1]
    for s in range(4):
        for b in range(2):
            pltpu.make_async_copy(
                here.at[pl.ds(0, ROWS)],
                others.at[b, pl.ds(s * ROWS, ROWS)],
                sems.at[2 * s + b],
            ).wait()
    row = lax.broadcasted_iota(jnp.int32, (ROWS, 4 * ROWS), 0)
    col = lax.broadcasted_iota(jnp.int32, (ROWS, 4 * ROWS), 1)
    for b in range(2):
        mine = z_ref[b * ROWS : (b + 1) * ROWS]
        logits = t * lax.dot_general(
            mine, others[b], (((1,), (1,)), ((), ())), preferred_element_type=F32
        ) + bias
        prob = jax.nn.sigmoid(logits) - jnp.where(row == col, 1.0, 0.0)
        weight = (prob * (1.0 / ROWS)).astype(BF)
        dz = t * jnp.dot(weight, others[b], preferred_element_type=F32)
        u = u_ref[b * ROWS : (b + 1) * ROWS]
        rn = rn_ref[b * ROWS : (b + 1) * ROWS, :1]
        inner = jnp.sum(u * dz, axis=-1, keepdims=True)
        dx_ref[b * ROWS : (b + 1) * ROWS] = ((dz - u * inner) * rn).astype(BF)


def pairs(flags, scale, z, *rest):
    rows = 2 * ROWS
    return pl.pallas_call(
        pairs_kernel,
        name="pairs",
        out_shape=jax.ShapeDtypeStruct((rows, D), BF),
        in_specs=[SMEM, SMEM] + [VMEM] * 3 + [ANY] * 10,
        out_specs=VMEM,
        scratch_shapes=[
            pltpu.VMEM((2, 4 * ROWS, D), BF),
            pltpu.SemaphoreType.DMA((8,)),
        ],
        compiler_params=PARAMS,
        cost_estimate=pl.CostEstimate(
            flops=16 * rows * ROWS * D, bytes_accessed=14 * rows * D, transcendentals=rows * 512
        ),
    )(flags, scale, z, *rest)


def near_kernel(ft, dx, feats_end, dx_end, feats_mid, dx_mid, inner_ref, outer_ref):
    dx_own = dx[...]
    dx_other = dx_mid[...]
    inner_ref[...] = (
        jnp.dot(ft[CHIP : 2 * CHIP], dx_own, preferred_element_type=F32)
        + jnp.dot(feats_end[:CHIP], dx_end[...], preferred_element_type=F32)
        + jnp.dot(feats_mid[:CHIP], dx_other, preferred_element_type=F32)
    )
    outer_ref[...] = jnp.dot(ft[:CHIP], dx_own, preferred_element_type=F32) + jnp.dot(
        feats_mid[CHIP:], dx_other, preferred_element_type=F32
    )


def near(ft, dx, feats_end, dx_end, feats_mid, dx_mid):
    return pl.pallas_call(
        near_kernel,
        name="near",
        out_shape=(
            jax.ShapeDtypeStruct((CHIP, D), F32),
            jax.ShapeDtypeStruct((CHIP, D), F32),
        ),
        in_specs=[VMEM] * 6,
        out_specs=(VMEM,) * 2,
        compiler_params=PARAMS,
        cost_estimate=pl.CostEstimate(
            flops=20 * CHIP * ROWS * D, bytes_accessed=14 * CHIP * D, transcendentals=0
        ),
    )(ft, dx, feats_end, dx_end, feats_mid, dx_mid)


def far_kernel(flags, outer_ref, feats, dx, same, crossed, part):
    c = flags[0]
    part[...] = outer_ref[...] + jnp.dot(
        feats[CHIP:], dx[...], preferred_element_type=F32
    )
    mine = pl.ds(pl.multiple_of(c * CORE, CORE), CORE)
    theirs = pl.ds(pl.multiple_of((1 - c) * CORE, CORE), CORE)
    same[...] = part[mine].astype(BF)
    crossed[...] = part[theirs].astype(BF)


def far(flags, outer, feats, dx):
    return pl.pallas_call(
        far_kernel,
        name="far",
        out_shape=(
            jax.ShapeDtypeStruct((CORE, D), BF),
            jax.ShapeDtypeStruct((CORE, D), BF),
            jax.ShapeDtypeStruct((CHIP, D), F32),
        ),
        in_specs=[SMEM] + [VMEM] * 3,
        out_specs=(VMEM,) * 3,
        compiler_params=PARAMS,
        cost_estimate=pl.CostEstimate(
            flops=4 * CHIP * ROWS * D, bytes_accessed=14 * CHIP * D, transcendentals=0
        ),
    )(flags, outer, feats, dx)


def rest_kernel(flags, inner_ref, feats, dx, part, keep, swap, total):
    c = flags[0]
    mine = pl.ds(pl.multiple_of(c * CORE, CORE), CORE)
    theirs = pl.ds(pl.multiple_of((1 - c) * CORE, CORE), CORE)

    @pl.when(flags[4] == 1)
    def _():
        total[...] = inner_ref[...] + jnp.dot(
            feats[:CHIP], dx[...], preferred_element_type=F32
        )
        keep[...] = total[mine]
        swap[...] = total[theirs].astype(BF)

    @pl.when(flags[4] == 0)
    def _():
        keep[...] = part[mine]
        swap[...] = part[theirs].astype(BF)


def rest(flags, *parts):
    return pl.pallas_call(
        rest_kernel,
        name="rest",
        out_shape=(
            jax.ShapeDtypeStruct((CORE, D), F32),
            jax.ShapeDtypeStruct((CORE, D), BF),
        ),
        in_specs=[SMEM] + [VMEM] * 4,
        out_specs=(VMEM, VMEM),
        scratch_shapes=[pltpu.VMEM((CHIP, D), F32)],
        compiler_params=PARAMS,
        cost_estimate=pl.CostEstimate(
            flops=4 * CHIP * ROWS * D, bytes_accessed=14 * CHIP * D, transcendentals=0
        ),
    )(flags, *parts)


def finish_kernel(flags, same, crossed, swap, keep, image_ref, text_ref):
    own = keep[...] + same[...].astype(F32)
    other = swap[...].astype(F32) + crossed[...].astype(F32)

    @pl.when(flags[0] == 0)
    def _():
        image_ref[0] = own
        text_ref[0] = other

    @pl.when(flags[0] == 1)
    def _():
        image_ref[0] = other
        text_ref[0] = own


def finish(flags, *parts):
    shape = jax.ShapeDtypeStruct((1, CORE, D), F32)
    return pl.pallas_call(
        finish_kernel,
        name="finish",
        out_shape=(shape, shape),
        in_specs=[SMEM] + [VMEM] * 4,
        out_specs=(VMEM, VMEM),
        compiler_params=PARAMS,
        cost_estimate=pl.CostEstimate(
            flops=4 * CORE * D, bytes_accessed=18 * CORE * D, transcendentals=0
        ),
    )(flags, *parts)


def on_device(pictures, captions, picture_head, caption_head, sharpness, shift_term):
    c = lax.axis_index("c")
    y = lax.axis_index("y")
    zl = lax.axis_index("zl")
    yy = jnp.where(c == 0, y, 7 - y)
    flags = jnp.stack([c, yy, zl, zl >= 2, (zl == 1) | (zl == 2)]).astype(jnp.int32)
    scale = jnp.concatenate([sharpness, shift_term])

    received = send(jnp.where(c == 0, captions, pictures), other_core)
    z, u, rn = project(flags, pictures, captions, received, picture_head, caption_head)

    one = send(z, first_hop)
    cross_one = send(z, first_crossing)
    here = send(z, other_core)
    ft = turn(flags, pictures, captions, received)
    one, ft = lax.optimization_barrier((one, ft))
    two = send(one, second_hop)
    ft_end = send(ft[CHIP:], inward)
    ft_mid = send(ft[2 * CHIP :], middle)
    cross_two = send(one, later_crossing)
    cross_three = send(two, later_crossing)
    second = send(cross_one, from_second)
    three = send(choose(flags, two, cross_one, cross_two), third_hop)
    ft_far = send(ft_end[CHIP:], middle)
    dx = pairs(
        flags, scale, z, u, rn,
        here, one, two, three, cross_one, cross_two, cross_three, second, ft_mid, ft_far,
    )

    dx_end = send(dx, inward)
    dx_mid = send(dx, middle)
    dx_far = send(dx_end, middle)
    inner, outer = near(ft, dx, ft_end, dx_end, ft_mid, dx_mid)
    same, crossed, part = far(flags, outer, ft_far, dx_far)
    same = send(same, outward)
    crossed = send(crossed, outward_cross)
    keep, swap = rest(flags, inner, ft_far, dx_far, part)
    swap = send(swap, other_core)
    return finish(flags, same, crossed, swap, keep)


def solution(mesh):
    physical = Mesh(mesh.devices.reshape(SIZES), NAMES)
    rows = P(NAMES, None)
    grad = P(("x", "zh", "y"), ("zl", "c"), None)
    return jax.shard_map(
        on_device,
        mesh=physical,
        in_specs=(rows, rows, P(), P(), P(), P()),
        out_specs=(grad, grad),
        check_vma=False,
    )
```

time: 137 us -> 150 us (1.095)
  starting transfers between devices: 40.5 us -> 74.3 us
  waiting for transfers between devices: 75.4 us -> 54.8 us
  local copies, waits for them, and re-layouts: 5.64 us -> 2.45 us
  Pallas kernels: 11.5 us -> 14.5 us
    ppermute x20 -> x18, starting transfers between devices: 40.5 us -> 74.3 us  [send(): return lax.ppermute(value, NAMES, pairs_of(rule))]
    ppermute x20 -> x18, waiting for transfers between devices: 75.4 us -> 54.8 us  [send(): return lax.ppermute(value, NAMES, pairs_of(rule))]
    unnamed x12 -> x16, local copies, waits for them, and re-layouts: 5.43 us -> 1.69 us
    pallas_call x4, Pallas kernels: 4.75 us -> 7.67 us  [the longest x1 5.35 us: project(): pl.pallas_call(project_kernel, name='project', out_shape=(jax.ShapeDtypeS...]
  transfers between devices with their start and end apart: 20 -> 18, of which waited for: 7 -> 8; matrix products, arithmetic and copies ran while one was open for 0% -> 1% of each run, Pallas kernels for 4% -> 2%
where the time goes in v2:
time: 150 us; the launch traced here: 149 us
  starting transfers between devices  74.3 us (50%)
  waiting for transfers between devices  54.8 us (37%)
  Pallas kernels  14.5 us (10%)
  local copies, waits for them, and re-layouts  2.45 us (2%)
  between operations  2.28 us (2%)
    ppermute x18, starting transfers between devices, send(): return lax.ppermute(value, NAMES, pairs_of(rule))  74.3 us
    ppermute x18, waiting for transfers between devices, send(): return lax.ppermute(value, NAMES, pairs_of(rule))  54.8 us
    pallas_call x1, Pallas kernels, project(): pl.pallas_call(project_kernel, name='project', out_shape=(jax.ShapeDtypeS...  5.35 us
  transfers between devices with their start and end apart: 18, of which 8 were waited for; matrix products, arithmetic and copies ran while one was open for 1% of the time, Pallas kernels for 2%

profile of v2, /device:TPU:1, one launch (start us, length us, event | category | flops | bytes accessed | tf_op | source)
XLA Modules:
  0.0 149.3 jit_solution(9578563348616979135)
XLA Ops:
  0.6 1.0 broadcast_select_fusion
  1.6 16.1 %collective-permute-start = (bf16[128,1152]{1,0:T(8,128)(2,1)S(1)}, bf16[128,1152]{1,0:T(8,128)(2,1)S(1)}, u32[]{:S(2)}, u32[]{:S(2)}) collective-permute-start(bf16[128,1152]{1,0:T(8,128)(2,1)S(1)} %broadcast_select_fusion), channel_id=1, source_target_pairs={{0,1},{1,0},{2,3},{3,2},{4,5},{5,4},{6,7},{7,6},{8,9},{9,8},{10,11... | collective-permute-start | bytes 884744 | tf_op jit(solution)/shard_map/ppermute | solution.py:43
  17.7 0.7 stack.31.flags
  18.4 0.0 copy-start
  18.4 0.0 copy-start.1
  18.4 0.0 copy-start.7
  18.4 0.5 collective-permute-done.recv
  18.9 0.0 copy-start.2
  18.9 0.7 copy-done.2
  19.6 5.4 %project.1 = (bf16[256,1152]{1,0:T(8,128)(2,1)}, f32[256,1152]{1,0:T(8,128)}, f32[256,128]{1,0:T(8,128)}) custom-call(s32[5]{0:T(128)} %stack.31.flags, bf16[128,1152]{1,0:T(8,128)(2,1)} %pictures.3, bf16[128,1152]{1,0:T(8,128)(2,1)} %captions.3, bf16[128,1152]{1,0:T(8,128)(2,1)} %copy-done.2, bf16[1152,1152]{1,0:T(8,128)(2,1)} %wp.1, bf16[1152,1152]{1,0:T(8,128)(2,1)} %wc.1), custom_call_target="tpu_custom_call" | custom-call | flops 679477248 | bytes 5013504 | tf_op jit(solution)/shard_map/project/pallas_call | solution.py:155
  25.0 1.9 %collective-permute-start.1 = (bf16[256,1152]{1,0:T(8,128)(2,1)}, bf16[256,1152]{1,0:T(8,128)(2,1)S(1)}, u32[]{:S(2)}, u32[]{:S(2)}) collective-permute-start(bf16[256,1152]{1,0:T(8,128)(2,1)} %get-tuple-element.14.z_ref), channel_id=1, source_target_pairs={{1,8},{3,10},{5,12},{7,14},{8,1},{9,16},{10,3},{11,18},{12,5},{13,... | collective-permute-start | bytes 1769480 | tf_op jit(solution)/shard_map/ppermute | solution.py:43
  26.9 0.7 collective-permute-start.4
  27.6 0.0 copy-done
  27.6 0.0 copy-done.1
  27.6 0.0 copy-done.7
  27.6 0.0 copy-start.3
  27.7 1.0 copy-done.3
  28.6 0.0 copy-start.5
  28.6 1.0 turn.1.ft
  29.6 6.8 %collective-permute-done.1.one = bf16[256,1152]{1,0:T(8,128)(2,1)S(1)} collective-permute-done((bf16[256,1152]{1,0:T(8,128)(2,1)}, bf16[256,1152]{1,0:T(8,128)(2,1)S(1)}, u32[]{:S(2)}, u32[]{:S(2)}) %collective-permute-start.1) | collective-permute-done | bytes 589856 | tf_op jit(solution)/shard_map/ppermute | solution.py:43
  36.4 7.4 %collective-permute-start.5 = (bf16[256,1152]{1,0:T(8,128)(2,1)S(1)}, bf16[256,1152]{1,0:T(8,128)(2,1)S(1)}, u32[]{:S(2)}, u32[]{:S(2)}) collective-permute-start(bf16[256,1152]{1,0:T(8,128)(2,1)S(1)} %collective-permute-done.1.one), channel_id=1, source_target_pairs={{1,1017},{3,1019},{5,1021},{7,1023},{56,64},{58,66},{60,68},{62,70... | collective-permute-start | bytes 1769480 | tf_op jit(solution)/shard_map/ppermute | solution.py:43
  43.8 1.3 collective-permute-start.3
  45.1 0.0 copy-done.5
  45.1 1.9 %collective-permute-start.2 = (bf16[256,1152]{1,0:T(8,128)(2,1)S(1)}, bf16[256,1152]{1,0:T(8,128)(2,1)S(1)}, u32[]{:S(2)}, u32[]{:S(2)}) collective-permute-start(bf16[256,1152]{1,0:T(8,128)(2,1)S(1)} %copy-done.5), channel_id=1, source_target_pairs={{0,1},{1,0},{2,3},{3,2},{4,5},{5,4},{6,7},{7,6},{8,9},{9,8},{10,11... | collective-permute-start | bytes 1769480 | tf_op jit(solution)/shard_map/ppermute | solution.py:43
  47.1 0.0 copy-start.4
  47.1 0.0 copy-start.6
  47.1 1.4 collective-permute-start.10
  48.6 0.0 collective-permute-done.4.cross_one
  48.6 0.7 collective-permute-start.8
  49.3 5.2 %collective-permute-done.5.cross_two = bf16[256,1152]{1,0:T(8,128)(2,1)S(1)} collective-permute-done((bf16[256,1152]{1,0:T(8,128)(2,1)S(1)}, bf16[256,1152]{1,0:T(8,128)(2,1)S(1)}, u32[]{:S(2)}, u32[]{:S(2)}) %collective-permute-start.5) | collective-permute-done | bytes 589856 | tf_op jit(solution)/shard_map/ppermute | solution.py:43
  54.5 0.3 collective-permute-done.3.two
  54.7 0.7 choose.1
  55.4 1.3 collective-permute-start.6
  56.7 14.9 %collective-permute-start.7 = (bf16[256,1152]{1,0:T(8,128)(2,1)S(1)}, bf16[256,1152]{1,0:T(8,128)(2,1)S(1)}, u32[]{:S(2)}, u32[]{:S(2)}) collective-permute-start(bf16[256,1152]{1,0:T(8,128)(2,1)S(1)} %collective-permute-done.3.two), channel_id=1, source_target_pairs={{1,1017},{3,1019},{5,1021},{7,1023},{56,64},{58,66},{60,68},{62,70... | collective-permute-start | bytes 1769480 | tf_op jit(solution)/shard_map/ppermute | solution.py:43
  71.6 0.0 collective-permute-done.10.feats_end
  71.6 0.7 collective-permute-start.9
  72.4 0.0 collective-permute-done.2.here
  72.4 0.7 collective-permute-start.11
  74.3 0.1 pad_maximum_fusion.scale
  74.4 0.0 collective-permute-done.9.early_mid.feats_mid
  74.4 0.0 collective-permute-done.8.second
  74.4 0.0 collective-permute-done.11.early_far.feats
  74.4 0.0 collective-permute-done.6.three
  74.4 5.4 %collective-permute-done.7.cross_three = bf16[256,1152]{1,0:T(8,128)(2,1)S(1)} collective-permute-done((bf16[256,1152]{1,0:T(8,128)(2,1)S(1)}, bf16[256,1152]{1,0:T(8,128)(2,1)S(1)}, u32[]{:S(2)}, u32[]{:S(2)}) %collective-permute-start.7) | collective-permute-done | bytes 589856 | tf_op jit(solution)/shard_map/ppermute | solution.py:43
  79.8 0.0 copy-done.4
  79.9 0.0 copy-done.6
  79.9 2.8 %pairs.1.dx = bf16[256,1152]{1,0:T(8,128)(2,1)S(1)} custom-call(s32[5]{0:T(128)S(1)} %copy-done.7, f32[2]{0:T(128)S(1)} %pad_maximum_fusion.scale, bf16[256,1152]{1,0:T(8,128)(2,1)S(1)} %copy-done.5, f32[256,1152]{1,0:T(8,128)S(1)} %copy-done.4, f32[256,128]{1,0:T(8,128)S(1)} %copy-done.6, bf16[256,1152]{1,0:T(8,128)(2,1)S(1)} %collective-permute-done.2.here, ...), custom_call_target="tpu_custom_call" | custom-call | flops 603979776 | bytes 4128768 | tf_op jit(solution)/shard_map/pairs/pallas_call | solution.py:312
  82.7 17.9 %collective-permute-start.12 = (bf16[256,1152]{1,0:T(8,128)(2,1)S(1)}, bf16[256,1152]{1,0:T(8,128)(2,1)S(1)}, u32[]{:S(2)}, u32[]{:S(2)}) collective-permute-start(bf16[256,1152]{1,0:T(8,128)(2,1)S(1)} %pairs.1.dx), channel_id=1, source_target_pairs={{0,2},{1,3},{6,4},{7,5},{8,10},{9,11},{14,12},{15,13},{16,18},{17,... | collective-permute-start | bytes 1769480 | tf_op jit(solution)/shard_map/ppermute | solution.py:43
  100.6 0.7 collective-permute-start.13
  101.3 11.3 %collective-permute-done.12.dx_end = bf16[256,1152]{1,0:T(8,128)(2,1)S(1)} collective-permute-done((bf16[256,1152]{1,0:T(8,128)(2,1)S(1)}, bf16[256,1152]{1,0:T(8,128)(2,1)S(1)}, u32[]{:S(2)}, u32[]{:S(2)}) %collective-permute-start.12) | collective-permute-done | bytes 589856 | tf_op jit(solution)/shard_map/ppermute | solution.py:43
  112.6 0.7 collective-permute-start.14
  113.3 0.0 collective-permute-done.13.dx_mid
  113.3 1.1 near.1
  114.5 0.0 collective-permute-done.14.dx
  114.5 1.0 far.1
  115.5 1.3 collective-permute-start.15
  116.8 1.3 collective-permute-start.16
  118.1 0.6 rest.1
  118.7 3.4 %collective-permute-start.17 = (bf16[144,1152]{1,0:T(8,128)(2,1)S(1)}, bf16[144,1152]{1,0:T(8,128)(2,1)S(1)}, u32[]{:S(2)}, u32[]{:S(2)}) collective-permute-start(bf16[144,1152]{1,0:T(8,128)(2,1)S(1)} %get-tuple-element.24), channel_id=1, source_target_pairs={{0,1},{1,0},{2,3},{3,2},{4,5},{5,4},{6,7},{7,6},{8,9},{9,8},{10,11... | collective-permute-start | bytes 995336 | tf_op jit(solution)/shard_map/ppermute | solution.py:43
  122.1 15.9 %collective-permute-done.15.same = bf16[144,1152]{1,0:T(8,128)(2,1)S(1)} collective-permute-done((bf16[144,1152]{1,0:T(8,128)(2,1)S(1)}, bf16[144,1152]{1,0:T(8,128)(2,1)S(1)}, u32[]{:S(2)}, u32[]{:S(2)}) %collective-permute-start.15) | collective-permute-done | bytes 331808 | tf_op jit(solution)/shard_map/ppermute | solution.py:43
  138.0 9.5 %collective-permute-done.16.crossed = bf16[144,1152]{1,0:T(8,128)(2,1)S(1)} collective-permute-done((bf16[144,1152]{1,0:T(8,128)(2,1)S(1)}, bf16[144,1152]{1,0:T(8,128)(2,1)S(1)}, u32[]{:S(2)}, u32[]{:S(2)}) %collective-permute-start.16) | collective-permute-done | bytes 331808 | tf_op jit(solution)/shard_map/ppermute | solution.py:43
  147.5 0.0 collective-permute-done.17.swap
  147.5 1.9 %finish.1 = (f32[1,144,1152]{2,1,0:T(8,128)}, f32[1,144,1152]{2,1,0:T(8,128)}) custom-call(s32[5]{0:T(128)S(1)} %copy-done.7, bf16[144,1152]{1,0:T(8,128)(2,1)S(1)} %collective-permute-done.15.same, bf16[144,1152]{1,0:T(8,128)(2,1)S(1)} %collective-permute-done.16.crossed, bf16[144,1152]{1,0:T(8,128)(2,1)S(1)} %collective-permute-done.17.swap, ...), custom_call_target="tpu_custom_call" | custom-call | flops 663552 | bytes 2985984 | tf_op jit(solution)/shard_map/finish/pallas_call | solution.py:442
  (3 shorter events, 0.1 us)
Async XLA Ops:
  1.6 17.3 %collective-permute-start = (bf16[128,1152]{1,0:T(8,128)(2,1)S(1)}, bf16[128,1152]{1,0:T(8,128)(2,1)S(1)}, u32[]{:S(2)}, u32[]{:S(2)}) collective-permute-start(bf16[128,1152]{1,0:T(8,128)(2,1)S(1)} %broadcast_select_fusion), channel_id=1, source_target_pairs={{0,1},{1,0},{2,3},{3,2},{4,5},{5,4},{6,7},{7,6},{8,9},{9,8},{10,11... | collective-permute-start | bytes 884744 | tf_op jit(solution)/shard_map/ppermute | solution.py:43
  18.4 9.2 %copy-start = (bf16[128,1152]{1,0:T(8,128)(2,1)S(1)}, bf16[128,1152]{1,0:T(8,128)(2,1)}, u32[]{:S(2)}) copy-start(bf16[128,1152]{1,0:T(8,128)(2,1)} %pictures.3) | copy-start | bytes 884740
  18.4 9.2 %copy-start.1 = (bf16[128,1152]{1,0:T(8,128)(2,1)S(1)}, bf16[128,1152]{1,0:T(8,128)(2,1)}, u32[]{:S(2)}) copy-start(bf16[128,1152]{1,0:T(8,128)(2,1)} %captions.3) | copy-start | bytes 884740
  18.4 9.2 %copy-start.7 = (s32[5]{0:T(128)S(1)}, s32[5]{0:T(128)}, u32[]{:S(2)}) copy-start(s32[5]{0:T(128)} %stack.31.flags) | copy-start | bytes 64
  18.9 0.7 copy-start.2
  25.0 11.4 %collective-permute-start.1 = (bf16[256,1152]{1,0:T(8,128)(2,1)}, bf16[256,1152]{1,0:T(8,128)(2,1)S(1)}, u32[]{:S(2)}, u32[]{:S(2)}) collective-permute-start(bf16[256,1152]{1,0:T(8,128)(2,1)} %get-tuple-element.14.z_ref), channel_id=1, source_target_pairs={{1,8},{3,10},{5,12},{7,14},{8,1},{9,16},{10,3},{11,18},{12,5},{13,... | collective-permute-start | bytes 1769480 | tf_op jit(solution)/shard_map/ppermute | solution.py:43
  26.9 21.7 %collective-permute-start.4 = (bf16[256,1152]{1,0:T(8,128)(2,1)}, bf16[256,1152]{1,0:T(8,128)(2,1)S(1)}, u32[]{:S(2)}, u32[]{:S(2)}) collective-permute-start(bf16[256,1152]{1,0:T(8,128)(2,1)} %get-tuple-element.14.z_ref), channel_id=1, source_target_pairs={{0,1009},{2,1011},{4,1013},{6,1015},{57,72},{59,74},{61,76},{63,78... | collective-permute-start | bytes 1769480 | tf_op jit(solution)/shard_map/ppermute | solution.py:43
  27.6 1.0 copy-start.3
  28.6 16.5 %copy-start.5 = (bf16[256,1152]{1,0:T(8,128)(2,1)S(1)}, bf16[256,1152]{1,0:T(8,128)(2,1)}, u32[]{:S(2)}) copy-start(bf16[256,1152]{1,0:T(8,128)(2,1)} %get-tuple-element.14.z_ref) | copy-start | bytes 1769476
  36.4 18.1 %collective-permute-start.5 = (bf16[256,1152]{1,0:T(8,128)(2,1)S(1)}, bf16[256,1152]{1,0:T(8,128)(2,1)S(1)}, u32[]{:S(2)}, u32[]{:S(2)}) collective-permute-start(bf16[256,1152]{1,0:T(8,128)(2,1)S(1)} %collective-permute-done.1.one), channel_id=1, source_target_pairs={{1,1017},{3,1019},{5,1021},{7,1023},{56,64},{58,66},{60,68},{62,70... | collective-permute-start | bytes 1769480 | tf_op jit(solution)/shard_map/ppermute | solution.py:43
  43.8 10.9 %collective-permute-start.3 = (bf16[256,1152]{1,0:T(8,128)(2,1)S(1)}, bf16[256,1152]{1,0:T(8,128)(2,1)S(1)}, u32[]{:S(2)}, u32[]{:S(2)}) collective-permute-start(bf16[256,1152]{1,0:T(8,128)(2,1)S(1)} %collective-permute-done.1.one), channel_id=1, source_target_pairs={{8,16},{9,1},{10,18},{11,3},{12,20},{13,5},{14,22},{15,7},{16,24},... | collective-permute-start | bytes 1769480 | tf_op jit(solution)/shard_map/ppermute | solution.py:43
  45.1 27.2 %collective-permute-start.2 = (bf16[256,1152]{1,0:T(8,128)(2,1)S(1)}, bf16[256,1152]{1,0:T(8,128)(2,1)S(1)}, u32[]{:S(2)}, u32[]{:S(2)}) collective-permute-start(bf16[256,1152]{1,0:T(8,128)(2,1)S(1)} %copy-done.5), channel_id=1, source_target_pairs={{0,1},{1,0},{2,3},{3,2},{4,5},{5,4},{6,7},{7,6},{8,9},{9,8},{10,11... | collective-permute-start | bytes 1769480 | tf_op jit(solution)/shard_map/ppermute | solution.py:43
  47.1 32.8 %copy-start.4 = (f32[256,1152]{1,0:T(8,128)S(1)}, f32[256,1152]{1,0:T(8,128)}, u32[]{:S(2)}) copy-start(f32[256,1152]{1,0:T(8,128)} %get-tuple-element.16.u_ref) | copy-start | bytes 3538948
  47.1 32.7 %copy-start.6 = (f32[256,128]{1,0:T(8,128)S(1)}, f32[256,128]{1,0:T(8,128)}, u32[]{:S(2)}) copy-start(f32[256,128]{1,0:T(8,128)} %get-tuple-element.17.rn_ref) | copy-start | bytes 393220
  47.1 24.5 %collective-permute-start.10 = (bf16[864,256]{1,0:T(8,128)(2,1)S(1)}, bf16[864,256]{1,0:T(8,128)(2,1)S(1)}, u32[]{:S(2)}, u32[]{:S(2)}) collective-permute-start(bf16[864,256]{1,0:T(8,128)(2,1)S(1)} %slice.10), channel_id=1, source_target_pairs={{0,2},{1,3},{6,4},{7,5},{8,10},{9,11},{14,12},{15,13},{16,18},{17,... | collective-permute-start | bytes 1327112 | tf_op jit(solution)/shard_map/ppermute | solution.py:43
  48.6 25.8 %collective-permute-start.8 = (bf16[256,1152]{1,0:T(8,128)(2,1)S(1)}, bf16[256,1152]{1,0:T(8,128)(2,1)S(1)}, u32[]{:S(2)}, u32[]{:S(2)}) collective-permute-start(bf16[256,1152]{1,0:T(8,128)(2,1)S(1)} %collective-permute-done.4.cross_one), channel_id=1, source_target_pairs={{8,0},{10,2},{12,4},{14,6},{49,57},{51,59},{53,61},{55,63},{72,64}... | collective-permute-start | bytes 1769480 | tf_op jit(solution)/shard_map/ppermute | solution.py:43
  55.4 19.0 %collective-permute-start.6 = (bf16[256,1152]{1,0:T(8,128)(2,1)S(1)}, bf16[256,1152]{1,0:T(8,128)(2,1)S(1)}, u32[]{:S(2)}, u32[]{:S(2)}) collective-permute-start(bf16[256,1152]{1,0:T(8,128)(2,1)S(1)} %choose.1), channel_id=1, source_target_pairs={{0,8},{2,10},{4,12},{6,14},{8,16},{9,1},{10,18},{11,3},{12,20},{13... | collective-permute-start | bytes 1769480 | tf_op jit(solution)/shard_map/ppermute | solution.py:43
  56.7 23.1 %collective-permute-start.7 = (bf16[256,1152]{1,0:T(8,128)(2,1)S(1)}, bf16[256,1152]{1,0:T(8,128)(2,1)S(1)}, u32[]{:S(2)}, u32[]{:S(2)}) collective-permute-start(bf16[256,1152]{1,0:T(8,128)(2,1)S(1)} %collective-permute-done.3.two), channel_id=1, source_target_pairs={{1,1017},{3,1019},{5,1021},{7,1023},{56,64},{58,66},{60,68},{62,70... | collective-permute-start | bytes 1769480 | tf_op jit(solution)/shard_map/ppermute | solution.py:43
  71.6 2.8 %collective-permute-start.9 = (bf16[576,256]{1,0:T(8,128)(2,1)S(1)}, bf16[576,256]{1,0:T(8,128)(2,1)S(1)}, u32[]{:S(2)}, u32[]{:S(2)}) collective-permute-start(bf16[576,256]{1,0:T(8,128)(2,1)S(1)} %slice.9), channel_id=1, source_target_pairs={{2,4},{3,5},{4,2},{5,3},{10,12},{11,13},{12,10},{13,11},{18,20},{1... | collective-permute-start | bytes 884744 | tf_op jit(solution)/shard_map/ppermute | solution.py:43
  72.4 2.1 %collective-permute-start.11 = (bf16[576,256]{1,0:T(8,128)(2,1)S(1)}, bf16[576,256]{1,0:T(8,128)(2,1)S(1)}, u32[]{:S(2)}, u32[]{:S(2)}) collective-permute-start(bf16[576,256]{1,0:T(8,128)(2,1)S(1)} %slice.12), channel_id=1, source_target_pairs={{2,4},{3,5},{4,2},{5,3},{10,12},{11,13},{12,10},{13,11},{18,20},{1... | collective-permute-start | bytes 884744 | tf_op jit(solution)/shard_map/ppermute | solution.py:43
  82.7 29.9 %collective-permute-start.12 = (bf16[256,1152]{1,0:T(8,128)(2,1)S(1)}, bf16[256,1152]{1,0:T(8,128)(2,1)S(1)}, u32[]{:S(2)}, u32[]{:S(2)}) collective-permute-start(bf16[256,1152]{1,0:T(8,128)(2,1)S(1)} %pairs.1.dx), channel_id=1, source_target_pairs={{0,2},{1,3},{6,4},{7,5},{8,10},{9,11},{14,12},{15,13},{16,18},{17,... | collective-permute-start | bytes 1769480 | tf_op jit(solution)/shard_map/ppermute | solution.py:43
  100.6 12.7 %collective-permute-start.13 = (bf16[256,1152]{1,0:T(8,128)(2,1)S(1)}, bf16[256,1152]{1,0:T(8,128)(2,1)S(1)}, u32[]{:S(2)}, u32[]{:S(2)}) collective-permute-start(bf16[256,1152]{1,0:T(8,128)(2,1)S(1)} %pairs.1.dx), channel_id=1, source_target_pairs={{2,4},{3,5},{4,2},{5,3},{10,12},{11,13},{12,10},{13,11},{18,20},{1... | collective-permute-start | bytes 1769480 | tf_op jit(solution)/shard_map/ppermute | solution.py:43
  112.6 1.9 %collective-permute-start.14 = (bf16[256,1152]{1,0:T(8,128)(2,1)S(1)}, bf16[256,1152]{1,0:T(8,128)(2,1)S(1)}, u32[]{:S(2)}, u32[]{:S(2)}) collective-permute-start(bf16[256,1152]{1,0:T(8,128)(2,1)S(1)} %collective-permute-done.12.dx_end), channel_id=1, source_target_pairs={{2,4},{3,5},{4,2},{5,3},{10,12},{11,13},{12,10},{13,11},{18,20},{1... | collective-permute-start | bytes 1769480 | tf_op jit(solution)/shard_map/ppermute | solution.py:43
  115.5 22.5 %collective-permute-start.15 = (bf16[144,1152]{1,0:T(8,128)(2,1)S(1)}, bf16[144,1152]{1,0:T(8,128)(2,1)S(1)}, u32[]{:S(2)}, u32[]{:S(2)}) collective-permute-start(bf16[144,1152]{1,0:T(8,128)(2,1)S(1)} %get-tuple-element.20), channel_id=1, source_target_pairs={{2,0},{3,1},{4,6},{5,7},{10,8},{11,9},{12,14},{13,15},{18,16},{19,... | collective-permute-start | bytes 995336 | tf_op jit(solution)/shard_map/ppermute | solution.py:43
  116.8 30.7 %collective-permute-start.16 = (bf16[144,1152]{1,0:T(8,128)(2,1)S(1)}, bf16[144,1152]{1,0:T(8,128)(2,1)S(1)}, u32[]{:S(2)}, u32[]{:S(2)}) collective-permute-start(bf16[144,1152]{1,0:T(8,128)(2,1)S(1)} %get-tuple-element.21), channel_id=1, source_target_pairs={{2,1},{3,0},{4,7},{5,6},{10,9},{11,8},{12,15},{13,14},{18,17},{19,... | collective-permute-start | bytes 995336 | tf_op jit(solution)/shard_map/ppermute | solution.py:43
  118.7 28.7 %collective-permute-start.17 = (bf16[144,1152]{1,0:T(8,128)(2,1)S(1)}, bf16[144,1152]{1,0:T(8,128)(2,1)S(1)}, u32[]{:S(2)}, u32[]{:S(2)}) collective-permute-start(bf16[144,1152]{1,0:T(8,128)(2,1)S(1)} %get-tuple-element.24), channel_id=1, source_target_pairs={{0,1},{1,0},{2,3},{3,2},{4,5},{5,4},{6,7},{7,6},{8,9},{9,8},{10,11... | collective-permute-start | bytes 995336 | tf_op jit(solution)/shard_map/ppermute | solution.py:43

commit v3 on v2

v3 whole, which is shorter than its diff:
```python
import functools

import jax
import jax.numpy as jnp
from jax import lax
from jax.experimental import pallas as pl
from jax.experimental.pallas import tpu as pltpu
from jax.sharding import Mesh, PartitionSpec as P

NAMES = ("x", "zh", "y", "zl", "c")
NX, NZH, NY, NZL, NC = SIZES = (8, 2, 8, 4, 2)
ROWS = 128
D = 1152
CHIP = 288
CORE = 144
LEFT = 512
HALVES = (slice(0, LEFT), slice(LEFT, D))
EPS = 1e-06
BF = jnp.bfloat16
F32 = jnp.float32
PROJECT_LIMIT = 51
VMEM = pl.BlockSpec(memory_space=pltpu.VMEM)
SMEM = pl.BlockSpec(memory_space=pltpu.SMEM)
ANY = pl.BlockSpec(memory_space=pl.ANY)
HBM = pl.BlockSpec(memory_space=pltpu.HBM)
PARAMS = pltpu.CompilerParams(vmem_limit_bytes=32 * 1024 * 1024)


def index_of(x, zh, y, zl, c):
    return (((x * NZH + zh) * NY + y) * NZL + zl) * NC + c


def pairs_of(rule):
    found = []
    for x in range(NX):
        for zh in range(NZH):
            for y in range(NY):
                for zl in range(NZL):
                    for c in range(NC):
                        target = rule(x, zh, y, zl, c)
                        if target is not None:
                            found.append((index_of(x, zh, y, zl, c), index_of(*target)))
    return found


def send(value, rule):
    return lax.ppermute(value, NAMES, pairs_of(rule))


def other_core(x, zh, y, zl, c):
    return (x, zh, y, zl, 1 - c)


def first_hop(x, zh, y, zl, c):
    if c == 1:
        return (x, zh, y + 1, zl, 0) if y < 7 else None
    return (x, zh, y - 1, zl, 1) if y > 0 else None


def second_hop(x, zh, y, zl, c):
    if not 1 <= y <= 6:
        return None
    return (x, zh, y + 1 if c == 0 else y - 1, zl, c)


def third_hop(x, zh, y, zl, c):
    if c == 0:
        return (x, zh, y + 1, zl, 0) if y < 7 else None
    return (x, zh, y - 1, zl, 1) if y > 0 else None


def above(x, zh, column):
    return (x, 1, column) if zh == 0 else ((x + 1) % NX, 0, column)


def below(x, zh, column):
    return (x, 0, column) if zh == 1 else ((x - 1) % NX, 1, column)


def first_crossing(x, zh, y, zl, c):
    if c == 1 and y >= 6:
        return (*above(x, zh, y - 6), zl, 0)
    if c == 0 and y <= 1:
        return (*below(x, zh, y + 6), zl, 1)
    return None


def second_crossing(x, zh, y, zl, c):
    if c == 0 and y == 6:
        return (*above(x, zh, 0), zl, 0)
    if c == 1 and y == 1:
        return (*below(x, zh, 7), zl, 1)
    return None


def from_second(x, zh, y, zl, c):
    if c == 0 and y == 1:
        return (x, zh, 0, zl, 0)
    if c == 1 and y == 6:
        return (x, zh, 7, zl, 1)
    return None


def inward(x, zh, y, zl, c):
    return {0: (x, zh, y, 1, c), 3: (x, zh, y, 2, c)}.get(zl)


def middle(x, zh, y, zl, c):
    return {1: (x, zh, y, 2, c), 2: (x, zh, y, 1, c)}.get(zl)


def outward(x, zh, y, zl, c):
    return {1: (x, zh, y, 0, c), 2: (x, zh, y, 3, c)}.get(zl)


def outward_cross(x, zh, y, zl, c):
    return {1: (x, zh, y, 0, 1 - c), 2: (x, zh, y, 3, 1 - c)}.get(zl)


def project_kernel(
    flags, own, recv, wp, wc, z_ref, u_ref, rn_ref, f_ref, w_ref, sems
):
    c = flags[0]
    parts = 3
    width = D // parts

    def fetch(head):
        for j in range(parts):
            cols = pl.ds(j * width, width)
            pltpu.make_async_copy(head.at[:, cols], w_ref.at[j], sems.at[j]).start()

    @pl.when(c == 0)
    def _():
        fetch(wp)

    @pl.when(c == 1)
    def _():
        fetch(wc)

    f_ref[:ROWS] = own[...]
    f_ref[ROWS:] = recv[...]
    total = jnp.zeros((2 * ROWS, 1), F32)
    for j in range(parts):
        cols = pl.ds(j * width, width)
        pltpu.make_async_copy(wp.at[:, cols], w_ref.at[j], sems.at[j]).wait()
        x = jnp.dot(f_ref[...], w_ref[j], preferred_element_type=F32)
        u_ref[:, cols] = x
        total = total + jnp.sum(x * x, axis=-1, keepdims=True)
    rn = 1.0 / jnp.sqrt(total + EPS)
    rn_ref[...] = jnp.broadcast_to(rn, (2 * ROWS, 128))
    u = u_ref[...] * rn
    u_ref[...] = u
    z_ref[...] = u.astype(BF)


def project(flags, own, recv, wp, wc):
    rows = 2 * ROWS
    return pl.pallas_call(
        project_kernel,
        name="project",
        out_shape=(
            jax.ShapeDtypeStruct((rows, D), BF),
            jax.ShapeDtypeStruct((rows, D), F32),
            jax.ShapeDtypeStruct((rows, 128), F32),
        ),
        in_specs=[SMEM, VMEM, VMEM, HBM, HBM],
        out_specs=(VMEM,) * 3,
        scratch_shapes=[
            pltpu.VMEM((rows, D), BF),
            pltpu.VMEM((3, D, D // 3), BF),
            pltpu.SemaphoreType.DMA((3,)),
        ],
        compiler_params=pltpu.CompilerParams(vmem_limit_bytes=PROJECT_LIMIT * 1024 * 1024),
        cost_estimate=pl.CostEstimate(
            flops=2 * rows * D * D, bytes_accessed=2 * D * D + 8 * rows * D, transcendentals=0
        ),
    )(flags, own, recv, wp, wc)


def turn_kernel(flags, own, recv, ft_ref, turned):
    mirror = flags[3]
    turned[:, :ROWS] = own[...].T
    turned[:, ROWS:] = recv[...].T
    for j in range(4):
        start = pl.multiple_of(jnp.where(mirror == 1, 3 - j, j) * CHIP, CHIP)
        ft_ref[j * CHIP : (j + 1) * CHIP] = turned[pl.ds(start, CHIP)]


def turn(flags, own, recv):
    return pl.pallas_call(
        turn_kernel,
        name="turn",
        out_shape=jax.ShapeDtypeStruct((D, 2 * ROWS), BF),
        in_specs=[SMEM, VMEM, VMEM],
        out_specs=VMEM,
        scratch_shapes=[pltpu.VMEM((D, 2 * ROWS), BF)],
        compiler_params=PARAMS,
        cost_estimate=pl.CostEstimate(
            flops=0, bytes_accessed=8 * ROWS * D, transcendentals=0
        ),
    )(flags, own, recv)


def choose_kernel(flags, two, cross_one, out_ref, sem):
    place = flags[1]

    @pl.when(place <= 1)
    def _():
        pltpu.make_async_copy(cross_one, out_ref, sem).start()

    @pl.when(place > 1)
    def _():
        pltpu.make_async_copy(two, out_ref, sem).start()

    pltpu.make_async_copy(two, out_ref, sem).wait()


def choose(flags, two, cross_one):
    return pl.pallas_call(
        choose_kernel,
        name="choose",
        out_shape=jax.ShapeDtypeStruct((2 * ROWS, D), BF),
        in_specs=[SMEM] + [ANY] * 2,
        out_specs=VMEM,
        scratch_shapes=[pltpu.SemaphoreType.DMA(())],
        compiler_params=PARAMS,
        cost_estimate=pl.CostEstimate(
            flops=0, bytes_accessed=8 * ROWS * D, transcendentals=0
        ),
    )(flags, two, cross_one)


def pairs_kernel(
    flags, scale, z_ref, u_ref, rn_ref,
    here, one, two, three, cross_one, cross_two, second, early_mid, early_far,
    dx_left, dx_right, others, sems,
):
    del early_mid, early_far
    place = flags[1]

    def fetch(source, s):
        for b in range(2):
            pltpu.make_async_copy(
                source.at[pl.ds((1 - b) * ROWS, ROWS)],
                others.at[b, pl.ds(s * ROWS, ROWS)],
                sems.at[2 * s + b],
            ).start()

    fetch(here, 0)

    @pl.when(place > 0)
    def _():
        fetch(one, 1)
        fetch(three, 3)

    @pl.when(place == 0)
    def _():
        fetch(second, 1)
        fetch(cross_two, 3)

    @pl.when(place <= 1)
    def _():
        fetch(cross_one, 2)

    @pl.when(place > 1)
    def _():
        fetch(two, 2)

    t = scale[0]
    bias = scale[1]
    for s in range(4):
        for b in range(2):
            pltpu.make_async_copy(
                here.at[pl.ds(0, ROWS)],
                others.at[b, pl.ds(s * ROWS, ROWS)],
                sems.at[2 * s + b],
            ).wait()
    row = lax.broadcasted_iota(jnp.int32, (ROWS, 4 * ROWS), 0)
    col = lax.broadcasted_iota(jnp.int32, (ROWS, 4 * ROWS), 1)
    for b in range(2):
        mine = z_ref[b * ROWS : (b + 1) * ROWS]
        logits = t * lax.dot_general(
            mine, others[b], (((1,), (1,)), ((), ())), preferred_element_type=F32
        ) + bias
        prob = jax.nn.sigmoid(logits) - jnp.where(row == col, 1.0, 0.0)
        weight = (prob * (1.0 / ROWS)).astype(BF)
        dz = t * jnp.dot(weight, others[b], preferred_element_type=F32)
        u = u_ref[b * ROWS : (b + 1) * ROWS]
        rn = rn_ref[b * ROWS : (b + 1) * ROWS, :1]
        inner = jnp.sum(u * dz, axis=-1, keepdims=True)
        dx = ((dz - u * inner) * rn).astype(BF)
        for cols, dx_ref in zip(HALVES, (dx_left, dx_right)):
            dx_ref[b * ROWS : (b + 1) * ROWS] = dx[:, cols]


def pairs(flags, scale, z, *rest):
    rows = 2 * ROWS
    return pl.pallas_call(
        pairs_kernel,
        name="pairs",
        out_shape=(
            jax.ShapeDtypeStruct((rows, LEFT), BF),
            jax.ShapeDtypeStruct((rows, D - LEFT), BF),
        ),
        in_specs=[SMEM, SMEM] + [VMEM] * 3 + [ANY] * 9,
        out_specs=(VMEM, VMEM),
        scratch_shapes=[
            pltpu.VMEM((2, 4 * ROWS, D), BF),
            pltpu.SemaphoreType.DMA((8,)),
        ],
        compiler_params=PARAMS,
        cost_estimate=pl.CostEstimate(
            flops=16 * rows * ROWS * D, bytes_accessed=14 * rows * D, transcendentals=rows * 512
        ),
    )(flags, scale, z, *rest)


def near_kernel(ft, feats_end, feats_mid, *refs):
    inner_ref, outer_ref = refs[6:]
    for cols, dx, dx_end, dx_mid in zip(HALVES, refs[:2], refs[2:4], refs[4:6]):
        dx_own = dx[...]
        dx_other = dx_mid[...]
        inner_ref[:, cols] = (
            jnp.dot(ft[CHIP : 2 * CHIP], dx_own, preferred_element_type=F32)
            + jnp.dot(feats_end[:CHIP], dx_end[...], preferred_element_type=F32)
            + jnp.dot(feats_mid[:CHIP], dx_other, preferred_element_type=F32)
        )
        outer_ref[:, cols] = jnp.dot(
            ft[:CHIP], dx_own, preferred_element_type=F32
        ) + jnp.dot(feats_mid[CHIP:], dx_other, preferred_element_type=F32)


def near(ft, feats_end, feats_mid, *dxs):
    return pl.pallas_call(
        near_kernel,
        name="near",
        out_shape=(
            jax.ShapeDtypeStruct((CHIP, D), F32),
            jax.ShapeDtypeStruct((CHIP, D), F32),
        ),
        in_specs=[VMEM] * 9,
        out_specs=(VMEM, VMEM),
        compiler_params=PARAMS,
        cost_estimate=pl.CostEstimate(
            flops=20 * CHIP * ROWS * D, bytes_accessed=14 * CHIP * D, transcendentals=0
        ),
    )(ft, feats_end, feats_mid, *dxs)


def far_kernel(half, flags, outer_ref, feats, dx, *refs):
    same, crossed, part = refs[-3:]
    c = flags[0]
    part[...] = outer_ref[:, HALVES[half]] + jnp.dot(
        feats[CHIP:], dx[...], preferred_element_type=F32
    )
    mine = pl.ds(pl.multiple_of(c * CORE, CORE), CORE)
    theirs = pl.ds(pl.multiple_of((1 - c) * CORE, CORE), CORE)
    same[...] = part[mine].astype(BF)
    crossed[...] = part[theirs].astype(BF)


def far(half, flags, outer, feats, dx, *after):
    cols = dx.shape[1]
    return pl.pallas_call(
        functools.partial(far_kernel, half),
        name="far",
        out_shape=(
            jax.ShapeDtypeStruct((CORE, cols), BF),
            jax.ShapeDtypeStruct((CORE, cols), BF),
            jax.ShapeDtypeStruct((CHIP, cols), F32),
        ),
        in_specs=[SMEM] + [VMEM] * 3 + [ANY] * len(after),
        out_specs=(VMEM,) * 3,
        compiler_params=PARAMS,
        cost_estimate=pl.CostEstimate(
            flops=4 * CHIP * ROWS * cols, bytes_accessed=14 * CHIP * cols, transcendentals=0
        ),
    )(flags, outer, feats, dx, *after)


def rest_kernel(
    flags, inner_ref, feats, dx_left, dx_right, part_left, part_right,
    keep, swap_left, swap_right, total,
):
    c = flags[0]
    mine = pl.ds(pl.multiple_of(c * CORE, CORE), CORE)
    theirs = pl.ds(pl.multiple_of((1 - c) * CORE, CORE), CORE)

    @pl.when(flags[4] == 1)
    def _():
        for cols, dx in zip(HALVES, (dx_left, dx_right)):
            total[:, cols] = inner_ref[:, cols] + jnp.dot(
                feats[:CHIP], dx[...], preferred_element_type=F32
            )
        keep[...] = total[mine]
        swap_left[...] = total[theirs, :LEFT].astype(BF)
        swap_right[...] = total[theirs, LEFT:].astype(BF)

    @pl.when(flags[4] == 0)
    def _():
        for cols, part, swap in zip(
            HALVES, (part_left, part_right), (swap_left, swap_right)
        ):
            keep[:, cols] = part[mine]
            swap[...] = part[theirs].astype(BF)


def rest(flags, *parts):
    return pl.pallas_call(
        rest_kernel,
        name="rest",
        out_shape=(
            jax.ShapeDtypeStruct((CORE, D), F32),
            jax.ShapeDtypeStruct((CORE, LEFT), BF),
            jax.ShapeDtypeStruct((CORE, D - LEFT), BF),
        ),
        in_specs=[SMEM] + [VMEM] * 6,
        out_specs=(VMEM,) * 3,
        scratch_shapes=[pltpu.VMEM((CHIP, D), F32)],
        compiler_params=PARAMS,
        cost_estimate=pl.CostEstimate(
            flops=4 * CHIP * ROWS * D, bytes_accessed=14 * CHIP * D, transcendentals=0
        ),
    )(flags, *parts)


def finish_kernel(
    flags, same_left, crossed_left, same_right, crossed_right, swap_left, swap_right, keep,
    image_ref, text_ref,
):
    def put(own_ref, other_ref):
        for cols, same, crossed, swap in (
            (HALVES[0], same_left, crossed_left, swap_left),
            (HALVES[1], same_right, crossed_right, swap_right),
        ):
            own_ref[0, :, cols] = keep[:, cols] + same[...].astype(F32)
            other_ref[0, :, cols] = swap[...].astype(F32) + crossed[...].astype(F32)

    @pl.when(flags[0] == 0)
    def _():
        put(image_ref, text_ref)

    @pl.when(flags[0] == 1)
    def _():
        put(text_ref, image_ref)


def finish(flags, *parts):
    shape = jax.ShapeDtypeStruct((1, CORE, D), F32)
    return pl.pallas_call(
        finish_kernel,
        name="finish",
        out_shape=(shape, shape),
        in_specs=[SMEM] + [VMEM] * 7,
        out_specs=(VMEM, VMEM),
        compiler_params=PARAMS,
        cost_estimate=pl.CostEstimate(
            flops=4 * CORE * D, bytes_accessed=18 * CORE * D, transcendentals=0
        ),
    )(flags, *parts)


def on_device(pictures, captions, picture_head, caption_head, sharpness, shift_term):
    c = lax.axis_index("c")
    y = lax.axis_index("y")
    zl = lax.axis_index("zl")
    yy = jnp.where(c == 0, y, 7 - y)
    flags = jnp.stack([c, yy, zl, zl >= 2, (zl == 1) | (zl == 2)]).astype(jnp.int32)
    scale = jnp.concatenate([sharpness, shift_term])

    received = send(jnp.where(c == 0, captions, pictures), other_core)
    own = jnp.where(c == 0, pictures, captions)
    z, u, rn = project(flags, own, received, picture_head, caption_head)

    one = send(z, first_hop)
    cross_one = send(z, first_crossing)
    ft = turn(flags, own, received)
    one, ft = lax.optimization_barrier((one, ft))
    ft_end = send(ft[CHIP:], inward)
    ft_mid = send(ft[2 * CHIP :], middle)
    ft_far = send(ft_end[CHIP:], middle)
    two = send(one, second_hop)
    cross_two = send(one, second_crossing)
    second = send(cross_one, from_second)
    chosen, z_late = lax.optimization_barrier((choose(flags, two, cross_one), z))
    three = send(chosen, third_hop)
    here = send(z_late, other_core)
    dxs = pairs(
        flags, scale, z, u, rn, here, one, two, three, cross_one, cross_two, second, ft_mid, ft_far
    )

    ends = [send(dx, inward) for dx in dxs]
    mids = [send(dx, middle) for dx in dxs]
    inner, outer = near(ft, ft_end, ft_mid, *dxs, *ends, *mids)
    right, inner = lax.optimization_barrier((ends[1], inner))
    fars = [send(ends[0], middle), send(right, middle)]
    same_left, crossed_left, part_left = far(0, flags, outer, ft_far, fars[0])
    same_left = send(same_left, outward)
    crossed_left = send(crossed_left, outward_cross)
    same_right, crossed_right, part_right = far(1, flags, outer, ft_far, fars[1], part_left)
    same_right = send(same_right, outward)
    crossed_right = send(crossed_right, outward_cross)
    keep, *swaps = rest(flags, inner, ft_far, *fars, part_left, part_right)
    swaps, same_left, crossed_left = lax.optimization_barrier(
        (swaps, same_left, crossed_left)
    )
    swaps = [send(swap, other_core) for swap in swaps]
    return finish(
        flags, same_left, crossed_left, same_right, crossed_right, *swaps, keep
    )


def solution(mesh):
    physical = Mesh(mesh.devices.reshape(SIZES), NAMES)
    rows = P(NAMES, None)
    grad = P(("x", "zh", "y"), ("zl", "c"), None)
    return jax.shard_map(
        on_device,
        mesh=physical,
        in_specs=(rows, rows, P(), P(), P(), P()),
        out_specs=(grad, grad),
        check_vma=False,
    )
```

time: 150 us -> 128 us (0.85)
  starting transfers between devices: 74.3 us -> 47 us
  waiting for transfers between devices: 54.8 us -> 63.7 us
  local copies, waits for them, and re-layouts: 2.45 us -> 0.16 us
    ppermute x18 -> x23, starting transfers between devices: 74.3 us -> 47 us  [send(): return lax.ppermute(value, NAMES, pairs_of(rule))]
    ppermute x18 -> x23, waiting for transfers between devices: 54.8 us -> 63.7 us  [send(): return lax.ppermute(value, NAMES, pairs_of(rule))]
    pallas_call x1, Pallas kernels: 5.35 us -> 3.58 us  [project(): pl.pallas_call(project_kernel, name='project', out_shape=(jax.ShapeDtypeS...]
    unnamed x16 -> x0, local copies, waits for them, and re-layouts: 1.69 us -> none
    pallas_call x2 -> x3, Pallas kernels: 3.82 us -> 4.47 us  [the longest x1 2.81 us: pairs(): pl.pallas_call(pairs_kernel, name='pairs', out_shape=(jax.ShapeDtypeStruc...]
  transfers between devices with their start and end apart: 18 -> 23, of which waited for: 8 -> 10; matrix products, arithmetic and copies ran while one was open for 1% -> 0% of each run, Pallas kernels for 2% -> 4%
where the time goes in v3:
time: 128 us; the launch traced here: 127 us
  waiting for transfers between devices  63.7 us (50%)
  starting transfers between devices  47 us (37%)
  Pallas kernels  13.1 us (10%)
  between operations  2.29 us (2%)
    ppermute x23, waiting for transfers between devices, send(): return lax.ppermute(value, NAMES, pairs_of(rule))  63.7 us
    ppermute x23, starting transfers between devices, send(): return lax.ppermute(value, NAMES, pairs_of(rule))  47 us
    pallas_call x1, Pallas kernels, project(): pl.pallas_call(project_kernel, name='project', out_shape=(jax.ShapeDtypeS...  3.58 us
    pallas_call x1, Pallas kernels, pairs(): pl.pallas_call(pairs_kernel, name='pairs', out_shape=(jax.ShapeDtypeStruc...  2.81 us
  transfers between devices with their start and end apart: 23, of which 10 were waited for; matrix products, arithmetic and copies ran while one was open for 0% of the time, Pallas kernels for 4%

profile of v3, /device:TPU:1, one launch (start us, length us, event | category | flops | bytes accessed | tf_op | source)
XLA Modules:
  0.0 127.3 jit_solution(4470846237787302106)
XLA Ops:
  0.6 1.1 broadcast_select_fusion
  1.7 16.1 %collective-permute-start = (bf16[128,1152]{1,0:T(8,128)(2,1)S(1)}, bf16[128,1152]{1,0:T(8,128)(2,1)S(1)}, u32[]{:S(2)}, u32[]{:S(2)}) collective-permute-start(bf16[128,1152]{1,0:T(8,128)(2,1)S(1)} %get-tuple-element.54), channel_id=1, source_target_pairs={{0,1},{1,0},{2,3},{3,2},{4,5},{5,4},{6,7},{7,6},{8,9},{9,8},{10,11... | collective-permute-start | bytes 884744 | tf_op jit(solution)/shard_map/ppermute | solution.py:47
  17.8 0.1 stack.31.flags
  17.9 1.1 collective-permute-done.recv
  19.0 3.6 %project.1 = (bf16[256,1152]{1,0:T(8,128)(2,1)S(1)}, f32[256,1152]{1,0:T(8,128)S(1)}, f32[256,128]{1,0:T(8,128)S(1)}) custom-call(s32[5]{0:T(128)S(1)} %stack.31.flags, bf16[128,1152]{1,0:T(8,128)(2,1)S(1)} %get-tuple-element.55.own, bf16[128,1152]{1,0:T(8,128)(2,1)S(1)} %collective-permute-done.recv, bf16[1152,1152]{1,0:T(8,128)(2,1)} %wp.1, ...), custom_call_target="tpu_custom_call" | custom-call | flops 679477248 | bytes 5013504 | tf_op jit(solution)/shard_map/project/pallas_call | solution.py:158
  22.6 1.9 %collective-permute-start.1 = (bf16[256,1152]{1,0:T(8,128)(2,1)S(1)}, bf16[256,1152]{1,0:T(8,128)(2,1)S(1)}, u32[]{:S(2)}, u32[]{:S(2)}) collective-permute-start(bf16[256,1152]{1,0:T(8,128)(2,1)S(1)} %get-tuple-element.32.z_ref), channel_id=1, source_target_pairs={{1,8},{3,10},{5,12},{7,14},{8,1},{9,16},{10,3},{11,18},{12,5},{13,... | collective-permute-start | bytes 1769480 | tf_op jit(solution)/shard_map/ppermute | solution.py:47
  24.5 0.7 collective-permute-start.3
  25.2 0.8 turn.1.ft
  26.0 12.4 %collective-permute-done.1.one = bf16[256,1152]{1,0:T(8,128)(2,1)S(1)} collective-permute-done((bf16[256,1152]{1,0:T(8,128)(2,1)S(1)}, bf16[256,1152]{1,0:T(8,128)(2,1)S(1)}, u32[]{:S(2)}, u32[]{:S(2)}) %collective-permute-start.1) | collective-permute-done | bytes 589856 | tf_op jit(solution)/shard_map/ppermute | solution.py:47
  38.4 1.3 %collective-permute-start.2 = (bf16[256,1152]{1,0:T(8,128)(2,1)S(1)}, bf16[256,1152]{1,0:T(8,128)(2,1)S(1)}, u32[]{:S(2)}, u32[]{:S(2)}) collective-permute-start(bf16[256,1152]{1,0:T(8,128)(2,1)S(1)} %collective-permute-done.1.one), channel_id=1, source_target_pairs={{8,16},{9,1},{10,18},{11,3},{12,20},{13,5},{14,22},{15,7},{16,24},... | collective-permute-start | bytes 1769480 | tf_op jit(solution)/shard_map/ppermute | solution.py:47
  39.8 1.3 %collective-permute-start.9 = (bf16[864,256]{1,0:T(8,128)(2,1)S(1)}, bf16[864,256]{1,0:T(8,128)(2,1)S(1)}, u32[]{:S(2)}, u32[]{:S(2)}) collective-permute-start(bf16[864,256]{1,0:T(8,128)(2,1)S(1)} %slice.10), channel_id=1, source_target_pairs={{0,2},{1,3},{6,4},{7,5},{8,10},{9,11},{14,12},{15,13},{16,18},{17,... | collective-permute-start | bytes 1327112 | tf_op jit(solution)/shard_map/ppermute | solution.py:47
  41.1 0.7 collective-permute-start.6
  41.8 0.7 collective-permute-start.8
  42.5 0.0 collective-permute-done.3.cross_one
  42.5 0.7 collective-permute-start.7
  43.2 11.6 %collective-permute-done.2.two = bf16[256,1152]{1,0:T(8,128)(2,1)S(1)} collective-permute-done((bf16[256,1152]{1,0:T(8,128)(2,1)S(1)}, bf16[256,1152]{1,0:T(8,128)(2,1)S(1)}, u32[]{:S(2)}, u32[]{:S(2)}) %collective-permute-start.2) | collective-permute-done | bytes 589856 | tf_op jit(solution)/shard_map/ppermute | solution.py:47
  54.8 0.7 choose.1
  55.5 1.9 %collective-permute-start.4 = (bf16[256,1152]{1,0:T(8,128)(2,1)S(1)}, bf16[256,1152]{1,0:T(8,128)(2,1)S(1)}, u32[]{:S(2)}, u32[]{:S(2)}) collective-permute-start(bf16[256,1152]{1,0:T(8,128)(2,1)S(1)} %get-tuple-element.32.z_ref), channel_id=1, source_target_pairs={{0,1},{1,0},{2,3},{3,2},{4,5},{5,4},{6,7},{7,6},{8,9},{9,8},{10,11... | collective-permute-start | bytes 1769480 | tf_op jit(solution)/shard_map/ppermute | solution.py:47
  57.4 9.8 %collective-permute-done.9.feats_end = bf16[864,256]{1,0:T(8,128)(2,1)S(1)} collective-permute-done((bf16[864,256]{1,0:T(8,128)(2,1)S(1)}, bf16[864,256]{1,0:T(8,128)(2,1)S(1)}, u32[]{:S(2)}, u32[]{:S(2)}) %collective-permute-start.9) | collective-permute-done | bytes 442400 | tf_op jit(solution)/shard_map/ppermute | solution.py:47
  67.2 1.3 %collective-permute-start.5 = (bf16[256,1152]{1,0:T(8,128)(2,1)S(1)}, bf16[256,1152]{1,0:T(8,128)(2,1)S(1)}, u32[]{:S(2)}, u32[]{:S(2)}) collective-permute-start(bf16[256,1152]{1,0:T(8,128)(2,1)S(1)} %choose.1), channel_id=1, source_target_pairs={{0,8},{2,10},{4,12},{6,14},{8,16},{9,1},{10,18},{11,3},{12,20},{13... | collective-permute-start | bytes 1769480 | tf_op jit(solution)/shard_map/ppermute | solution.py:47
  68.5 0.0 collective-permute-done.8.early_mid.feats_mid
  68.5 0.7 collective-permute-start.10
  70.5 0.1 pad_maximum_fusion.scale
  70.6 0.0 collective-permute-done.6.cross_two
  70.6 0.0 collective-permute-done.7.second
  70.6 0.0 collective-permute-done.10.early_far.feats
  70.6 0.0 collective-permute-done.4.here
  70.6 7.2 %collective-permute-done.5.three = bf16[256,1152]{1,0:T(8,128)(2,1)S(1)} collective-permute-done((bf16[256,1152]{1,0:T(8,128)(2,1)S(1)}, bf16[256,1152]{1,0:T(8,128)(2,1)S(1)}, u32[]{:S(2)}, u32[]{:S(2)}) %collective-permute-start.5) | collective-permute-done | bytes 589856 | tf_op jit(solution)/shard_map/ppermute | solution.py:47
  77.8 2.8 %pairs.1 = (bf16[256,512]{1,0:T(8,128)(2,1)S(1)}, bf16[256,640]{1,0:T(8,128)(2,1)S(1)}) custom-call(s32[5]{0:T(128)S(1)} %stack.31.flags, f32[2]{0:T(128)S(1)} %pad_maximum_fusion.scale, bf16[256,1152]{1,0:T(8,128)(2,1)S(1)} %get-tuple-element.32.z_ref, f32[256,1152]{1,0:T(8,128)S(1)} %get-tuple-element.29.u_ref, f32[256,128]{1,0:T(8,128)S(1)} %get-tuple-element.30.rn_ref, ...), custom_call_target="tpu_custom_call" | custom-call | flops 603979776 | bytes 4128768 | tf_op jit(solution)/shard_map/pairs/pallas_call | solution.py:298
  80.6 4.7 %collective-permute-start.11 = (bf16[256,640]{1,0:T(8,128)(2,1)S(1)}, bf16[256,640]{1,0:T(8,128)(2,1)S(1)}, u32[]{:S(2)}, u32[]{:S(2)}) collective-permute-start(bf16[256,640]{1,0:T(8,128)(2,1)S(1)} %get-tuple-element.35.refs_1_), channel_id=1, source_target_pairs={{0,2},{1,3},{6,4},{7,5},{8,10},{9,11},{14,12},{15,13},{16,18},{17,... | collective-permute-start | bytes 983048 | tf_op jit(solution)/shard_map/ppermute | solution.py:47
  85.3 0.7 collective-permute-start.14
  86.0 2.8 %collective-permute-start.12 = (bf16[256,512]{1,0:T(8,128)(2,1)S(1)}, bf16[256,512]{1,0:T(8,128)(2,1)S(1)}, u32[]{:S(2)}, u32[]{:S(2)}) collective-permute-start(bf16[256,512]{1,0:T(8,128)(2,1)S(1)} %get-tuple-element.36.refs_0_), channel_id=1, source_target_pairs={{0,2},{1,3},{6,4},{7,5},{8,10},{9,11},{14,12},{15,13},{16,18},{17,... | collective-permute-start | bytes 786440 | tf_op jit(solution)/shard_map/ppermute | solution.py:47
  88.9 0.7 collective-permute-start.13
  89.6 7.1 %collective-permute-done.12.refs_2_ = bf16[256,512]{1,0:T(8,128)(2,1)S(1)} collective-permute-done((bf16[256,512]{1,0:T(8,128)(2,1)S(1)}, bf16[256,512]{1,0:T(8,128)(2,1)S(1)}, u32[]{:S(2)}, u32[]{:S(2)}) %collective-permute-start.12) | collective-permute-done | bytes 262176 | tf_op jit(solution)/shard_map/ppermute | solution.py:47
  96.7 0.7 collective-permute-start.15
  97.3 0.0 collective-permute-done.13.refs_4_
  97.3 0.0 collective-permute-done.11.refs_3_
  97.3 0.0 collective-permute-done.14.refs_5_
  97.4 1.2 near.1
  98.5 0.7 collective-permute-start.16
  99.2 0.0 collective-permute-done.15.dx.dx_left
  99.2 0.8 far.2
  100.0 1.3 %collective-permute-start.17 = (bf16[144,512]{1,0:T(8,128)(2,1)S(1)}, bf16[144,512]{1,0:T(8,128)(2,1)S(1)}, u32[]{:S(2)}, u32[]{:S(2)}) collective-permute-start(bf16[144,512]{1,0:T(8,128)(2,1)S(1)} %get-tuple-element.45), channel_id=1, source_target_pairs={{2,0},{3,1},{4,6},{5,7},{10,8},{11,9},{12,14},{13,15},{18,16},{19,... | collective-permute-start | bytes 442376 | tf_op jit(solution)/shard_map/ppermute | solution.py:47
  101.3 1.3 %collective-permute-start.18 = (bf16[144,512]{1,0:T(8,128)(2,1)S(1)}, bf16[144,512]{1,0:T(8,128)(2,1)S(1)}, u32[]{:S(2)}, u32[]{:S(2)}) collective-permute-start(bf16[144,512]{1,0:T(8,128)(2,1)S(1)} %get-tuple-element.46), channel_id=1, source_target_pairs={{2,1},{3,0},{4,7},{5,6},{10,9},{11,8},{12,15},{13,14},{18,17},{19,... | collective-permute-start | bytes 442376 | tf_op jit(solution)/shard_map/ppermute | solution.py:47
  102.6 0.0 collective-permute-done.16.dx.dx_right
  102.6 0.9 far.3
  103.5 1.3 %collective-permute-start.19 = (bf16[144,640]{1,0:T(8,128)(2,1)S(1)}, bf16[144,640]{1,0:T(8,128)(2,1)S(1)}, u32[]{:S(2)}, u32[]{:S(2)}) collective-permute-start(bf16[144,640]{1,0:T(8,128)(2,1)S(1)} %get-tuple-element.49), channel_id=1, source_target_pairs={{2,0},{3,1},{4,6},{5,7},{10,8},{11,9},{12,14},{13,15},{18,16},{19,... | collective-permute-start | bytes 552968 | tf_op jit(solution)/shard_map/ppermute | solution.py:47
  104.8 1.3 %collective-permute-start.20 = (bf16[144,640]{1,0:T(8,128)(2,1)S(1)}, bf16[144,640]{1,0:T(8,128)(2,1)S(1)}, u32[]{:S(2)}, u32[]{:S(2)}) collective-permute-start(bf16[144,640]{1,0:T(8,128)(2,1)S(1)} %get-tuple-element.50), channel_id=1, source_target_pairs={{2,1},{3,0},{4,7},{5,6},{10,9},{11,8},{12,15},{13,14},{18,17},{19,... | collective-permute-start | bytes 552968 | tf_op jit(solution)/shard_map/ppermute | solution.py:47
  106.1 0.6 rest.1
  106.7 4.2 %collective-permute-done.17.same_left = bf16[144,512]{1,0:T(8,128)(2,1)S(1)} collective-permute-done((bf16[144,512]{1,0:T(8,128)(2,1)S(1)}, bf16[144,512]{1,0:T(8,128)(2,1)S(1)}, u32[]{:S(2)}, u32[]{:S(2)}) %collective-permute-start.17) | collective-permute-done | bytes 147488 | tf_op jit(solution)/shard_map/ppermute | solution.py:47
  111.0 7.0 %collective-permute-done.18.crossed_left = bf16[144,512]{1,0:T(8,128)(2,1)S(1)} collective-permute-done((bf16[144,512]{1,0:T(8,128)(2,1)S(1)}, bf16[144,512]{1,0:T(8,128)(2,1)S(1)}, u32[]{:S(2)}, u32[]{:S(2)}) %collective-permute-start.18) | collective-permute-done | bytes 147488 | tf_op jit(solution)/shard_map/ppermute | solution.py:47
  117.9 1.9 %collective-permute-start.22 = (bf16[144,640]{1,0:T(8,128)(2,1)S(1)}, bf16[144,640]{1,0:T(8,128)(2,1)S(1)}, u32[]{:S(2)}, u32[]{:S(2)}) collective-permute-start(bf16[144,640]{1,0:T(8,128)(2,1)S(1)} %get-tuple-element.52), channel_id=1, source_target_pairs={{0,1},{1,0},{2,3},{3,2},{4,5},{5,4},{6,7},{7,6},{8,9},{9,8},{10,11... | collective-permute-start | bytes 552968 | tf_op jit(solution)/shard_map/ppermute | solution.py:47
  119.9 2.4 %collective-permute-start.21 = (bf16[144,512]{1,0:T(8,128)(2,1)S(1)}, bf16[144,512]{1,0:T(8,128)(2,1)S(1)}, u32[]{:S(2)}, u32[]{:S(2)}) collective-permute-start(bf16[144,512]{1,0:T(8,128)(2,1)S(1)} %get-tuple-element.51), channel_id=1, source_target_pairs={{0,1},{1,0},{2,3},{3,2},{4,5},{5,4},{6,7},{7,6},{8,9},{9,8},{10,11... | collective-permute-start | bytes 442376 | tf_op jit(solution)/shard_map/ppermute | solution.py:47
  122.3 1.0 collective-permute-done.21.swap_left
  123.3 0.0 collective-permute-done.19.same_right
  123.3 2.3 %collective-permute-done.20.crossed_right = bf16[144,640]{1,0:T(8,128)(2,1)S(1)} collective-permute-done((bf16[144,640]{1,0:T(8,128)(2,1)S(1)}, bf16[144,640]{1,0:T(8,128)(2,1)S(1)}, u32[]{:S(2)}, u32[]{:S(2)}) %collective-permute-start.20) | collective-permute-done | bytes 184352 | tf_op jit(solution)/shard_map/ppermute | solution.py:47
  125.6 0.0 collective-permute-done.22.swap_right
  125.6 1.7 %finish.1 = (f32[1,144,1152]{2,1,0:T(8,128)}, f32[1,144,1152]{2,1,0:T(8,128)}) custom-call(s32[5]{0:T(128)S(1)} %stack.31.flags, bf16[144,512]{1,0:T(8,128)(2,1)S(1)} %collective-permute-done.17.same_left, bf16[144,512]{1,0:T(8,128)(2,1)S(1)} %collective-permute-done.18.crossed_left, bf16[144,640]{1,0:T(8,128)(2,1)S(1)} %collective-permute-done.19.same_right, ...), custom_call_target="tpu_custom_call" | custom-call | flops 663552 | bytes 2985984 | tf_op jit(solution)/shard_map/finish/pallas_call | solution.py:450
  (3 shorter events, 0.1 us)
Async XLA Ops:
  1.7 17.3 %collective-permute-start = (bf16[128,1152]{1,0:T(8,128)(2,1)S(1)}, bf16[128,1152]{1,0:T(8,128)(2,1)S(1)}, u32[]{:S(2)}, u32[]{:S(2)}) collective-permute-start(bf16[128,1152]{1,0:T(8,128)(2,1)S(1)} %get-tuple-element.54), channel_id=1, source_target_pairs={{0,1},{1,0},{2,3},{3,2},{4,5},{5,4},{6,7},{7,6},{8,9},{9,8},{10,11... | collective-permute-start | bytes 884744 | tf_op jit(solution)/shard_map/ppermute | solution.py:47
  22.6 15.8 %collective-permute-start.1 = (bf16[256,1152]{1,0:T(8,128)(2,1)S(1)}, bf16[256,1152]{1,0:T(8,128)(2,1)S(1)}, u32[]{:S(2)}, u32[]{:S(2)}) collective-permute-start(bf16[256,1152]{1,0:T(8,128)(2,1)S(1)} %get-tuple-element.32.z_ref), channel_id=1, source_target_pairs={{1,8},{3,10},{5,12},{7,14},{8,1},{9,16},{10,3},{11,18},{12,5},{13,... | collective-permute-start | bytes 1769480 | tf_op jit(solution)/shard_map/ppermute | solution.py:47
  24.5 18.0 %collective-permute-start.3 = (bf16[256,1152]{1,0:T(8,128)(2,1)S(1)}, bf16[256,1152]{1,0:T(8,128)(2,1)S(1)}, u32[]{:S(2)}, u32[]{:S(2)}) collective-permute-start(bf16[256,1152]{1,0:T(8,128)(2,1)S(1)} %get-tuple-element.32.z_ref), channel_id=1, source_target_pairs={{0,1009},{2,1011},{4,1013},{6,1015},{8,1017},{10,1019},{12,1021},{... | collective-permute-start | bytes 1769480 | tf_op jit(solution)/shard_map/ppermute | solution.py:47
  38.4 16.4 %collective-permute-start.2 = (bf16[256,1152]{1,0:T(8,128)(2,1)S(1)}, bf16[256,1152]{1,0:T(8,128)(2,1)S(1)}, u32[]{:S(2)}, u32[]{:S(2)}) collective-permute-start(bf16[256,1152]{1,0:T(8,128)(2,1)S(1)} %collective-permute-done.1.one), channel_id=1, source_target_pairs={{8,16},{9,1},{10,18},{11,3},{12,20},{13,5},{14,22},{15,7},{16,24},... | collective-permute-start | bytes 1769480 | tf_op jit(solution)/shard_map/ppermute | solution.py:47
  39.8 27.4 %collective-permute-start.9 = (bf16[864,256]{1,0:T(8,128)(2,1)S(1)}, bf16[864,256]{1,0:T(8,128)(2,1)S(1)}, u32[]{:S(2)}, u32[]{:S(2)}) collective-permute-start(bf16[864,256]{1,0:T(8,128)(2,1)S(1)} %slice.10), channel_id=1, source_target_pairs={{0,2},{1,3},{6,4},{7,5},{8,10},{9,11},{14,12},{15,13},{16,18},{17,... | collective-permute-start | bytes 1327112 | tf_op jit(solution)/shard_map/ppermute | solution.py:47
  41.1 29.5 %collective-permute-start.6 = (bf16[256,1152]{1,0:T(8,128)(2,1)S(1)}, bf16[256,1152]{1,0:T(8,128)(2,1)S(1)}, u32[]{:S(2)}, u32[]{:S(2)}) collective-permute-start(bf16[256,1152]{1,0:T(8,128)(2,1)S(1)} %collective-permute-done.1.one), channel_id=1, source_target_pairs={{9,1017},{11,1019},{13,1021},{15,1023},{48,64},{50,66},{52,68},{54... | collective-permute-start | bytes 1769480 | tf_op jit(solution)/shard_map/ppermute | solution.py:47
  41.8 26.7 %collective-permute-start.8 = (bf16[576,256]{1,0:T(8,128)(2,1)S(1)}, bf16[576,256]{1,0:T(8,128)(2,1)S(1)}, u32[]{:S(2)}, u32[]{:S(2)}) collective-permute-start(bf16[576,256]{1,0:T(8,128)(2,1)S(1)} %slice.9), channel_id=1, source_target_pairs={{2,4},{3,5},{4,2},{5,3},{10,12},{11,13},{12,10},{13,11},{18,20},{1... | collective-permute-start | bytes 884744 | tf_op jit(solution)/shard_map/ppermute | solution.py:47
  42.5 28.1 %collective-permute-start.7 = (bf16[256,1152]{1,0:T(8,128)(2,1)S(1)}, bf16[256,1152]{1,0:T(8,128)(2,1)S(1)}, u32[]{:S(2)}, u32[]{:S(2)}) collective-permute-start(bf16[256,1152]{1,0:T(8,128)(2,1)S(1)} %collective-permute-done.3.cross_one), channel_id=1, source_target_pairs={{8,0},{10,2},{12,4},{14,6},{49,57},{51,59},{53,61},{55,63},{72,64}... | collective-permute-start | bytes 1769480 | tf_op jit(solution)/shard_map/ppermute | solution.py:47
  55.5 15.1 %collective-permute-start.4 = (bf16[256,1152]{1,0:T(8,128)(2,1)S(1)}, bf16[256,1152]{1,0:T(8,128)(2,1)S(1)}, u32[]{:S(2)}, u32[]{:S(2)}) collective-permute-start(bf16[256,1152]{1,0:T(8,128)(2,1)S(1)} %get-tuple-element.32.z_ref), channel_id=1, source_target_pairs={{0,1},{1,0},{2,3},{3,2},{4,5},{5,4},{6,7},{7,6},{8,9},{9,8},{10,11... | collective-permute-start | bytes 1769480 | tf_op jit(solution)/shard_map/ppermute | solution.py:47
  67.2 10.6 %collective-permute-start.5 = (bf16[256,1152]{1,0:T(8,128)(2,1)S(1)}, bf16[256,1152]{1,0:T(8,128)(2,1)S(1)}, u32[]{:S(2)}, u32[]{:S(2)}) collective-permute-start(bf16[256,1152]{1,0:T(8,128)(2,1)S(1)} %choose.1), channel_id=1, source_target_pairs={{0,8},{2,10},{4,12},{6,14},{8,16},{9,1},{10,18},{11,3},{12,20},{13... | collective-permute-start | bytes 1769480 | tf_op jit(solution)/shard_map/ppermute | solution.py:47
  68.5 2.1 %collective-permute-start.10 = (bf16[576,256]{1,0:T(8,128)(2,1)S(1)}, bf16[576,256]{1,0:T(8,128)(2,1)S(1)}, u32[]{:S(2)}, u32[]{:S(2)}) collective-permute-start(bf16[576,256]{1,0:T(8,128)(2,1)S(1)} %slice.12), channel_id=1, source_target_pairs={{2,4},{3,5},{4,2},{5,3},{10,12},{11,13},{12,10},{13,11},{18,20},{1... | collective-permute-start | bytes 884744 | tf_op jit(solution)/shard_map/ppermute | solution.py:47
  80.6 16.7 %collective-permute-start.11 = (bf16[256,640]{1,0:T(8,128)(2,1)S(1)}, bf16[256,640]{1,0:T(8,128)(2,1)S(1)}, u32[]{:S(2)}, u32[]{:S(2)}) collective-permute-start(bf16[256,640]{1,0:T(8,128)(2,1)S(1)} %get-tuple-element.35.refs_1_), channel_id=1, source_target_pairs={{0,2},{1,3},{6,4},{7,5},{8,10},{9,11},{14,12},{15,13},{16,18},{17,... | collective-permute-start | bytes 983048 | tf_op jit(solution)/shard_map/ppermute | solution.py:47
  85.3 12.0 %collective-permute-start.14 = (bf16[256,640]{1,0:T(8,128)(2,1)S(1)}, bf16[256,640]{1,0:T(8,128)(2,1)S(1)}, u32[]{:S(2)}, u32[]{:S(2)}) collective-permute-start(bf16[256,640]{1,0:T(8,128)(2,1)S(1)} %get-tuple-element.35.refs_1_), channel_id=1, source_target_pairs={{2,4},{3,5},{4,2},{5,3},{10,12},{11,13},{12,10},{13,11},{18,20},{1... | collective-permute-start | bytes 983048 | tf_op jit(solution)/shard_map/ppermute | solution.py:47
  86.0 10.6 %collective-permute-start.12 = (bf16[256,512]{1,0:T(8,128)(2,1)S(1)}, bf16[256,512]{1,0:T(8,128)(2,1)S(1)}, u32[]{:S(2)}, u32[]{:S(2)}) collective-permute-start(bf16[256,512]{1,0:T(8,128)(2,1)S(1)} %get-tuple-element.36.refs_0_), channel_id=1, source_target_pairs={{0,2},{1,3},{6,4},{7,5},{8,10},{9,11},{14,12},{15,13},{16,18},{17,... | collective-permute-start | bytes 786440 | tf_op jit(solution)/shard_map/ppermute | solution.py:47
  88.9 8.4 %collective-permute-start.13 = (bf16[256,512]{1,0:T(8,128)(2,1)S(1)}, bf16[256,512]{1,0:T(8,128)(2,1)S(1)}, u32[]{:S(2)}, u32[]{:S(2)}) collective-permute-start(bf16[256,512]{1,0:T(8,128)(2,1)S(1)} %get-tuple-element.36.refs_0_), channel_id=1, source_target_pairs={{2,4},{3,5},{4,2},{5,3},{10,12},{11,13},{12,10},{13,11},{18,20},{1... | collective-permute-start | bytes 786440 | tf_op jit(solution)/shard_map/ppermute | solution.py:47
  96.7 2.6 %collective-permute-start.15 = (bf16[256,512]{1,0:T(8,128)(2,1)S(1)}, bf16[256,512]{1,0:T(8,128)(2,1)S(1)}, u32[]{:S(2)}, u32[]{:S(2)}) collective-permute-start(bf16[256,512]{1,0:T(8,128)(2,1)S(1)} %collective-permute-done.12.refs_2_), channel_id=1, source_target_pairs={{2,4},{3,5},{4,2},{5,3},{10,12},{11,13},{12,10},{13,11},{18,20},{1... | collective-permute-start | bytes 786440 | tf_op jit(solution)/shard_map/ppermute | solution.py:47
  98.5 4.1 %collective-permute-start.16 = (bf16[256,640]{1,0:T(8,128)(2,1)S(1)}, bf16[256,640]{1,0:T(8,128)(2,1)S(1)}, u32[]{:S(2)}, u32[]{:S(2)}) collective-permute-start(bf16[256,640]{1,0:T(8,128)(2,1)S(1)} %collective-permute-done.11.refs_3_), channel_id=1, source_target_pairs={{2,4},{3,5},{4,2},{5,3},{10,12},{11,13},{12,10},{13,11},{18,20},{1... | collective-permute-start | bytes 983048 | tf_op jit(solution)/shard_map/ppermute | solution.py:47
  100.0 10.9 %collective-permute-start.17 = (bf16[144,512]{1,0:T(8,128)(2,1)S(1)}, bf16[144,512]{1,0:T(8,128)(2,1)S(1)}, u32[]{:S(2)}, u32[]{:S(2)}) collective-permute-start(bf16[144,512]{1,0:T(8,128)(2,1)S(1)} %get-tuple-element.45), channel_id=1, source_target_pairs={{2,0},{3,1},{4,6},{5,7},{10,8},{11,9},{12,14},{13,15},{18,16},{19,... | collective-permute-start | bytes 442376 | tf_op jit(solution)/shard_map/ppermute | solution.py:47
  101.3 16.6 %collective-permute-start.18 = (bf16[144,512]{1,0:T(8,128)(2,1)S(1)}, bf16[144,512]{1,0:T(8,128)(2,1)S(1)}, u32[]{:S(2)}, u32[]{:S(2)}) collective-permute-start(bf16[144,512]{1,0:T(8,128)(2,1)S(1)} %get-tuple-element.46), channel_id=1, source_target_pairs={{2,1},{3,0},{4,7},{5,6},{10,9},{11,8},{12,15},{13,14},{18,17},{19,... | collective-permute-start | bytes 442376 | tf_op jit(solution)/shard_map/ppermute | solution.py:47
  103.5 19.8 %collective-permute-start.19 = (bf16[144,640]{1,0:T(8,128)(2,1)S(1)}, bf16[144,640]{1,0:T(8,128)(2,1)S(1)}, u32[]{:S(2)}, u32[]{:S(2)}) collective-permute-start(bf16[144,640]{1,0:T(8,128)(2,1)S(1)} %get-tuple-element.49), channel_id=1, source_target_pairs={{2,0},{3,1},{4,6},{5,7},{10,8},{11,9},{12,14},{13,15},{18,16},{19,... | collective-permute-start | bytes 552968 | tf_op jit(solution)/shard_map/ppermute | solution.py:47
  104.8 20.8 %collective-permute-start.20 = (bf16[144,640]{1,0:T(8,128)(2,1)S(1)}, bf16[144,640]{1,0:T(8,128)(2,1)S(1)}, u32[]{:S(2)}, u32[]{:S(2)}) collective-permute-start(bf16[144,640]{1,0:T(8,128)(2,1)S(1)} %get-tuple-element.50), channel_id=1, source_target_pairs={{2,1},{3,0},{4,7},{5,6},{10,9},{11,8},{12,15},{13,14},{18,17},{19,... | collective-permute-start | bytes 552968 | tf_op jit(solution)/shard_map/ppermute | solution.py:47
  117.9 7.6 %collective-permute-start.22 = (bf16[144,640]{1,0:T(8,128)(2,1)S(1)}, bf16[144,640]{1,0:T(8,128)(2,1)S(1)}, u32[]{:S(2)}, u32[]{:S(2)}) collective-permute-start(bf16[144,640]{1,0:T(8,128)(2,1)S(1)} %get-tuple-element.52), channel_id=1, source_target_pairs={{0,1},{1,0},{2,3},{3,2},{4,5},{5,4},{6,7},{7,6},{8,9},{9,8},{10,11... | collective-permute-start | bytes 552968 | tf_op jit(solution)/shard_map/ppermute | solution.py:47
  119.9 3.4 %collective-permute-start.21 = (bf16[144,512]{1,0:T(8,128)(2,1)S(1)}, bf16[144,512]{1,0:T(8,128)(2,1)S(1)}, u32[]{:S(2)}, u32[]{:S(2)}) collective-permute-start(bf16[144,512]{1,0:T(8,128)(2,1)S(1)} %get-tuple-element.51), channel_id=1, source_target_pairs={{0,1},{1,0},{2,3},{3,2},{4,5},{5,4},{6,7},{7,6},{8,9},{9,8},{10,11... | collective-permute-start | bytes 442376 | tf_op jit(solution)/shard_map/ppermute | solution.py:47

commit v4 on v3

--- a/solution.py
+++ b/solution.py
@@ -78,25 +78,33 @@
 
 
 def first_crossing(x, zh, y, zl, c):
-    if c == 1 and y >= 6:
-        return (*above(x, zh, y - 6), zl, 0)
-    if c == 0 and y <= 1:
-        return (*below(x, zh, y + 6), zl, 1)
+    if c == 1 and y in (5, 7):
+        return (*above(x, zh, 1 if y == 7 else 5), zl, 0)
+    if c == 0 and y in (0, 2):
+        return (*below(x, zh, 6 if y == 0 else 2), zl, 1)
     return None
 
 
 def second_crossing(x, zh, y, zl, c):
-    if c == 0 and y == 6:
+    if c == 0 and y == 7:
         return (*above(x, zh, 0), zl, 0)
-    if c == 1 and y == 1:
+    if c == 1 and y == 0:
         return (*below(x, zh, 7), zl, 1)
     return None
 
 
-def from_second(x, zh, y, zl, c):
+def from_near(x, zh, y, zl, c):
     if c == 0 and y == 1:
         return (x, zh, 0, zl, 0)
     if c == 1 and y == 6:
+        return (x, zh, 7, zl, 1)
+    return None
+
+
+def from_afar(x, zh, y, zl, c):
+    if c == 0 and y == 5:
+        return (x, zh, 0, zl, 0)
+    if c == 1 and y == 2:
         return (x, zh, 7, zl, 1)
     return None
 
@@ -201,10 +209,14 @@
     )(flags, own, recv)
 
 
-def choose_kernel(flags, two, cross_one, out_ref, sem):
+def choose_kernel(flags, two, cross_one, cross_two, out_ref, sem):
     place = flags[1]
 
-    @pl.when(place <= 1)
+    @pl.when(place == 0)
+    def _():
+        pltpu.make_async_copy(cross_two, out_ref, sem).start()
+
+    @pl.when(place == 1)
     def _():
         pltpu.make_async_copy(cross_one, out_ref, sem).start()
 
@@ -215,24 +227,24 @@
     pltpu.make_async_copy(two, out_ref, sem).wait()
 
 
-def choose(flags, two, cross_one):
+def choose(flags, two, cross_one, cross_two):
     return pl.pallas_call(
         choose_kernel,
         name="choose",
         out_shape=jax.ShapeDtypeStruct((2 * ROWS, D), BF),
-        in_specs=[SMEM] + [ANY] * 2,
+        in_specs=[SMEM] + [ANY] * 3,
         out_specs=VMEM,
         scratch_shapes=[pltpu.SemaphoreType.DMA(())],
         compiler_params=PARAMS,
         cost_estimate=pl.CostEstimate(
             flops=0, bytes_accessed=8 * ROWS * D, transcendentals=0
         ),
-    )(flags, two, cross_one)
+    )(flags, two, cross_one, cross_two)
 
 
 def pairs_kernel(
     flags, scale, z_ref, u_ref, rn_ref,
-    here, one, two, three, cross_one, cross_two, second, early_mid, early_far,
+    here, one, two, three, cross_one, cross_two, near_one, afar_one, early_mid, early_far,
     dx_left, dx_right, others, sems,
 ):
     del early_mid, early_far
@@ -255,10 +267,11 @@
 
     @pl.when(place == 0)
     def _():
-        fetch(second, 1)
-        fetch(cross_two, 3)
-
-    @pl.when(place <= 1)
+        fetch(near_one, 1)
+        fetch(cross_two, 2)
+        fetch(afar_one, 3)
+
+    @pl.when(place == 1)
     def _():
         fetch(cross_one, 2)
 
@@ -302,7 +315,7 @@
             jax.ShapeDtypeStruct((rows, LEFT), BF),
             jax.ShapeDtypeStruct((rows, D - LEFT), BF),
         ),
-        in_specs=[SMEM, SMEM] + [VMEM] * 3 + [ANY] * 9,
+        in_specs=[SMEM, SMEM] + [VMEM] * 3 + [ANY] * 10,
         out_specs=(VMEM, VMEM),
         scratch_shapes=[
             pltpu.VMEM((2, 4 * ROWS, D), BF),
@@ -476,17 +489,18 @@
     cross_one = send(z, first_crossing)
     ft = turn(flags, own, received)
     one, ft = lax.optimization_barrier((one, ft))
+    two = send(one, second_hop)
+    cross_two = send(one, second_crossing)
     ft_end = send(ft[CHIP:], inward)
     ft_mid = send(ft[2 * CHIP :], middle)
+    near_one = send(cross_one, from_near)
+    afar_one = send(cross_one, from_afar)
     ft_far = send(ft_end[CHIP:], middle)
-    two = send(one, second_hop)
-    cross_two = send(one, second_crossing)
-    second = send(cross_one, from_second)
-    chosen, z_late = lax.optimization_barrier((choose(flags, two, cross_one), z))
-    three = send(chosen, third_hop)
-    here = send(z_late, other_core)
+    three = send(choose(flags, two, cross_one, cross_two), third_hop)
+    here = send(z, other_core)
     dxs = pairs(
-        flags, scale, z, u, rn, here, one, two, three, cross_one, cross_two, second, ft_mid, ft_far
+        flags, scale, z, u, rn, here, one, two, three,
+        cross_one, cross_two, near_one, afar_one, ft_mid, ft_far,
     )
 
     ends = [send(dx, inward) for dx in dxs]

time: 128 us -> 128 us (level)
  the two profiles are of different devices: /device:TPU:1 before, /device:TPU:15 now
where the time goes in v4:
time: 128 us; the launch traced here: 127 us
  starting transfers between devices  65.7 us (51%)
  waiting for transfers between devices  44.6 us (35%)
  Pallas kernels  13.1 us (10%)
  between operations  2.31 us (2%)
    ppermute x24, starting transfers between devices, send(): return lax.ppermute(value, NAMES, pairs_of(rule))  65.7 us
    ppermute x24, waiting for transfers between devices, send(): return lax.ppermute(value, NAMES, pairs_of(rule))  44.6 us
    pallas_call x1, Pallas kernels, project(): pl.pallas_call(project_kernel, name='project', out_shape=(jax.ShapeDtypeS...  3.58 us
    pallas_call x1, Pallas kernels, pairs(): pl.pallas_call(pairs_kernel, name='pairs', out_shape=(jax.ShapeDtypeStruc...  2.81 us
  transfers between devices with their start and end apart: 24, of which 9 were waited for; matrix products, arithmetic and copies ran while one was open for 0% of the time, Pallas kernels for 4%

profile of v4, /device:TPU:15, one launch (start us, length us, event | category | flops | bytes accessed | tf_op | source)
XLA Modules:
  0.0 127.0 jit_solution(2300088148634837176)
XLA Ops:
  0.6 1.1 broadcast_select_fusion
  1.7 2.6 %collective-permute-start = (bf16[128,1152]{1,0:T(8,128)(2,1)S(1)}, bf16[128,1152]{1,0:T(8,128)(2,1)S(1)}, u32[]{:S(2)}, u32[]{:S(2)}) collective-permute-start(bf16[128,1152]{1,0:T(8,128)(2,1)S(1)} %get-tuple-element.50), channel_id=1, source_target_pairs={{0,1},{1,0},{2,3},{3,2},{4,5},{5,4},{6,7},{7,6},{8,9},{9,8},{10,11... | collective-permute-start | bytes 884744 | tf_op jit(solution)/shard_map/ppermute | solution.py:47
  4.4 0.1 stack.31.flags
  4.4 1.1 collective-permute-done.recv
  5.5 3.6 %project.1 = (bf16[256,1152]{1,0:T(8,128)(2,1)S(1)}, f32[256,1152]{1,0:T(8,128)S(1)}, f32[256,128]{1,0:T(8,128)S(1)}) custom-call(s32[5]{0:T(128)S(1)} %stack.31.flags, bf16[128,1152]{1,0:T(8,128)(2,1)S(1)} %get-tuple-element.51.own, bf16[128,1152]{1,0:T(8,128)(2,1)S(1)} %collective-permute-done.recv, bf16[1152,1152]{1,0:T(8,128)(2,1)} %wp.1, ...), custom_call_target="tpu_custom_call" | custom-call | flops 679477248 | bytes 5013504 | tf_op jit(solution)/shard_map/project/pallas_call | solution.py:166
  9.1 3.6 %collective-permute-start.2 = (bf16[256,1152]{1,0:T(8,128)(2,1)S(1)}, bf16[256,1152]{1,0:T(8,128)(2,1)S(1)}, u32[]{:S(2)}, u32[]{:S(2)}) collective-permute-start(bf16[256,1152]{1,0:T(8,128)(2,1)S(1)} %get-tuple-element.26.z_ref), channel_id=1, source_target_pairs={{1,8},{3,10},{5,12},{7,14},{8,1},{9,16},{10,3},{11,18},{12,5},{13,... | collective-permute-start | bytes 1769480 | tf_op jit(solution)/shard_map/ppermute | solution.py:47
  12.7 0.7 collective-permute-start.4
  13.4 0.8 turn.1.ft
  14.2 6.1 %collective-permute-done.2.one = bf16[256,1152]{1,0:T(8,128)(2,1)S(1)} collective-permute-done((bf16[256,1152]{1,0:T(8,128)(2,1)S(1)}, bf16[256,1152]{1,0:T(8,128)(2,1)S(1)}, u32[]{:S(2)}, u32[]{:S(2)}) %collective-permute-start.2) | collective-permute-done | bytes 589856 | tf_op jit(solution)/shard_map/ppermute | solution.py:47
  20.3 10.5 %collective-permute-start.5 = (bf16[256,1152]{1,0:T(8,128)(2,1)S(1)}, bf16[256,1152]{1,0:T(8,128)(2,1)S(1)}, u32[]{:S(2)}, u32[]{:S(2)}) collective-permute-start(bf16[256,1152]{1,0:T(8,128)(2,1)S(1)} %collective-permute-done.2.one), channel_id=1, source_target_pairs={{1,1017},{3,1019},{5,1021},{7,1023},{56,64},{58,66},{60,68},{62,70... | collective-permute-start | bytes 1769480 | tf_op jit(solution)/shard_map/ppermute | solution.py:47
  30.9 1.3 %collective-permute-start.3 = (bf16[256,1152]{1,0:T(8,128)(2,1)S(1)}, bf16[256,1152]{1,0:T(8,128)(2,1)S(1)}, u32[]{:S(2)}, u32[]{:S(2)}) collective-permute-start(bf16[256,1152]{1,0:T(8,128)(2,1)S(1)} %collective-permute-done.2.one), channel_id=1, source_target_pairs={{8,16},{9,1},{10,18},{11,3},{12,20},{13,5},{14,22},{15,7},{16,24},... | collective-permute-start | bytes 1769480 | tf_op jit(solution)/shard_map/ppermute | solution.py:47
  32.2 4.3 %collective-permute-start.1 = (bf16[256,1152]{1,0:T(8,128)(2,1)S(1)}, bf16[256,1152]{1,0:T(8,128)(2,1)S(1)}, u32[]{:S(2)}, u32[]{:S(2)}) collective-permute-start(bf16[256,1152]{1,0:T(8,128)(2,1)S(1)} %get-tuple-element.26.z_ref), channel_id=1, source_target_pairs={{0,1},{1,0},{2,3},{3,2},{4,5},{5,4},{6,7},{7,6},{8,9},{9,8},{10,11... | collective-permute-start | bytes 1769480 | tf_op jit(solution)/shard_map/ppermute | solution.py:47
  36.5 4.0 %collective-permute-start.10 = (bf16[864,256]{1,0:T(8,128)(2,1)S(1)}, bf16[864,256]{1,0:T(8,128)(2,1)S(1)}, u32[]{:S(2)}, u32[]{:S(2)}) collective-permute-start(bf16[864,256]{1,0:T(8,128)(2,1)S(1)} %slice.10), channel_id=1, source_target_pairs={{0,2},{1,3},{6,4},{7,5},{8,10},{9,11},{14,12},{15,13},{16,18},{17,... | collective-permute-start | bytes 1327112 | tf_op jit(solution)/shard_map/ppermute | solution.py:47
  40.6 0.0 collective-permute-done.4.cross_one
  40.6 0.7 collective-permute-start.8
  41.3 1.6 %collective-permute-done.5.cross_two = bf16[256,1152]{1,0:T(8,128)(2,1)S(1)} collective-permute-done((bf16[256,1152]{1,0:T(8,128)(2,1)S(1)}, bf16[256,1152]{1,0:T(8,128)(2,1)S(1)}, u32[]{:S(2)}, u32[]{:S(2)}) %collective-permute-start.5) | collective-permute-done | bytes 589856 | tf_op jit(solution)/shard_map/ppermute | solution.py:47
  42.9 0.7 collective-permute-start.7
  43.5 0.0 collective-permute-done.3.two
  43.6 0.7 choose.1
  44.3 1.3 %collective-permute-start.6 = (bf16[256,1152]{1,0:T(8,128)(2,1)S(1)}, bf16[256,1152]{1,0:T(8,128)(2,1)S(1)}, u32[]{:S(2)}, u32[]{:S(2)}) collective-permute-start(bf16[256,1152]{1,0:T(8,128)(2,1)S(1)} %choose.1), channel_id=1, source_target_pairs={{0,8},{2,10},{4,12},{6,14},{8,16},{9,1},{10,18},{11,3},{12,20},{13... | collective-permute-start | bytes 1769480 | tf_op jit(solution)/shard_map/ppermute | solution.py:47
  45.6 10.4 %collective-permute-done.10.feats_end = bf16[864,256]{1,0:T(8,128)(2,1)S(1)} collective-permute-done((bf16[864,256]{1,0:T(8,128)(2,1)S(1)}, bf16[864,256]{1,0:T(8,128)(2,1)S(1)}, u32[]{:S(2)}, u32[]{:S(2)}) %collective-permute-start.10) | collective-permute-done | bytes 442400 | tf_op jit(solution)/shard_map/ppermute | solution.py:47
  56.0 0.7 collective-permute-start.9
  56.7 0.0 collective-permute-done.1.here
  56.7 0.7 collective-permute-start.11
  58.7 0.1 pad_maximum_fusion.scale
  58.7 0.0 collective-permute-done.9.early_mid.feats_mid
  58.7 0.0 collective-permute-done.8.afar_one
  58.7 0.0 collective-permute-done.7.near_one
  58.7 0.0 collective-permute-done.11.early_far.feats
  58.8 1.1 collective-permute-done.6.three
  59.9 2.8 %pairs.1 = (bf16[256,512]{1,0:T(8,128)(2,1)S(1)}, bf16[256,640]{1,0:T(8,128)(2,1)S(1)}) custom-call(s32[5]{0:T(128)S(1)} %stack.31.flags, f32[2]{0:T(128)S(1)} %pad_maximum_fusion.scale, bf16[256,1152]{1,0:T(8,128)(2,1)S(1)} %get-tuple-element.26.z_ref, f32[256,1152]{1,0:T(8,128)S(1)} %get-tuple-element.27.u_ref, f32[256,128]{1,0:T(8,128)S(1)} %get-tuple-element.28.rn_ref, ...), custom_call_target="tpu_custom_call" | custom-call | flops 603979776 | bytes 4128768 | tf_op jit(solution)/shard_map/pairs/pallas_call | solution.py:311
  62.7 0.7 collective-permute-start.15
  63.4 21.2 %collective-permute-start.12 = (bf16[256,640]{1,0:T(8,128)(2,1)S(1)}, bf16[256,640]{1,0:T(8,128)(2,1)S(1)}, u32[]{:S(2)}, u32[]{:S(2)}) collective-permute-start(bf16[256,640]{1,0:T(8,128)(2,1)S(1)} %get-tuple-element.31.refs_1_), channel_id=1, source_target_pairs={{0,2},{1,3},{6,4},{7,5},{8,10},{9,11},{14,12},{15,13},{16,18},{17,... | collective-permute-start | bytes 983048 | tf_op jit(solution)/shard_map/ppermute | solution.py:47
  84.6 1.3 %collective-permute-start.13 = (bf16[256,512]{1,0:T(8,128)(2,1)S(1)}, bf16[256,512]{1,0:T(8,128)(2,1)S(1)}, u32[]{:S(2)}, u32[]{:S(2)}) collective-permute-start(bf16[256,512]{1,0:T(8,128)(2,1)S(1)} %get-tuple-element.32.refs_0_), channel_id=1, source_target_pairs={{0,2},{1,3},{6,4},{7,5},{8,10},{9,11},{14,12},{15,13},{16,18},{17,... | collective-permute-start | bytes 786440 | tf_op jit(solution)/shard_map/ppermute | solution.py:47
  85.9 0.7 collective-permute-start.14
  86.6 6.2 %collective-permute-done.13.refs_2_ = bf16[256,512]{1,0:T(8,128)(2,1)S(1)} collective-permute-done((bf16[256,512]{1,0:T(8,128)(2,1)S(1)}, bf16[256,512]{1,0:T(8,128)(2,1)S(1)}, u32[]{:S(2)}, u32[]{:S(2)}) %collective-permute-start.13) | collective-permute-done | bytes 262176 | tf_op jit(solution)/shard_map/ppermute | solution.py:47
  92.8 0.7 collective-permute-start.16
  93.5 0.0 collective-permute-done.14.refs_4_
  93.5 0.0 collective-permute-done.15.refs_5_
  93.5 0.0 collective-permute-done.12.refs_3_
  93.5 1.2 near.1
  94.7 0.7 collective-permute-start.17
  95.3 0.0 collective-permute-done.16.dx.dx_left
  95.4 0.8 far.2
  96.2 1.3 %collective-permute-start.18 = (bf16[144,512]{1,0:T(8,128)(2,1)S(1)}, bf16[144,512]{1,0:T(8,128)(2,1)S(1)}, u32[]{:S(2)}, u32[]{:S(2)}) collective-permute-start(bf16[144,512]{1,0:T(8,128)(2,1)S(1)} %get-tuple-element.41), channel_id=1, source_target_pairs={{2,0},{3,1},{4,6},{5,7},{10,8},{11,9},{12,14},{13,15},{18,16},{19,... | collective-permute-start | bytes 442376 | tf_op jit(solution)/shard_map/ppermute | solution.py:47
  97.5 1.3 %collective-permute-start.19 = (bf16[144,512]{1,0:T(8,128)(2,1)S(1)}, bf16[144,512]{1,0:T(8,128)(2,1)S(1)}, u32[]{:S(2)}, u32[]{:S(2)}) collective-permute-start(bf16[144,512]{1,0:T(8,128)(2,1)S(1)} %get-tuple-element.42), channel_id=1, source_target_pairs={{2,1},{3,0},{4,7},{5,6},{10,9},{11,8},{12,15},{13,14},{18,17},{19,... | collective-permute-start | bytes 442376 | tf_op jit(solution)/shard_map/ppermute | solution.py:47
  98.8 0.0 collective-permute-done.17.dx.dx_right
  98.8 0.9 far.3
  99.7 1.3 %collective-permute-start.20 = (bf16[144,640]{1,0:T(8,128)(2,1)S(1)}, bf16[144,640]{1,0:T(8,128)(2,1)S(1)}, u32[]{:S(2)}, u32[]{:S(2)}) collective-permute-start(bf16[144,640]{1,0:T(8,128)(2,1)S(1)} %get-tuple-element.45), channel_id=1, source_target_pairs={{2,0},{3,1},{4,6},{5,7},{10,8},{11,9},{12,14},{13,15},{18,16},{19,... | collective-permute-start | bytes 552968 | tf_op jit(solution)/shard_map/ppermute | solution.py:47
  101.0 1.3 %collective-permute-start.21 = (bf16[144,640]{1,0:T(8,128)(2,1)S(1)}, bf16[144,640]{1,0:T(8,128)(2,1)S(1)}, u32[]{:S(2)}, u32[]{:S(2)}) collective-permute-start(bf16[144,640]{1,0:T(8,128)(2,1)S(1)} %get-tuple-element.46), channel_id=1, source_target_pairs={{2,1},{3,0},{4,7},{5,6},{10,9},{11,8},{12,15},{13,14},{18,17},{19,... | collective-permute-start | bytes 552968 | tf_op jit(solution)/shard_map/ppermute | solution.py:47
  102.3 0.6 rest.1
  102.9 3.8 %collective-permute-done.18.same_left = bf16[144,512]{1,0:T(8,128)(2,1)S(1)} collective-permute-done((bf16[144,512]{1,0:T(8,128)(2,1)S(1)}, bf16[144,512]{1,0:T(8,128)(2,1)S(1)}, u32[]{:S(2)}, u32[]{:S(2)}) %collective-permute-start.18) | collective-permute-done | bytes 147488 | tf_op jit(solution)/shard_map/ppermute | solution.py:47
  106.7 13.3 %collective-permute-done.19.crossed_left = bf16[144,512]{1,0:T(8,128)(2,1)S(1)} collective-permute-done((bf16[144,512]{1,0:T(8,128)(2,1)S(1)}, bf16[144,512]{1,0:T(8,128)(2,1)S(1)}, u32[]{:S(2)}, u32[]{:S(2)}) %collective-permute-start.19) | collective-permute-done | bytes 147488 | tf_op jit(solution)/shard_map/ppermute | solution.py:47
  120.0 1.9 %collective-permute-start.23 = (bf16[144,640]{1,0:T(8,128)(2,1)S(1)}, bf16[144,640]{1,0:T(8,128)(2,1)S(1)}, u32[]{:S(2)}, u32[]{:S(2)}) collective-permute-start(bf16[144,640]{1,0:T(8,128)(2,1)S(1)} %get-tuple-element.48), channel_id=1, source_target_pairs={{0,1},{1,0},{2,3},{3,2},{4,5},{5,4},{6,7},{7,6},{8,9},{9,8},{10,11... | collective-permute-start | bytes 552968 | tf_op jit(solution)/shard_map/ppermute | solution.py:47
  121.9 2.4 %collective-permute-start.22 = (bf16[144,512]{1,0:T(8,128)(2,1)S(1)}, bf16[144,512]{1,0:T(8,128)(2,1)S(1)}, u32[]{:S(2)}, u32[]{:S(2)}) collective-permute-start(bf16[144,512]{1,0:T(8,128)(2,1)S(1)} %get-tuple-element.47), channel_id=1, source_target_pairs={{0,1},{1,0},{2,3},{3,2},{4,5},{5,4},{6,7},{7,6},{8,9},{9,8},{10,11... | collective-permute-start | bytes 442376 | tf_op jit(solution)/shard_map/ppermute | solution.py:47
  124.3 1.0 collective-permute-done.22.swap_left
  125.3 0.0 collective-permute-done.20.same_right
  125.3 0.0 collective-permute-done.21.crossed_right
  125.3 0.0 collective-permute-done.23.swap_right
  125.3 1.7 %finish.1 = (f32[1,144,1152]{2,1,0:T(8,128)}, f32[1,144,1152]{2,1,0:T(8,128)}) custom-call(s32[5]{0:T(128)S(1)} %stack.31.flags, bf16[144,512]{1,0:T(8,128)(2,1)S(1)} %collective-permute-done.18.same_left, bf16[144,512]{1,0:T(8,128)(2,1)S(1)} %collective-permute-done.19.crossed_left, bf16[144,640]{1,0:T(8,128)(2,1)S(1)} %collective-permute-done.20.same_right, ...), custom_call_target="tpu_custom_call" | custom-call | flops 663552 | bytes 2985984 | tf_op jit(solution)/shard_map/finish/pallas_call | solution.py:463
  (3 shorter events, 0.1 us)
Async XLA Ops:
  1.7 3.8 %collective-permute-start = (bf16[128,1152]{1,0:T(8,128)(2,1)S(1)}, bf16[128,1152]{1,0:T(8,128)(2,1)S(1)}, u32[]{:S(2)}, u32[]{:S(2)}) collective-permute-start(bf16[128,1152]{1,0:T(8,128)(2,1)S(1)} %get-tuple-element.50), channel_id=1, source_target_pairs={{0,1},{1,0},{2,3},{3,2},{4,5},{5,4},{6,7},{7,6},{8,9},{9,8},{10,11... | collective-permute-start | bytes 884744 | tf_op jit(solution)/shard_map/ppermute | solution.py:47
  9.1 11.2 %collective-permute-start.2 = (bf16[256,1152]{1,0:T(8,128)(2,1)S(1)}, bf16[256,1152]{1,0:T(8,128)(2,1)S(1)}, u32[]{:S(2)}, u32[]{:S(2)}) collective-permute-start(bf16[256,1152]{1,0:T(8,128)(2,1)S(1)} %get-tuple-element.26.z_ref), channel_id=1, source_target_pairs={{1,8},{3,10},{5,12},{7,14},{8,1},{9,16},{10,3},{11,18},{12,5},{13,... | collective-permute-start | bytes 1769480 | tf_op jit(solution)/shard_map/ppermute | solution.py:47
  12.7 27.9 %collective-permute-start.4 = (bf16[256,1152]{1,0:T(8,128)(2,1)S(1)}, bf16[256,1152]{1,0:T(8,128)(2,1)S(1)}, u32[]{:S(2)}, u32[]{:S(2)}) collective-permute-start(bf16[256,1152]{1,0:T(8,128)(2,1)S(1)} %get-tuple-element.26.z_ref), channel_id=1, source_target_pairs={{0,1009},{2,1011},{4,1013},{6,1015},{16,977},{18,979},{20,981},{22... | collective-permute-start | bytes 1769480 | tf_op jit(solution)/shard_map/ppermute | solution.py:47
  20.3 22.5 %collective-permute-start.5 = (bf16[256,1152]{1,0:T(8,128)(2,1)S(1)}, bf16[256,1152]{1,0:T(8,128)(2,1)S(1)}, u32[]{:S(2)}, u32[]{:S(2)}) collective-permute-start(bf16[256,1152]{1,0:T(8,128)(2,1)S(1)} %collective-permute-done.2.one), channel_id=1, source_target_pairs={{1,1017},{3,1019},{5,1021},{7,1023},{56,64},{58,66},{60,68},{62,70... | collective-permute-start | bytes 1769480 | tf_op jit(solution)/shard_map/ppermute | solution.py:47
  30.9 12.7 %collective-permute-start.3 = (bf16[256,1152]{1,0:T(8,128)(2,1)S(1)}, bf16[256,1152]{1,0:T(8,128)(2,1)S(1)}, u32[]{:S(2)}, u32[]{:S(2)}) collective-permute-start(bf16[256,1152]{1,0:T(8,128)(2,1)S(1)} %collective-permute-done.2.one), channel_id=1, source_target_pairs={{8,16},{9,1},{10,18},{11,3},{12,20},{13,5},{14,22},{15,7},{16,24},... | collective-permute-start | bytes 1769480 | tf_op jit(solution)/shard_map/ppermute | solution.py:47
  32.2 24.5 %collective-permute-start.1 = (bf16[256,1152]{1,0:T(8,128)(2,1)S(1)}, bf16[256,1152]{1,0:T(8,128)(2,1)S(1)}, u32[]{:S(2)}, u32[]{:S(2)}) collective-permute-start(bf16[256,1152]{1,0:T(8,128)(2,1)S(1)} %get-tuple-element.26.z_ref), channel_id=1, source_target_pairs={{0,1},{1,0},{2,3},{3,2},{4,5},{5,4},{6,7},{7,6},{8,9},{9,8},{10,11... | collective-permute-start | bytes 1769480 | tf_op jit(solution)/shard_map/ppermute | solution.py:47
  36.5 19.4 %collective-permute-start.10 = (bf16[864,256]{1,0:T(8,128)(2,1)S(1)}, bf16[864,256]{1,0:T(8,128)(2,1)S(1)}, u32[]{:S(2)}, u32[]{:S(2)}) collective-permute-start(bf16[864,256]{1,0:T(8,128)(2,1)S(1)} %slice.10), channel_id=1, source_target_pairs={{0,2},{1,3},{6,4},{7,5},{8,10},{9,11},{14,12},{15,13},{16,18},{17,... | collective-permute-start | bytes 1327112 | tf_op jit(solution)/shard_map/ppermute | solution.py:47
  40.6 18.2 %collective-permute-start.8 = (bf16[256,1152]{1,0:T(8,128)(2,1)S(1)}, bf16[256,1152]{1,0:T(8,128)(2,1)S(1)}, u32[]{:S(2)}, u32[]{:S(2)}) collective-permute-start(bf16[256,1152]{1,0:T(8,128)(2,1)S(1)} %collective-permute-done.4.cross_one), channel_id=1, source_target_pairs={{17,57},{19,59},{21,61},{23,63},{40,0},{42,2},{44,4},{46,6},{81,12... | collective-permute-start | bytes 1769480 | tf_op jit(solution)/shard_map/ppermute | solution.py:47
  42.9 15.9 %collective-permute-start.7 = (bf16[256,1152]{1,0:T(8,128)(2,1)S(1)}, bf16[256,1152]{1,0:T(8,128)(2,1)S(1)}, u32[]{:S(2)}, u32[]{:S(2)}) collective-permute-start(bf16[256,1152]{1,0:T(8,128)(2,1)S(1)} %collective-permute-done.4.cross_one), channel_id=1, source_target_pairs={{8,0},{10,2},{12,4},{14,6},{49,57},{51,59},{53,61},{55,63},{72,64}... | collective-permute-start | bytes 1769480 | tf_op jit(solution)/shard_map/ppermute | solution.py:47
  44.3 15.6 %collective-permute-start.6 = (bf16[256,1152]{1,0:T(8,128)(2,1)S(1)}, bf16[256,1152]{1,0:T(8,128)(2,1)S(1)}, u32[]{:S(2)}, u32[]{:S(2)}) collective-permute-start(bf16[256,1152]{1,0:T(8,128)(2,1)S(1)} %choose.1), channel_id=1, source_target_pairs={{0,8},{2,10},{4,12},{6,14},{8,16},{9,1},{10,18},{11,3},{12,20},{13... | collective-permute-start | bytes 1769480 | tf_op jit(solution)/shard_map/ppermute | solution.py:47
  56.0 2.8 %collective-permute-start.9 = (bf16[576,256]{1,0:T(8,128)(2,1)S(1)}, bf16[576,256]{1,0:T(8,128)(2,1)S(1)}, u32[]{:S(2)}, u32[]{:S(2)}) collective-permute-start(bf16[576,256]{1,0:T(8,128)(2,1)S(1)} %slice.9), channel_id=1, source_target_pairs={{2,4},{3,5},{4,2},{5,3},{10,12},{11,13},{12,10},{13,11},{18,20},{1... | collective-permute-start | bytes 884744 | tf_op jit(solution)/shard_map/ppermute | solution.py:47
  56.7 2.1 %collective-permute-start.11 = (bf16[576,256]{1,0:T(8,128)(2,1)S(1)}, bf16[576,256]{1,0:T(8,128)(2,1)S(1)}, u32[]{:S(2)}, u32[]{:S(2)}) collective-permute-start(bf16[576,256]{1,0:T(8,128)(2,1)S(1)} %slice.12), channel_id=1, source_target_pairs={{2,4},{3,5},{4,2},{5,3},{10,12},{11,13},{12,10},{13,11},{18,20},{1... | collective-permute-start | bytes 884744 | tf_op jit(solution)/shard_map/ppermute | solution.py:47
  62.7 30.8 %collective-permute-start.15 = (bf16[256,640]{1,0:T(8,128)(2,1)S(1)}, bf16[256,640]{1,0:T(8,128)(2,1)S(1)}, u32[]{:S(2)}, u32[]{:S(2)}) collective-permute-start(bf16[256,640]{1,0:T(8,128)(2,1)S(1)} %get-tuple-element.31.refs_1_), channel_id=1, source_target_pairs={{2,4},{3,5},{4,2},{5,3},{10,12},{11,13},{12,10},{13,11},{18,20},{1... | collective-permute-start | bytes 983048 | tf_op jit(solution)/shard_map/ppermute | solution.py:47
  63.4 30.1 %collective-permute-start.12 = (bf16[256,640]{1,0:T(8,128)(2,1)S(1)}, bf16[256,640]{1,0:T(8,128)(2,1)S(1)}, u32[]{:S(2)}, u32[]{:S(2)}) collective-permute-start(bf16[256,640]{1,0:T(8,128)(2,1)S(1)} %get-tuple-element.31.refs_1_), channel_id=1, source_target_pairs={{0,2},{1,3},{6,4},{7,5},{8,10},{9,11},{14,12},{15,13},{16,18},{17,... | collective-permute-start | bytes 983048 | tf_op jit(solution)/shard_map/ppermute | solution.py:47
  84.6 8.2 %collective-permute-start.13 = (bf16[256,512]{1,0:T(8,128)(2,1)S(1)}, bf16[256,512]{1,0:T(8,128)(2,1)S(1)}, u32[]{:S(2)}, u32[]{:S(2)}) collective-permute-start(bf16[256,512]{1,0:T(8,128)(2,1)S(1)} %get-tuple-element.32.refs_0_), channel_id=1, source_target_pairs={{0,2},{1,3},{6,4},{7,5},{8,10},{9,11},{14,12},{15,13},{16,18},{17,... | collective-permute-start | bytes 786440 | tf_op jit(solution)/shard_map/ppermute | solution.py:47
  85.9 7.6 %collective-permute-start.14 = (bf16[256,512]{1,0:T(8,128)(2,1)S(1)}, bf16[256,512]{1,0:T(8,128)(2,1)S(1)}, u32[]{:S(2)}, u32[]{:S(2)}) collective-permute-start(bf16[256,512]{1,0:T(8,128)(2,1)S(1)} %get-tuple-element.32.refs_0_), channel_id=1, source_target_pairs={{2,4},{3,5},{4,2},{5,3},{10,12},{11,13},{12,10},{13,11},{18,20},{1... | collective-permute-start | bytes 786440 | tf_op jit(solution)/shard_map/ppermute | solution.py:47
  92.8 2.6 %collective-permute-start.16 = (bf16[256,512]{1,0:T(8,128)(2,1)S(1)}, bf16[256,512]{1,0:T(8,128)(2,1)S(1)}, u32[]{:S(2)}, u32[]{:S(2)}) collective-permute-start(bf16[256,512]{1,0:T(8,128)(2,1)S(1)} %collective-permute-done.13.refs_2_), channel_id=1, source_target_pairs={{2,4},{3,5},{4,2},{5,3},{10,12},{11,13},{12,10},{13,11},{18,20},{1... | collective-permute-start | bytes 786440 | tf_op jit(solution)/shard_map/ppermute | solution.py:47
  94.7 4.1 %collective-permute-start.17 = (bf16[256,640]{1,0:T(8,128)(2,1)S(1)}, bf16[256,640]{1,0:T(8,128)(2,1)S(1)}, u32[]{:S(2)}, u32[]{:S(2)}) collective-permute-start(bf16[256,640]{1,0:T(8,128)(2,1)S(1)} %collective-permute-done.12.refs_3_), channel_id=1, source_target_pairs={{2,4},{3,5},{4,2},{5,3},{10,12},{11,13},{12,10},{13,11},{18,20},{1... | collective-permute-start | bytes 983048 | tf_op jit(solution)/shard_map/ppermute | solution.py:47
  96.2 10.5 %collective-permute-start.18 = (bf16[144,512]{1,0:T(8,128)(2,1)S(1)}, bf16[144,512]{1,0:T(8,128)(2,1)S(1)}, u32[]{:S(2)}, u32[]{:S(2)}) collective-permute-start(bf16[144,512]{1,0:T(8,128)(2,1)S(1)} %get-tuple-element.41), channel_id=1, source_target_pairs={{2,0},{3,1},{4,6},{5,7},{10,8},{11,9},{12,14},{13,15},{18,16},{19,... | collective-permute-start | bytes 442376 | tf_op jit(solution)/shard_map/ppermute | solution.py:47
  97.5 22.5 %collective-permute-start.19 = (bf16[144,512]{1,0:T(8,128)(2,1)S(1)}, bf16[144,512]{1,0:T(8,128)(2,1)S(1)}, u32[]{:S(2)}, u32[]{:S(2)}) collective-permute-start(bf16[144,512]{1,0:T(8,128)(2,1)S(1)} %get-tuple-element.42), channel_id=1, source_target_pairs={{2,1},{3,0},{4,7},{5,6},{10,9},{11,8},{12,15},{13,14},{18,17},{19,... | collective-permute-start | bytes 442376 | tf_op jit(solution)/shard_map/ppermute | solution.py:47
  99.7 25.6 %collective-permute-start.20 = (bf16[144,640]{1,0:T(8,128)(2,1)S(1)}, bf16[144,640]{1,0:T(8,128)(2,1)S(1)}, u32[]{:S(2)}, u32[]{:S(2)}) collective-permute-start(bf16[144,640]{1,0:T(8,128)(2,1)S(1)} %get-tuple-element.45), channel_id=1, source_target_pairs={{2,0},{3,1},{4,6},{5,7},{10,8},{11,9},{12,14},{13,15},{18,16},{19,... | collective-permute-start | bytes 552968 | tf_op jit(solution)/shard_map/ppermute | solution.py:47
  101.0 24.3 %collective-permute-start.21 = (bf16[144,640]{1,0:T(8,128)(2,1)S(1)}, bf16[144,640]{1,0:T(8,128)(2,1)S(1)}, u32[]{:S(2)}, u32[]{:S(2)}) collective-permute-start(bf16[144,640]{1,0:T(8,128)(2,1)S(1)} %get-tuple-element.46), channel_id=1, source_target_pairs={{2,1},{3,0},{4,7},{5,6},{10,9},{11,8},{12,15},{13,14},{18,17},{19,... | collective-permute-start | bytes 552968 | tf_op jit(solution)/shard_map/ppermute | solution.py:47
  120.0 5.3 %collective-permute-start.23 = (bf16[144,640]{1,0:T(8,128)(2,1)S(1)}, bf16[144,640]{1,0:T(8,128)(2,1)S(1)}, u32[]{:S(2)}, u32[]{:S(2)}) collective-permute-start(bf16[144,640]{1,0:T(8,128)(2,1)S(1)} %get-tuple-element.48), channel_id=1, source_target_pairs={{0,1},{1,0},{2,3},{3,2},{4,5},{5,4},{6,7},{7,6},{8,9},{9,8},{10,11... | collective-permute-start | bytes 552968 | tf_op jit(solution)/shard_map/ppermute | solution.py:47
  121.9 3.4 %collective-permute-start.22 = (bf16[144,512]{1,0:T(8,128)(2,1)S(1)}, bf16[144,512]{1,0:T(8,128)(2,1)S(1)}, u32[]{:S(2)}, u32[]{:S(2)}) collective-permute-start(bf16[144,512]{1,0:T(8,128)(2,1)S(1)} %get-tuple-element.47), channel_id=1, source_target_pairs={{0,1},{1,0},{2,3},{3,2},{4,5},{5,4},{6,7},{7,6},{8,9},{9,8},{10,11... | collective-permute-start | bytes 442376 | tf_op jit(solution)/shard_map/ppermute | solution.py:47

commit v5 on v4

--- a/solution.py
+++ b/solution.py
@@ -115,6 +115,10 @@
 
 def middle(x, zh, y, zl, c):
     return {1: (x, zh, y, 2, c), 2: (x, zh, y, 1, c)}.get(zl)
+
+
+def inward_far(x, zh, y, zl, c):
+    return {0: (x, zh, y, 2, c), 3: (x, zh, y, 1, c)}.get(zl)
 
 
 def outward(x, zh, y, zl, c):
@@ -488,14 +492,15 @@
     one = send(z, first_hop)
     cross_one = send(z, first_crossing)
     ft = turn(flags, own, received)
-    one, ft = lax.optimization_barrier((one, ft))
+    ft_end = send(ft[CHIP : 2 * CHIP], inward)
+    ft_mid = send(ft[2 * CHIP :], middle)
+    ft_far = send(ft[2 * CHIP :], inward_far)
+    one, ft_end = lax.optimization_barrier((one, ft_end))
     two = send(one, second_hop)
     cross_two = send(one, second_crossing)
-    ft_end = send(ft[CHIP:], inward)
-    ft_mid = send(ft[2 * CHIP :], middle)
     near_one = send(cross_one, from_near)
     afar_one = send(cross_one, from_afar)
-    ft_far = send(ft_end[CHIP:], middle)
+    two, ft_mid = lax.optimization_barrier((two, ft_mid))
     three = send(choose(flags, two, cross_one, cross_two), third_hop)
     here = send(z, other_core)
     dxs = pairs(

time: 128 us -> 131 us (1.023)
  the two profiles are of different devices: /device:TPU:15 before, /device:TPU:1 now
where the time goes in v5:
time: 131 us
  starting transfers between devices  72.3 us (55%)
  waiting for transfers between devices  41.8 us (32%)
  Pallas kernels  13.1 us (10%)
  between operations  2.29 us (2%)
    ppermute x24, starting transfers between devices, send(): return lax.ppermute(value, NAMES, pairs_of(rule))  72.3 us
    ppermute x24, waiting for transfers between devices, send(): return lax.ppermute(value, NAMES, pairs_of(rule))  41.8 us
    pallas_call x1, Pallas kernels, project(): pl.pallas_call(project_kernel, name='project', out_shape=(jax.ShapeDtypeS...  3.58 us
    pallas_call x1, Pallas kernels, pairs(): pl.pallas_call(pairs_kernel, name='pairs', out_shape=(jax.ShapeDtypeStruc...  2.81 us
  transfers between devices with their start and end apart: 24, of which 11 were waited for; matrix products, arithmetic and copies ran while one was open for 0% of the time, Pallas kernels for 4%

profile of v5, /device:TPU:1, one launch (start us, length us, event | category | flops | bytes accessed | tf_op | source)
XLA Modules:
  0.0 130.8 jit_solution(4912518599501737242)
XLA Ops:
  0.6 1.1 broadcast_select_fusion
  1.7 16.1 %collective-permute-start = (bf16[128,1152]{1,0:T(8,128)(2,1)S(1)}, bf16[128,1152]{1,0:T(8,128)(2,1)S(1)}, u32[]{:S(2)}, u32[]{:S(2)}) collective-permute-start(bf16[128,1152]{1,0:T(8,128)(2,1)S(1)} %get-tuple-element.54), channel_id=1, source_target_pairs={{0,1},{1,0},{2,3},{3,2},{4,5},{5,4},{6,7},{7,6},{8,9},{9,8},{10,11... | collective-permute-start | bytes 884744 | tf_op jit(solution)/shard_map/ppermute | solution.py:47
  17.8 0.1 stack.31.flags
  17.9 1.1 collective-permute-done.recv
  19.0 3.6 %project.1 = (bf16[256,1152]{1,0:T(8,128)(2,1)S(1)}, f32[256,1152]{1,0:T(8,128)S(1)}, f32[256,128]{1,0:T(8,128)S(1)}) custom-call(s32[5]{0:T(128)S(1)} %stack.31.flags, bf16[128,1152]{1,0:T(8,128)(2,1)S(1)} %get-tuple-element.55.own, bf16[128,1152]{1,0:T(8,128)(2,1)S(1)} %collective-permute-done.recv, bf16[1152,1152]{1,0:T(8,128)(2,1)} %wp.1, ...), custom_call_target="tpu_custom_call" | custom-call | flops 679477248 | bytes 5013504 | tf_op jit(solution)/shard_map/project/pallas_call | solution.py:170
  22.6 1.9 %collective-permute-start.2 = (bf16[256,1152]{1,0:T(8,128)(2,1)S(1)}, bf16[256,1152]{1,0:T(8,128)(2,1)S(1)}, u32[]{:S(2)}, u32[]{:S(2)}) collective-permute-start(bf16[256,1152]{1,0:T(8,128)(2,1)S(1)} %get-tuple-element.28.z_ref), channel_id=1, source_target_pairs={{1,8},{3,10},{5,12},{7,14},{8,1},{9,16},{10,3},{11,18},{12,5},{13,... | collective-permute-start | bytes 1769480 | tf_op jit(solution)/shard_map/ppermute | solution.py:47
  24.5 0.8 turn.1.ft
  25.3 1.3 collective-permute-start.3
  26.6 0.7 collective-permute-start.6
  27.4 2.3 %collective-permute-done.3.feats_end = bf16[288,256]{1,0:T(8,128)(2,1)S(1)} collective-permute-done((bf16[288,256]{1,0:T(8,128)(2,1)S(1)}, bf16[288,256]{1,0:T(8,128)(2,1)S(1)}, u32[]{:S(2)}, u32[]{:S(2)}) %collective-permute-start.3) | collective-permute-done | bytes 147488 | tf_op jit(solution)/shard_map/ppermute | solution.py:47
  29.6 4.2 %collective-permute-done.2.one = bf16[256,1152]{1,0:T(8,128)(2,1)S(1)} collective-permute-done((bf16[256,1152]{1,0:T(8,128)(2,1)S(1)}, bf16[256,1152]{1,0:T(8,128)(2,1)S(1)}, u32[]{:S(2)}, u32[]{:S(2)}) %collective-permute-start.2) | collective-permute-done | bytes 589856 | tf_op jit(solution)/shard_map/ppermute | solution.py:47
  33.8 1.3 collective-permute-start.4
  35.1 7.2 %collective-permute-start.7 = (bf16[256,1152]{1,0:T(8,128)(2,1)S(1)}, bf16[256,1152]{1,0:T(8,128)(2,1)S(1)}, u32[]{:S(2)}, u32[]{:S(2)}) collective-permute-start(bf16[256,1152]{1,0:T(8,128)(2,1)S(1)} %collective-permute-done.2.one), channel_id=1, source_target_pairs={{1,1017},{3,1019},{5,1021},{7,1023},{56,64},{58,66},{60,68},{62,70... | collective-permute-start | bytes 1769480 | tf_op jit(solution)/shard_map/ppermute | solution.py:47
  42.3 0.7 collective-permute-start.5
  43.0 1.9 %collective-permute-start.1 = (bf16[256,1152]{1,0:T(8,128)(2,1)S(1)}, bf16[256,1152]{1,0:T(8,128)(2,1)S(1)}, u32[]{:S(2)}, u32[]{:S(2)}) collective-permute-start(bf16[256,1152]{1,0:T(8,128)(2,1)S(1)} %get-tuple-element.28.z_ref), channel_id=1, source_target_pairs={{0,1},{1,0},{2,3},{3,2},{4,5},{5,4},{6,7},{7,6},{8,9},{9,8},{10,11... | collective-permute-start | bytes 1769480 | tf_op jit(solution)/shard_map/ppermute | solution.py:47
  45.0 0.0 collective-permute-done.6.cross_one
  45.0 0.7 collective-permute-start.10
  45.7 0.0 collective-permute-done.5.early_mid.feats_mid
  45.7 0.7 collective-permute-start.9
  46.4 0.0 collective-permute-done.4.two
  46.4 5.9 %collective-permute-done.7.cross_two = bf16[256,1152]{1,0:T(8,128)(2,1)S(1)} collective-permute-done((bf16[256,1152]{1,0:T(8,128)(2,1)S(1)}, bf16[256,1152]{1,0:T(8,128)(2,1)S(1)}, u32[]{:S(2)}, u32[]{:S(2)}) %collective-permute-start.7) | collective-permute-done | bytes 589856 | tf_op jit(solution)/shard_map/ppermute | solution.py:47
  52.3 0.7 choose.1
  53.0 1.3 collective-permute-start.8
  54.3 12.2 %collective-permute-start.11 = (bf16[576,256]{1,0:T(8,128)(2,1)S(1)}, bf16[576,256]{1,0:T(8,128)(2,1)S(1)}, u32[]{:S(2)}, u32[]{:S(2)}) collective-permute-start(bf16[576,256]{1,0:T(8,128)(2,1)S(1)} %slice.10), channel_id=1, source_target_pairs={{0,4},{1,5},{6,2},{7,3},{8,12},{9,13},{14,10},{15,11},{16,20},{17,... | collective-permute-start | bytes 884744 | tf_op jit(solution)/shard_map/ppermute | solution.py:47
  67.8 0.1 pad_maximum_fusion.scale
  67.9 2.3 %collective-permute-done.11.early_far.feats = bf16[576,256]{1,0:T(8,128)(2,1)S(1)} collective-permute-done((bf16[576,256]{1,0:T(8,128)(2,1)S(1)}, bf16[576,256]{1,0:T(8,128)(2,1)S(1)}, u32[]{:S(2)}, u32[]{:S(2)}) %collective-permute-start.11) | collective-permute-done | bytes 294944 | tf_op jit(solution)/shard_map/ppermute | solution.py:47
  70.1 0.0 collective-permute-done.1.here
  70.1 0.0 collective-permute-done.10.afar_one
  70.1 0.0 collective-permute-done.9.near_one
  70.1 0.7 collective-permute-done.8.three
  70.8 2.8 %pairs.1 = (bf16[256,512]{1,0:T(8,128)(2,1)S(1)}, bf16[256,640]{1,0:T(8,128)(2,1)S(1)}) custom-call(s32[5]{0:T(128)S(1)} %stack.31.flags, f32[2]{0:T(128)S(1)} %pad_maximum_fusion.scale, bf16[256,1152]{1,0:T(8,128)(2,1)S(1)} %get-tuple-element.28.z_ref, f32[256,1152]{1,0:T(8,128)S(1)} %get-tuple-element.29.u_ref, f32[256,128]{1,0:T(8,128)S(1)} %get-tuple-element.30.rn_ref, ...), custom_call_target="tpu_custom_call" | custom-call | flops 603979776 | bytes 4128768 | tf_op jit(solution)/shard_map/pairs/pallas_call | solution.py:315
  73.6 0.7 collective-permute-start.15
  74.3 12.8 %collective-permute-start.12 = (bf16[256,640]{1,0:T(8,128)(2,1)S(1)}, bf16[256,640]{1,0:T(8,128)(2,1)S(1)}, u32[]{:S(2)}, u32[]{:S(2)}) collective-permute-start(bf16[256,640]{1,0:T(8,128)(2,1)S(1)} %get-tuple-element.34.refs_1_), channel_id=1, source_target_pairs={{0,2},{1,3},{6,4},{7,5},{8,10},{9,11},{14,12},{15,13},{16,18},{17,... | collective-permute-start | bytes 983048 | tf_op jit(solution)/shard_map/ppermute | solution.py:47
  87.2 1.3 collective-permute-start.13
  88.5 0.7 collective-permute-start.14
  89.2 10.7 %collective-permute-done.13.refs_2_ = bf16[256,512]{1,0:T(8,128)(2,1)S(1)} collective-permute-done((bf16[256,512]{1,0:T(8,128)(2,1)S(1)}, bf16[256,512]{1,0:T(8,128)(2,1)S(1)}, u32[]{:S(2)}, u32[]{:S(2)}) %collective-permute-start.13) | collective-permute-done | bytes 262176 | tf_op jit(solution)/shard_map/ppermute | solution.py:47
  99.9 0.7 collective-permute-start.16
  100.6 0.0 collective-permute-done.14.refs_4_
  100.6 0.0 collective-permute-done.15.refs_5_
  100.6 0.0 collective-permute-done.12.refs_3_
  100.6 1.1 near.1
  101.8 0.7 collective-permute-start.17
  102.5 0.0 collective-permute-done.16.dx.dx_left
  102.5 0.8 far.2
  103.3 1.3 collective-permute-start.18
  104.6 1.3 collective-permute-start.19
  105.9 0.0 collective-permute-done.17.dx.dx_right
  105.9 0.9 far.3
  106.8 1.3 collective-permute-start.20
  108.1 1.3 collective-permute-start.21
  109.4 0.6 rest.1
  110.0 5.7 %collective-permute-done.18.same_left = bf16[144,512]{1,0:T(8,128)(2,1)S(1)} collective-permute-done((bf16[144,512]{1,0:T(8,128)(2,1)S(1)}, bf16[144,512]{1,0:T(8,128)(2,1)S(1)}, u32[]{:S(2)}, u32[]{:S(2)}) %collective-permute-start.18) | collective-permute-done | bytes 147488 | tf_op jit(solution)/shard_map/ppermute | solution.py:47
  115.7 4.7 %collective-permute-done.19.crossed_left = bf16[144,512]{1,0:T(8,128)(2,1)S(1)} collective-permute-done((bf16[144,512]{1,0:T(8,128)(2,1)S(1)}, bf16[144,512]{1,0:T(8,128)(2,1)S(1)}, u32[]{:S(2)}, u32[]{:S(2)}) %collective-permute-start.19) | collective-permute-done | bytes 147488 | tf_op jit(solution)/shard_map/ppermute | solution.py:47
  120.4 1.9 %collective-permute-start.23 = (bf16[144,640]{1,0:T(8,128)(2,1)S(1)}, bf16[144,640]{1,0:T(8,128)(2,1)S(1)}, u32[]{:S(2)}, u32[]{:S(2)}) collective-permute-start(bf16[144,640]{1,0:T(8,128)(2,1)S(1)} %get-tuple-element.52), channel_id=1, source_target_pairs={{0,1},{1,0},{2,3},{3,2},{4,5},{5,4},{6,7},{7,6},{8,9},{9,8},{10,11... | collective-permute-start | bytes 552968 | tf_op jit(solution)/shard_map/ppermute | solution.py:47
  122.3 2.4 %collective-permute-start.22 = (bf16[144,512]{1,0:T(8,128)(2,1)S(1)}, bf16[144,512]{1,0:T(8,128)(2,1)S(1)}, u32[]{:S(2)}, u32[]{:S(2)}) collective-permute-start(bf16[144,512]{1,0:T(8,128)(2,1)S(1)} %get-tuple-element.51), channel_id=1, source_target_pairs={{0,1},{1,0},{2,3},{3,2},{4,5},{5,4},{6,7},{7,6},{8,9},{9,8},{10,11... | collective-permute-start | bytes 442376 | tf_op jit(solution)/shard_map/ppermute | solution.py:47
  124.7 1.0 collective-permute-done.22.swap_left
  125.7 0.0 collective-permute-done.20.same_right
  125.7 3.3 %collective-permute-done.21.crossed_right = bf16[144,640]{1,0:T(8,128)(2,1)S(1)} collective-permute-done((bf16[144,640]{1,0:T(8,128)(2,1)S(1)}, bf16[144,640]{1,0:T(8,128)(2,1)S(1)}, u32[]{:S(2)}, u32[]{:S(2)}) %collective-permute-start.21) | collective-permute-done | bytes 184352 | tf_op jit(solution)/shard_map/ppermute | solution.py:47
  129.1 0.0 collective-permute-done.23.swap_right
  129.1 1.7 %finish.1 = (f32[1,144,1152]{2,1,0:T(8,128)}, f32[1,144,1152]{2,1,0:T(8,128)}) custom-call(s32[5]{0:T(128)S(1)} %stack.31.flags, bf16[144,512]{1,0:T(8,128)(2,1)S(1)} %collective-permute-done.18.same_left, bf16[144,512]{1,0:T(8,128)(2,1)S(1)} %collective-permute-done.19.crossed_left, bf16[144,640]{1,0:T(8,128)(2,1)S(1)} %collective-permute-done.20.same_right, ...), custom_call_target="tpu_custom_call" | custom-call | flops 663552 | bytes 2985984 | tf_op jit(solution)/shard_map/finish/pallas_call | solution.py:467
  (2 shorter events, 0.0 us)
Async XLA Ops:
  1.7 17.3 %collective-permute-start = (bf16[128,1152]{1,0:T(8,128)(2,1)S(1)}, bf16[128,1152]{1,0:T(8,128)(2,1)S(1)}, u32[]{:S(2)}, u32[]{:S(2)}) collective-permute-start(bf16[128,1152]{1,0:T(8,128)(2,1)S(1)} %get-tuple-element.54), channel_id=1, source_target_pairs={{0,1},{1,0},{2,3},{3,2},{4,5},{5,4},{6,7},{7,6},{8,9},{9,8},{10,11... | collective-permute-start | bytes 884744 | tf_op jit(solution)/shard_map/ppermute | solution.py:47
  22.6 11.2 %collective-permute-start.2 = (bf16[256,1152]{1,0:T(8,128)(2,1)S(1)}, bf16[256,1152]{1,0:T(8,128)(2,1)S(1)}, u32[]{:S(2)}, u32[]{:S(2)}) collective-permute-start(bf16[256,1152]{1,0:T(8,128)(2,1)S(1)} %get-tuple-element.28.z_ref), channel_id=1, source_target_pairs={{1,8},{3,10},{5,12},{7,14},{8,1},{9,16},{10,3},{11,18},{12,5},{13,... | collective-permute-start | bytes 1769480 | tf_op jit(solution)/shard_map/ppermute | solution.py:47
  25.3 4.3 %collective-permute-start.3 = (bf16[288,256]{1,0:T(8,128)(2,1)S(1)}, bf16[288,256]{1,0:T(8,128)(2,1)S(1)}, u32[]{:S(2)}, u32[]{:S(2)}) collective-permute-start(bf16[288,256]{1,0:T(8,128)(2,1)S(1)} %slice.9), channel_id=1, source_target_pairs={{0,2},{1,3},{6,4},{7,5},{8,10},{9,11},{14,12},{15,13},{16,18},{17,... | collective-permute-start | bytes 442376 | tf_op jit(solution)/shard_map/ppermute | solution.py:47
  26.6 18.3 %collective-permute-start.6 = (bf16[256,1152]{1,0:T(8,128)(2,1)S(1)}, bf16[256,1152]{1,0:T(8,128)(2,1)S(1)}, u32[]{:S(2)}, u32[]{:S(2)}) collective-permute-start(bf16[256,1152]{1,0:T(8,128)(2,1)S(1)} %get-tuple-element.28.z_ref), channel_id=1, source_target_pairs={{0,1009},{2,1011},{4,1013},{6,1015},{16,977},{18,979},{20,981},{22... | collective-permute-start | bytes 1769480 | tf_op jit(solution)/shard_map/ppermute | solution.py:47
  33.8 12.6 %collective-permute-start.4 = (bf16[256,1152]{1,0:T(8,128)(2,1)S(1)}, bf16[256,1152]{1,0:T(8,128)(2,1)S(1)}, u32[]{:S(2)}, u32[]{:S(2)}) collective-permute-start(bf16[256,1152]{1,0:T(8,128)(2,1)S(1)} %collective-permute-done.2.one), channel_id=1, source_target_pairs={{8,16},{9,1},{10,18},{11,3},{12,20},{13,5},{14,22},{15,7},{16,24},... | collective-permute-start | bytes 1769480 | tf_op jit(solution)/shard_map/ppermute | solution.py:47
  35.1 17.2 %collective-permute-start.7 = (bf16[256,1152]{1,0:T(8,128)(2,1)S(1)}, bf16[256,1152]{1,0:T(8,128)(2,1)S(1)}, u32[]{:S(2)}, u32[]{:S(2)}) collective-permute-start(bf16[256,1152]{1,0:T(8,128)(2,1)S(1)} %collective-permute-done.2.one), channel_id=1, source_target_pairs={{1,1017},{3,1019},{5,1021},{7,1023},{56,64},{58,66},{60,68},{62,70... | collective-permute-start | bytes 1769480 | tf_op jit(solution)/shard_map/ppermute | solution.py:47
  42.3 3.3 %collective-permute-start.5 = (bf16[576,256]{1,0:T(8,128)(2,1)S(1)}, bf16[576,256]{1,0:T(8,128)(2,1)S(1)}, u32[]{:S(2)}, u32[]{:S(2)}) collective-permute-start(bf16[576,256]{1,0:T(8,128)(2,1)S(1)} %slice.10), channel_id=1, source_target_pairs={{2,4},{3,5},{4,2},{5,3},{10,12},{11,13},{12,10},{13,11},{18,20},{1... | collective-permute-start | bytes 884744 | tf_op jit(solution)/shard_map/ppermute | solution.py:47
  43.0 27.1 %collective-permute-start.1 = (bf16[256,1152]{1,0:T(8,128)(2,1)S(1)}, bf16[256,1152]{1,0:T(8,128)(2,1)S(1)}, u32[]{:S(2)}, u32[]{:S(2)}) collective-permute-start(bf16[256,1152]{1,0:T(8,128)(2,1)S(1)} %get-tuple-element.28.z_ref), channel_id=1, source_target_pairs={{0,1},{1,0},{2,3},{3,2},{4,5},{5,4},{6,7},{7,6},{8,9},{9,8},{10,11... | collective-permute-start | bytes 1769480 | tf_op jit(solution)/shard_map/ppermute | solution.py:47
  45.0 25.1 %collective-permute-start.10 = (bf16[256,1152]{1,0:T(8,128)(2,1)S(1)}, bf16[256,1152]{1,0:T(8,128)(2,1)S(1)}, u32[]{:S(2)}, u32[]{:S(2)}) collective-permute-start(bf16[256,1152]{1,0:T(8,128)(2,1)S(1)} %collective-permute-done.6.cross_one), channel_id=1, source_target_pairs={{17,57},{19,59},{21,61},{23,63},{40,0},{42,2},{44,4},{46,6},{81,12... | collective-permute-start | bytes 1769480 | tf_op jit(solution)/shard_map/ppermute | solution.py:47
  45.7 24.4 %collective-permute-start.9 = (bf16[256,1152]{1,0:T(8,128)(2,1)S(1)}, bf16[256,1152]{1,0:T(8,128)(2,1)S(1)}, u32[]{:S(2)}, u32[]{:S(2)}) collective-permute-start(bf16[256,1152]{1,0:T(8,128)(2,1)S(1)} %collective-permute-done.6.cross_one), channel_id=1, source_target_pairs={{8,0},{10,2},{12,4},{14,6},{49,57},{51,59},{53,61},{55,63},{72,64}... | collective-permute-start | bytes 1769480 | tf_op jit(solution)/shard_map/ppermute | solution.py:47
  53.0 17.8 %collective-permute-start.8 = (bf16[256,1152]{1,0:T(8,128)(2,1)S(1)}, bf16[256,1152]{1,0:T(8,128)(2,1)S(1)}, u32[]{:S(2)}, u32[]{:S(2)}) collective-permute-start(bf16[256,1152]{1,0:T(8,128)(2,1)S(1)} %choose.1), channel_id=1, source_target_pairs={{0,8},{2,10},{4,12},{6,14},{8,16},{9,1},{10,18},{11,3},{12,20},{13... | collective-permute-start | bytes 1769480 | tf_op jit(solution)/shard_map/ppermute | solution.py:47
  54.3 15.9 %collective-permute-start.11 = (bf16[576,256]{1,0:T(8,128)(2,1)S(1)}, bf16[576,256]{1,0:T(8,128)(2,1)S(1)}, u32[]{:S(2)}, u32[]{:S(2)}) collective-permute-start(bf16[576,256]{1,0:T(8,128)(2,1)S(1)} %slice.10), channel_id=1, source_target_pairs={{0,4},{1,5},{6,2},{7,3},{8,12},{9,13},{14,10},{15,11},{16,20},{17,... | collective-permute-start | bytes 884744 | tf_op jit(solution)/shard_map/ppermute | solution.py:47
  73.6 27.0 %collective-permute-start.15 = (bf16[256,640]{1,0:T(8,128)(2,1)S(1)}, bf16[256,640]{1,0:T(8,128)(2,1)S(1)}, u32[]{:S(2)}, u32[]{:S(2)}) collective-permute-start(bf16[256,640]{1,0:T(8,128)(2,1)S(1)} %get-tuple-element.34.refs_1_), channel_id=1, source_target_pairs={{2,4},{3,5},{4,2},{5,3},{10,12},{11,13},{12,10},{13,11},{18,20},{1... | collective-permute-start | bytes 983048 | tf_op jit(solution)/shard_map/ppermute | solution.py:47
  74.3 26.3 %collective-permute-start.12 = (bf16[256,640]{1,0:T(8,128)(2,1)S(1)}, bf16[256,640]{1,0:T(8,128)(2,1)S(1)}, u32[]{:S(2)}, u32[]{:S(2)}) collective-permute-start(bf16[256,640]{1,0:T(8,128)(2,1)S(1)} %get-tuple-element.34.refs_1_), channel_id=1, source_target_pairs={{0,2},{1,3},{6,4},{7,5},{8,10},{9,11},{14,12},{15,13},{16,18},{17,... | collective-permute-start | bytes 983048 | tf_op jit(solution)/shard_map/ppermute | solution.py:47
  87.2 12.7 %collective-permute-start.13 = (bf16[256,512]{1,0:T(8,128)(2,1)S(1)}, bf16[256,512]{1,0:T(8,128)(2,1)S(1)}, u32[]{:S(2)}, u32[]{:S(2)}) collective-permute-start(bf16[256,512]{1,0:T(8,128)(2,1)S(1)} %get-tuple-element.36.refs_0_), channel_id=1, source_target_pairs={{0,2},{1,3},{6,4},{7,5},{8,10},{9,11},{14,12},{15,13},{16,18},{17,... | collective-permute-start | bytes 786440 | tf_op jit(solution)/shard_map/ppermute | solution.py:47
  88.5 12.1 %collective-permute-start.14 = (bf16[256,512]{1,0:T(8,128)(2,1)S(1)}, bf16[256,512]{1,0:T(8,128)(2,1)S(1)}, u32[]{:S(2)}, u32[]{:S(2)}) collective-permute-start(bf16[256,512]{1,0:T(8,128)(2,1)S(1)} %get-tuple-element.36.refs_0_), channel_id=1, source_target_pairs={{2,4},{3,5},{4,2},{5,3},{10,12},{11,13},{12,10},{13,11},{18,20},{1... | collective-permute-start | bytes 786440 | tf_op jit(solution)/shard_map/ppermute | solution.py:47
  99.9 2.6 %collective-permute-start.16 = (bf16[256,512]{1,0:T(8,128)(2,1)S(1)}, bf16[256,512]{1,0:T(8,128)(2,1)S(1)}, u32[]{:S(2)}, u32[]{:S(2)}) collective-permute-start(bf16[256,512]{1,0:T(8,128)(2,1)S(1)} %collective-permute-done.13.refs_2_), channel_id=1, source_target_pairs={{2,4},{3,5},{4,2},{5,3},{10,12},{11,13},{12,10},{13,11},{18,20},{1... | collective-permute-start | bytes 786440 | tf_op jit(solution)/shard_map/ppermute | solution.py:47
  101.8 4.1 %collective-permute-start.17 = (bf16[256,640]{1,0:T(8,128)(2,1)S(1)}, bf16[256,640]{1,0:T(8,128)(2,1)S(1)}, u32[]{:S(2)}, u32[]{:S(2)}) collective-permute-start(bf16[256,640]{1,0:T(8,128)(2,1)S(1)} %collective-permute-done.12.refs_3_), channel_id=1, source_target_pairs={{2,4},{3,5},{4,2},{5,3},{10,12},{11,13},{12,10},{13,11},{18,20},{1... | collective-permute-start | bytes 983048 | tf_op jit(solution)/shard_map/ppermute | solution.py:47
  103.3 12.4 %collective-permute-start.18 = (bf16[144,512]{1,0:T(8,128)(2,1)S(1)}, bf16[144,512]{1,0:T(8,128)(2,1)S(1)}, u32[]{:S(2)}, u32[]{:S(2)}) collective-permute-start(bf16[144,512]{1,0:T(8,128)(2,1)S(1)} %get-tuple-element.45), channel_id=1, source_target_pairs={{2,0},{3,1},{4,6},{5,7},{10,8},{11,9},{12,14},{13,15},{18,16},{19,... | collective-permute-start | bytes 442376 | tf_op jit(solution)/shard_map/ppermute | solution.py:47
  104.6 15.8 %collective-permute-start.19 = (bf16[144,512]{1,0:T(8,128)(2,1)S(1)}, bf16[144,512]{1,0:T(8,128)(2,1)S(1)}, u32[]{:S(2)}, u32[]{:S(2)}) collective-permute-start(bf16[144,512]{1,0:T(8,128)(2,1)S(1)} %get-tuple-element.46), channel_id=1, source_target_pairs={{2,1},{3,0},{4,7},{5,6},{10,9},{11,8},{12,15},{13,14},{18,17},{19,... | collective-permute-start | bytes 442376 | tf_op jit(solution)/shard_map/ppermute | solution.py:47
  106.8 19.0 %collective-permute-start.20 = (bf16[144,640]{1,0:T(8,128)(2,1)S(1)}, bf16[144,640]{1,0:T(8,128)(2,1)S(1)}, u32[]{:S(2)}, u32[]{:S(2)}) collective-permute-start(bf16[144,640]{1,0:T(8,128)(2,1)S(1)} %get-tuple-element.49), channel_id=1, source_target_pairs={{2,0},{3,1},{4,6},{5,7},{10,8},{11,9},{12,14},{13,15},{18,16},{19,... | collective-permute-start | bytes 552968 | tf_op jit(solution)/shard_map/ppermute | solution.py:47
  108.1 21.0 %collective-permute-start.21 = (bf16[144,640]{1,0:T(8,128)(2,1)S(1)}, bf16[144,640]{1,0:T(8,128)(2,1)S(1)}, u32[]{:S(2)}, u32[]{:S(2)}) collective-permute-start(bf16[144,640]{1,0:T(8,128)(2,1)S(1)} %get-tuple-element.50), channel_id=1, source_target_pairs={{2,1},{3,0},{4,7},{5,6},{10,9},{11,8},{12,15},{13,14},{18,17},{19,... | collective-permute-start | bytes 552968 | tf_op jit(solution)/shard_map/ppermute | solution.py:47
  120.4 8.7 %collective-permute-start.23 = (bf16[144,640]{1,0:T(8,128)(2,1)S(1)}, bf16[144,640]{1,0:T(8,128)(2,1)S(1)}, u32[]{:S(2)}, u32[]{:S(2)}) collective-permute-start(bf16[144,640]{1,0:T(8,128)(2,1)S(1)} %get-tuple-element.52), channel_id=1, source_target_pairs={{0,1},{1,0},{2,3},{3,2},{4,5},{5,4},{6,7},{7,6},{8,9},{9,8},{10,11... | collective-permute-start | bytes 552968 | tf_op jit(solution)/shard_map/ppermute | solution.py:47
  122.3 3.4 %collective-permute-start.22 = (bf16[144,512]{1,0:T(8,128)(2,1)S(1)}, bf16[144,512]{1,0:T(8,128)(2,1)S(1)}, u32[]{:S(2)}, u32[]{:S(2)}) collective-permute-start(bf16[144,512]{1,0:T(8,128)(2,1)S(1)} %get-tuple-element.51), channel_id=1, source_target_pairs={{0,1},{1,0},{2,3},{3,2},{4,5},{5,4},{6,7},{7,6},{8,9},{9,8},{10,11... | collective-permute-start | bytes 442376 | tf_op jit(solution)/shard_map/ppermute | solution.py:47

commit v6 on v5

--- a/solution.py
+++ b/solution.py
@@ -18,7 +18,7 @@
 EPS = 1e-06
 BF = jnp.bfloat16
 F32 = jnp.float32
-PROJECT_LIMIT = 51
+PROJECT_LIMIT = 49
 VMEM = pl.BlockSpec(memory_space=pltpu.VMEM)
 SMEM = pl.BlockSpec(memory_space=pltpu.SMEM)
 ANY = pl.BlockSpec(memory_space=pl.ANY)
@@ -77,19 +77,11 @@
     return (x, 0, column) if zh == 1 else ((x - 1) % NX, 1, column)
 
 
-def first_crossing(x, zh, y, zl, c):
-    if c == 1 and y in (5, 7):
-        return (*above(x, zh, 1 if y == 7 else 5), zl, 0)
-    if c == 0 and y in (0, 2):
-        return (*below(x, zh, 6 if y == 0 else 2), zl, 1)
-    return None
-
-
-def second_crossing(x, zh, y, zl, c):
-    if c == 0 and y == 7:
-        return (*above(x, zh, 0), zl, 0)
-    if c == 1 and y == 0:
-        return (*below(x, zh, 7), zl, 1)
+def crossing(x, zh, y, zl, c):
+    if c == 1 and y >= 5:
+        return (*above(x, zh, {7: 1, 6: 0, 5: 5}[y]), zl, 0)
+    if c == 0 and y <= 2:
+        return (*below(x, zh, {0: 6, 1: 7, 2: 2}[y]), zl, 1)
     return None
 
 
@@ -129,9 +121,13 @@
     return {1: (x, zh, y, 0, 1 - c), 2: (x, zh, y, 3, 1 - c)}.get(zl)
 
 
-def project_kernel(
-    flags, own, recv, wp, wc, z_ref, u_ref, rn_ref, f_ref, w_ref, sems
-):
+def normalised(x):
+    total = jnp.sum(x * x, axis=-1, keepdims=True)
+    rn = 1.0 / jnp.sqrt(total + EPS)
+    return x * rn, jnp.broadcast_to(rn, (ROWS, 128))
+
+
+def project_own_kernel(flags, own, wp, wc, w_ref, z_ref, u_ref, rn_ref, sems):
     c = flags[0]
     parts = 3
     width = D // parts
@@ -139,7 +135,7 @@
     def fetch(head):
         for j in range(parts):
             cols = pl.ds(j * width, width)
-            pltpu.make_async_copy(head.at[:, cols], w_ref.at[j], sems.at[j]).start()
+            pltpu.make_async_copy(head.at[:, cols], w_ref.at[:, cols], sems.at[j]).start()
 
     @pl.when(c == 0)
     def _():
@@ -149,44 +145,60 @@
     def _():
         fetch(wc)
 
-    f_ref[:ROWS] = own[...]
-    f_ref[ROWS:] = recv[...]
-    total = jnp.zeros((2 * ROWS, 1), F32)
     for j in range(parts):
         cols = pl.ds(j * width, width)
-        pltpu.make_async_copy(wp.at[:, cols], w_ref.at[j], sems.at[j]).wait()
-        x = jnp.dot(f_ref[...], w_ref[j], preferred_element_type=F32)
-        u_ref[:, cols] = x
-        total = total + jnp.sum(x * x, axis=-1, keepdims=True)
-    rn = 1.0 / jnp.sqrt(total + EPS)
-    rn_ref[...] = jnp.broadcast_to(rn, (2 * ROWS, 128))
-    u = u_ref[...] * rn
+        pltpu.make_async_copy(wp.at[:, cols], w_ref.at[:, cols], sems.at[j]).wait()
+        u_ref[:, cols] = jnp.dot(own[...], w_ref[:, cols], preferred_element_type=F32)
+    u, rn_ref[...] = normalised(u_ref[...])
     u_ref[...] = u
     z_ref[...] = u.astype(BF)
 
 
-def project(flags, own, recv, wp, wc):
-    rows = 2 * ROWS
-    return pl.pallas_call(
-        project_kernel,
-        name="project",
+def project_own(flags, own, wp, wc):
+    return pl.pallas_call(
+        project_own_kernel,
+        name="project_own",
         out_shape=(
-            jax.ShapeDtypeStruct((rows, D), BF),
-            jax.ShapeDtypeStruct((rows, D), F32),
-            jax.ShapeDtypeStruct((rows, 128), F32),
-        ),
-        in_specs=[SMEM, VMEM, VMEM, HBM, HBM],
+            jax.ShapeDtypeStruct((D, D), BF),
+            jax.ShapeDtypeStruct((ROWS, D), BF),
+            jax.ShapeDtypeStruct((ROWS, D), F32),
+            jax.ShapeDtypeStruct((ROWS, 128), F32),
+        ),
+        in_specs=[SMEM, VMEM, HBM, HBM],
+        out_specs=(VMEM,) * 4,
+        scratch_shapes=[pltpu.SemaphoreType.DMA((3,))],
+        compiler_params=pltpu.CompilerParams(vmem_limit_bytes=PROJECT_LIMIT * 1024 * 1024),
+        cost_estimate=pl.CostEstimate(
+            flops=2 * ROWS * D * D, bytes_accessed=2 * D * D + 8 * ROWS * D, transcendentals=0
+        ),
+    )(flags, own, wp, wc)
+
+
+def project_other_kernel(recv, w_ref, z_own, z_ref, u_ref, rn_ref):
+    z_ref[:ROWS] = z_own[...]
+    u, rn_ref[...] = normalised(
+        jnp.dot(recv[...], w_ref[...], preferred_element_type=F32)
+    )
+    u_ref[...] = u
+    z_ref[ROWS:] = u.astype(BF)
+
+
+def project_other(recv, w, z_own):
+    return pl.pallas_call(
+        project_other_kernel,
+        name="project_other",
+        out_shape=(
+            jax.ShapeDtypeStruct((2 * ROWS, D), BF),
+            jax.ShapeDtypeStruct((ROWS, D), F32),
+            jax.ShapeDtypeStruct((ROWS, 128), F32),
+        ),
+        in_specs=[VMEM] * 3,
         out_specs=(VMEM,) * 3,
-        scratch_shapes=[
-            pltpu.VMEM((rows, D), BF),
-            pltpu.VMEM((3, D, D // 3), BF),
-            pltpu.SemaphoreType.DMA((3,)),
-        ],
-        compiler_params=pltpu.CompilerParams(vmem_limit_bytes=PROJECT_LIMIT * 1024 * 1024),
-        cost_estimate=pl.CostEstimate(
-            flops=2 * rows * D * D, bytes_accessed=2 * D * D + 8 * rows * D, transcendentals=0
-        ),
-    )(flags, own, recv, wp, wc)
+        compiler_params=PARAMS,
+        cost_estimate=pl.CostEstimate(
+            flops=2 * ROWS * D * D, bytes_accessed=2 * D * D + 8 * ROWS * D, transcendentals=0
+        ),
+    )(recv, w, z_own)
 
 
 def turn_kernel(flags, own, recv, ft_ref, turned):
@@ -213,16 +225,12 @@
     )(flags, own, recv)
 
 
-def choose_kernel(flags, two, cross_one, cross_two, out_ref, sem):
+def choose_kernel(flags, two, cross, out_ref, sem):
     place = flags[1]
 
-    @pl.when(place == 0)
-    def _():
-        pltpu.make_async_copy(cross_two, out_ref, sem).start()
-
-    @pl.when(place == 1)
-    def _():
-        pltpu.make_async_copy(cross_one, out_ref, sem).start()
+    @pl.when(place <= 1)
+    def _():
+        pltpu.make_async_copy(cross, out_ref, sem).start()
 
     @pl.when(place > 1)
     def _():
@@ -231,24 +239,24 @@
     pltpu.make_async_copy(two, out_ref, sem).wait()
 
 
-def choose(flags, two, cross_one, cross_two):
+def choose(flags, two, cross):
     return pl.pallas_call(
         choose_kernel,
         name="choose",
         out_shape=jax.ShapeDtypeStruct((2 * ROWS, D), BF),
-        in_specs=[SMEM] + [ANY] * 3,
+        in_specs=[SMEM] + [ANY] * 2,
         out_specs=VMEM,
         scratch_shapes=[pltpu.SemaphoreType.DMA(())],
         compiler_params=PARAMS,
         cost_estimate=pl.CostEstimate(
             flops=0, bytes_accessed=8 * ROWS * D, transcendentals=0
         ),
-    )(flags, two, cross_one, cross_two)
+    )(flags, two, cross)
 
 
 def pairs_kernel(
-    flags, scale, z_ref, u_ref, rn_ref,
-    here, one, two, three, cross_one, cross_two, near_one, afar_one, early_mid, early_far,
+    flags, scale, z_ref, u_own, u_other, rn_own, rn_other,
+    here, one, two, three, cross, near_one, afar_one, early_mid, early_far,
     dx_left, dx_right, others, sems,
 ):
     del early_mid, early_far
@@ -272,12 +280,11 @@
     @pl.when(place == 0)
     def _():
         fetch(near_one, 1)
-        fetch(cross_two, 2)
         fetch(afar_one, 3)
 
-    @pl.when(place == 1)
-    def _():
-        fetch(cross_one, 2)
+    @pl.when(place <= 1)
+    def _():
+        fetch(cross, 2)
 
     @pl.when(place > 1)
     def _():
@@ -302,8 +309,8 @@
         prob = jax.nn.sigmoid(logits) - jnp.where(row == col, 1.0, 0.0)
         weight = (prob * (1.0 / ROWS)).astype(BF)
         dz = t * jnp.dot(weight, others[b], preferred_element_type=F32)
-        u = u_ref[b * ROWS : (b + 1) * ROWS]
-        rn = rn_ref[b * ROWS : (b + 1) * ROWS, :1]
+        u = (u_own, u_other)[b][...]
+        rn = (rn_own, rn_other)[b][:, :1]
         inner = jnp.sum(u * dz, axis=-1, keepdims=True)
         dx = ((dz - u * inner) * rn).astype(BF)
         for cols, dx_ref in zip(HALVES, (dx_left, dx_right)):
@@ -319,7 +326,7 @@
             jax.ShapeDtypeStruct((rows, LEFT), BF),
             jax.ShapeDtypeStruct((rows, D - LEFT), BF),
         ),
-        in_specs=[SMEM, SMEM] + [VMEM] * 3 + [ANY] * 10,
+        in_specs=[SMEM, SMEM] + [VMEM] * 5 + [ANY] * 9,
         out_specs=(VMEM, VMEM),
         scratch_shapes=[
             pltpu.VMEM((2, 4 * ROWS, D), BF),
@@ -487,25 +494,25 @@
 
     received = send(jnp.where(c == 0, captions, pictures), other_core)
     own = jnp.where(c == 0, pictures, captions)
-    z, u, rn = project(flags, own, received, picture_head, caption_head)
+    head, z_own, u_own, rn_own = project_own(flags, own, picture_head, caption_head)
+    z, u_other, rn_other = project_other(received, head, z_own)
 
     one = send(z, first_hop)
-    cross_one = send(z, first_crossing)
+    cross = send(z, crossing)
     ft = turn(flags, own, received)
     ft_end = send(ft[CHIP : 2 * CHIP], inward)
     ft_mid = send(ft[2 * CHIP :], middle)
     ft_far = send(ft[2 * CHIP :], inward_far)
     one, ft_end = lax.optimization_barrier((one, ft_end))
     two = send(one, second_hop)
-    cross_two = send(one, second_crossing)
-    near_one = send(cross_one, from_near)
-    afar_one = send(cross_one, from_afar)
-    two, ft_mid = lax.optimization_barrier((two, ft_mid))
-    three = send(choose(flags, two, cross_one, cross_two), third_hop)
+    near_one = send(cross, from_near)
+    afar_one = send(cross, from_afar)
+    two, ft_far = lax.optimization_barrier((two, ft_far))
+    three = send(choose(flags, two, cross), third_hop)
     here = send(z, other_core)
     dxs = pairs(
-        flags, scale, z, u, rn, here, one, two, three,
-        cross_one, cross_two, near_one, afar_one, ft_mid, ft_far,
+        flags, scale, z, u_own, u_other, rn_own, rn_other, here, one, two, three,
+        cross, near_one, afar_one, ft_mid, ft_far,
     )
 
     ends = [send(dx, inward) for dx in dxs]

time: 131 us -> 126 us (0.962)
  starting transfers between devices: 72.3 us -> 54.9 us
  waiting for transfers between devices: 41.8 us -> 54 us
    ppermute x24 -> x23, starting transfers between devices: 72.3 us -> 54.9 us  [send(): return lax.ppermute(value, NAMES, pairs_of(rule))]
    ppermute x24 -> x23, waiting for transfers between devices: 41.8 us -> 54 us  [send(): return lax.ppermute(value, NAMES, pairs_of(rule))]
    pallas_call x1 -> x2, Pallas kernels: 3.58 us -> 3.65 us  [the longest x1 2.89 us: project_own(): pl.pallas_call(project_own_kernel, name='project_own', out_shape=(jax.Sha...]
  transfers between devices with their start and end apart: 24 -> 23, of which waited for: 11 -> 9; matrix products, arithmetic and copies ran while one was open for 0% -> 0% of each run, Pallas kernels for 4% -> 6%
where the time goes in v6:
time: 126 us
  starting transfers between devices  54.9 us (44%)
  waiting for transfers between devices  54 us (43%)
  Pallas kernels  13.1 us (10%)
  between operations  2.29 us (2%)
    ppermute x23, starting transfers between devices, send(): return lax.ppermute(value, NAMES, pairs_of(rule))  54.9 us
    ppermute x23, waiting for transfers between devices, send(): return lax.ppermute(value, NAMES, pairs_of(rule))  54 us
    pallas_call x1, Pallas kernels, project_own(): pl.pallas_call(project_own_kernel, name='project_own', out_shape=(jax.Sha...  2.89 us
    pallas_call x1, Pallas kernels, pairs(): pl.pallas_call(pairs_kernel, name='pairs', out_shape=(jax.ShapeDtypeStruc...  2.81 us
  transfers between devices with their start and end apart: 23, of which 9 were waited for; matrix products, arithmetic and copies ran while one was open for 0% of the time, Pallas kernels for 6%

profile of v6, /device:TPU:1, one launch (start us, length us, event | category | flops | bytes accessed | tf_op | source)
XLA Modules:
  0.0 125.6 jit_solution(5003800677333316674)
XLA Ops:
  0.6 1.1 broadcast_select_fusion
  1.7 16.1 %collective-permute-start = (bf16[128,1152]{1,0:T(8,128)(2,1)S(1)}, bf16[128,1152]{1,0:T(8,128)(2,1)S(1)}, u32[]{:S(2)}, u32[]{:S(2)}) collective-permute-start(bf16[128,1152]{1,0:T(8,128)(2,1)S(1)} %get-tuple-element.63), channel_id=1, source_target_pairs={{0,1},{1,0},{2,3},{3,2},{4,5},{5,4},{6,7},{7,6},{8,9},{9,8},{10,11... | collective-permute-start | bytes 884744 | tf_op jit(solution)/shard_map/ppermute | solution.py:47
  17.8 0.1 stack.31.flags
  17.9 2.9 %project_own.1 = (bf16[1152,1152]{1,0:T(8,128)(2,1)S(1)}, bf16[128,1152]{1,0:T(8,128)(2,1)S(1)}, f32[128,1152]{1,0:T(8,128)S(1)}, f32[128,128]{1,0:T(8,128)S(1)}) custom-call(s32[5]{0:T(128)S(1)} %stack.31.flags, bf16[128,1152]{1,0:T(8,128)(2,1)S(1)} %get-tuple-element.62.own, bf16[1152,1152]{1,0:T(8,128)(2,1)} %wp.1, bf16[1152,1152]{1,0:T(8,128)(2,1)} %wc.1), custom_call_target="tpu_custom_call" | custom-call | flops 339738624 | bytes 3833856 | tf_op jit(solution)/shard_map/project_own/pallas_call | solution.py:158
  20.8 0.0 collective-permute-done.recv
  20.8 0.8 project_other.1
  21.6 1.9 %collective-permute-start.2 = (bf16[256,1152]{1,0:T(8,128)(2,1)S(1)}, bf16[256,1152]{1,0:T(8,128)(2,1)S(1)}, u32[]{:S(2)}, u32[]{:S(2)}) collective-permute-start(bf16[256,1152]{1,0:T(8,128)(2,1)S(1)} %get-tuple-element.34.z_ref), channel_id=1, source_target_pairs={{1,8},{3,10},{5,12},{7,14},{8,1},{9,16},{10,3},{11,18},{12,5},{13,... | collective-permute-start | bytes 1769480 | tf_op jit(solution)/shard_map/ppermute | solution.py:47
  23.5 0.8 turn.1.ft
  24.3 1.3 %collective-permute-start.3 = (bf16[288,256]{1,0:T(8,128)(2,1)S(1)}, bf16[288,256]{1,0:T(8,128)(2,1)S(1)}, u32[]{:S(2)}, u32[]{:S(2)}) collective-permute-start(bf16[288,256]{1,0:T(8,128)(2,1)S(1)} %slice.9), channel_id=1, source_target_pairs={{0,2},{1,3},{6,4},{7,5},{8,10},{9,11},{14,12},{15,13},{16,18},{17,... | collective-permute-start | bytes 442376 | tf_op jit(solution)/shard_map/ppermute | solution.py:47
  25.7 0.7 collective-permute-start.6
  26.4 1.9 %collective-permute-done.3.feats_end = bf16[288,256]{1,0:T(8,128)(2,1)S(1)} collective-permute-done((bf16[288,256]{1,0:T(8,128)(2,1)S(1)}, bf16[288,256]{1,0:T(8,128)(2,1)S(1)}, u32[]{:S(2)}, u32[]{:S(2)}) %collective-permute-start.3) | collective-permute-done | bytes 147488 | tf_op jit(solution)/shard_map/ppermute | solution.py:47
  28.3 4.5 %collective-permute-done.2.one = bf16[256,1152]{1,0:T(8,128)(2,1)S(1)} collective-permute-done((bf16[256,1152]{1,0:T(8,128)(2,1)S(1)}, bf16[256,1152]{1,0:T(8,128)(2,1)S(1)}, u32[]{:S(2)}, u32[]{:S(2)}) %collective-permute-start.2) | collective-permute-done | bytes 589856 | tf_op jit(solution)/shard_map/ppermute | solution.py:47
  32.8 1.3 %collective-permute-start.4 = (bf16[256,1152]{1,0:T(8,128)(2,1)S(1)}, bf16[256,1152]{1,0:T(8,128)(2,1)S(1)}, u32[]{:S(2)}, u32[]{:S(2)}) collective-permute-start(bf16[256,1152]{1,0:T(8,128)(2,1)S(1)} %collective-permute-done.2.one), channel_id=1, source_target_pairs={{8,16},{9,1},{10,18},{11,3},{12,20},{13,5},{14,22},{15,7},{16,24},... | collective-permute-start | bytes 1769480 | tf_op jit(solution)/shard_map/ppermute | solution.py:47
  34.1 1.3 %collective-permute-start.5 = (bf16[576,256]{1,0:T(8,128)(2,1)S(1)}, bf16[576,256]{1,0:T(8,128)(2,1)S(1)}, u32[]{:S(2)}, u32[]{:S(2)}) collective-permute-start(bf16[576,256]{1,0:T(8,128)(2,1)S(1)} %slice.10), channel_id=1, source_target_pairs={{0,4},{1,5},{6,2},{7,3},{8,12},{9,13},{14,10},{15,11},{16,20},{17,... | collective-permute-start | bytes 884744 | tf_op jit(solution)/shard_map/ppermute | solution.py:47
  35.4 8.1 %collective-permute-start.1 = (bf16[256,1152]{1,0:T(8,128)(2,1)S(1)}, bf16[256,1152]{1,0:T(8,128)(2,1)S(1)}, u32[]{:S(2)}, u32[]{:S(2)}) collective-permute-start(bf16[256,1152]{1,0:T(8,128)(2,1)S(1)} %get-tuple-element.34.z_ref), channel_id=1, source_target_pairs={{0,1},{1,0},{2,3},{3,2},{4,5},{5,4},{6,7},{7,6},{8,9},{9,8},{10,11... | collective-permute-start | bytes 1769480 | tf_op jit(solution)/shard_map/ppermute | solution.py:47
  43.6 0.0 collective-permute-done.6.cross
  43.6 0.7 collective-permute-start.9
  44.3 0.7 collective-permute-start.8
  45.0 7.8 %collective-permute-done.5.early_far.feats = bf16[576,256]{1,0:T(8,128)(2,1)S(1)} collective-permute-done((bf16[576,256]{1,0:T(8,128)(2,1)S(1)}, bf16[576,256]{1,0:T(8,128)(2,1)S(1)}, u32[]{:S(2)}, u32[]{:S(2)}) %collective-permute-start.5) | collective-permute-done | bytes 294944 | tf_op jit(solution)/shard_map/ppermute | solution.py:47
  52.8 0.0 collective-permute-done.4.two
  52.8 0.7 choose.1
  53.4 1.3 %collective-permute-start.7 = (bf16[256,1152]{1,0:T(8,128)(2,1)S(1)}, bf16[256,1152]{1,0:T(8,128)(2,1)S(1)}, u32[]{:S(2)}, u32[]{:S(2)}) collective-permute-start(bf16[256,1152]{1,0:T(8,128)(2,1)S(1)} %choose.1), channel_id=1, source_target_pairs={{0,8},{2,10},{4,12},{6,14},{8,16},{9,1},{10,18},{11,3},{12,20},{13... | collective-permute-start | bytes 1769480 | tf_op jit(solution)/shard_map/ppermute | solution.py:47
  54.7 0.7 collective-permute-start.10
  56.7 0.1 pad_maximum_fusion.scale
  56.8 0.0 collective-permute-done.10.early_mid.feats_mid
  56.8 0.0 collective-permute-done.1.here
  56.8 0.0 collective-permute-done.9.afar_one
  56.8 0.0 collective-permute-done.8.near_one
  56.8 15.1 %collective-permute-done.7.three = bf16[256,1152]{1,0:T(8,128)(2,1)S(1)} collective-permute-done((bf16[256,1152]{1,0:T(8,128)(2,1)S(1)}, bf16[256,1152]{1,0:T(8,128)(2,1)S(1)}, u32[]{:S(2)}, u32[]{:S(2)}) %collective-permute-start.7) | collective-permute-done | bytes 589856 | tf_op jit(solution)/shard_map/ppermute | solution.py:47
  71.9 2.8 %pairs.1 = (bf16[256,512]{1,0:T(8,128)(2,1)S(1)}, bf16[256,640]{1,0:T(8,128)(2,1)S(1)}) custom-call(s32[5]{0:T(128)S(1)} %stack.31.flags, f32[2]{0:T(128)S(1)} %pad_maximum_fusion.scale, bf16[256,1152]{1,0:T(8,128)(2,1)S(1)} %get-tuple-element.34.z_ref, f32[128,1152]{1,0:T(8,128)S(1)} %get-tuple-element.35.u_own, f32[128,1152]{1,0:T(8,128)S(1)} %get-tuple-element.36.u_other, ...), custom_call_target="tpu_custom_call" | custom-call | flops 603979776 | bytes 4128768 | tf_op jit(solution)/shard_map/pairs/pallas_call | solution.py:322
  74.7 0.7 collective-permute-start.14
  75.4 7.3 %collective-permute-start.11 = (bf16[256,640]{1,0:T(8,128)(2,1)S(1)}, bf16[256,640]{1,0:T(8,128)(2,1)S(1)}, u32[]{:S(2)}, u32[]{:S(2)}) collective-permute-start(bf16[256,640]{1,0:T(8,128)(2,1)S(1)} %get-tuple-element.42.refs_1_), channel_id=1, source_target_pairs={{0,2},{1,3},{6,4},{7,5},{8,10},{9,11},{14,12},{15,13},{16,18},{17,... | collective-permute-start | bytes 983048 | tf_op jit(solution)/shard_map/ppermute | solution.py:47
  82.8 1.3 %collective-permute-start.12 = (bf16[256,512]{1,0:T(8,128)(2,1)S(1)}, bf16[256,512]{1,0:T(8,128)(2,1)S(1)}, u32[]{:S(2)}, u32[]{:S(2)}) collective-permute-start(bf16[256,512]{1,0:T(8,128)(2,1)S(1)} %get-tuple-element.44.refs_0_), channel_id=1, source_target_pairs={{0,2},{1,3},{6,4},{7,5},{8,10},{9,11},{14,12},{15,13},{16,18},{17,... | collective-permute-start | bytes 786440 | tf_op jit(solution)/shard_map/ppermute | solution.py:47
  84.1 0.7 collective-permute-start.13
  84.8 9.9 %collective-permute-done.12.refs_2_ = bf16[256,512]{1,0:T(8,128)(2,1)S(1)} collective-permute-done((bf16[256,512]{1,0:T(8,128)(2,1)S(1)}, bf16[256,512]{1,0:T(8,128)(2,1)S(1)}, u32[]{:S(2)}, u32[]{:S(2)}) %collective-permute-start.12) | collective-permute-done | bytes 262176 | tf_op jit(solution)/shard_map/ppermute | solution.py:47
  94.7 0.7 collective-permute-start.15
  95.4 0.0 collective-permute-done.13.refs_4_
  95.4 0.0 collective-permute-done.14.refs_5_
  95.4 0.0 collective-permute-done.11.refs_3_
  95.4 1.1 near.1
  96.6 0.7 collective-permute-start.16
  97.3 0.0 collective-permute-done.15.dx.dx_left
  97.3 0.8 far.2
  98.1 1.3 %collective-permute-start.17 = (bf16[144,512]{1,0:T(8,128)(2,1)S(1)}, bf16[144,512]{1,0:T(8,128)(2,1)S(1)}, u32[]{:S(2)}, u32[]{:S(2)}) collective-permute-start(bf16[144,512]{1,0:T(8,128)(2,1)S(1)} %get-tuple-element.53), channel_id=1, source_target_pairs={{2,0},{3,1},{4,6},{5,7},{10,8},{11,9},{12,14},{13,15},{18,16},{19,... | collective-permute-start | bytes 442376 | tf_op jit(solution)/shard_map/ppermute | solution.py:47
  99.4 1.3 %collective-permute-start.18 = (bf16[144,512]{1,0:T(8,128)(2,1)S(1)}, bf16[144,512]{1,0:T(8,128)(2,1)S(1)}, u32[]{:S(2)}, u32[]{:S(2)}) collective-permute-start(bf16[144,512]{1,0:T(8,128)(2,1)S(1)} %get-tuple-element.54), channel_id=1, source_target_pairs={{2,1},{3,0},{4,7},{5,6},{10,9},{11,8},{12,15},{13,14},{18,17},{19,... | collective-permute-start | bytes 442376 | tf_op jit(solution)/shard_map/ppermute | solution.py:47
  100.7 0.0 collective-permute-done.16.dx.dx_right
  100.7 0.9 far.3
  101.6 1.3 %collective-permute-start.19 = (bf16[144,640]{1,0:T(8,128)(2,1)S(1)}, bf16[144,640]{1,0:T(8,128)(2,1)S(1)}, u32[]{:S(2)}, u32[]{:S(2)}) collective-permute-start(bf16[144,640]{1,0:T(8,128)(2,1)S(1)} %get-tuple-element.57), channel_id=1, source_target_pairs={{2,0},{3,1},{4,6},{5,7},{10,8},{11,9},{12,14},{13,15},{18,16},{19,... | collective-permute-start | bytes 552968 | tf_op jit(solution)/shard_map/ppermute | solution.py:47
  102.9 1.3 %collective-permute-start.20 = (bf16[144,640]{1,0:T(8,128)(2,1)S(1)}, bf16[144,640]{1,0:T(8,128)(2,1)S(1)}, u32[]{:S(2)}, u32[]{:S(2)}) collective-permute-start(bf16[144,640]{1,0:T(8,128)(2,1)S(1)} %get-tuple-element.58), channel_id=1, source_target_pairs={{2,1},{3,0},{4,7},{5,6},{10,9},{11,8},{12,15},{13,14},{18,17},{19,... | collective-permute-start | bytes 552968 | tf_op jit(solution)/shard_map/ppermute | solution.py:47
  104.2 0.6 rest.1
  104.8 4.8 %collective-permute-done.17.same_left = bf16[144,512]{1,0:T(8,128)(2,1)S(1)} collective-permute-done((bf16[144,512]{1,0:T(8,128)(2,1)S(1)}, bf16[144,512]{1,0:T(8,128)(2,1)S(1)}, u32[]{:S(2)}, u32[]{:S(2)}) %collective-permute-start.17) | collective-permute-done | bytes 147488 | tf_op jit(solution)/shard_map/ppermute | solution.py:47
  109.7 7.1 %collective-permute-done.18.crossed_left = bf16[144,512]{1,0:T(8,128)(2,1)S(1)} collective-permute-done((bf16[144,512]{1,0:T(8,128)(2,1)S(1)}, bf16[144,512]{1,0:T(8,128)(2,1)S(1)}, u32[]{:S(2)}, u32[]{:S(2)}) %collective-permute-start.18) | collective-permute-done | bytes 147488 | tf_op jit(solution)/shard_map/ppermute | solution.py:47
  116.7 1.9 %collective-permute-start.22 = (bf16[144,640]{1,0:T(8,128)(2,1)S(1)}, bf16[144,640]{1,0:T(8,128)(2,1)S(1)}, u32[]{:S(2)}, u32[]{:S(2)}) collective-permute-start(bf16[144,640]{1,0:T(8,128)(2,1)S(1)} %get-tuple-element.60), channel_id=1, source_target_pairs={{0,1},{1,0},{2,3},{3,2},{4,5},{5,4},{6,7},{7,6},{8,9},{9,8},{10,11... | collective-permute-start | bytes 552968 | tf_op jit(solution)/shard_map/ppermute | solution.py:47
  118.7 2.4 %collective-permute-start.21 = (bf16[144,512]{1,0:T(8,128)(2,1)S(1)}, bf16[144,512]{1,0:T(8,128)(2,1)S(1)}, u32[]{:S(2)}, u32[]{:S(2)}) collective-permute-start(bf16[144,512]{1,0:T(8,128)(2,1)S(1)} %get-tuple-element.59), channel_id=1, source_target_pairs={{0,1},{1,0},{2,3},{3,2},{4,5},{5,4},{6,7},{7,6},{8,9},{9,8},{10,11... | collective-permute-start | bytes 442376 | tf_op jit(solution)/shard_map/ppermute | solution.py:47
  121.1 1.0 collective-permute-done.21.swap_left
  122.1 0.0 collective-permute-done.19.same_right
  122.1 1.8 %collective-permute-done.20.crossed_right = bf16[144,640]{1,0:T(8,128)(2,1)S(1)} collective-permute-done((bf16[144,640]{1,0:T(8,128)(2,1)S(1)}, bf16[144,640]{1,0:T(8,128)(2,1)S(1)}, u32[]{:S(2)}, u32[]{:S(2)}) %collective-permute-start.20) | collective-permute-done | bytes 184352 | tf_op jit(solution)/shard_map/ppermute | solution.py:47
  123.9 0.0 collective-permute-done.22.swap_right
  123.9 1.7 %finish.1 = (f32[1,144,1152]{2,1,0:T(8,128)}, f32[1,144,1152]{2,1,0:T(8,128)}) custom-call(s32[5]{0:T(128)S(1)} %stack.31.flags, bf16[144,512]{1,0:T(8,128)(2,1)S(1)} %collective-permute-done.17.same_left, bf16[144,512]{1,0:T(8,128)(2,1)S(1)} %collective-permute-done.18.crossed_left, bf16[144,640]{1,0:T(8,128)(2,1)S(1)} %collective-permute-done.19.same_right, ...), custom_call_target="tpu_custom_call" | custom-call | flops 663552 | bytes 2985984 | tf_op jit(solution)/shard_map/finish/pallas_call | solution.py:474
  (2 shorter events, 0.0 us)
Async XLA Ops:
  1.7 19.1 %collective-permute-start = (bf16[128,1152]{1,0:T(8,128)(2,1)S(1)}, bf16[128,1152]{1,0:T(8,128)(2,1)S(1)}, u32[]{:S(2)}, u32[]{:S(2)}) collective-permute-start(bf16[128,1152]{1,0:T(8,128)(2,1)S(1)} %get-tuple-element.63), channel_id=1, source_target_pairs={{0,1},{1,0},{2,3},{3,2},{4,5},{5,4},{6,7},{7,6},{8,9},{9,8},{10,11... | collective-permute-start | bytes 884744 | tf_op jit(solution)/shard_map/ppermute | solution.py:47
  21.6 11.2 %collective-permute-start.2 = (bf16[256,1152]{1,0:T(8,128)(2,1)S(1)}, bf16[256,1152]{1,0:T(8,128)(2,1)S(1)}, u32[]{:S(2)}, u32[]{:S(2)}) collective-permute-start(bf16[256,1152]{1,0:T(8,128)(2,1)S(1)} %get-tuple-element.34.z_ref), channel_id=1, source_target_pairs={{1,8},{3,10},{5,12},{7,14},{8,1},{9,16},{10,3},{11,18},{12,5},{13,... | collective-permute-start | bytes 1769480 | tf_op jit(solution)/shard_map/ppermute | solution.py:47
  24.3 3.9 %collective-permute-start.3 = (bf16[288,256]{1,0:T(8,128)(2,1)S(1)}, bf16[288,256]{1,0:T(8,128)(2,1)S(1)}, u32[]{:S(2)}, u32[]{:S(2)}) collective-permute-start(bf16[288,256]{1,0:T(8,128)(2,1)S(1)} %slice.9), channel_id=1, source_target_pairs={{0,2},{1,3},{6,4},{7,5},{8,10},{9,11},{14,12},{15,13},{16,18},{17,... | collective-permute-start | bytes 442376 | tf_op jit(solution)/shard_map/ppermute | solution.py:47
  25.7 17.9 %collective-permute-start.6 = (bf16[256,1152]{1,0:T(8,128)(2,1)S(1)}, bf16[256,1152]{1,0:T(8,128)(2,1)S(1)}, u32[]{:S(2)}, u32[]{:S(2)}) collective-permute-start(bf16[256,1152]{1,0:T(8,128)(2,1)S(1)} %get-tuple-element.34.z_ref), channel_id=1, source_target_pairs={{0,1009},{2,1011},{4,1013},{6,1015},{8,1017},{10,1019},{12,1021},{... | collective-permute-start | bytes 1769480 | tf_op jit(solution)/shard_map/ppermute | solution.py:47
  32.8 20.0 %collective-permute-start.4 = (bf16[256,1152]{1,0:T(8,128)(2,1)S(1)}, bf16[256,1152]{1,0:T(8,128)(2,1)S(1)}, u32[]{:S(2)}, u32[]{:S(2)}) collective-permute-start(bf16[256,1152]{1,0:T(8,128)(2,1)S(1)} %collective-permute-done.2.one), channel_id=1, source_target_pairs={{8,16},{9,1},{10,18},{11,3},{12,20},{13,5},{14,22},{15,7},{16,24},... | collective-permute-start | bytes 1769480 | tf_op jit(solution)/shard_map/ppermute | solution.py:47
  34.1 18.6 %collective-permute-start.5 = (bf16[576,256]{1,0:T(8,128)(2,1)S(1)}, bf16[576,256]{1,0:T(8,128)(2,1)S(1)}, u32[]{:S(2)}, u32[]{:S(2)}) collective-permute-start(bf16[576,256]{1,0:T(8,128)(2,1)S(1)} %slice.10), channel_id=1, source_target_pairs={{0,4},{1,5},{6,2},{7,3},{8,12},{9,13},{14,10},{15,11},{16,20},{17,... | collective-permute-start | bytes 884744 | tf_op jit(solution)/shard_map/ppermute | solution.py:47
  35.4 21.4 %collective-permute-start.1 = (bf16[256,1152]{1,0:T(8,128)(2,1)S(1)}, bf16[256,1152]{1,0:T(8,128)(2,1)S(1)}, u32[]{:S(2)}, u32[]{:S(2)}) collective-permute-start(bf16[256,1152]{1,0:T(8,128)(2,1)S(1)} %get-tuple-element.34.z_ref), channel_id=1, source_target_pairs={{0,1},{1,0},{2,3},{3,2},{4,5},{5,4},{6,7},{7,6},{8,9},{9,8},{10,11... | collective-permute-start | bytes 1769480 | tf_op jit(solution)/shard_map/ppermute | solution.py:47
  43.6 13.2 %collective-permute-start.9 = (bf16[256,1152]{1,0:T(8,128)(2,1)S(1)}, bf16[256,1152]{1,0:T(8,128)(2,1)S(1)}, u32[]{:S(2)}, u32[]{:S(2)}) collective-permute-start(bf16[256,1152]{1,0:T(8,128)(2,1)S(1)} %collective-permute-done.6.cross), channel_id=1, source_target_pairs={{17,57},{19,59},{21,61},{23,63},{40,0},{42,2},{44,4},{46,6},{81,12... | collective-permute-start | bytes 1769480 | tf_op jit(solution)/shard_map/ppermute | solution.py:47
  44.3 12.5 %collective-permute-start.8 = (bf16[256,1152]{1,0:T(8,128)(2,1)S(1)}, bf16[256,1152]{1,0:T(8,128)(2,1)S(1)}, u32[]{:S(2)}, u32[]{:S(2)}) collective-permute-start(bf16[256,1152]{1,0:T(8,128)(2,1)S(1)} %collective-permute-done.6.cross), channel_id=1, source_target_pairs={{8,0},{10,2},{12,4},{14,6},{49,57},{51,59},{53,61},{55,63},{72,64}... | collective-permute-start | bytes 1769480 | tf_op jit(solution)/shard_map/ppermute | solution.py:47
  53.4 18.5 %collective-permute-start.7 = (bf16[256,1152]{1,0:T(8,128)(2,1)S(1)}, bf16[256,1152]{1,0:T(8,128)(2,1)S(1)}, u32[]{:S(2)}, u32[]{:S(2)}) collective-permute-start(bf16[256,1152]{1,0:T(8,128)(2,1)S(1)} %choose.1), channel_id=1, source_target_pairs={{0,8},{2,10},{4,12},{6,14},{8,16},{9,1},{10,18},{11,3},{12,20},{13... | collective-permute-start | bytes 1769480 | tf_op jit(solution)/shard_map/ppermute | solution.py:47
  54.7 2.1 %collective-permute-start.10 = (bf16[576,256]{1,0:T(8,128)(2,1)S(1)}, bf16[576,256]{1,0:T(8,128)(2,1)S(1)}, u32[]{:S(2)}, u32[]{:S(2)}) collective-permute-start(bf16[576,256]{1,0:T(8,128)(2,1)S(1)} %slice.10), channel_id=1, source_target_pairs={{2,4},{3,5},{4,2},{5,3},{10,12},{11,13},{12,10},{13,11},{18,20},{1... | collective-permute-start | bytes 884744 | tf_op jit(solution)/shard_map/ppermute | solution.py:47
  74.7 20.7 %collective-permute-start.14 = (bf16[256,640]{1,0:T(8,128)(2,1)S(1)}, bf16[256,640]{1,0:T(8,128)(2,1)S(1)}, u32[]{:S(2)}, u32[]{:S(2)}) collective-permute-start(bf16[256,640]{1,0:T(8,128)(2,1)S(1)} %get-tuple-element.42.refs_1_), channel_id=1, source_target_pairs={{2,4},{3,5},{4,2},{5,3},{10,12},{11,13},{12,10},{13,11},{18,20},{1... | collective-permute-start | bytes 983048 | tf_op jit(solution)/shard_map/ppermute | solution.py:47
  75.4 20.0 %collective-permute-start.11 = (bf16[256,640]{1,0:T(8,128)(2,1)S(1)}, bf16[256,640]{1,0:T(8,128)(2,1)S(1)}, u32[]{:S(2)}, u32[]{:S(2)}) collective-permute-start(bf16[256,640]{1,0:T(8,128)(2,1)S(1)} %get-tuple-element.42.refs_1_), channel_id=1, source_target_pairs={{0,2},{1,3},{6,4},{7,5},{8,10},{9,11},{14,12},{15,13},{16,18},{17,... | collective-permute-start | bytes 983048 | tf_op jit(solution)/shard_map/ppermute | solution.py:47
  82.8 11.9 %collective-permute-start.12 = (bf16[256,512]{1,0:T(8,128)(2,1)S(1)}, bf16[256,512]{1,0:T(8,128)(2,1)S(1)}, u32[]{:S(2)}, u32[]{:S(2)}) collective-permute-start(bf16[256,512]{1,0:T(8,128)(2,1)S(1)} %get-tuple-element.44.refs_0_), channel_id=1, source_target_pairs={{0,2},{1,3},{6,4},{7,5},{8,10},{9,11},{14,12},{15,13},{16,18},{17,... | collective-permute-start | bytes 786440 | tf_op jit(solution)/shard_map/ppermute | solution.py:47
  84.1 11.3 %collective-permute-start.13 = (bf16[256,512]{1,0:T(8,128)(2,1)S(1)}, bf16[256,512]{1,0:T(8,128)(2,1)S(1)}, u32[]{:S(2)}, u32[]{:S(2)}) collective-permute-start(bf16[256,512]{1,0:T(8,128)(2,1)S(1)} %get-tuple-element.44.refs_0_), channel_id=1, source_target_pairs={{2,4},{3,5},{4,2},{5,3},{10,12},{11,13},{12,10},{13,11},{18,20},{1... | collective-permute-start | bytes 786440 | tf_op jit(solution)/shard_map/ppermute | solution.py:47
  94.7 2.5 %collective-permute-start.15 = (bf16[256,512]{1,0:T(8,128)(2,1)S(1)}, bf16[256,512]{1,0:T(8,128)(2,1)S(1)}, u32[]{:S(2)}, u32[]{:S(2)}) collective-permute-start(bf16[256,512]{1,0:T(8,128)(2,1)S(1)} %collective-permute-done.12.refs_2_), channel_id=1, source_target_pairs={{2,4},{3,5},{4,2},{5,3},{10,12},{11,13},{12,10},{13,11},{18,20},{1... | collective-permute-start | bytes 786440 | tf_op jit(solution)/shard_map/ppermute | solution.py:47
  96.6 4.1 %collective-permute-start.16 = (bf16[256,640]{1,0:T(8,128)(2,1)S(1)}, bf16[256,640]{1,0:T(8,128)(2,1)S(1)}, u32[]{:S(2)}, u32[]{:S(2)}) collective-permute-start(bf16[256,640]{1,0:T(8,128)(2,1)S(1)} %collective-permute-done.11.refs_3_), channel_id=1, source_target_pairs={{2,4},{3,5},{4,2},{5,3},{10,12},{11,13},{12,10},{13,11},{18,20},{1... | collective-permute-start | bytes 983048 | tf_op jit(solution)/shard_map/ppermute | solution.py:47
  98.1 11.6 %collective-permute-start.17 = (bf16[144,512]{1,0:T(8,128)(2,1)S(1)}, bf16[144,512]{1,0:T(8,128)(2,1)S(1)}, u32[]{:S(2)}, u32[]{:S(2)}) collective-permute-start(bf16[144,512]{1,0:T(8,128)(2,1)S(1)} %get-tuple-element.53), channel_id=1, source_target_pairs={{2,0},{3,1},{4,6},{5,7},{10,8},{11,9},{12,14},{13,15},{18,16},{19,... | collective-permute-start | bytes 442376 | tf_op jit(solution)/shard_map/ppermute | solution.py:47
  99.4 17.4 %collective-permute-start.18 = (bf16[144,512]{1,0:T(8,128)(2,1)S(1)}, bf16[144,512]{1,0:T(8,128)(2,1)S(1)}, u32[]{:S(2)}, u32[]{:S(2)}) collective-permute-start(bf16[144,512]{1,0:T(8,128)(2,1)S(1)} %get-tuple-element.54), channel_id=1, source_target_pairs={{2,1},{3,0},{4,7},{5,6},{10,9},{11,8},{12,15},{13,14},{18,17},{19,... | collective-permute-start | bytes 442376 | tf_op jit(solution)/shard_map/ppermute | solution.py:47
  101.6 20.5 %collective-permute-start.19 = (bf16[144,640]{1,0:T(8,128)(2,1)S(1)}, bf16[144,640]{1,0:T(8,128)(2,1)S(1)}, u32[]{:S(2)}, u32[]{:S(2)}) collective-permute-start(bf16[144,640]{1,0:T(8,128)(2,1)S(1)} %get-tuple-element.57), channel_id=1, source_target_pairs={{2,0},{3,1},{4,6},{5,7},{10,8},{11,9},{12,14},{13,15},{18,16},{19,... | collective-permute-start | bytes 552968 | tf_op jit(solution)/shard_map/ppermute | solution.py:47
  102.9 21.0 %collective-permute-start.20 = (bf16[144,640]{1,0:T(8,128)(2,1)S(1)}, bf16[144,640]{1,0:T(8,128)(2,1)S(1)}, u32[]{:S(2)}, u32[]{:S(2)}) collective-permute-start(bf16[144,640]{1,0:T(8,128)(2,1)S(1)} %get-tuple-element.58), channel_id=1, source_target_pairs={{2,1},{3,0},{4,7},{5,6},{10,9},{11,8},{12,15},{13,14},{18,17},{19,... | collective-permute-start | bytes 552968 | tf_op jit(solution)/shard_map/ppermute | solution.py:47
  116.7 7.1 %collective-permute-start.22 = (bf16[144,640]{1,0:T(8,128)(2,1)S(1)}, bf16[144,640]{1,0:T(8,128)(2,1)S(1)}, u32[]{:S(2)}, u32[]{:S(2)}) collective-permute-start(bf16[144,640]{1,0:T(8,128)(2,1)S(1)} %get-tuple-element.60), channel_id=1, source_target_pairs={{0,1},{1,0},{2,3},{3,2},{4,5},{5,4},{6,7},{7,6},{8,9},{9,8},{10,11... | collective-permute-start | bytes 552968 | tf_op jit(solution)/shard_map/ppermute | solution.py:47
  118.7 3.4 %collective-permute-start.21 = (bf16[144,512]{1,0:T(8,128)(2,1)S(1)}, bf16[144,512]{1,0:T(8,128)(2,1)S(1)}, u32[]{:S(2)}, u32[]{:S(2)}) collective-permute-start(bf16[144,512]{1,0:T(8,128)(2,1)S(1)} %get-tuple-element.59), channel_id=1, source_target_pairs={{0,1},{1,0},{2,3},{3,2},{4,5},{5,4},{6,7},{7,6},{8,9},{9,8},{10,11... | collective-permute-start | bytes 442376 | tf_op jit(solution)/shard_map/ppermute | solution.py:47

commit v7 on v6

--- a/solution.py
+++ b/solution.py
@@ -77,11 +77,19 @@
     return (x, 0, column) if zh == 1 else ((x - 1) % NX, 1, column)
 
 
-def crossing(x, zh, y, zl, c):
-    if c == 1 and y >= 5:
-        return (*above(x, zh, {7: 1, 6: 0, 5: 5}[y]), zl, 0)
-    if c == 0 and y <= 2:
-        return (*below(x, zh, {0: 6, 1: 7, 2: 2}[y]), zl, 1)
+def first_crossing(x, zh, y, zl, c):
+    if c == 1 and y >= 6:
+        return (*above(x, zh, y - 6), zl, 0)
+    if c == 0 and y <= 1:
+        return (*below(x, zh, 6 + y), zl, 1)
+    return None
+
+
+def second_crossing(x, zh, y, zl, c):
+    if c == 0 and y == 6:
+        return (*above(x, zh, 0), zl, 0)
+    if c == 1 and y == 1:
+        return (*below(x, zh, 7), zl, 1)
     return None
 
 
@@ -89,14 +97,6 @@
     if c == 0 and y == 1:
         return (x, zh, 0, zl, 0)
     if c == 1 and y == 6:
-        return (x, zh, 7, zl, 1)
-    return None
-
-
-def from_afar(x, zh, y, zl, c):
-    if c == 0 and y == 5:
-        return (x, zh, 0, zl, 0)
-    if c == 1 and y == 2:
         return (x, zh, 7, zl, 1)
     return None
 
@@ -256,10 +256,9 @@
 
 def pairs_kernel(
     flags, scale, z_ref, u_own, u_other, rn_own, rn_other,
-    here, one, two, three, cross, near_one, afar_one, early_mid, early_far,
-    dx_left, dx_right, others, sems,
+    here, one, two, three, cross, near_one, cross_two, *refs
 ):
-    del early_mid, early_far
+    dx_left, dx_right, others, sems = refs[-4:]
     place = flags[1]
 
     def fetch(source, s):
@@ -280,7 +279,7 @@
     @pl.when(place == 0)
     def _():
         fetch(near_one, 1)
-        fetch(afar_one, 3)
+        fetch(cross_two, 3)
 
     @pl.when(place <= 1)
     def _():
@@ -326,7 +325,7 @@
             jax.ShapeDtypeStruct((rows, LEFT), BF),
             jax.ShapeDtypeStruct((rows, D - LEFT), BF),
         ),
-        in_specs=[SMEM, SMEM] + [VMEM] * 5 + [ANY] * 9,
+        in_specs=[SMEM, SMEM] + [VMEM] * 5 + [ANY] * 10,
         out_specs=(VMEM, VMEM),
         scratch_shapes=[
             pltpu.VMEM((2, 4 * ROWS, D), BF),
@@ -498,21 +497,21 @@
     z, u_other, rn_other = project_other(received, head, z_own)
 
     one = send(z, first_hop)
-    cross = send(z, crossing)
+    cross = send(z, first_crossing)
     ft = turn(flags, own, received)
+    one, ft = lax.optimization_barrier((one, ft))
     ft_end = send(ft[CHIP : 2 * CHIP], inward)
     ft_mid = send(ft[2 * CHIP :], middle)
     ft_far = send(ft[2 * CHIP :], inward_far)
-    one, ft_end = lax.optimization_barrier((one, ft_end))
     two = send(one, second_hop)
+    cross_two = send(one, second_crossing)
     near_one = send(cross, from_near)
-    afar_one = send(cross, from_afar)
     two, ft_far = lax.optimization_barrier((two, ft_far))
     three = send(choose(flags, two, cross), third_hop)
     here = send(z, other_core)
     dxs = pairs(
         flags, scale, z, u_own, u_other, rn_own, rn_other, here, one, two, three,
-        cross, near_one, afar_one, ft_mid, ft_far,
+        cross, near_one, cross_two, ft_mid, ft_far, ft_end,
     )
 
     ends = [send(dx, inward) for dx in dxs]

time: 126 us -> 130 us (1.032)
  the two profiles are of different devices: /device:TPU:1 before, /device:TPU:113 now
where the time goes in v7:
time: 130 us; the launch traced here: 129 us
  starting transfers between devices  73.6 us (57%)
  waiting for transfers between devices  38.9 us (30%)
  Pallas kernels  13.1 us (10%)
  between operations  2.3 us (2%)
    ppermute x23, starting transfers between devices, send(): return lax.ppermute(value, NAMES, pairs_of(rule))  73.6 us
    ppermute x23, waiting for transfers between devices, send(): return lax.ppermute(value, NAMES, pairs_of(rule))  38.9 us
    pallas_call x1, Pallas kernels, project_own(): pl.pallas_call(project_own_kernel, name='project_own', out_shape=(jax.Sha...  2.89 us
    pallas_call x1, Pallas kernels, pairs(): pl.pallas_call(pairs_kernel, name='pairs', out_shape=(jax.ShapeDtypeStruc...  2.84 us
  transfers between devices with their start and end apart: 23, of which 8 were waited for; matrix products, arithmetic and copies ran while one was open for 0% of the time, Pallas kernels for 6%

profile of v7, /device:TPU:113, one launch (start us, length us, event | category | flops | bytes accessed | tf_op | source)
XLA Modules:
  0.0 129.2 jit_solution(8259658828758561299)
XLA Ops:
  0.6 1.1 broadcast_select_fusion
  1.7 2.6 %collective-permute-start = (bf16[128,1152]{1,0:T(8,128)(2,1)S(1)}, bf16[128,1152]{1,0:T(8,128)(2,1)S(1)}, u32[]{:S(2)}, u32[]{:S(2)}) collective-permute-start(bf16[128,1152]{1,0:T(8,128)(2,1)S(1)} %get-tuple-element.63), channel_id=1, source_target_pairs={{0,1},{1,0},{2,3},{3,2},{4,5},{5,4},{6,7},{7,6},{8,9},{9,8},{10,11... | collective-permute-start | bytes 884744 | tf_op jit(solution)/shard_map/ppermute | solution.py:47
  4.4 0.1 stack.31.flags
  4.4 2.9 %project_own.1 = (bf16[1152,1152]{1,0:T(8,128)(2,1)S(1)}, bf16[128,1152]{1,0:T(8,128)(2,1)S(1)}, f32[128,1152]{1,0:T(8,128)S(1)}, f32[128,128]{1,0:T(8,128)S(1)}) custom-call(s32[5]{0:T(128)S(1)} %stack.31.flags, bf16[128,1152]{1,0:T(8,128)(2,1)S(1)} %get-tuple-element.62.own, bf16[1152,1152]{1,0:T(8,128)(2,1)} %wp.1, bf16[1152,1152]{1,0:T(8,128)(2,1)} %wc.1), custom_call_target="tpu_custom_call" | custom-call | flops 339738624 | bytes 3833856 | tf_op jit(solution)/shard_map/project_own/pallas_call | solution.py:158
  7.3 0.0 collective-permute-done.recv
  7.4 0.8 project_other.1
  8.1 0.7 collective-permute-start.2
  8.8 15.4 %collective-permute-start.5 = (bf16[256,1152]{1,0:T(8,128)(2,1)S(1)}, bf16[256,1152]{1,0:T(8,128)(2,1)S(1)}, u32[]{:S(2)}, u32[]{:S(2)}) collective-permute-start(bf16[256,1152]{1,0:T(8,128)(2,1)S(1)} %get-tuple-element.34.z_ref), channel_id=1, source_target_pairs={{0,1009},{2,1011},{4,1013},{6,1015},{8,1017},{10,1019},{12,1021},{... | collective-permute-start | bytes 1769480 | tf_op jit(solution)/shard_map/ppermute | solution.py:47
  24.2 0.8 turn.1.ft
  25.0 0.0 collective-permute-done.2.one
  25.0 0.7 collective-permute-start.3
  25.7 5.8 %collective-permute-start.4 = (bf16[576,256]{1,0:T(8,128)(2,1)S(1)}, bf16[576,256]{1,0:T(8,128)(2,1)S(1)}, u32[]{:S(2)}, u32[]{:S(2)}) collective-permute-start(bf16[576,256]{1,0:T(8,128)(2,1)S(1)} %slice.7), channel_id=1, source_target_pairs={{0,4},{1,5},{6,2},{7,3},{8,12},{9,13},{14,10},{15,11},{16,20},{17,... | collective-permute-start | bytes 884744 | tf_op jit(solution)/shard_map/ppermute | solution.py:47
  31.6 1.9 %collective-permute-start.1 = (bf16[256,1152]{1,0:T(8,128)(2,1)S(1)}, bf16[256,1152]{1,0:T(8,128)(2,1)S(1)}, u32[]{:S(2)}, u32[]{:S(2)}) collective-permute-start(bf16[256,1152]{1,0:T(8,128)(2,1)S(1)} %get-tuple-element.34.z_ref), channel_id=1, source_target_pairs={{0,1},{1,0},{2,3},{3,2},{4,5},{5,4},{6,7},{7,6},{8,9},{9,8},{10,11... | collective-permute-start | bytes 1769480 | tf_op jit(solution)/shard_map/ppermute | solution.py:47
  33.5 1.3 %collective-permute-start.8 = (bf16[256,1152]{1,0:T(8,128)(2,1)S(1)}, bf16[256,1152]{1,0:T(8,128)(2,1)S(1)}, u32[]{:S(2)}, u32[]{:S(2)}) collective-permute-start(bf16[256,1152]{1,0:T(8,128)(2,1)S(1)} %collective-permute-done.2.one), channel_id=1, source_target_pairs={{9,1017},{11,1019},{13,1021},{15,1023},{48,64},{50,66},{52,68},{54... | collective-permute-start | bytes 1769480 | tf_op jit(solution)/shard_map/ppermute | solution.py:47
  34.8 6.6 %collective-permute-done.5.cross = bf16[256,1152]{1,0:T(8,128)(2,1)S(1)} collective-permute-done((bf16[256,1152]{1,0:T(8,128)(2,1)S(1)}, bf16[256,1152]{1,0:T(8,128)(2,1)S(1)}, u32[]{:S(2)}, u32[]{:S(2)}) %collective-permute-start.5) | collective-permute-done | bytes 589856 | tf_op jit(solution)/shard_map/ppermute | solution.py:47
  41.4 1.3 collective-permute-start.7
  42.7 7.5 %collective-permute-done.4.refs_1_.feats = bf16[576,256]{1,0:T(8,128)(2,1)S(1)} collective-permute-done((bf16[576,256]{1,0:T(8,128)(2,1)S(1)}, bf16[576,256]{1,0:T(8,128)(2,1)S(1)}, u32[]{:S(2)}, u32[]{:S(2)}) %collective-permute-start.4) | collective-permute-done | bytes 294944 | tf_op jit(solution)/shard_map/ppermute | solution.py:47
  50.2 0.0 collective-permute-done.3.two
  50.2 0.7 choose.1
  50.9 1.3 %collective-permute-start.6 = (bf16[256,1152]{1,0:T(8,128)(2,1)S(1)}, bf16[256,1152]{1,0:T(8,128)(2,1)S(1)}, u32[]{:S(2)}, u32[]{:S(2)}) collective-permute-start(bf16[256,1152]{1,0:T(8,128)(2,1)S(1)} %choose.1), channel_id=1, source_target_pairs={{0,8},{2,10},{4,12},{6,14},{8,16},{9,1},{10,18},{11,3},{12,20},{13... | collective-permute-start | bytes 1769480 | tf_op jit(solution)/shard_map/ppermute | solution.py:47
  52.2 0.7 collective-permute-start.9
  52.9 0.0 collective-permute-done.1.here
  52.9 21.5 %collective-permute-start.10 = (bf16[288,256]{1,0:T(8,128)(2,1)S(1)}, bf16[288,256]{1,0:T(8,128)(2,1)S(1)}, u32[]{:S(2)}, u32[]{:S(2)}) collective-permute-start(bf16[288,256]{1,0:T(8,128)(2,1)S(1)} %slice.8), channel_id=1, source_target_pairs={{0,2},{1,3},{6,4},{7,5},{8,10},{9,11},{14,12},{15,13},{16,18},{17,... | collective-permute-start | bytes 442376 | tf_op jit(solution)/shard_map/ppermute | solution.py:47
  75.7 0.1 pad_maximum_fusion.scale
  75.8 1.4 %collective-permute-done.10.refs_2_.feats_end = bf16[288,256]{1,0:T(8,128)(2,1)S(1)} collective-permute-done((bf16[288,256]{1,0:T(8,128)(2,1)S(1)}, bf16[288,256]{1,0:T(8,128)(2,1)S(1)}, u32[]{:S(2)}, u32[]{:S(2)}) %collective-permute-start.10) | collective-permute-done | bytes 147488 | tf_op jit(solution)/shard_map/ppermute | solution.py:47
  77.2 0.0 collective-permute-done.9.refs_0_.feats_mid
  77.2 0.0 collective-permute-done.7.near_one
  77.2 0.0 collective-permute-done.8.cross_two
  77.3 0.0 collective-permute-done.6.three
  77.3 2.8 %pairs.1 = (bf16[256,512]{1,0:T(8,128)(2,1)S(1)}, bf16[256,640]{1,0:T(8,128)(2,1)S(1)}) custom-call(s32[5]{0:T(128)S(1)} %stack.31.flags, f32[2]{0:T(128)S(1)} %pad_maximum_fusion.scale, bf16[256,1152]{1,0:T(8,128)(2,1)S(1)} %get-tuple-element.34.z_ref, f32[128,1152]{1,0:T(8,128)S(1)} %get-tuple-element.35.u_own, f32[128,1152]{1,0:T(8,128)S(1)} %get-tuple-element.36.u_other, ...), custom_call_target="tpu_custom_call" | custom-call | flops 603979776 | bytes 4128768 | tf_op jit(solution)/shard_map/pairs/pallas_call | solution.py:321
  80.1 0.7 collective-permute-start.14
  80.8 6.9 %collective-permute-start.11 = (bf16[256,640]{1,0:T(8,128)(2,1)S(1)}, bf16[256,640]{1,0:T(8,128)(2,1)S(1)}, u32[]{:S(2)}, u32[]{:S(2)}) collective-permute-start(bf16[256,640]{1,0:T(8,128)(2,1)S(1)} %get-tuple-element.43.refs_1_), channel_id=1, source_target_pairs={{0,2},{1,3},{6,4},{7,5},{8,10},{9,11},{14,12},{15,13},{16,18},{17,... | collective-permute-start | bytes 983048 | tf_op jit(solution)/shard_map/ppermute | solution.py:47
  87.7 1.3 %collective-permute-start.12 = (bf16[256,512]{1,0:T(8,128)(2,1)S(1)}, bf16[256,512]{1,0:T(8,128)(2,1)S(1)}, u32[]{:S(2)}, u32[]{:S(2)}) collective-permute-start(bf16[256,512]{1,0:T(8,128)(2,1)S(1)} %get-tuple-element.44.refs_0_), channel_id=1, source_target_pairs={{0,2},{1,3},{6,4},{7,5},{8,10},{9,11},{14,12},{15,13},{16,18},{17,... | collective-permute-start | bytes 786440 | tf_op jit(solution)/shard_map/ppermute | solution.py:47
  89.0 0.7 collective-permute-start.13
  89.7 9.1 %collective-permute-done.12.refs_2_ = bf16[256,512]{1,0:T(8,128)(2,1)S(1)} collective-permute-done((bf16[256,512]{1,0:T(8,128)(2,1)S(1)}, bf16[256,512]{1,0:T(8,128)(2,1)S(1)}, u32[]{:S(2)}, u32[]{:S(2)}) %collective-permute-start.12) | collective-permute-done | bytes 262176 | tf_op jit(solution)/shard_map/ppermute | solution.py:47
  98.8 0.7 collective-permute-start.15
  99.5 0.0 collective-permute-done.13.refs_4_
  99.5 0.0 collective-permute-done.14.refs_5_
  99.5 0.0 collective-permute-done.11.refs_3_
  99.5 1.1 near.1
  100.7 0.7 collective-permute-start.16
  101.3 0.0 collective-permute-done.15.dx.dx_left
  101.4 0.8 far.2
  102.2 1.3 %collective-permute-start.17 = (bf16[144,512]{1,0:T(8,128)(2,1)S(1)}, bf16[144,512]{1,0:T(8,128)(2,1)S(1)}, u32[]{:S(2)}, u32[]{:S(2)}) collective-permute-start(bf16[144,512]{1,0:T(8,128)(2,1)S(1)} %get-tuple-element.53), channel_id=1, source_target_pairs={{2,0},{3,1},{4,6},{5,7},{10,8},{11,9},{12,14},{13,15},{18,16},{19,... | collective-permute-start | bytes 442376 | tf_op jit(solution)/shard_map/ppermute | solution.py:47
  103.5 1.3 %collective-permute-start.18 = (bf16[144,512]{1,0:T(8,128)(2,1)S(1)}, bf16[144,512]{1,0:T(8,128)(2,1)S(1)}, u32[]{:S(2)}, u32[]{:S(2)}) collective-permute-start(bf16[144,512]{1,0:T(8,128)(2,1)S(1)} %get-tuple-element.54), channel_id=1, source_target_pairs={{2,1},{3,0},{4,7},{5,6},{10,9},{11,8},{12,15},{13,14},{18,17},{19,... | collective-permute-start | bytes 442376 | tf_op jit(solution)/shard_map/ppermute | solution.py:47
  104.8 0.0 collective-permute-done.16.dx.dx_right
  104.8 0.9 far.3
  105.6 1.3 %collective-permute-start.19 = (bf16[144,640]{1,0:T(8,128)(2,1)S(1)}, bf16[144,640]{1,0:T(8,128)(2,1)S(1)}, u32[]{:S(2)}, u32[]{:S(2)}) collective-permute-start(bf16[144,640]{1,0:T(8,128)(2,1)S(1)} %get-tuple-element.57), channel_id=1, source_target_pairs={{2,0},{3,1},{4,6},{5,7},{10,8},{11,9},{12,14},{13,15},{18,16},{19,... | collective-permute-start | bytes 552968 | tf_op jit(solution)/shard_map/ppermute | solution.py:47
  106.9 1.3 %collective-permute-start.20 = (bf16[144,640]{1,0:T(8,128)(2,1)S(1)}, bf16[144,640]{1,0:T(8,128)(2,1)S(1)}, u32[]{:S(2)}, u32[]{:S(2)}) collective-permute-start(bf16[144,640]{1,0:T(8,128)(2,1)S(1)} %get-tuple-element.58), channel_id=1, source_target_pairs={{2,1},{3,0},{4,7},{5,6},{10,9},{11,8},{12,15},{13,14},{18,17},{19,... | collective-permute-start | bytes 552968 | tf_op jit(solution)/shard_map/ppermute | solution.py:47
  108.2 0.6 rest.1
  108.9 3.8 %collective-permute-done.17.same_left = bf16[144,512]{1,0:T(8,128)(2,1)S(1)} collective-permute-done((bf16[144,512]{1,0:T(8,128)(2,1)S(1)}, bf16[144,512]{1,0:T(8,128)(2,1)S(1)}, u32[]{:S(2)}, u32[]{:S(2)}) %collective-permute-start.17) | collective-permute-done | bytes 147488 | tf_op jit(solution)/shard_map/ppermute | solution.py:47
  112.7 6.7 %collective-permute-done.18.crossed_left = bf16[144,512]{1,0:T(8,128)(2,1)S(1)} collective-permute-done((bf16[144,512]{1,0:T(8,128)(2,1)S(1)}, bf16[144,512]{1,0:T(8,128)(2,1)S(1)}, u32[]{:S(2)}, u32[]{:S(2)}) %collective-permute-start.18) | collective-permute-done | bytes 147488 | tf_op jit(solution)/shard_map/ppermute | solution.py:47
  119.4 1.9 %collective-permute-start.22 = (bf16[144,640]{1,0:T(8,128)(2,1)S(1)}, bf16[144,640]{1,0:T(8,128)(2,1)S(1)}, u32[]{:S(2)}, u32[]{:S(2)}) collective-permute-start(bf16[144,640]{1,0:T(8,128)(2,1)S(1)} %get-tuple-element.60), channel_id=1, source_target_pairs={{0,1},{1,0},{2,3},{3,2},{4,5},{5,4},{6,7},{7,6},{8,9},{9,8},{10,11... | collective-permute-start | bytes 552968 | tf_op jit(solution)/shard_map/ppermute | solution.py:47
  121.3 2.4 %collective-permute-start.21 = (bf16[144,512]{1,0:T(8,128)(2,1)S(1)}, bf16[144,512]{1,0:T(8,128)(2,1)S(1)}, u32[]{:S(2)}, u32[]{:S(2)}) collective-permute-start(bf16[144,512]{1,0:T(8,128)(2,1)S(1)} %get-tuple-element.59), channel_id=1, source_target_pairs={{0,1},{1,0},{2,3},{3,2},{4,5},{5,4},{6,7},{7,6},{8,9},{9,8},{10,11... | collective-permute-start | bytes 442376 | tf_op jit(solution)/shard_map/ppermute | solution.py:47
  123.8 1.0 collective-permute-done.21.swap_left
  124.7 0.0 collective-permute-done.19.same_right
  124.8 2.7 %collective-permute-done.20.crossed_right = bf16[144,640]{1,0:T(8,128)(2,1)S(1)} collective-permute-done((bf16[144,640]{1,0:T(8,128)(2,1)S(1)}, bf16[144,640]{1,0:T(8,128)(2,1)S(1)}, u32[]{:S(2)}, u32[]{:S(2)}) %collective-permute-start.20) | collective-permute-done | bytes 184352 | tf_op jit(solution)/shard_map/ppermute | solution.py:47
  127.5 0.0 collective-permute-done.22.swap_right
  127.5 1.7 %finish.1 = (f32[1,144,1152]{2,1,0:T(8,128)}, f32[1,144,1152]{2,1,0:T(8,128)}) custom-call(s32[5]{0:T(128)S(1)} %stack.31.flags, bf16[144,512]{1,0:T(8,128)(2,1)S(1)} %collective-permute-done.17.same_left, bf16[144,512]{1,0:T(8,128)(2,1)S(1)} %collective-permute-done.18.crossed_left, bf16[144,640]{1,0:T(8,128)(2,1)S(1)} %collective-permute-done.19.same_right, ...), custom_call_target="tpu_custom_call" | custom-call | flops 663552 | bytes 2985984 | tf_op jit(solution)/shard_map/finish/pallas_call | solution.py:473
  (2 shorter events, 0.0 us)
Async XLA Ops:
  1.7 5.6 %collective-permute-start = (bf16[128,1152]{1,0:T(8,128)(2,1)S(1)}, bf16[128,1152]{1,0:T(8,128)(2,1)S(1)}, u32[]{:S(2)}, u32[]{:S(2)}) collective-permute-start(bf16[128,1152]{1,0:T(8,128)(2,1)S(1)} %get-tuple-element.63), channel_id=1, source_target_pairs={{0,1},{1,0},{2,3},{3,2},{4,5},{5,4},{6,7},{7,6},{8,9},{9,8},{10,11... | collective-permute-start | bytes 884744 | tf_op jit(solution)/shard_map/ppermute | solution.py:47
  8.1 16.9 %collective-permute-start.2 = (bf16[256,1152]{1,0:T(8,128)(2,1)S(1)}, bf16[256,1152]{1,0:T(8,128)(2,1)S(1)}, u32[]{:S(2)}, u32[]{:S(2)}) collective-permute-start(bf16[256,1152]{1,0:T(8,128)(2,1)S(1)} %get-tuple-element.34.z_ref), channel_id=1, source_target_pairs={{1,8},{3,10},{5,12},{7,14},{8,1},{9,16},{10,3},{11,18},{12,5},{13,... | collective-permute-start | bytes 1769480 | tf_op jit(solution)/shard_map/ppermute | solution.py:47
  8.8 32.6 %collective-permute-start.5 = (bf16[256,1152]{1,0:T(8,128)(2,1)S(1)}, bf16[256,1152]{1,0:T(8,128)(2,1)S(1)}, u32[]{:S(2)}, u32[]{:S(2)}) collective-permute-start(bf16[256,1152]{1,0:T(8,128)(2,1)S(1)} %get-tuple-element.34.z_ref), channel_id=1, source_target_pairs={{0,1009},{2,1011},{4,1013},{6,1015},{8,1017},{10,1019},{12,1021},{... | collective-permute-start | bytes 1769480 | tf_op jit(solution)/shard_map/ppermute | solution.py:47
  25.0 25.2 %collective-permute-start.3 = (bf16[256,1152]{1,0:T(8,128)(2,1)S(1)}, bf16[256,1152]{1,0:T(8,128)(2,1)S(1)}, u32[]{:S(2)}, u32[]{:S(2)}) collective-permute-start(bf16[256,1152]{1,0:T(8,128)(2,1)S(1)} %collective-permute-done.2.one), channel_id=1, source_target_pairs={{8,16},{9,1},{10,18},{11,3},{12,20},{13,5},{14,22},{15,7},{16,24},... | collective-permute-start | bytes 1769480 | tf_op jit(solution)/shard_map/ppermute | solution.py:47
  25.7 24.4 %collective-permute-start.4 = (bf16[576,256]{1,0:T(8,128)(2,1)S(1)}, bf16[576,256]{1,0:T(8,128)(2,1)S(1)}, u32[]{:S(2)}, u32[]{:S(2)}) collective-permute-start(bf16[576,256]{1,0:T(8,128)(2,1)S(1)} %slice.7), channel_id=1, source_target_pairs={{0,4},{1,5},{6,2},{7,3},{8,12},{9,13},{14,10},{15,11},{16,20},{17,... | collective-permute-start | bytes 884744 | tf_op jit(solution)/shard_map/ppermute | solution.py:47
  31.6 21.3 %collective-permute-start.1 = (bf16[256,1152]{1,0:T(8,128)(2,1)S(1)}, bf16[256,1152]{1,0:T(8,128)(2,1)S(1)}, u32[]{:S(2)}, u32[]{:S(2)}) collective-permute-start(bf16[256,1152]{1,0:T(8,128)(2,1)S(1)} %get-tuple-element.34.z_ref), channel_id=1, source_target_pairs={{0,1},{1,0},{2,3},{3,2},{4,5},{5,4},{6,7},{7,6},{8,9},{9,8},{10,11... | collective-permute-start | bytes 1769480 | tf_op jit(solution)/shard_map/ppermute | solution.py:47
  33.5 43.7 %collective-permute-start.8 = (bf16[256,1152]{1,0:T(8,128)(2,1)S(1)}, bf16[256,1152]{1,0:T(8,128)(2,1)S(1)}, u32[]{:S(2)}, u32[]{:S(2)}) collective-permute-start(bf16[256,1152]{1,0:T(8,128)(2,1)S(1)} %collective-permute-done.2.one), channel_id=1, source_target_pairs={{9,1017},{11,1019},{13,1021},{15,1023},{48,64},{50,66},{52,68},{54... | collective-permute-start | bytes 1769480 | tf_op jit(solution)/shard_map/ppermute | solution.py:47
  41.4 35.8 %collective-permute-start.7 = (bf16[256,1152]{1,0:T(8,128)(2,1)S(1)}, bf16[256,1152]{1,0:T(8,128)(2,1)S(1)}, u32[]{:S(2)}, u32[]{:S(2)}) collective-permute-start(bf16[256,1152]{1,0:T(8,128)(2,1)S(1)} %collective-permute-done.5.cross), channel_id=1, source_target_pairs={{8,0},{10,2},{12,4},{14,6},{49,57},{51,59},{53,61},{55,63},{72,64}... | collective-permute-start | bytes 1769480 | tf_op jit(solution)/shard_map/ppermute | solution.py:47
  50.9 26.4 %collective-permute-start.6 = (bf16[256,1152]{1,0:T(8,128)(2,1)S(1)}, bf16[256,1152]{1,0:T(8,128)(2,1)S(1)}, u32[]{:S(2)}, u32[]{:S(2)}) collective-permute-start(bf16[256,1152]{1,0:T(8,128)(2,1)S(1)} %choose.1), channel_id=1, source_target_pairs={{0,8},{2,10},{4,12},{6,14},{8,16},{9,1},{10,18},{11,3},{12,20},{13... | collective-permute-start | bytes 1769480 | tf_op jit(solution)/shard_map/ppermute | solution.py:47
  52.2 25.0 %collective-permute-start.9 = (bf16[576,256]{1,0:T(8,128)(2,1)S(1)}, bf16[576,256]{1,0:T(8,128)(2,1)S(1)}, u32[]{:S(2)}, u32[]{:S(2)}) collective-permute-start(bf16[576,256]{1,0:T(8,128)(2,1)S(1)} %slice.7), channel_id=1, source_target_pairs={{2,4},{3,5},{4,2},{5,3},{10,12},{11,13},{12,10},{13,11},{18,20},{1... | collective-permute-start | bytes 884744 | tf_op jit(solution)/shard_map/ppermute | solution.py:47
  52.9 24.3 %collective-permute-start.10 = (bf16[288,256]{1,0:T(8,128)(2,1)S(1)}, bf16[288,256]{1,0:T(8,128)(2,1)S(1)}, u32[]{:S(2)}, u32[]{:S(2)}) collective-permute-start(bf16[288,256]{1,0:T(8,128)(2,1)S(1)} %slice.8), channel_id=1, source_target_pairs={{0,2},{1,3},{6,4},{7,5},{8,10},{9,11},{14,12},{15,13},{16,18},{17,... | collective-permute-start | bytes 442376 | tf_op jit(solution)/shard_map/ppermute | solution.py:47
  80.1 19.4 %collective-permute-start.14 = (bf16[256,640]{1,0:T(8,128)(2,1)S(1)}, bf16[256,640]{1,0:T(8,128)(2,1)S(1)}, u32[]{:S(2)}, u32[]{:S(2)}) collective-permute-start(bf16[256,640]{1,0:T(8,128)(2,1)S(1)} %get-tuple-element.43.refs_1_), channel_id=1, source_target_pairs={{2,4},{3,5},{4,2},{5,3},{10,12},{11,13},{12,10},{13,11},{18,20},{1... | collective-permute-start | bytes 983048 | tf_op jit(solution)/shard_map/ppermute | solution.py:47
  80.8 18.7 %collective-permute-start.11 = (bf16[256,640]{1,0:T(8,128)(2,1)S(1)}, bf16[256,640]{1,0:T(8,128)(2,1)S(1)}, u32[]{:S(2)}, u32[]{:S(2)}) collective-permute-start(bf16[256,640]{1,0:T(8,128)(2,1)S(1)} %get-tuple-element.43.refs_1_), channel_id=1, source_target_pairs={{0,2},{1,3},{6,4},{7,5},{8,10},{9,11},{14,12},{15,13},{16,18},{17,... | collective-permute-start | bytes 983048 | tf_op jit(solution)/shard_map/ppermute | solution.py:47
  87.7 11.1 %collective-permute-start.12 = (bf16[256,512]{1,0:T(8,128)(2,1)S(1)}, bf16[256,512]{1,0:T(8,128)(2,1)S(1)}, u32[]{:S(2)}, u32[]{:S(2)}) collective-permute-start(bf16[256,512]{1,0:T(8,128)(2,1)S(1)} %get-tuple-element.44.refs_0_), channel_id=1, source_target_pairs={{0,2},{1,3},{6,4},{7,5},{8,10},{9,11},{14,12},{15,13},{16,18},{17,... | collective-permute-start | bytes 786440 | tf_op jit(solution)/shard_map/ppermute | solution.py:47
  89.0 10.5 %collective-permute-start.13 = (bf16[256,512]{1,0:T(8,128)(2,1)S(1)}, bf16[256,512]{1,0:T(8,128)(2,1)S(1)}, u32[]{:S(2)}, u32[]{:S(2)}) collective-permute-start(bf16[256,512]{1,0:T(8,128)(2,1)S(1)} %get-tuple-element.44.refs_0_), channel_id=1, source_target_pairs={{2,4},{3,5},{4,2},{5,3},{10,12},{11,13},{12,10},{13,11},{18,20},{1... | collective-permute-start | bytes 786440 | tf_op jit(solution)/shard_map/ppermute | solution.py:47
  98.8 2.6 %collective-permute-start.15 = (bf16[256,512]{1,0:T(8,128)(2,1)S(1)}, bf16[256,512]{1,0:T(8,128)(2,1)S(1)}, u32[]{:S(2)}, u32[]{:S(2)}) collective-permute-start(bf16[256,512]{1,0:T(8,128)(2,1)S(1)} %collective-permute-done.12.refs_2_), channel_id=1, source_target_pairs={{2,4},{3,5},{4,2},{5,3},{10,12},{11,13},{12,10},{13,11},{18,20},{1... | collective-permute-start | bytes 786440 | tf_op jit(solution)/shard_map/ppermute | solution.py:47
  100.7 4.1 %collective-permute-start.16 = (bf16[256,640]{1,0:T(8,128)(2,1)S(1)}, bf16[256,640]{1,0:T(8,128)(2,1)S(1)}, u32[]{:S(2)}, u32[]{:S(2)}) collective-permute-start(bf16[256,640]{1,0:T(8,128)(2,1)S(1)} %collective-permute-done.11.refs_3_), channel_id=1, source_target_pairs={{2,4},{3,5},{4,2},{5,3},{10,12},{11,13},{12,10},{13,11},{18,20},{1... | collective-permute-start | bytes 983048 | tf_op jit(solution)/shard_map/ppermute | solution.py:47
  102.2 10.5 %collective-permute-start.17 = (bf16[144,512]{1,0:T(8,128)(2,1)S(1)}, bf16[144,512]{1,0:T(8,128)(2,1)S(1)}, u32[]{:S(2)}, u32[]{:S(2)}) collective-permute-start(bf16[144,512]{1,0:T(8,128)(2,1)S(1)} %get-tuple-element.53), channel_id=1, source_target_pairs={{2,0},{3,1},{4,6},{5,7},{10,8},{11,9},{12,14},{13,15},{18,16},{19,... | collective-permute-start | bytes 442376 | tf_op jit(solution)/shard_map/ppermute | solution.py:47
  103.5 16.0 %collective-permute-start.18 = (bf16[144,512]{1,0:T(8,128)(2,1)S(1)}, bf16[144,512]{1,0:T(8,128)(2,1)S(1)}, u32[]{:S(2)}, u32[]{:S(2)}) collective-permute-start(bf16[144,512]{1,0:T(8,128)(2,1)S(1)} %get-tuple-element.54), channel_id=1, source_target_pairs={{2,1},{3,0},{4,7},{5,6},{10,9},{11,8},{12,15},{13,14},{18,17},{19,... | collective-permute-start | bytes 442376 | tf_op jit(solution)/shard_map/ppermute | solution.py:47
  105.6 19.1 %collective-permute-start.19 = (bf16[144,640]{1,0:T(8,128)(2,1)S(1)}, bf16[144,640]{1,0:T(8,128)(2,1)S(1)}, u32[]{:S(2)}, u32[]{:S(2)}) collective-permute-start(bf16[144,640]{1,0:T(8,128)(2,1)S(1)} %get-tuple-element.57), channel_id=1, source_target_pairs={{2,0},{3,1},{4,6},{5,7},{10,8},{11,9},{12,14},{13,15},{18,16},{19,... | collective-permute-start | bytes 552968 | tf_op jit(solution)/shard_map/ppermute | solution.py:47
  106.9 20.5 %collective-permute-start.20 = (bf16[144,640]{1,0:T(8,128)(2,1)S(1)}, bf16[144,640]{1,0:T(8,128)(2,1)S(1)}, u32[]{:S(2)}, u32[]{:S(2)}) collective-permute-start(bf16[144,640]{1,0:T(8,128)(2,1)S(1)} %get-tuple-element.58), channel_id=1, source_target_pairs={{2,1},{3,0},{4,7},{5,6},{10,9},{11,8},{12,15},{13,14},{18,17},{19,... | collective-permute-start | bytes 552968 | tf_op jit(solution)/shard_map/ppermute | solution.py:47
  119.4 8.0 %collective-permute-start.22 = (bf16[144,640]{1,0:T(8,128)(2,1)S(1)}, bf16[144,640]{1,0:T(8,128)(2,1)S(1)}, u32[]{:S(2)}, u32[]{:S(2)}) collective-permute-start(bf16[144,640]{1,0:T(8,128)(2,1)S(1)} %get-tuple-element.60), channel_id=1, source_target_pairs={{0,1},{1,0},{2,3},{3,2},{4,5},{5,4},{6,7},{7,6},{8,9},{9,8},{10,11... | collective-permute-start | bytes 552968 | tf_op jit(solution)/shard_map/ppermute | solution.py:47
  121.3 3.4 %collective-permute-start.21 = (bf16[144,512]{1,0:T(8,128)(2,1)S(1)}, bf16[144,512]{1,0:T(8,128)(2,1)S(1)}, u32[]{:S(2)}, u32[]{:S(2)}) collective-permute-start(bf16[144,512]{1,0:T(8,128)(2,1)S(1)} %get-tuple-element.59), channel_id=1, source_target_pairs={{0,1},{1,0},{2,3},{3,2},{4,5},{5,4},{6,7},{7,6},{8,9},{9,8},{10,11... | collective-permute-start | bytes 442376 | tf_op jit(solution)/shard_map/ppermute | solution.py:47

commit v8 on v7

--- a/solution.py
+++ b/solution.py
@@ -506,12 +506,12 @@
     two = send(one, second_hop)
     cross_two = send(one, second_crossing)
     near_one = send(cross, from_near)
-    two, ft_far = lax.optimization_barrier((two, ft_far))
+    two, ft_mid = lax.optimization_barrier((two, ft_mid))
     three = send(choose(flags, two, cross), third_hop)
     here = send(z, other_core)
     dxs = pairs(
         flags, scale, z, u_own, u_other, rn_own, rn_other, here, one, two, three,
-        cross, near_one, cross_two, ft_mid, ft_far, ft_end,
+        cross, near_one, cross_two, ft_far, ft_mid, ft_end,
     )
 
     ends = [send(dx, inward) for dx in dxs]

time: 130 us -> 129 us (level)
  starting transfers between devices: 73.6 us -> 67.7 us
  waiting for transfers between devices: 38.9 us -> 43.5 us
    ppermute x23, starting transfers between devices: 73.6 us -> 67.7 us  [send(): return lax.ppermute(value, NAMES, pairs_of(rule))]
    ppermute x23, waiting for transfers between devices: 38.9 us -> 43.5 us  [send(): return lax.ppermute(value, NAMES, pairs_of(rule))]
  transfers between devices with their start and end apart: 23 -> 23, of which waited for: 8 -> 7; matrix products, arithmetic and copies ran while one was open for 0% -> 0% of each run, Pallas kernels for 6% -> 6%
where the time goes in v8:
time: 129 us; the launch traced here: 128 us
  starting transfers between devices  67.7 us (52%)
  waiting for transfers between devices  43.5 us (34%)
  Pallas kernels  13.1 us (10%)
  between operations  2.32 us (2%)
    ppermute x23, starting transfers between devices, send(): return lax.ppermute(value, NAMES, pairs_of(rule))  67.7 us
    ppermute x23, waiting for transfers between devices, send(): return lax.ppermute(value, NAMES, pairs_of(rule))  43.5 us
    pallas_call x1, Pallas kernels, project_own(): pl.pallas_call(project_own_kernel, name='project_own', out_shape=(jax.Sha...  2.89 us
    pallas_call x1, Pallas kernels, pairs(): pl.pallas_call(pairs_kernel, name='pairs', out_shape=(jax.ShapeDtypeStruc...  2.82 us
  transfers between devices with their start and end apart: 23, of which 7 were waited for; matrix products, arithmetic and copies ran while one was open for 0% of the time, Pallas kernels for 6%

profile of v8, /device:TPU:113, one launch (start us, length us, event | category | flops | bytes accessed | tf_op | source)
XLA Modules:
  0.0 127.9 jit_solution(6745350791432478943)
XLA Ops:
  0.6 1.1 broadcast_select_fusion
  1.7 2.6 %collective-permute-start = (bf16[128,1152]{1,0:T(8,128)(2,1)S(1)}, bf16[128,1152]{1,0:T(8,128)(2,1)S(1)}, u32[]{:S(2)}, u32[]{:S(2)}) collective-permute-start(bf16[128,1152]{1,0:T(8,128)(2,1)S(1)} %get-tuple-element.63), channel_id=1, source_target_pairs={{0,1},{1,0},{2,3},{3,2},{4,5},{5,4},{6,7},{7,6},{8,9},{9,8},{10,11... | collective-permute-start | bytes 884744 | tf_op jit(solution)/shard_map/ppermute | solution.py:47
  4.4 0.1 stack.31.flags
  4.4 2.9 %project_own.1 = (bf16[1152,1152]{1,0:T(8,128)(2,1)S(1)}, bf16[128,1152]{1,0:T(8,128)(2,1)S(1)}, f32[128,1152]{1,0:T(8,128)S(1)}, f32[128,128]{1,0:T(8,128)S(1)}) custom-call(s32[5]{0:T(128)S(1)} %stack.31.flags, bf16[128,1152]{1,0:T(8,128)(2,1)S(1)} %get-tuple-element.62.own, bf16[1152,1152]{1,0:T(8,128)(2,1)} %wp.1, bf16[1152,1152]{1,0:T(8,128)(2,1)} %wc.1), custom_call_target="tpu_custom_call" | custom-call | flops 339738624 | bytes 3833856 | tf_op jit(solution)/shard_map/project_own/pallas_call | solution.py:158
  7.3 0.0 collective-permute-done.recv
  7.4 0.8 project_other.1
  8.1 0.7 collective-permute-start.2
  8.8 15.4 %collective-permute-start.5 = (bf16[256,1152]{1,0:T(8,128)(2,1)S(1)}, bf16[256,1152]{1,0:T(8,128)(2,1)S(1)}, u32[]{:S(2)}, u32[]{:S(2)}) collective-permute-start(bf16[256,1152]{1,0:T(8,128)(2,1)S(1)} %get-tuple-element.34.z_ref), channel_id=1, source_target_pairs={{0,1009},{2,1011},{4,1013},{6,1015},{8,1017},{10,1019},{12,1021},{... | collective-permute-start | bytes 1769480 | tf_op jit(solution)/shard_map/ppermute | solution.py:47
  24.2 0.8 turn.1.ft
  25.0 0.0 collective-permute-done.2.one
  25.0 0.7 collective-permute-start.3
  25.7 0.7 collective-permute-start.4
  26.4 1.9 %collective-permute-start.1 = (bf16[256,1152]{1,0:T(8,128)(2,1)S(1)}, bf16[256,1152]{1,0:T(8,128)(2,1)S(1)}, u32[]{:S(2)}, u32[]{:S(2)}) collective-permute-start(bf16[256,1152]{1,0:T(8,128)(2,1)S(1)} %get-tuple-element.34.z_ref), channel_id=1, source_target_pairs={{0,1},{1,0},{2,3},{3,2},{4,5},{5,4},{6,7},{7,6},{8,9},{9,8},{10,11... | collective-permute-start | bytes 1769480 | tf_op jit(solution)/shard_map/ppermute | solution.py:47
  28.3 1.3 %collective-permute-start.8 = (bf16[256,1152]{1,0:T(8,128)(2,1)S(1)}, bf16[256,1152]{1,0:T(8,128)(2,1)S(1)}, u32[]{:S(2)}, u32[]{:S(2)}) collective-permute-start(bf16[256,1152]{1,0:T(8,128)(2,1)S(1)} %collective-permute-done.2.one), channel_id=1, source_target_pairs={{9,1017},{11,1019},{13,1021},{15,1023},{48,64},{50,66},{52,68},{54... | collective-permute-start | bytes 1769480 | tf_op jit(solution)/shard_map/ppermute | solution.py:47
  29.6 11.9 %collective-permute-done.5.cross = bf16[256,1152]{1,0:T(8,128)(2,1)S(1)} collective-permute-done((bf16[256,1152]{1,0:T(8,128)(2,1)S(1)}, bf16[256,1152]{1,0:T(8,128)(2,1)S(1)}, u32[]{:S(2)}, u32[]{:S(2)}) %collective-permute-start.5) | collective-permute-done | bytes 589856 | tf_op jit(solution)/shard_map/ppermute | solution.py:47
  41.5 1.3 %collective-permute-start.7 = (bf16[256,1152]{1,0:T(8,128)(2,1)S(1)}, bf16[256,1152]{1,0:T(8,128)(2,1)S(1)}, u32[]{:S(2)}, u32[]{:S(2)}) collective-permute-start(bf16[256,1152]{1,0:T(8,128)(2,1)S(1)} %collective-permute-done.5.cross), channel_id=1, source_target_pairs={{8,0},{10,2},{12,4},{14,6},{49,57},{51,59},{53,61},{55,63},{72,64}... | collective-permute-start | bytes 1769480 | tf_op jit(solution)/shard_map/ppermute | solution.py:47
  42.8 0.0 collective-permute-done.4.refs_1_.feats_mid
  42.8 0.0 collective-permute-done.3.two
  42.8 0.7 choose.1
  43.5 4.1 %collective-permute-start.6 = (bf16[256,1152]{1,0:T(8,128)(2,1)S(1)}, bf16[256,1152]{1,0:T(8,128)(2,1)S(1)}, u32[]{:S(2)}, u32[]{:S(2)}) collective-permute-start(bf16[256,1152]{1,0:T(8,128)(2,1)S(1)} %choose.1), channel_id=1, source_target_pairs={{0,8},{2,10},{4,12},{6,14},{8,16},{9,1},{10,18},{11,3},{12,20},{13... | collective-permute-start | bytes 1769480 | tf_op jit(solution)/shard_map/ppermute | solution.py:47
  47.6 19.0 %collective-permute-start.9 = (bf16[576,256]{1,0:T(8,128)(2,1)S(1)}, bf16[576,256]{1,0:T(8,128)(2,1)S(1)}, u32[]{:S(2)}, u32[]{:S(2)}) collective-permute-start(bf16[576,256]{1,0:T(8,128)(2,1)S(1)} %slice.7), channel_id=1, source_target_pairs={{0,4},{1,5},{6,2},{7,3},{8,12},{9,13},{14,10},{15,11},{16,20},{17,... | collective-permute-start | bytes 884744 | tf_op jit(solution)/shard_map/ppermute | solution.py:47
  66.6 0.0 collective-permute-done.1.here
  66.6 1.3 %collective-permute-start.10 = (bf16[288,256]{1,0:T(8,128)(2,1)S(1)}, bf16[288,256]{1,0:T(8,128)(2,1)S(1)}, u32[]{:S(2)}, u32[]{:S(2)}) collective-permute-start(bf16[288,256]{1,0:T(8,128)(2,1)S(1)} %slice.8), channel_id=1, source_target_pairs={{0,2},{1,3},{6,4},{7,5},{8,10},{9,11},{14,12},{15,13},{16,18},{17,... | collective-permute-start | bytes 442376 | tf_op jit(solution)/shard_map/ppermute | solution.py:47
  69.2 0.1 pad_maximum_fusion.scale
  69.3 7.0 %collective-permute-done.10.refs_2_.feats_end = bf16[288,256]{1,0:T(8,128)(2,1)S(1)} collective-permute-done((bf16[288,256]{1,0:T(8,128)(2,1)S(1)}, bf16[288,256]{1,0:T(8,128)(2,1)S(1)}, u32[]{:S(2)}, u32[]{:S(2)}) %collective-permute-start.10) | collective-permute-done | bytes 147488 | tf_op jit(solution)/shard_map/ppermute | solution.py:47
  76.2 0.0 collective-permute-done.9.refs_0_.feats
  76.2 0.0 collective-permute-done.7.near_one
  76.2 0.0 collective-permute-done.8.cross_two
  76.2 0.0 collective-permute-done.6.three
  76.2 2.8 %pairs.1 = (bf16[256,512]{1,0:T(8,128)(2,1)S(1)}, bf16[256,640]{1,0:T(8,128)(2,1)S(1)}) custom-call(s32[5]{0:T(128)S(1)} %stack.31.flags, f32[2]{0:T(128)S(1)} %pad_maximum_fusion.scale, bf16[256,1152]{1,0:T(8,128)(2,1)S(1)} %get-tuple-element.34.z_ref, f32[128,1152]{1,0:T(8,128)S(1)} %get-tuple-element.35.u_own, f32[128,1152]{1,0:T(8,128)S(1)} %get-tuple-element.36.u_other, ...), custom_call_target="tpu_custom_call" | custom-call | flops 603979776 | bytes 4128768 | tf_op jit(solution)/shard_map/pairs/pallas_call | solution.py:321
  79.1 0.7 collective-permute-start.14
  79.8 5.4 %collective-permute-start.11 = (bf16[256,640]{1,0:T(8,128)(2,1)S(1)}, bf16[256,640]{1,0:T(8,128)(2,1)S(1)}, u32[]{:S(2)}, u32[]{:S(2)}) collective-permute-start(bf16[256,640]{1,0:T(8,128)(2,1)S(1)} %get-tuple-element.43.refs_1_), channel_id=1, source_target_pairs={{0,2},{1,3},{6,4},{7,5},{8,10},{9,11},{14,12},{15,13},{16,18},{17,... | collective-permute-start | bytes 983048 | tf_op jit(solution)/shard_map/ppermute | solution.py:47
  85.1 1.3 %collective-permute-start.12 = (bf16[256,512]{1,0:T(8,128)(2,1)S(1)}, bf16[256,512]{1,0:T(8,128)(2,1)S(1)}, u32[]{:S(2)}, u32[]{:S(2)}) collective-permute-start(bf16[256,512]{1,0:T(8,128)(2,1)S(1)} %get-tuple-element.44.refs_0_), channel_id=1, source_target_pairs={{0,2},{1,3},{6,4},{7,5},{8,10},{9,11},{14,12},{15,13},{16,18},{17,... | collective-permute-start | bytes 786440 | tf_op jit(solution)/shard_map/ppermute | solution.py:47
  86.4 0.7 collective-permute-start.13
  87.1 9.9 %collective-permute-done.12.refs_2_ = bf16[256,512]{1,0:T(8,128)(2,1)S(1)} collective-permute-done((bf16[256,512]{1,0:T(8,128)(2,1)S(1)}, bf16[256,512]{1,0:T(8,128)(2,1)S(1)}, u32[]{:S(2)}, u32[]{:S(2)}) %collective-permute-start.12) | collective-permute-done | bytes 262176 | tf_op jit(solution)/shard_map/ppermute | solution.py:47
  97.1 0.7 collective-permute-start.15
  97.7 0.0 collective-permute-done.13.refs_4_
  97.8 0.0 collective-permute-done.14.refs_5_
  97.8 0.0 collective-permute-done.11.refs_3_
  97.8 1.1 near.1
  98.9 0.7 collective-permute-start.16
  99.6 0.0 collective-permute-done.15.dx.dx_left
  99.6 0.8 far.2
  100.4 1.3 %collective-permute-start.17 = (bf16[144,512]{1,0:T(8,128)(2,1)S(1)}, bf16[144,512]{1,0:T(8,128)(2,1)S(1)}, u32[]{:S(2)}, u32[]{:S(2)}) collective-permute-start(bf16[144,512]{1,0:T(8,128)(2,1)S(1)} %get-tuple-element.53), channel_id=1, source_target_pairs={{2,0},{3,1},{4,6},{5,7},{10,8},{11,9},{12,14},{13,15},{18,16},{19,... | collective-permute-start | bytes 442376 | tf_op jit(solution)/shard_map/ppermute | solution.py:47
  101.7 1.3 %collective-permute-start.18 = (bf16[144,512]{1,0:T(8,128)(2,1)S(1)}, bf16[144,512]{1,0:T(8,128)(2,1)S(1)}, u32[]{:S(2)}, u32[]{:S(2)}) collective-permute-start(bf16[144,512]{1,0:T(8,128)(2,1)S(1)} %get-tuple-element.54), channel_id=1, source_target_pairs={{2,1},{3,0},{4,7},{5,6},{10,9},{11,8},{12,15},{13,14},{18,17},{19,... | collective-permute-start | bytes 442376 | tf_op jit(solution)/shard_map/ppermute | solution.py:47
  103.0 0.0 collective-permute-done.16.dx.dx_right
  103.1 0.9 far.3
  103.9 1.3 %collective-permute-start.19 = (bf16[144,640]{1,0:T(8,128)(2,1)S(1)}, bf16[144,640]{1,0:T(8,128)(2,1)S(1)}, u32[]{:S(2)}, u32[]{:S(2)}) collective-permute-start(bf16[144,640]{1,0:T(8,128)(2,1)S(1)} %get-tuple-element.57), channel_id=1, source_target_pairs={{2,0},{3,1},{4,6},{5,7},{10,8},{11,9},{12,14},{13,15},{18,16},{19,... | collective-permute-start | bytes 552968 | tf_op jit(solution)/shard_map/ppermute | solution.py:47
  105.2 1.3 %collective-permute-start.20 = (bf16[144,640]{1,0:T(8,128)(2,1)S(1)}, bf16[144,640]{1,0:T(8,128)(2,1)S(1)}, u32[]{:S(2)}, u32[]{:S(2)}) collective-permute-start(bf16[144,640]{1,0:T(8,128)(2,1)S(1)} %get-tuple-element.58), channel_id=1, source_target_pairs={{2,1},{3,0},{4,7},{5,6},{10,9},{11,8},{12,15},{13,14},{18,17},{19,... | collective-permute-start | bytes 552968 | tf_op jit(solution)/shard_map/ppermute | solution.py:47
  106.5 0.6 rest.1
  107.2 4.8 %collective-permute-done.17.same_left = bf16[144,512]{1,0:T(8,128)(2,1)S(1)} collective-permute-done((bf16[144,512]{1,0:T(8,128)(2,1)S(1)}, bf16[144,512]{1,0:T(8,128)(2,1)S(1)}, u32[]{:S(2)}, u32[]{:S(2)}) %collective-permute-start.17) | collective-permute-done | bytes 147488 | tf_op jit(solution)/shard_map/ppermute | solution.py:47
  112.0 5.6 %collective-permute-done.18.crossed_left = bf16[144,512]{1,0:T(8,128)(2,1)S(1)} collective-permute-done((bf16[144,512]{1,0:T(8,128)(2,1)S(1)}, bf16[144,512]{1,0:T(8,128)(2,1)S(1)}, u32[]{:S(2)}, u32[]{:S(2)}) %collective-permute-start.18) | collective-permute-done | bytes 147488 | tf_op jit(solution)/shard_map/ppermute | solution.py:47
  117.6 1.9 %collective-permute-start.22 = (bf16[144,640]{1,0:T(8,128)(2,1)S(1)}, bf16[144,640]{1,0:T(8,128)(2,1)S(1)}, u32[]{:S(2)}, u32[]{:S(2)}) collective-permute-start(bf16[144,640]{1,0:T(8,128)(2,1)S(1)} %get-tuple-element.60), channel_id=1, source_target_pairs={{0,1},{1,0},{2,3},{3,2},{4,5},{5,4},{6,7},{7,6},{8,9},{9,8},{10,11... | collective-permute-start | bytes 552968 | tf_op jit(solution)/shard_map/ppermute | solution.py:47
  119.5 2.4 %collective-permute-start.21 = (bf16[144,512]{1,0:T(8,128)(2,1)S(1)}, bf16[144,512]{1,0:T(8,128)(2,1)S(1)}, u32[]{:S(2)}, u32[]{:S(2)}) collective-permute-start(bf16[144,512]{1,0:T(8,128)(2,1)S(1)} %get-tuple-element.59), channel_id=1, source_target_pairs={{0,1},{1,0},{2,3},{3,2},{4,5},{5,4},{6,7},{7,6},{8,9},{9,8},{10,11... | collective-permute-start | bytes 442376 | tf_op jit(solution)/shard_map/ppermute | solution.py:47
  121.9 1.0 collective-permute-done.21.swap_left
  122.9 0.0 collective-permute-done.19.same_right
  122.9 3.3 %collective-permute-done.20.crossed_right = bf16[144,640]{1,0:T(8,128)(2,1)S(1)} collective-permute-done((bf16[144,640]{1,0:T(8,128)(2,1)S(1)}, bf16[144,640]{1,0:T(8,128)(2,1)S(1)}, u32[]{:S(2)}, u32[]{:S(2)}) %collective-permute-start.20) | collective-permute-done | bytes 184352 | tf_op jit(solution)/shard_map/ppermute | solution.py:47
  126.2 0.0 collective-permute-done.22.swap_right
  126.2 1.7 %finish.1 = (f32[1,144,1152]{2,1,0:T(8,128)}, f32[1,144,1152]{2,1,0:T(8,128)}) custom-call(s32[5]{0:T(128)S(1)} %stack.31.flags, bf16[144,512]{1,0:T(8,128)(2,1)S(1)} %collective-permute-done.17.same_left, bf16[144,512]{1,0:T(8,128)(2,1)S(1)} %collective-permute-done.18.crossed_left, bf16[144,640]{1,0:T(8,128)(2,1)S(1)} %collective-permute-done.19.same_right, ...), custom_call_target="tpu_custom_call" | custom-call | flops 663552 | bytes 2985984 | tf_op jit(solution)/shard_map/finish/pallas_call | solution.py:473
  (2 shorter events, 0.0 us)
Async XLA Ops:
  1.7 5.6 %collective-permute-start = (bf16[128,1152]{1,0:T(8,128)(2,1)S(1)}, bf16[128,1152]{1,0:T(8,128)(2,1)S(1)}, u32[]{:S(2)}, u32[]{:S(2)}) collective-permute-start(bf16[128,1152]{1,0:T(8,128)(2,1)S(1)} %get-tuple-element.63), channel_id=1, source_target_pairs={{0,1},{1,0},{2,3},{3,2},{4,5},{5,4},{6,7},{7,6},{8,9},{9,8},{10,11... | collective-permute-start | bytes 884744 | tf_op jit(solution)/shard_map/ppermute | solution.py:47
  8.1 16.9 %collective-permute-start.2 = (bf16[256,1152]{1,0:T(8,128)(2,1)S(1)}, bf16[256,1152]{1,0:T(8,128)(2,1)S(1)}, u32[]{:S(2)}, u32[]{:S(2)}) collective-permute-start(bf16[256,1152]{1,0:T(8,128)(2,1)S(1)} %get-tuple-element.34.z_ref), channel_id=1, source_target_pairs={{1,8},{3,10},{5,12},{7,14},{8,1},{9,16},{10,3},{11,18},{12,5},{13,... | collective-permute-start | bytes 1769480 | tf_op jit(solution)/shard_map/ppermute | solution.py:47
  8.8 32.7 %collective-permute-start.5 = (bf16[256,1152]{1,0:T(8,128)(2,1)S(1)}, bf16[256,1152]{1,0:T(8,128)(2,1)S(1)}, u32[]{:S(2)}, u32[]{:S(2)}) collective-permute-start(bf16[256,1152]{1,0:T(8,128)(2,1)S(1)} %get-tuple-element.34.z_ref), channel_id=1, source_target_pairs={{0,1009},{2,1011},{4,1013},{6,1015},{8,1017},{10,1019},{12,1021},{... | collective-permute-start | bytes 1769480 | tf_op jit(solution)/shard_map/ppermute | solution.py:47
  25.0 17.8 %collective-permute-start.3 = (bf16[256,1152]{1,0:T(8,128)(2,1)S(1)}, bf16[256,1152]{1,0:T(8,128)(2,1)S(1)}, u32[]{:S(2)}, u32[]{:S(2)}) collective-permute-start(bf16[256,1152]{1,0:T(8,128)(2,1)S(1)} %collective-permute-done.2.one), channel_id=1, source_target_pairs={{8,16},{9,1},{10,18},{11,3},{12,20},{13,5},{14,22},{15,7},{16,24},... | collective-permute-start | bytes 1769480 | tf_op jit(solution)/shard_map/ppermute | solution.py:47
  25.7 17.1 %collective-permute-start.4 = (bf16[576,256]{1,0:T(8,128)(2,1)S(1)}, bf16[576,256]{1,0:T(8,128)(2,1)S(1)}, u32[]{:S(2)}, u32[]{:S(2)}) collective-permute-start(bf16[576,256]{1,0:T(8,128)(2,1)S(1)} %slice.7), channel_id=1, source_target_pairs={{2,4},{3,5},{4,2},{5,3},{10,12},{11,13},{12,10},{13,11},{18,20},{1... | collective-permute-start | bytes 884744 | tf_op jit(solution)/shard_map/ppermute | solution.py:47
  26.4 40.1 %collective-permute-start.1 = (bf16[256,1152]{1,0:T(8,128)(2,1)S(1)}, bf16[256,1152]{1,0:T(8,128)(2,1)S(1)}, u32[]{:S(2)}, u32[]{:S(2)}) collective-permute-start(bf16[256,1152]{1,0:T(8,128)(2,1)S(1)} %get-tuple-element.34.z_ref), channel_id=1, source_target_pairs={{0,1},{1,0},{2,3},{3,2},{4,5},{5,4},{6,7},{7,6},{8,9},{9,8},{10,11... | collective-permute-start | bytes 1769480 | tf_op jit(solution)/shard_map/ppermute | solution.py:47
  28.3 47.9 %collective-permute-start.8 = (bf16[256,1152]{1,0:T(8,128)(2,1)S(1)}, bf16[256,1152]{1,0:T(8,128)(2,1)S(1)}, u32[]{:S(2)}, u32[]{:S(2)}) collective-permute-start(bf16[256,1152]{1,0:T(8,128)(2,1)S(1)} %collective-permute-done.2.one), channel_id=1, source_target_pairs={{9,1017},{11,1019},{13,1021},{15,1023},{48,64},{50,66},{52,68},{54... | collective-permute-start | bytes 1769480 | tf_op jit(solution)/shard_map/ppermute | solution.py:47
  41.5 34.7 %collective-permute-start.7 = (bf16[256,1152]{1,0:T(8,128)(2,1)S(1)}, bf16[256,1152]{1,0:T(8,128)(2,1)S(1)}, u32[]{:S(2)}, u32[]{:S(2)}) collective-permute-start(bf16[256,1152]{1,0:T(8,128)(2,1)S(1)} %collective-permute-done.5.cross), channel_id=1, source_target_pairs={{8,0},{10,2},{12,4},{14,6},{49,57},{51,59},{53,61},{55,63},{72,64}... | collective-permute-start | bytes 1769480 | tf_op jit(solution)/shard_map/ppermute | solution.py:47
  43.5 32.7 %collective-permute-start.6 = (bf16[256,1152]{1,0:T(8,128)(2,1)S(1)}, bf16[256,1152]{1,0:T(8,128)(2,1)S(1)}, u32[]{:S(2)}, u32[]{:S(2)}) collective-permute-start(bf16[256,1152]{1,0:T(8,128)(2,1)S(1)} %choose.1), channel_id=1, source_target_pairs={{0,8},{2,10},{4,12},{6,14},{8,16},{9,1},{10,18},{11,3},{12,20},{13... | collective-permute-start | bytes 1769480 | tf_op jit(solution)/shard_map/ppermute | solution.py:47
  47.6 28.6 %collective-permute-start.9 = (bf16[576,256]{1,0:T(8,128)(2,1)S(1)}, bf16[576,256]{1,0:T(8,128)(2,1)S(1)}, u32[]{:S(2)}, u32[]{:S(2)}) collective-permute-start(bf16[576,256]{1,0:T(8,128)(2,1)S(1)} %slice.7), channel_id=1, source_target_pairs={{0,4},{1,5},{6,2},{7,3},{8,12},{9,13},{14,10},{15,11},{16,20},{17,... | collective-permute-start | bytes 884744 | tf_op jit(solution)/shard_map/ppermute | solution.py:47
  66.6 9.6 %collective-permute-start.10 = (bf16[288,256]{1,0:T(8,128)(2,1)S(1)}, bf16[288,256]{1,0:T(8,128)(2,1)S(1)}, u32[]{:S(2)}, u32[]{:S(2)}) collective-permute-start(bf16[288,256]{1,0:T(8,128)(2,1)S(1)} %slice.8), channel_id=1, source_target_pairs={{0,2},{1,3},{6,4},{7,5},{8,10},{9,11},{14,12},{15,13},{16,18},{17,... | collective-permute-start | bytes 442376 | tf_op jit(solution)/shard_map/ppermute | solution.py:47
  79.1 18.7 %collective-permute-start.14 = (bf16[256,640]{1,0:T(8,128)(2,1)S(1)}, bf16[256,640]{1,0:T(8,128)(2,1)S(1)}, u32[]{:S(2)}, u32[]{:S(2)}) collective-permute-start(bf16[256,640]{1,0:T(8,128)(2,1)S(1)} %get-tuple-element.43.refs_1_), channel_id=1, source_target_pairs={{2,4},{3,5},{4,2},{5,3},{10,12},{11,13},{12,10},{13,11},{18,20},{1... | collective-permute-start | bytes 983048 | tf_op jit(solution)/shard_map/ppermute | solution.py:47
  79.8 18.0 %collective-permute-start.11 = (bf16[256,640]{1,0:T(8,128)(2,1)S(1)}, bf16[256,640]{1,0:T(8,128)(2,1)S(1)}, u32[]{:S(2)}, u32[]{:S(2)}) collective-permute-start(bf16[256,640]{1,0:T(8,128)(2,1)S(1)} %get-tuple-element.43.refs_1_), channel_id=1, source_target_pairs={{0,2},{1,3},{6,4},{7,5},{8,10},{9,11},{14,12},{15,13},{16,18},{17,... | collective-permute-start | bytes 983048 | tf_op jit(solution)/shard_map/ppermute | solution.py:47
  85.1 11.9 %collective-permute-start.12 = (bf16[256,512]{1,0:T(8,128)(2,1)S(1)}, bf16[256,512]{1,0:T(8,128)(2,1)S(1)}, u32[]{:S(2)}, u32[]{:S(2)}) collective-permute-start(bf16[256,512]{1,0:T(8,128)(2,1)S(1)} %get-tuple-element.44.refs_0_), channel_id=1, source_target_pairs={{0,2},{1,3},{6,4},{7,5},{8,10},{9,11},{14,12},{15,13},{16,18},{17,... | collective-permute-start | bytes 786440 | tf_op jit(solution)/shard_map/ppermute | solution.py:47
  86.4 11.3 %collective-permute-start.13 = (bf16[256,512]{1,0:T(8,128)(2,1)S(1)}, bf16[256,512]{1,0:T(8,128)(2,1)S(1)}, u32[]{:S(2)}, u32[]{:S(2)}) collective-permute-start(bf16[256,512]{1,0:T(8,128)(2,1)S(1)} %get-tuple-element.44.refs_0_), channel_id=1, source_target_pairs={{2,4},{3,5},{4,2},{5,3},{10,12},{11,13},{12,10},{13,11},{18,20},{1... | collective-permute-start | bytes 786440 | tf_op jit(solution)/shard_map/ppermute | solution.py:47
  97.1 2.6 %collective-permute-start.15 = (bf16[256,512]{1,0:T(8,128)(2,1)S(1)}, bf16[256,512]{1,0:T(8,128)(2,1)S(1)}, u32[]{:S(2)}, u32[]{:S(2)}) collective-permute-start(bf16[256,512]{1,0:T(8,128)(2,1)S(1)} %collective-permute-done.12.refs_2_), channel_id=1, source_target_pairs={{2,4},{3,5},{4,2},{5,3},{10,12},{11,13},{12,10},{13,11},{18,20},{1... | collective-permute-start | bytes 786440 | tf_op jit(solution)/shard_map/ppermute | solution.py:47
  98.9 4.1 %collective-permute-start.16 = (bf16[256,640]{1,0:T(8,128)(2,1)S(1)}, bf16[256,640]{1,0:T(8,128)(2,1)S(1)}, u32[]{:S(2)}, u32[]{:S(2)}) collective-permute-start(bf16[256,640]{1,0:T(8,128)(2,1)S(1)} %collective-permute-done.11.refs_3_), channel_id=1, source_target_pairs={{2,4},{3,5},{4,2},{5,3},{10,12},{11,13},{12,10},{13,11},{18,20},{1... | collective-permute-start | bytes 983048 | tf_op jit(solution)/shard_map/ppermute | solution.py:47
  100.4 11.6 %collective-permute-start.17 = (bf16[144,512]{1,0:T(8,128)(2,1)S(1)}, bf16[144,512]{1,0:T(8,128)(2,1)S(1)}, u32[]{:S(2)}, u32[]{:S(2)}) collective-permute-start(bf16[144,512]{1,0:T(8,128)(2,1)S(1)} %get-tuple-element.53), channel_id=1, source_target_pairs={{2,0},{3,1},{4,6},{5,7},{10,8},{11,9},{12,14},{13,15},{18,16},{19,... | collective-permute-start | bytes 442376 | tf_op jit(solution)/shard_map/ppermute | solution.py:47
  101.7 15.8 %collective-permute-start.18 = (bf16[144,512]{1,0:T(8,128)(2,1)S(1)}, bf16[144,512]{1,0:T(8,128)(2,1)S(1)}, u32[]{:S(2)}, u32[]{:S(2)}) collective-permute-start(bf16[144,512]{1,0:T(8,128)(2,1)S(1)} %get-tuple-element.54), channel_id=1, source_target_pairs={{2,1},{3,0},{4,7},{5,6},{10,9},{11,8},{12,15},{13,14},{18,17},{19,... | collective-permute-start | bytes 442376 | tf_op jit(solution)/shard_map/ppermute | solution.py:47
  103.9 19.0 %collective-permute-start.19 = (bf16[144,640]{1,0:T(8,128)(2,1)S(1)}, bf16[144,640]{1,0:T(8,128)(2,1)S(1)}, u32[]{:S(2)}, u32[]{:S(2)}) collective-permute-start(bf16[144,640]{1,0:T(8,128)(2,1)S(1)} %get-tuple-element.57), channel_id=1, source_target_pairs={{2,0},{3,1},{4,6},{5,7},{10,8},{11,9},{12,14},{13,15},{18,16},{19,... | collective-permute-start | bytes 552968 | tf_op jit(solution)/shard_map/ppermute | solution.py:47
  105.2 21.0 %collective-permute-start.20 = (bf16[144,640]{1,0:T(8,128)(2,1)S(1)}, bf16[144,640]{1,0:T(8,128)(2,1)S(1)}, u32[]{:S(2)}, u32[]{:S(2)}) collective-permute-start(bf16[144,640]{1,0:T(8,128)(2,1)S(1)} %get-tuple-element.58), channel_id=1, source_target_pairs={{2,1},{3,0},{4,7},{5,6},{10,9},{11,8},{12,15},{13,14},{18,17},{19,... | collective-permute-start | bytes 552968 | tf_op jit(solution)/shard_map/ppermute | solution.py:47
  117.6 8.6 %collective-permute-start.22 = (bf16[144,640]{1,0:T(8,128)(2,1)S(1)}, bf16[144,640]{1,0:T(8,128)(2,1)S(1)}, u32[]{:S(2)}, u32[]{:S(2)}) collective-permute-start(bf16[144,640]{1,0:T(8,128)(2,1)S(1)} %get-tuple-element.60), channel_id=1, source_target_pairs={{0,1},{1,0},{2,3},{3,2},{4,5},{5,4},{6,7},{7,6},{8,9},{9,8},{10,11... | collective-permute-start | bytes 552968 | tf_op jit(solution)/shard_map/ppermute | solution.py:47
  119.5 3.4 %collective-permute-start.21 = (bf16[144,512]{1,0:T(8,128)(2,1)S(1)}, bf16[144,512]{1,0:T(8,128)(2,1)S(1)}, u32[]{:S(2)}, u32[]{:S(2)}) collective-permute-start(bf16[144,512]{1,0:T(8,128)(2,1)S(1)} %get-tuple-element.59), channel_id=1, source_target_pairs={{0,1},{1,0},{2,3},{3,2},{4,5},{5,4},{6,7},{7,6},{8,9},{9,8},{10,11... | collective-permute-start | bytes 442376 | tf_op jit(solution)/shard_map/ppermute | solution.py:47

commit v9 on v8

--- a/solution.py
+++ b/solution.py
@@ -506,7 +506,6 @@
     two = send(one, second_hop)
     cross_two = send(one, second_crossing)
     near_one = send(cross, from_near)
-    two, ft_mid = lax.optimization_barrier((two, ft_mid))
     three = send(choose(flags, two, cross), third_hop)
     here = send(z, other_core)
     dxs = pairs(

time: 129 us -> 124 us (0.961)
  the two profiles are of different devices: /device:TPU:113 before, /device:TPU:17 now
where the time goes in v9:
time: 124 us; the launch traced here: 123 us
  starting transfers between devices  68.3 us (55%)
  waiting for transfers between devices  38 us (31%)
  Pallas kernels  13.1 us (11%)
  between operations  2.3 us (2%)
    ppermute x23, starting transfers between devices, send(): return lax.ppermute(value, NAMES, pairs_of(rule))  68.3 us
    ppermute x23, waiting for transfers between devices, send(): return lax.ppermute(value, NAMES, pairs_of(rule))  38 us
    pallas_call x1, Pallas kernels, project_own(): pl.pallas_call(project_own_kernel, name='project_own', out_shape=(jax.Sha...  2.89 us
    pallas_call x1, Pallas kernels, pairs(): pl.pallas_call(pairs_kernel, name='pairs', out_shape=(jax.ShapeDtypeStruc...  2.82 us
  transfers between devices with their start and end apart: 23, of which 7 were waited for; matrix products, arithmetic and copies ran while one was open for 0% of the time, Pallas kernels for 6%

profile of v9, /device:TPU:17, one launch (start us, length us, event | category | flops | bytes accessed | tf_op | source)
XLA Modules:
  0.0 123.1 jit_solution(17305736150788089833)
XLA Ops:
  0.6 1.1 broadcast_select_fusion
  1.7 2.6 %collective-permute-start = (bf16[128,1152]{1,0:T(8,128)(2,1)S(1)}, bf16[128,1152]{1,0:T(8,128)(2,1)S(1)}, u32[]{:S(2)}, u32[]{:S(2)}) collective-permute-start(bf16[128,1152]{1,0:T(8,128)(2,1)S(1)} %get-tuple-element.59), channel_id=1, source_target_pairs={{0,1},{1,0},{2,3},{3,2},{4,5},{5,4},{6,7},{7,6},{8,9},{9,8},{10,11... | collective-permute-start | bytes 884744 | tf_op jit(solution)/shard_map/ppermute | solution.py:47
  4.4 0.1 stack.31.flags
  4.4 2.9 %project_own.1 = (bf16[1152,1152]{1,0:T(8,128)(2,1)S(1)}, bf16[128,1152]{1,0:T(8,128)(2,1)S(1)}, f32[128,1152]{1,0:T(8,128)S(1)}, f32[128,128]{1,0:T(8,128)S(1)}) custom-call(s32[5]{0:T(128)S(1)} %stack.31.flags, bf16[128,1152]{1,0:T(8,128)(2,1)S(1)} %get-tuple-element.58.own, bf16[1152,1152]{1,0:T(8,128)(2,1)} %wp.1, bf16[1152,1152]{1,0:T(8,128)(2,1)} %wc.1), custom_call_target="tpu_custom_call" | custom-call | flops 339738624 | bytes 3833856 | tf_op jit(solution)/shard_map/project_own/pallas_call | solution.py:158
  7.3 0.0 collective-permute-done.recv
  7.4 0.8 project_other.1
  8.1 3.2 %collective-permute-start.2 = (bf16[256,1152]{1,0:T(8,128)(2,1)S(1)}, bf16[256,1152]{1,0:T(8,128)(2,1)S(1)}, u32[]{:S(2)}, u32[]{:S(2)}) collective-permute-start(bf16[256,1152]{1,0:T(8,128)(2,1)S(1)} %get-tuple-element.32.z_ref), channel_id=1, source_target_pairs={{1,8},{3,10},{5,12},{7,14},{8,1},{9,16},{10,3},{11,18},{12,5},{13,... | collective-permute-start | bytes 1769480 | tf_op jit(solution)/shard_map/ppermute | solution.py:47
  11.3 0.7 collective-permute-start.4
  12.0 0.8 turn.1.ft
  12.8 6.5 %collective-permute-done.2.one = bf16[256,1152]{1,0:T(8,128)(2,1)S(1)} collective-permute-done((bf16[256,1152]{1,0:T(8,128)(2,1)S(1)}, bf16[256,1152]{1,0:T(8,128)(2,1)S(1)}, u32[]{:S(2)}, u32[]{:S(2)}) %collective-permute-start.2) | collective-permute-done | bytes 589856 | tf_op jit(solution)/shard_map/ppermute | solution.py:47
  19.3 18.9 %collective-permute-start.3 = (bf16[256,1152]{1,0:T(8,128)(2,1)S(1)}, bf16[256,1152]{1,0:T(8,128)(2,1)S(1)}, u32[]{:S(2)}, u32[]{:S(2)}) collective-permute-start(bf16[256,1152]{1,0:T(8,128)(2,1)S(1)} %collective-permute-done.2.one), channel_id=1, source_target_pairs={{8,16},{9,1},{10,18},{11,3},{12,20},{13,5},{14,22},{15,7},{16,24},... | collective-permute-start | bytes 1769480 | tf_op jit(solution)/shard_map/ppermute | solution.py:47
  38.2 1.9 %collective-permute-start.1 = (bf16[256,1152]{1,0:T(8,128)(2,1)S(1)}, bf16[256,1152]{1,0:T(8,128)(2,1)S(1)}, u32[]{:S(2)}, u32[]{:S(2)}) collective-permute-start(bf16[256,1152]{1,0:T(8,128)(2,1)S(1)} %get-tuple-element.32.z_ref), channel_id=1, source_target_pairs={{0,1},{1,0},{2,3},{3,2},{4,5},{5,4},{6,7},{7,6},{8,9},{9,8},{10,11... | collective-permute-start | bytes 1769480 | tf_op jit(solution)/shard_map/ppermute | solution.py:47
  40.1 7.6 %collective-permute-start.7 = (bf16[256,1152]{1,0:T(8,128)(2,1)S(1)}, bf16[256,1152]{1,0:T(8,128)(2,1)S(1)}, u32[]{:S(2)}, u32[]{:S(2)}) collective-permute-start(bf16[256,1152]{1,0:T(8,128)(2,1)S(1)} %collective-permute-done.2.one), channel_id=1, source_target_pairs={{9,1017},{11,1019},{13,1021},{15,1023},{48,64},{50,66},{52,68},{54... | collective-permute-start | bytes 1769480 | tf_op jit(solution)/shard_map/ppermute | solution.py:47
  47.7 0.0 collective-permute-done.4.cross
  47.7 0.7 collective-permute-start.6
  48.4 0.0 collective-permute-done.3.two
  48.4 0.7 choose.1
  49.1 1.9 %collective-permute-start.5 = (bf16[256,1152]{1,0:T(8,128)(2,1)S(1)}, bf16[256,1152]{1,0:T(8,128)(2,1)S(1)}, u32[]{:S(2)}, u32[]{:S(2)}) collective-permute-start(bf16[256,1152]{1,0:T(8,128)(2,1)S(1)} %choose.1), channel_id=1, source_target_pairs={{0,8},{2,10},{4,12},{6,14},{8,16},{9,1},{10,18},{11,3},{12,20},{13... | collective-permute-start | bytes 1769480 | tf_op jit(solution)/shard_map/ppermute | solution.py:47
  51.1 4.0 %collective-permute-start.10 = (bf16[288,256]{1,0:T(8,128)(2,1)S(1)}, bf16[288,256]{1,0:T(8,128)(2,1)S(1)}, u32[]{:S(2)}, u32[]{:S(2)}) collective-permute-start(bf16[288,256]{1,0:T(8,128)(2,1)S(1)} %slice.8), channel_id=1, source_target_pairs={{0,2},{1,3},{6,4},{7,5},{8,10},{9,11},{14,12},{15,13},{16,18},{17,... | collective-permute-start | bytes 442376 | tf_op jit(solution)/shard_map/ppermute | solution.py:47
  55.1 0.0 collective-permute-done.1.here
  55.1 0.7 collective-permute-start.9
  55.8 2.8 %collective-permute-done.10.refs_2_.feats_end = bf16[288,256]{1,0:T(8,128)(2,1)S(1)} collective-permute-done((bf16[288,256]{1,0:T(8,128)(2,1)S(1)}, bf16[288,256]{1,0:T(8,128)(2,1)S(1)}, u32[]{:S(2)}, u32[]{:S(2)}) %collective-permute-start.10) | collective-permute-done | bytes 147488 | tf_op jit(solution)/shard_map/ppermute | solution.py:47
  58.6 6.1 %collective-permute-start.8 = (bf16[576,256]{1,0:T(8,128)(2,1)S(1)}, bf16[576,256]{1,0:T(8,128)(2,1)S(1)}, u32[]{:S(2)}, u32[]{:S(2)}) collective-permute-start(bf16[576,256]{1,0:T(8,128)(2,1)S(1)} %slice.7), channel_id=1, source_target_pairs={{0,4},{1,5},{6,2},{7,3},{8,12},{9,13},{14,10},{15,11},{16,20},{17,... | collective-permute-start | bytes 884744 | tf_op jit(solution)/shard_map/ppermute | solution.py:47
  66.1 0.1 pad_maximum_fusion.scale
  66.2 0.0 collective-permute-done.9.refs_1_.feats_mid
  66.2 4.1 %collective-permute-done.8.refs_0_.feats = bf16[576,256]{1,0:T(8,128)(2,1)S(1)} collective-permute-done((bf16[576,256]{1,0:T(8,128)(2,1)S(1)}, bf16[576,256]{1,0:T(8,128)(2,1)S(1)}, u32[]{:S(2)}, u32[]{:S(2)}) %collective-permute-start.8) | collective-permute-done | bytes 294944 | tf_op jit(solution)/shard_map/ppermute | solution.py:47
  70.3 0.0 collective-permute-done.6.near_one
  70.3 0.0 collective-permute-done.7.cross_two
  70.3 0.0 collective-permute-done.5.three
  70.3 2.8 %pairs.1 = (bf16[256,512]{1,0:T(8,128)(2,1)S(1)}, bf16[256,640]{1,0:T(8,128)(2,1)S(1)}) custom-call(s32[5]{0:T(128)S(1)} %stack.31.flags, f32[2]{0:T(128)S(1)} %pad_maximum_fusion.scale, bf16[256,1152]{1,0:T(8,128)(2,1)S(1)} %get-tuple-element.32.z_ref, f32[128,1152]{1,0:T(8,128)S(1)} %get-tuple-element.33.u_own, f32[128,1152]{1,0:T(8,128)S(1)} %get-tuple-element.34.u_other, ...), custom_call_target="tpu_custom_call" | custom-call | flops 603979776 | bytes 4128768 | tf_op jit(solution)/shard_map/pairs/pallas_call | solution.py:321
  73.1 0.7 collective-permute-start.14
  73.8 6.5 %collective-permute-start.11 = (bf16[256,640]{1,0:T(8,128)(2,1)S(1)}, bf16[256,640]{1,0:T(8,128)(2,1)S(1)}, u32[]{:S(2)}, u32[]{:S(2)}) collective-permute-start(bf16[256,640]{1,0:T(8,128)(2,1)S(1)} %get-tuple-element.39.refs_1_), channel_id=1, source_target_pairs={{0,2},{1,3},{6,4},{7,5},{8,10},{9,11},{14,12},{15,13},{16,18},{17,... | collective-permute-start | bytes 983048 | tf_op jit(solution)/shard_map/ppermute | solution.py:47
  80.3 1.3 %collective-permute-start.12 = (bf16[256,512]{1,0:T(8,128)(2,1)S(1)}, bf16[256,512]{1,0:T(8,128)(2,1)S(1)}, u32[]{:S(2)}, u32[]{:S(2)}) collective-permute-start(bf16[256,512]{1,0:T(8,128)(2,1)S(1)} %get-tuple-element.40.refs_0_), channel_id=1, source_target_pairs={{0,2},{1,3},{6,4},{7,5},{8,10},{9,11},{14,12},{15,13},{16,18},{17,... | collective-permute-start | bytes 786440 | tf_op jit(solution)/shard_map/ppermute | solution.py:47
  81.7 0.7 collective-permute-start.13
  82.3 8.6 %collective-permute-done.12.refs_2_ = bf16[256,512]{1,0:T(8,128)(2,1)S(1)} collective-permute-done((bf16[256,512]{1,0:T(8,128)(2,1)S(1)}, bf16[256,512]{1,0:T(8,128)(2,1)S(1)}, u32[]{:S(2)}, u32[]{:S(2)}) %collective-permute-start.12) | collective-permute-done | bytes 262176 | tf_op jit(solution)/shard_map/ppermute | solution.py:47
  90.9 0.7 collective-permute-start.15
  91.6 0.0 collective-permute-done.13.refs_4_
  91.6 0.0 collective-permute-done.14.refs_5_
  91.6 0.0 collective-permute-done.11.refs_3_
  91.6 1.1 near.1
  92.8 0.7 collective-permute-start.16
  93.5 0.0 collective-permute-done.15.dx.dx_left
  93.5 0.8 far.2
  94.3 1.3 %collective-permute-start.17 = (bf16[144,512]{1,0:T(8,128)(2,1)S(1)}, bf16[144,512]{1,0:T(8,128)(2,1)S(1)}, u32[]{:S(2)}, u32[]{:S(2)}) collective-permute-start(bf16[144,512]{1,0:T(8,128)(2,1)S(1)} %get-tuple-element.49), channel_id=1, source_target_pairs={{2,0},{3,1},{4,6},{5,7},{10,8},{11,9},{12,14},{13,15},{18,16},{19,... | collective-permute-start | bytes 442376 | tf_op jit(solution)/shard_map/ppermute | solution.py:47
  95.6 1.3 %collective-permute-start.18 = (bf16[144,512]{1,0:T(8,128)(2,1)S(1)}, bf16[144,512]{1,0:T(8,128)(2,1)S(1)}, u32[]{:S(2)}, u32[]{:S(2)}) collective-permute-start(bf16[144,512]{1,0:T(8,128)(2,1)S(1)} %get-tuple-element.50), channel_id=1, source_target_pairs={{2,1},{3,0},{4,7},{5,6},{10,9},{11,8},{12,15},{13,14},{18,17},{19,... | collective-permute-start | bytes 442376 | tf_op jit(solution)/shard_map/ppermute | solution.py:47
  96.9 0.0 collective-permute-done.16.dx.dx_right
  96.9 0.9 far.3
  97.8 1.3 %collective-permute-start.19 = (bf16[144,640]{1,0:T(8,128)(2,1)S(1)}, bf16[144,640]{1,0:T(8,128)(2,1)S(1)}, u32[]{:S(2)}, u32[]{:S(2)}) collective-permute-start(bf16[144,640]{1,0:T(8,128)(2,1)S(1)} %get-tuple-element.53), channel_id=1, source_target_pairs={{2,0},{3,1},{4,6},{5,7},{10,8},{11,9},{12,14},{13,15},{18,16},{19,... | collective-permute-start | bytes 552968 | tf_op jit(solution)/shard_map/ppermute | solution.py:47
  99.1 1.3 %collective-permute-start.20 = (bf16[144,640]{1,0:T(8,128)(2,1)S(1)}, bf16[144,640]{1,0:T(8,128)(2,1)S(1)}, u32[]{:S(2)}, u32[]{:S(2)}) collective-permute-start(bf16[144,640]{1,0:T(8,128)(2,1)S(1)} %get-tuple-element.54), channel_id=1, source_target_pairs={{2,1},{3,0},{4,7},{5,6},{10,9},{11,8},{12,15},{13,14},{18,17},{19,... | collective-permute-start | bytes 552968 | tf_op jit(solution)/shard_map/ppermute | solution.py:47
  100.4 0.6 rest.1
  101.0 3.8 %collective-permute-done.17.same_left = bf16[144,512]{1,0:T(8,128)(2,1)S(1)} collective-permute-done((bf16[144,512]{1,0:T(8,128)(2,1)S(1)}, bf16[144,512]{1,0:T(8,128)(2,1)S(1)}, u32[]{:S(2)}, u32[]{:S(2)}) %collective-permute-start.17) | collective-permute-done | bytes 147488 | tf_op jit(solution)/shard_map/ppermute | solution.py:47
  104.8 11.2 %collective-permute-done.18.crossed_left = bf16[144,512]{1,0:T(8,128)(2,1)S(1)} collective-permute-done((bf16[144,512]{1,0:T(8,128)(2,1)S(1)}, bf16[144,512]{1,0:T(8,128)(2,1)S(1)}, u32[]{:S(2)}, u32[]{:S(2)}) %collective-permute-start.18) | collective-permute-done | bytes 147488 | tf_op jit(solution)/shard_map/ppermute | solution.py:47
  116.0 1.9 %collective-permute-start.22 = (bf16[144,640]{1,0:T(8,128)(2,1)S(1)}, bf16[144,640]{1,0:T(8,128)(2,1)S(1)}, u32[]{:S(2)}, u32[]{:S(2)}) collective-permute-start(bf16[144,640]{1,0:T(8,128)(2,1)S(1)} %get-tuple-element.56), channel_id=1, source_target_pairs={{0,1},{1,0},{2,3},{3,2},{4,5},{5,4},{6,7},{7,6},{8,9},{9,8},{10,11... | collective-permute-start | bytes 552968 | tf_op jit(solution)/shard_map/ppermute | solution.py:47
  117.9 2.4 %collective-permute-start.21 = (bf16[144,512]{1,0:T(8,128)(2,1)S(1)}, bf16[144,512]{1,0:T(8,128)(2,1)S(1)}, u32[]{:S(2)}, u32[]{:S(2)}) collective-permute-start(bf16[144,512]{1,0:T(8,128)(2,1)S(1)} %get-tuple-element.55), channel_id=1, source_target_pairs={{0,1},{1,0},{2,3},{3,2},{4,5},{5,4},{6,7},{7,6},{8,9},{9,8},{10,11... | collective-permute-start | bytes 442376 | tf_op jit(solution)/shard_map/ppermute | solution.py:47
  120.3 1.0 collective-permute-done.21.swap_left
  121.3 0.0 collective-permute-done.19.same_right
  121.3 0.0 collective-permute-done.20.crossed_right
  121.4 0.0 collective-permute-done.22.swap_right
  121.4 1.7 %finish.1 = (f32[1,144,1152]{2,1,0:T(8,128)}, f32[1,144,1152]{2,1,0:T(8,128)}) custom-call(s32[5]{0:T(128)S(1)} %stack.31.flags, bf16[144,512]{1,0:T(8,128)(2,1)S(1)} %collective-permute-done.17.same_left, bf16[144,512]{1,0:T(8,128)(2,1)S(1)} %collective-permute-done.18.crossed_left, bf16[144,640]{1,0:T(8,128)(2,1)S(1)} %collective-permute-done.19.same_right, ...), custom_call_target="tpu_custom_call" | custom-call | flops 663552 | bytes 2985984 | tf_op jit(solution)/shard_map/finish/pallas_call | solution.py:473
  (2 shorter events, 0.0 us)
Async XLA Ops:
  1.7 5.6 %collective-permute-start = (bf16[128,1152]{1,0:T(8,128)(2,1)S(1)}, bf16[128,1152]{1,0:T(8,128)(2,1)S(1)}, u32[]{:S(2)}, u32[]{:S(2)}) collective-permute-start(bf16[128,1152]{1,0:T(8,128)(2,1)S(1)} %get-tuple-element.59), channel_id=1, source_target_pairs={{0,1},{1,0},{2,3},{3,2},{4,5},{5,4},{6,7},{7,6},{8,9},{9,8},{10,11... | collective-permute-start | bytes 884744 | tf_op jit(solution)/shard_map/ppermute | solution.py:47
  8.1 11.2 %collective-permute-start.2 = (bf16[256,1152]{1,0:T(8,128)(2,1)S(1)}, bf16[256,1152]{1,0:T(8,128)(2,1)S(1)}, u32[]{:S(2)}, u32[]{:S(2)}) collective-permute-start(bf16[256,1152]{1,0:T(8,128)(2,1)S(1)} %get-tuple-element.32.z_ref), channel_id=1, source_target_pairs={{1,8},{3,10},{5,12},{7,14},{8,1},{9,16},{10,3},{11,18},{12,5},{13,... | collective-permute-start | bytes 1769480 | tf_op jit(solution)/shard_map/ppermute | solution.py:47
  11.3 36.4 %collective-permute-start.4 = (bf16[256,1152]{1,0:T(8,128)(2,1)S(1)}, bf16[256,1152]{1,0:T(8,128)(2,1)S(1)}, u32[]{:S(2)}, u32[]{:S(2)}) collective-permute-start(bf16[256,1152]{1,0:T(8,128)(2,1)S(1)} %get-tuple-element.32.z_ref), channel_id=1, source_target_pairs={{0,1009},{2,1011},{4,1013},{6,1015},{8,1017},{10,1019},{12,1021},{... | collective-permute-start | bytes 1769480 | tf_op jit(solution)/shard_map/ppermute | solution.py:47
  19.3 29.1 %collective-permute-start.3 = (bf16[256,1152]{1,0:T(8,128)(2,1)S(1)}, bf16[256,1152]{1,0:T(8,128)(2,1)S(1)}, u32[]{:S(2)}, u32[]{:S(2)}) collective-permute-start(bf16[256,1152]{1,0:T(8,128)(2,1)S(1)} %collective-permute-done.2.one), channel_id=1, source_target_pairs={{8,16},{9,1},{10,18},{11,3},{12,20},{13,5},{14,22},{15,7},{16,24},... | collective-permute-start | bytes 1769480 | tf_op jit(solution)/shard_map/ppermute | solution.py:47
  38.2 16.9 %collective-permute-start.1 = (bf16[256,1152]{1,0:T(8,128)(2,1)S(1)}, bf16[256,1152]{1,0:T(8,128)(2,1)S(1)}, u32[]{:S(2)}, u32[]{:S(2)}) collective-permute-start(bf16[256,1152]{1,0:T(8,128)(2,1)S(1)} %get-tuple-element.32.z_ref), channel_id=1, source_target_pairs={{0,1},{1,0},{2,3},{3,2},{4,5},{5,4},{6,7},{7,6},{8,9},{9,8},{10,11... | collective-permute-start | bytes 1769480 | tf_op jit(solution)/shard_map/ppermute | solution.py:47
  40.1 30.1 %collective-permute-start.7 = (bf16[256,1152]{1,0:T(8,128)(2,1)S(1)}, bf16[256,1152]{1,0:T(8,128)(2,1)S(1)}, u32[]{:S(2)}, u32[]{:S(2)}) collective-permute-start(bf16[256,1152]{1,0:T(8,128)(2,1)S(1)} %collective-permute-done.2.one), channel_id=1, source_target_pairs={{9,1017},{11,1019},{13,1021},{15,1023},{48,64},{50,66},{52,68},{54... | collective-permute-start | bytes 1769480 | tf_op jit(solution)/shard_map/ppermute | solution.py:47
  47.7 22.6 %collective-permute-start.6 = (bf16[256,1152]{1,0:T(8,128)(2,1)S(1)}, bf16[256,1152]{1,0:T(8,128)(2,1)S(1)}, u32[]{:S(2)}, u32[]{:S(2)}) collective-permute-start(bf16[256,1152]{1,0:T(8,128)(2,1)S(1)} %collective-permute-done.4.cross), channel_id=1, source_target_pairs={{8,0},{10,2},{12,4},{14,6},{49,57},{51,59},{53,61},{55,63},{72,64}... | collective-permute-start | bytes 1769480 | tf_op jit(solution)/shard_map/ppermute | solution.py:47
  49.1 21.1 %collective-permute-start.5 = (bf16[256,1152]{1,0:T(8,128)(2,1)S(1)}, bf16[256,1152]{1,0:T(8,128)(2,1)S(1)}, u32[]{:S(2)}, u32[]{:S(2)}) collective-permute-start(bf16[256,1152]{1,0:T(8,128)(2,1)S(1)} %choose.1), channel_id=1, source_target_pairs={{0,8},{2,10},{4,12},{6,14},{8,16},{9,1},{10,18},{11,3},{12,20},{13... | collective-permute-start | bytes 1769480 | tf_op jit(solution)/shard_map/ppermute | solution.py:47
  51.1 7.6 %collective-permute-start.10 = (bf16[288,256]{1,0:T(8,128)(2,1)S(1)}, bf16[288,256]{1,0:T(8,128)(2,1)S(1)}, u32[]{:S(2)}, u32[]{:S(2)}) collective-permute-start(bf16[288,256]{1,0:T(8,128)(2,1)S(1)} %slice.8), channel_id=1, source_target_pairs={{0,2},{1,3},{6,4},{7,5},{8,10},{9,11},{14,12},{15,13},{16,18},{17,... | collective-permute-start | bytes 442376 | tf_op jit(solution)/shard_map/ppermute | solution.py:47
  55.1 11.0 %collective-permute-start.9 = (bf16[576,256]{1,0:T(8,128)(2,1)S(1)}, bf16[576,256]{1,0:T(8,128)(2,1)S(1)}, u32[]{:S(2)}, u32[]{:S(2)}) collective-permute-start(bf16[576,256]{1,0:T(8,128)(2,1)S(1)} %slice.7), channel_id=1, source_target_pairs={{2,4},{3,5},{4,2},{5,3},{10,12},{11,13},{12,10},{13,11},{18,20},{1... | collective-permute-start | bytes 884744 | tf_op jit(solution)/shard_map/ppermute | solution.py:47
  58.6 11.6 %collective-permute-start.8 = (bf16[576,256]{1,0:T(8,128)(2,1)S(1)}, bf16[576,256]{1,0:T(8,128)(2,1)S(1)}, u32[]{:S(2)}, u32[]{:S(2)}) collective-permute-start(bf16[576,256]{1,0:T(8,128)(2,1)S(1)} %slice.7), channel_id=1, source_target_pairs={{0,4},{1,5},{6,2},{7,3},{8,12},{9,13},{14,10},{15,11},{16,20},{17,... | collective-permute-start | bytes 884744 | tf_op jit(solution)/shard_map/ppermute | solution.py:47
  73.1 18.5 %collective-permute-start.14 = (bf16[256,640]{1,0:T(8,128)(2,1)S(1)}, bf16[256,640]{1,0:T(8,128)(2,1)S(1)}, u32[]{:S(2)}, u32[]{:S(2)}) collective-permute-start(bf16[256,640]{1,0:T(8,128)(2,1)S(1)} %get-tuple-element.39.refs_1_), channel_id=1, source_target_pairs={{2,4},{3,5},{4,2},{5,3},{10,12},{11,13},{12,10},{13,11},{18,20},{1... | collective-permute-start | bytes 983048 | tf_op jit(solution)/shard_map/ppermute | solution.py:47
  73.8 17.8 %collective-permute-start.11 = (bf16[256,640]{1,0:T(8,128)(2,1)S(1)}, bf16[256,640]{1,0:T(8,128)(2,1)S(1)}, u32[]{:S(2)}, u32[]{:S(2)}) collective-permute-start(bf16[256,640]{1,0:T(8,128)(2,1)S(1)} %get-tuple-element.39.refs_1_), channel_id=1, source_target_pairs={{0,2},{1,3},{6,4},{7,5},{8,10},{9,11},{14,12},{15,13},{16,18},{17,... | collective-permute-start | bytes 983048 | tf_op jit(solution)/shard_map/ppermute | solution.py:47
  80.3 10.6 %collective-permute-start.12 = (bf16[256,512]{1,0:T(8,128)(2,1)S(1)}, bf16[256,512]{1,0:T(8,128)(2,1)S(1)}, u32[]{:S(2)}, u32[]{:S(2)}) collective-permute-start(bf16[256,512]{1,0:T(8,128)(2,1)S(1)} %get-tuple-element.40.refs_0_), channel_id=1, source_target_pairs={{0,2},{1,3},{6,4},{7,5},{8,10},{9,11},{14,12},{15,13},{16,18},{17,... | collective-permute-start | bytes 786440 | tf_op jit(solution)/shard_map/ppermute | solution.py:47
  81.7 9.9 %collective-permute-start.13 = (bf16[256,512]{1,0:T(8,128)(2,1)S(1)}, bf16[256,512]{1,0:T(8,128)(2,1)S(1)}, u32[]{:S(2)}, u32[]{:S(2)}) collective-permute-start(bf16[256,512]{1,0:T(8,128)(2,1)S(1)} %get-tuple-element.40.refs_0_), channel_id=1, source_target_pairs={{2,4},{3,5},{4,2},{5,3},{10,12},{11,13},{12,10},{13,11},{18,20},{1... | collective-permute-start | bytes 786440 | tf_op jit(solution)/shard_map/ppermute | solution.py:47
  90.9 2.6 %collective-permute-start.15 = (bf16[256,512]{1,0:T(8,128)(2,1)S(1)}, bf16[256,512]{1,0:T(8,128)(2,1)S(1)}, u32[]{:S(2)}, u32[]{:S(2)}) collective-permute-start(bf16[256,512]{1,0:T(8,128)(2,1)S(1)} %collective-permute-done.12.refs_2_), channel_id=1, source_target_pairs={{2,4},{3,5},{4,2},{5,3},{10,12},{11,13},{12,10},{13,11},{18,20},{1... | collective-permute-start | bytes 786440 | tf_op jit(solution)/shard_map/ppermute | solution.py:47
  92.8 4.1 %collective-permute-start.16 = (bf16[256,640]{1,0:T(8,128)(2,1)S(1)}, bf16[256,640]{1,0:T(8,128)(2,1)S(1)}, u32[]{:S(2)}, u32[]{:S(2)}) collective-permute-start(bf16[256,640]{1,0:T(8,128)(2,1)S(1)} %collective-permute-done.11.refs_3_), channel_id=1, source_target_pairs={{2,4},{3,5},{4,2},{5,3},{10,12},{11,13},{12,10},{13,11},{18,20},{1... | collective-permute-start | bytes 983048 | tf_op jit(solution)/shard_map/ppermute | solution.py:47
  94.3 10.6 %collective-permute-start.17 = (bf16[144,512]{1,0:T(8,128)(2,1)S(1)}, bf16[144,512]{1,0:T(8,128)(2,1)S(1)}, u32[]{:S(2)}, u32[]{:S(2)}) collective-permute-start(bf16[144,512]{1,0:T(8,128)(2,1)S(1)} %get-tuple-element.49), channel_id=1, source_target_pairs={{2,0},{3,1},{4,6},{5,7},{10,8},{11,9},{12,14},{13,15},{18,16},{19,... | collective-permute-start | bytes 442376 | tf_op jit(solution)/shard_map/ppermute | solution.py:47
  95.6 20.4 %collective-permute-start.18 = (bf16[144,512]{1,0:T(8,128)(2,1)S(1)}, bf16[144,512]{1,0:T(8,128)(2,1)S(1)}, u32[]{:S(2)}, u32[]{:S(2)}) collective-permute-start(bf16[144,512]{1,0:T(8,128)(2,1)S(1)} %get-tuple-element.50), channel_id=1, source_target_pairs={{2,1},{3,0},{4,7},{5,6},{10,9},{11,8},{12,15},{13,14},{18,17},{19,... | collective-permute-start | bytes 442376 | tf_op jit(solution)/shard_map/ppermute | solution.py:47
  97.8 23.6 %collective-permute-start.19 = (bf16[144,640]{1,0:T(8,128)(2,1)S(1)}, bf16[144,640]{1,0:T(8,128)(2,1)S(1)}, u32[]{:S(2)}, u32[]{:S(2)}) collective-permute-start(bf16[144,640]{1,0:T(8,128)(2,1)S(1)} %get-tuple-element.53), channel_id=1, source_target_pairs={{2,0},{3,1},{4,6},{5,7},{10,8},{11,9},{12,14},{13,15},{18,16},{19,... | collective-permute-start | bytes 552968 | tf_op jit(solution)/shard_map/ppermute | solution.py:47
  99.1 22.3 %collective-permute-start.20 = (bf16[144,640]{1,0:T(8,128)(2,1)S(1)}, bf16[144,640]{1,0:T(8,128)(2,1)S(1)}, u32[]{:S(2)}, u32[]{:S(2)}) collective-permute-start(bf16[144,640]{1,0:T(8,128)(2,1)S(1)} %get-tuple-element.54), channel_id=1, source_target_pairs={{2,1},{3,0},{4,7},{5,6},{10,9},{11,8},{12,15},{13,14},{18,17},{19,... | collective-permute-start | bytes 552968 | tf_op jit(solution)/shard_map/ppermute | solution.py:47
  116.0 5.3 %collective-permute-start.22 = (bf16[144,640]{1,0:T(8,128)(2,1)S(1)}, bf16[144,640]{1,0:T(8,128)(2,1)S(1)}, u32[]{:S(2)}, u32[]{:S(2)}) collective-permute-start(bf16[144,640]{1,0:T(8,128)(2,1)S(1)} %get-tuple-element.56), channel_id=1, source_target_pairs={{0,1},{1,0},{2,3},{3,2},{4,5},{5,4},{6,7},{7,6},{8,9},{9,8},{10,11... | collective-permute-start | bytes 552968 | tf_op jit(solution)/shard_map/ppermute | solution.py:47
  117.9 3.4 %collective-permute-start.21 = (bf16[144,512]{1,0:T(8,128)(2,1)S(1)}, bf16[144,512]{1,0:T(8,128)(2,1)S(1)}, u32[]{:S(2)}, u32[]{:S(2)}) collective-permute-start(bf16[144,512]{1,0:T(8,128)(2,1)S(1)} %get-tuple-element.55), channel_id=1, source_target_pairs={{0,1},{1,0},{2,3},{3,2},{4,5},{5,4},{6,7},{7,6},{8,9},{9,8},{10,11... | collective-permute-start | bytes 442376 | tf_op jit(solution)/shard_map/ppermute | solution.py:47

commit v10 on v9

--- a/solution.py
+++ b/solution.py
@@ -506,6 +506,7 @@
     two = send(one, second_hop)
     cross_two = send(one, second_crossing)
     near_one = send(cross, from_near)
+    two, ft_end = lax.optimization_barrier((two, ft_end))
     three = send(choose(flags, two, cross), third_hop)
     here = send(z, other_core)
     dxs = pairs(

time: 124 us -> 130 us (1.048)
  the two profiles are of different devices: /device:TPU:17 before, /device:TPU:1 now
where the time goes in v10:
time: 130 us; the launch traced here: 127 us
  starting transfers between devices  56.9 us (44%)
  waiting for transfers between devices  53.8 us (41%)
  Pallas kernels  13.1 us (10%)
  between operations  2.29 us (2%)
    ppermute x23, starting transfers between devices, send(): return lax.ppermute(value, NAMES, pairs_of(rule))  56.9 us
    ppermute x23, waiting for transfers between devices, send(): return lax.ppermute(value, NAMES, pairs_of(rule))  53.8 us
    pallas_call x1, Pallas kernels, project_own(): pl.pallas_call(project_own_kernel, name='project_own', out_shape=(jax.Sha...  2.89 us
    pallas_call x1, Pallas kernels, pairs(): pl.pallas_call(pairs_kernel, name='pairs', out_shape=(jax.ShapeDtypeStruc...  2.81 us
  transfers between devices with their start and end apart: 23, of which 10 were waited for; matrix products, arithmetic and copies ran while one was open for 0% of the time, Pallas kernels for 6%

profile of v10, /device:TPU:1, one launch (start us, length us, event | category | flops | bytes accessed | tf_op | source)
XLA Modules:
  0.0 127.4 jit_solution(10862068724212402544)
XLA Ops:
  0.6 1.1 broadcast_select_fusion
  1.7 16.1 %collective-permute-start = (bf16[128,1152]{1,0:T(8,128)(2,1)S(1)}, bf16[128,1152]{1,0:T(8,128)(2,1)S(1)}, u32[]{:S(2)}, u32[]{:S(2)}) collective-permute-start(bf16[128,1152]{1,0:T(8,128)(2,1)S(1)} %get-tuple-element.63), channel_id=1, source_target_pairs={{0,1},{1,0},{2,3},{3,2},{4,5},{5,4},{6,7},{7,6},{8,9},{9,8},{10,11... | collective-permute-start | bytes 884744 | tf_op jit(solution)/shard_map/ppermute | solution.py:47
  17.8 0.1 stack.31.flags
  17.9 2.9 %project_own.1 = (bf16[1152,1152]{1,0:T(8,128)(2,1)S(1)}, bf16[128,1152]{1,0:T(8,128)(2,1)S(1)}, f32[128,1152]{1,0:T(8,128)S(1)}, f32[128,128]{1,0:T(8,128)S(1)}) custom-call(s32[5]{0:T(128)S(1)} %stack.31.flags, bf16[128,1152]{1,0:T(8,128)(2,1)S(1)} %get-tuple-element.62.own, bf16[1152,1152]{1,0:T(8,128)(2,1)} %wp.1, bf16[1152,1152]{1,0:T(8,128)(2,1)} %wc.1), custom_call_target="tpu_custom_call" | custom-call | flops 339738624 | bytes 3833856 | tf_op jit(solution)/shard_map/project_own/pallas_call | solution.py:158
  20.8 0.0 collective-permute-done.recv
  20.8 0.8 project_other.1
  21.6 1.9 %collective-permute-start.2 = (bf16[256,1152]{1,0:T(8,128)(2,1)S(1)}, bf16[256,1152]{1,0:T(8,128)(2,1)S(1)}, u32[]{:S(2)}, u32[]{:S(2)}) collective-permute-start(bf16[256,1152]{1,0:T(8,128)(2,1)S(1)} %get-tuple-element.34.z_ref), channel_id=1, source_target_pairs={{1,8},{3,10},{5,12},{7,14},{8,1},{9,16},{10,3},{11,18},{12,5},{13,... | collective-permute-start | bytes 1769480 | tf_op jit(solution)/shard_map/ppermute | solution.py:47
  23.5 0.7 collective-permute-start.5
  24.2 0.8 turn.1.ft
  25.0 12.0 %collective-permute-done.2.one = bf16[256,1152]{1,0:T(8,128)(2,1)S(1)} collective-permute-done((bf16[256,1152]{1,0:T(8,128)(2,1)S(1)}, bf16[256,1152]{1,0:T(8,128)(2,1)S(1)}, u32[]{:S(2)}, u32[]{:S(2)}) %collective-permute-start.2) | collective-permute-done | bytes 589856 | tf_op jit(solution)/shard_map/ppermute | solution.py:47
  37.1 1.3 %collective-permute-start.3 = (bf16[256,1152]{1,0:T(8,128)(2,1)S(1)}, bf16[256,1152]{1,0:T(8,128)(2,1)S(1)}, u32[]{:S(2)}, u32[]{:S(2)}) collective-permute-start(bf16[256,1152]{1,0:T(8,128)(2,1)S(1)} %collective-permute-done.2.one), channel_id=1, source_target_pairs={{8,16},{9,1},{10,18},{11,3},{12,20},{13,5},{14,22},{15,7},{16,24},... | collective-permute-start | bytes 1769480 | tf_op jit(solution)/shard_map/ppermute | solution.py:47
  38.4 1.9 %collective-permute-start.1 = (bf16[256,1152]{1,0:T(8,128)(2,1)S(1)}, bf16[256,1152]{1,0:T(8,128)(2,1)S(1)}, u32[]{:S(2)}, u32[]{:S(2)}) collective-permute-start(bf16[256,1152]{1,0:T(8,128)(2,1)S(1)} %get-tuple-element.34.z_ref), channel_id=1, source_target_pairs={{0,1},{1,0},{2,3},{3,2},{4,5},{5,4},{6,7},{7,6},{8,9},{9,8},{10,11... | collective-permute-start | bytes 1769480 | tf_op jit(solution)/shard_map/ppermute | solution.py:47
  40.3 1.3 %collective-permute-start.4 = (bf16[288,256]{1,0:T(8,128)(2,1)S(1)}, bf16[288,256]{1,0:T(8,128)(2,1)S(1)}, u32[]{:S(2)}, u32[]{:S(2)}) collective-permute-start(bf16[288,256]{1,0:T(8,128)(2,1)S(1)} %slice.7), channel_id=1, source_target_pairs={{0,2},{1,3},{6,4},{7,5},{8,10},{9,11},{14,12},{15,13},{16,18},{17,... | collective-permute-start | bytes 442376 | tf_op jit(solution)/shard_map/ppermute | solution.py:47
  41.6 0.7 collective-permute-start.8
  42.3 0.0 collective-permute-done.5.cross
  42.3 0.7 collective-permute-start.7
  43.0 4.4 %collective-permute-done.4.refs_2_.feats_end = bf16[288,256]{1,0:T(8,128)(2,1)S(1)} collective-permute-done((bf16[288,256]{1,0:T(8,128)(2,1)S(1)}, bf16[288,256]{1,0:T(8,128)(2,1)S(1)}, u32[]{:S(2)}, u32[]{:S(2)}) %collective-permute-start.4) | collective-permute-done | bytes 147488 | tf_op jit(solution)/shard_map/ppermute | solution.py:47
  47.4 0.3 collective-permute-done.3.two
  47.7 0.7 choose.1
  48.4 1.3 %collective-permute-start.6 = (bf16[256,1152]{1,0:T(8,128)(2,1)S(1)}, bf16[256,1152]{1,0:T(8,128)(2,1)S(1)}, u32[]{:S(2)}, u32[]{:S(2)}) collective-permute-start(bf16[256,1152]{1,0:T(8,128)(2,1)S(1)} %choose.1), channel_id=1, source_target_pairs={{0,8},{2,10},{4,12},{6,14},{8,16},{9,1},{10,18},{11,3},{12,20},{13... | collective-permute-start | bytes 1769480 | tf_op jit(solution)/shard_map/ppermute | solution.py:47
  49.7 0.7 collective-permute-start.10
  50.4 0.0 collective-permute-done.1.here
  50.4 6.5 %collective-permute-start.9 = (bf16[576,256]{1,0:T(8,128)(2,1)S(1)}, bf16[576,256]{1,0:T(8,128)(2,1)S(1)}, u32[]{:S(2)}, u32[]{:S(2)}) collective-permute-start(bf16[576,256]{1,0:T(8,128)(2,1)S(1)} %slice.8), channel_id=1, source_target_pairs={{0,4},{1,5},{6,2},{7,3},{8,12},{9,13},{14,10},{15,11},{16,20},{17,... | collective-permute-start | bytes 884744 | tf_op jit(solution)/shard_map/ppermute | solution.py:47
  58.2 0.1 pad_maximum_fusion.scale
  58.2 0.0 collective-permute-done.10.refs_1_.feats_mid
  58.2 12.0 %collective-permute-done.9.refs_0_.feats = bf16[576,256]{1,0:T(8,128)(2,1)S(1)} collective-permute-done((bf16[576,256]{1,0:T(8,128)(2,1)S(1)}, bf16[576,256]{1,0:T(8,128)(2,1)S(1)}, u32[]{:S(2)}, u32[]{:S(2)}) %collective-permute-start.9) | collective-permute-done | bytes 294944 | tf_op jit(solution)/shard_map/ppermute | solution.py:47
  70.2 0.0 collective-permute-done.7.near_one
  70.2 0.0 collective-permute-done.8.cross_two
  70.2 0.9 collective-permute-done.6.three
  71.2 2.8 %pairs.1 = (bf16[256,512]{1,0:T(8,128)(2,1)S(1)}, bf16[256,640]{1,0:T(8,128)(2,1)S(1)}) custom-call(s32[5]{0:T(128)S(1)} %stack.31.flags, f32[2]{0:T(128)S(1)} %pad_maximum_fusion.scale, bf16[256,1152]{1,0:T(8,128)(2,1)S(1)} %get-tuple-element.34.z_ref, f32[128,1152]{1,0:T(8,128)S(1)} %get-tuple-element.35.u_own, f32[128,1152]{1,0:T(8,128)S(1)} %get-tuple-element.36.u_other, ...), custom_call_target="tpu_custom_call" | custom-call | flops 603979776 | bytes 4128768 | tf_op jit(solution)/shard_map/pairs/pallas_call | solution.py:321
  74.0 0.7 collective-permute-start.14
  74.7 10.4 %collective-permute-start.11 = (bf16[256,640]{1,0:T(8,128)(2,1)S(1)}, bf16[256,640]{1,0:T(8,128)(2,1)S(1)}, u32[]{:S(2)}, u32[]{:S(2)}) collective-permute-start(bf16[256,640]{1,0:T(8,128)(2,1)S(1)} %get-tuple-element.43.refs_1_), channel_id=1, source_target_pairs={{0,2},{1,3},{6,4},{7,5},{8,10},{9,11},{14,12},{15,13},{16,18},{17,... | collective-permute-start | bytes 983048 | tf_op jit(solution)/shard_map/ppermute | solution.py:47
  85.1 1.3 %collective-permute-start.12 = (bf16[256,512]{1,0:T(8,128)(2,1)S(1)}, bf16[256,512]{1,0:T(8,128)(2,1)S(1)}, u32[]{:S(2)}, u32[]{:S(2)}) collective-permute-start(bf16[256,512]{1,0:T(8,128)(2,1)S(1)} %get-tuple-element.44.refs_0_), channel_id=1, source_target_pairs={{0,2},{1,3},{6,4},{7,5},{8,10},{9,11},{14,12},{15,13},{16,18},{17,... | collective-permute-start | bytes 786440 | tf_op jit(solution)/shard_map/ppermute | solution.py:47
  86.4 0.7 collective-permute-start.13
  87.1 9.0 %collective-permute-done.12.refs_2_ = bf16[256,512]{1,0:T(8,128)(2,1)S(1)} collective-permute-done((bf16[256,512]{1,0:T(8,128)(2,1)S(1)}, bf16[256,512]{1,0:T(8,128)(2,1)S(1)}, u32[]{:S(2)}, u32[]{:S(2)}) %collective-permute-start.12) | collective-permute-done | bytes 262176 | tf_op jit(solution)/shard_map/ppermute | solution.py:47
  96.2 0.7 collective-permute-start.15
  96.8 0.0 collective-permute-done.13.refs_4_
  96.9 0.0 collective-permute-done.14.refs_5_
  96.9 0.0 collective-permute-done.11.refs_3_
  96.9 1.2 near.1
  98.0 0.7 collective-permute-start.16
  98.7 0.0 collective-permute-done.15.dx.dx_left
  98.7 0.8 far.2
  99.6 1.3 %collective-permute-start.17 = (bf16[144,512]{1,0:T(8,128)(2,1)S(1)}, bf16[144,512]{1,0:T(8,128)(2,1)S(1)}, u32[]{:S(2)}, u32[]{:S(2)}) collective-permute-start(bf16[144,512]{1,0:T(8,128)(2,1)S(1)} %get-tuple-element.53), channel_id=1, source_target_pairs={{2,0},{3,1},{4,6},{5,7},{10,8},{11,9},{12,14},{13,15},{18,16},{19,... | collective-permute-start | bytes 442376 | tf_op jit(solution)/shard_map/ppermute | solution.py:47
  100.9 1.3 %collective-permute-start.18 = (bf16[144,512]{1,0:T(8,128)(2,1)S(1)}, bf16[144,512]{1,0:T(8,128)(2,1)S(1)}, u32[]{:S(2)}, u32[]{:S(2)}) collective-permute-start(bf16[144,512]{1,0:T(8,128)(2,1)S(1)} %get-tuple-element.54), channel_id=1, source_target_pairs={{2,1},{3,0},{4,7},{5,6},{10,9},{11,8},{12,15},{13,14},{18,17},{19,... | collective-permute-start | bytes 442376 | tf_op jit(solution)/shard_map/ppermute | solution.py:47
  102.2 0.0 collective-permute-done.16.dx.dx_right
  102.2 0.9 far.3
  103.0 1.3 %collective-permute-start.19 = (bf16[144,640]{1,0:T(8,128)(2,1)S(1)}, bf16[144,640]{1,0:T(8,128)(2,1)S(1)}, u32[]{:S(2)}, u32[]{:S(2)}) collective-permute-start(bf16[144,640]{1,0:T(8,128)(2,1)S(1)} %get-tuple-element.57), channel_id=1, source_target_pairs={{2,0},{3,1},{4,6},{5,7},{10,8},{11,9},{12,14},{13,15},{18,16},{19,... | collective-permute-start | bytes 552968 | tf_op jit(solution)/shard_map/ppermute | solution.py:47
  104.3 1.3 %collective-permute-start.20 = (bf16[144,640]{1,0:T(8,128)(2,1)S(1)}, bf16[144,640]{1,0:T(8,128)(2,1)S(1)}, u32[]{:S(2)}, u32[]{:S(2)}) collective-permute-start(bf16[144,640]{1,0:T(8,128)(2,1)S(1)} %get-tuple-element.58), channel_id=1, source_target_pairs={{2,1},{3,0},{4,7},{5,6},{10,9},{11,8},{12,15},{13,14},{18,17},{19,... | collective-permute-start | bytes 552968 | tf_op jit(solution)/shard_map/ppermute | solution.py:47
  105.6 0.6 rest.1
  106.3 4.9 %collective-permute-done.17.same_left = bf16[144,512]{1,0:T(8,128)(2,1)S(1)} collective-permute-done((bf16[144,512]{1,0:T(8,128)(2,1)S(1)}, bf16[144,512]{1,0:T(8,128)(2,1)S(1)}, u32[]{:S(2)}, u32[]{:S(2)}) %collective-permute-start.17) | collective-permute-done | bytes 147488 | tf_op jit(solution)/shard_map/ppermute | solution.py:47
  111.2 6.1 %collective-permute-done.18.crossed_left = bf16[144,512]{1,0:T(8,128)(2,1)S(1)} collective-permute-done((bf16[144,512]{1,0:T(8,128)(2,1)S(1)}, bf16[144,512]{1,0:T(8,128)(2,1)S(1)}, u32[]{:S(2)}, u32[]{:S(2)}) %collective-permute-start.18) | collective-permute-done | bytes 147488 | tf_op jit(solution)/shard_map/ppermute | solution.py:47
  117.3 1.9 %collective-permute-start.22 = (bf16[144,640]{1,0:T(8,128)(2,1)S(1)}, bf16[144,640]{1,0:T(8,128)(2,1)S(1)}, u32[]{:S(2)}, u32[]{:S(2)}) collective-permute-start(bf16[144,640]{1,0:T(8,128)(2,1)S(1)} %get-tuple-element.60), channel_id=1, source_target_pairs={{0,1},{1,0},{2,3},{3,2},{4,5},{5,4},{6,7},{7,6},{8,9},{9,8},{10,11... | collective-permute-start | bytes 552968 | tf_op jit(solution)/shard_map/ppermute | solution.py:47
  119.2 2.4 %collective-permute-start.21 = (bf16[144,512]{1,0:T(8,128)(2,1)S(1)}, bf16[144,512]{1,0:T(8,128)(2,1)S(1)}, u32[]{:S(2)}, u32[]{:S(2)}) collective-permute-start(bf16[144,512]{1,0:T(8,128)(2,1)S(1)} %get-tuple-element.59), channel_id=1, source_target_pairs={{0,1},{1,0},{2,3},{3,2},{4,5},{5,4},{6,7},{7,6},{8,9},{9,8},{10,11... | collective-permute-start | bytes 442376 | tf_op jit(solution)/shard_map/ppermute | solution.py:47
  121.6 1.0 collective-permute-done.21.swap_left
  122.6 0.0 collective-permute-done.19.same_right
  122.6 3.1 %collective-permute-done.20.crossed_right = bf16[144,640]{1,0:T(8,128)(2,1)S(1)} collective-permute-done((bf16[144,640]{1,0:T(8,128)(2,1)S(1)}, bf16[144,640]{1,0:T(8,128)(2,1)S(1)}, u32[]{:S(2)}, u32[]{:S(2)}) %collective-permute-start.20) | collective-permute-done | bytes 184352 | tf_op jit(solution)/shard_map/ppermute | solution.py:47
  125.7 0.0 collective-permute-done.22.swap_right
  125.7 1.7 %finish.1 = (f32[1,144,1152]{2,1,0:T(8,128)}, f32[1,144,1152]{2,1,0:T(8,128)}) custom-call(s32[5]{0:T(128)S(1)} %stack.31.flags, bf16[144,512]{1,0:T(8,128)(2,1)S(1)} %collective-permute-done.17.same_left, bf16[144,512]{1,0:T(8,128)(2,1)S(1)} %collective-permute-done.18.crossed_left, bf16[144,640]{1,0:T(8,128)(2,1)S(1)} %collective-permute-done.19.same_right, ...), custom_call_target="tpu_custom_call" | custom-call | flops 663552 | bytes 2985984 | tf_op jit(solution)/shard_map/finish/pallas_call | solution.py:473
  (2 shorter events, 0.0 us)
Async XLA Ops:
  1.7 19.1 %collective-permute-start = (bf16[128,1152]{1,0:T(8,128)(2,1)S(1)}, bf16[128,1152]{1,0:T(8,128)(2,1)S(1)}, u32[]{:S(2)}, u32[]{:S(2)}) collective-permute-start(bf16[128,1152]{1,0:T(8,128)(2,1)S(1)} %get-tuple-element.63), channel_id=1, source_target_pairs={{0,1},{1,0},{2,3},{3,2},{4,5},{5,4},{6,7},{7,6},{8,9},{9,8},{10,11... | collective-permute-start | bytes 884744 | tf_op jit(solution)/shard_map/ppermute | solution.py:47
  21.6 15.5 %collective-permute-start.2 = (bf16[256,1152]{1,0:T(8,128)(2,1)S(1)}, bf16[256,1152]{1,0:T(8,128)(2,1)S(1)}, u32[]{:S(2)}, u32[]{:S(2)}) collective-permute-start(bf16[256,1152]{1,0:T(8,128)(2,1)S(1)} %get-tuple-element.34.z_ref), channel_id=1, source_target_pairs={{1,8},{3,10},{5,12},{7,14},{8,1},{9,16},{10,3},{11,18},{12,5},{13,... | collective-permute-start | bytes 1769480 | tf_op jit(solution)/shard_map/ppermute | solution.py:47
  23.5 18.8 %collective-permute-start.5 = (bf16[256,1152]{1,0:T(8,128)(2,1)S(1)}, bf16[256,1152]{1,0:T(8,128)(2,1)S(1)}, u32[]{:S(2)}, u32[]{:S(2)}) collective-permute-start(bf16[256,1152]{1,0:T(8,128)(2,1)S(1)} %get-tuple-element.34.z_ref), channel_id=1, source_target_pairs={{0,1009},{2,1011},{4,1013},{6,1015},{8,1017},{10,1019},{12,1021},{... | collective-permute-start | bytes 1769480 | tf_op jit(solution)/shard_map/ppermute | solution.py:47
  37.1 10.6 %collective-permute-start.3 = (bf16[256,1152]{1,0:T(8,128)(2,1)S(1)}, bf16[256,1152]{1,0:T(8,128)(2,1)S(1)}, u32[]{:S(2)}, u32[]{:S(2)}) collective-permute-start(bf16[256,1152]{1,0:T(8,128)(2,1)S(1)} %collective-permute-done.2.one), channel_id=1, source_target_pairs={{8,16},{9,1},{10,18},{11,3},{12,20},{13,5},{14,22},{15,7},{16,24},... | collective-permute-start | bytes 1769480 | tf_op jit(solution)/shard_map/ppermute | solution.py:47
  38.4 12.0 %collective-permute-start.1 = (bf16[256,1152]{1,0:T(8,128)(2,1)S(1)}, bf16[256,1152]{1,0:T(8,128)(2,1)S(1)}, u32[]{:S(2)}, u32[]{:S(2)}) collective-permute-start(bf16[256,1152]{1,0:T(8,128)(2,1)S(1)} %get-tuple-element.34.z_ref), channel_id=1, source_target_pairs={{0,1},{1,0},{2,3},{3,2},{4,5},{5,4},{6,7},{7,6},{8,9},{9,8},{10,11... | collective-permute-start | bytes 1769480 | tf_op jit(solution)/shard_map/ppermute | solution.py:47
  40.3 7.1 %collective-permute-start.4 = (bf16[288,256]{1,0:T(8,128)(2,1)S(1)}, bf16[288,256]{1,0:T(8,128)(2,1)S(1)}, u32[]{:S(2)}, u32[]{:S(2)}) collective-permute-start(bf16[288,256]{1,0:T(8,128)(2,1)S(1)} %slice.7), channel_id=1, source_target_pairs={{0,2},{1,3},{6,4},{7,5},{8,10},{9,11},{14,12},{15,13},{16,18},{17,... | collective-permute-start | bytes 442376 | tf_op jit(solution)/shard_map/ppermute | solution.py:47
  41.6 28.6 %collective-permute-start.8 = (bf16[256,1152]{1,0:T(8,128)(2,1)S(1)}, bf16[256,1152]{1,0:T(8,128)(2,1)S(1)}, u32[]{:S(2)}, u32[]{:S(2)}) collective-permute-start(bf16[256,1152]{1,0:T(8,128)(2,1)S(1)} %collective-permute-done.2.one), channel_id=1, source_target_pairs={{9,1017},{11,1019},{13,1021},{15,1023},{48,64},{50,66},{52,68},{54... | collective-permute-start | bytes 1769480 | tf_op jit(solution)/shard_map/ppermute | solution.py:47
  42.3 27.9 %collective-permute-start.7 = (bf16[256,1152]{1,0:T(8,128)(2,1)S(1)}, bf16[256,1152]{1,0:T(8,128)(2,1)S(1)}, u32[]{:S(2)}, u32[]{:S(2)}) collective-permute-start(bf16[256,1152]{1,0:T(8,128)(2,1)S(1)} %collective-permute-done.5.cross), channel_id=1, source_target_pairs={{8,0},{10,2},{12,4},{14,6},{49,57},{51,59},{53,61},{55,63},{72,64}... | collective-permute-start | bytes 1769480 | tf_op jit(solution)/shard_map/ppermute | solution.py:47
  48.4 22.8 %collective-permute-start.6 = (bf16[256,1152]{1,0:T(8,128)(2,1)S(1)}, bf16[256,1152]{1,0:T(8,128)(2,1)S(1)}, u32[]{:S(2)}, u32[]{:S(2)}) collective-permute-start(bf16[256,1152]{1,0:T(8,128)(2,1)S(1)} %choose.1), channel_id=1, source_target_pairs={{0,8},{2,10},{4,12},{6,14},{8,16},{9,1},{10,18},{11,3},{12,20},{13... | collective-permute-start | bytes 1769480 | tf_op jit(solution)/shard_map/ppermute | solution.py:47
  49.7 8.5 %collective-permute-start.10 = (bf16[576,256]{1,0:T(8,128)(2,1)S(1)}, bf16[576,256]{1,0:T(8,128)(2,1)S(1)}, u32[]{:S(2)}, u32[]{:S(2)}) collective-permute-start(bf16[576,256]{1,0:T(8,128)(2,1)S(1)} %slice.8), channel_id=1, source_target_pairs={{2,4},{3,5},{4,2},{5,3},{10,12},{11,13},{12,10},{13,11},{18,20},{1... | collective-permute-start | bytes 884744 | tf_op jit(solution)/shard_map/ppermute | solution.py:47
  50.4 19.8 %collective-permute-start.9 = (bf16[576,256]{1,0:T(8,128)(2,1)S(1)}, bf16[576,256]{1,0:T(8,128)(2,1)S(1)}, u32[]{:S(2)}, u32[]{:S(2)}) collective-permute-start(bf16[576,256]{1,0:T(8,128)(2,1)S(1)} %slice.8), channel_id=1, source_target_pairs={{0,4},{1,5},{6,2},{7,3},{8,12},{9,13},{14,10},{15,11},{16,20},{17,... | collective-permute-start | bytes 884744 | tf_op jit(solution)/shard_map/ppermute | solution.py:47
  74.0 22.9 %collective-permute-start.14 = (bf16[256,640]{1,0:T(8,128)(2,1)S(1)}, bf16[256,640]{1,0:T(8,128)(2,1)S(1)}, u32[]{:S(2)}, u32[]{:S(2)}) collective-permute-start(bf16[256,640]{1,0:T(8,128)(2,1)S(1)} %get-tuple-element.43.refs_1_), channel_id=1, source_target_pairs={{2,4},{3,5},{4,2},{5,3},{10,12},{11,13},{12,10},{13,11},{18,20},{1... | collective-permute-start | bytes 983048 | tf_op jit(solution)/shard_map/ppermute | solution.py:47
  74.7 22.2 %collective-permute-start.11 = (bf16[256,640]{1,0:T(8,128)(2,1)S(1)}, bf16[256,640]{1,0:T(8,128)(2,1)S(1)}, u32[]{:S(2)}, u32[]{:S(2)}) collective-permute-start(bf16[256,640]{1,0:T(8,128)(2,1)S(1)} %get-tuple-element.43.refs_1_), channel_id=1, source_target_pairs={{0,2},{1,3},{6,4},{7,5},{8,10},{9,11},{14,12},{15,13},{16,18},{17,... | collective-permute-start | bytes 983048 | tf_op jit(solution)/shard_map/ppermute | solution.py:47
  85.1 11.0 %collective-permute-start.12 = (bf16[256,512]{1,0:T(8,128)(2,1)S(1)}, bf16[256,512]{1,0:T(8,128)(2,1)S(1)}, u32[]{:S(2)}, u32[]{:S(2)}) collective-permute-start(bf16[256,512]{1,0:T(8,128)(2,1)S(1)} %get-tuple-element.44.refs_0_), channel_id=1, source_target_pairs={{0,2},{1,3},{6,4},{7,5},{8,10},{9,11},{14,12},{15,13},{16,18},{17,... | collective-permute-start | bytes 786440 | tf_op jit(solution)/shard_map/ppermute | solution.py:47
  86.4 10.4 %collective-permute-start.13 = (bf16[256,512]{1,0:T(8,128)(2,1)S(1)}, bf16[256,512]{1,0:T(8,128)(2,1)S(1)}, u32[]{:S(2)}, u32[]{:S(2)}) collective-permute-start(bf16[256,512]{1,0:T(8,128)(2,1)S(1)} %get-tuple-element.44.refs_0_), channel_id=1, source_target_pairs={{2,4},{3,5},{4,2},{5,3},{10,12},{11,13},{12,10},{13,11},{18,20},{1... | collective-permute-start | bytes 786440 | tf_op jit(solution)/shard_map/ppermute | solution.py:47
  96.2 2.6 %collective-permute-start.15 = (bf16[256,512]{1,0:T(8,128)(2,1)S(1)}, bf16[256,512]{1,0:T(8,128)(2,1)S(1)}, u32[]{:S(2)}, u32[]{:S(2)}) collective-permute-start(bf16[256,512]{1,0:T(8,128)(2,1)S(1)} %collective-permute-done.12.refs_2_), channel_id=1, source_target_pairs={{2,4},{3,5},{4,2},{5,3},{10,12},{11,13},{12,10},{13,11},{18,20},{1... | collective-permute-start | bytes 786440 | tf_op jit(solution)/shard_map/ppermute | solution.py:47
  98.0 4.1 %collective-permute-start.16 = (bf16[256,640]{1,0:T(8,128)(2,1)S(1)}, bf16[256,640]{1,0:T(8,128)(2,1)S(1)}, u32[]{:S(2)}, u32[]{:S(2)}) collective-permute-start(bf16[256,640]{1,0:T(8,128)(2,1)S(1)} %collective-permute-done.11.refs_3_), channel_id=1, source_target_pairs={{2,4},{3,5},{4,2},{5,3},{10,12},{11,13},{12,10},{13,11},{18,20},{1... | collective-permute-start | bytes 983048 | tf_op jit(solution)/shard_map/ppermute | solution.py:47
  99.6 11.7 %collective-permute-start.17 = (bf16[144,512]{1,0:T(8,128)(2,1)S(1)}, bf16[144,512]{1,0:T(8,128)(2,1)S(1)}, u32[]{:S(2)}, u32[]{:S(2)}) collective-permute-start(bf16[144,512]{1,0:T(8,128)(2,1)S(1)} %get-tuple-element.53), channel_id=1, source_target_pairs={{2,0},{3,1},{4,6},{5,7},{10,8},{11,9},{12,14},{13,15},{18,16},{19,... | collective-permute-start | bytes 442376 | tf_op jit(solution)/shard_map/ppermute | solution.py:47
  100.9 16.4 %collective-permute-start.18 = (bf16[144,512]{1,0:T(8,128)(2,1)S(1)}, bf16[144,512]{1,0:T(8,128)(2,1)S(1)}, u32[]{:S(2)}, u32[]{:S(2)}) collective-permute-start(bf16[144,512]{1,0:T(8,128)(2,1)S(1)} %get-tuple-element.54), channel_id=1, source_target_pairs={{2,1},{3,0},{4,7},{5,6},{10,9},{11,8},{12,15},{13,14},{18,17},{19,... | collective-permute-start | bytes 442376 | tf_op jit(solution)/shard_map/ppermute | solution.py:47
  103.0 19.6 %collective-permute-start.19 = (bf16[144,640]{1,0:T(8,128)(2,1)S(1)}, bf16[144,640]{1,0:T(8,128)(2,1)S(1)}, u32[]{:S(2)}, u32[]{:S(2)}) collective-permute-start(bf16[144,640]{1,0:T(8,128)(2,1)S(1)} %get-tuple-element.57), channel_id=1, source_target_pairs={{2,0},{3,1},{4,6},{5,7},{10,8},{11,9},{12,14},{13,15},{18,16},{19,... | collective-permute-start | bytes 552968 | tf_op jit(solution)/shard_map/ppermute | solution.py:47
  104.3 21.4 %collective-permute-start.20 = (bf16[144,640]{1,0:T(8,128)(2,1)S(1)}, bf16[144,640]{1,0:T(8,128)(2,1)S(1)}, u32[]{:S(2)}, u32[]{:S(2)}) collective-permute-start(bf16[144,640]{1,0:T(8,128)(2,1)S(1)} %get-tuple-element.58), channel_id=1, source_target_pairs={{2,1},{3,0},{4,7},{5,6},{10,9},{11,8},{12,15},{13,14},{18,17},{19,... | collective-permute-start | bytes 552968 | tf_op jit(solution)/shard_map/ppermute | solution.py:47
  117.3 8.4 %collective-permute-start.22 = (bf16[144,640]{1,0:T(8,128)(2,1)S(1)}, bf16[144,640]{1,0:T(8,128)(2,1)S(1)}, u32[]{:S(2)}, u32[]{:S(2)}) collective-permute-start(bf16[144,640]{1,0:T(8,128)(2,1)S(1)} %get-tuple-element.60), channel_id=1, source_target_pairs={{0,1},{1,0},{2,3},{3,2},{4,5},{5,4},{6,7},{7,6},{8,9},{9,8},{10,11... | collective-permute-start | bytes 552968 | tf_op jit(solution)/shard_map/ppermute | solution.py:47
  119.2 3.4 %collective-permute-start.21 = (bf16[144,512]{1,0:T(8,128)(2,1)S(1)}, bf16[144,512]{1,0:T(8,128)(2,1)S(1)}, u32[]{:S(2)}, u32[]{:S(2)}) collective-permute-start(bf16[144,512]{1,0:T(8,128)(2,1)S(1)} %get-tuple-element.59), channel_id=1, source_target_pairs={{0,1},{1,0},{2,3},{3,2},{4,5},{5,4},{6,7},{7,6},{8,9},{9,8},{10,11... | collective-permute-start | bytes 442376 | tf_op jit(solution)/shard_map/ppermute | solution.py:47
